TPU v7x, 128 devices: a whole 4x4x4 slice. The times are simulated.
128 devices in a mesh: fsdp: 8 (over y, core), ctx: 8 (over z, x_lo), tp: 2 (over x_hi).
Axes of the slice: x: 4 (x_hi: 2, x_lo: 2; x = x_hi * 2 + x_lo), y: 4, z: 4, core: 2. Of those that a mesh axis runs over, the one named last changes fastest.
Arguments:
- x_prompt: bfloat16 [2, 8, 448, 2048], P(None, 'fsdp', 'ctx'), may hold values from -6 to 6
- x_cont: bfloat16 [2, 8, 512, 2048], P(None, 'fsdp', 'ctx'), may hold values from -6 to 6
- cot_prompt: bfloat16 [2, 8, 448, 2048], P(None, 'fsdp', 'ctx'), may hold values from -6 to 6
- cot_cont: bfloat16 [2, 8, 512, 2048], P(None, 'fsdp', 'ctx'), may hold values from -6 to 6
- ids_prompt: int32 [2, 8, 448, 8], P(None, 'fsdp', 'ctx'), may hold values from 0 to 63, all different within a row; in each aligned block of 56 rows (0 to 55, 56 to 111, ..., all dimensions but the last counted through in order) at most 7 rows name the same one
- ids_cont: int32 [2, 8, 512, 8], P(None, 'fsdp', 'ctx'), may hold values from 0 to 63, all different within a row; in each aligned block of 64 rows (0 to 63, 64 to 127, ..., all dimensions but the last counted through in order) at most 8 rows name the same one
- gates_prompt: float32 [2, 8, 448, 8], P(None, 'fsdp', 'ctx'), may hold values from 0 to 1, as said below
- gates_cont: float32 [2, 8, 512, 8], P(None, 'fsdp', 'ctx'), may hold values from 0 to 1, as said below
- norm_gain: bfloat16 [2048], P(('fsdp', 'ctx')), may hold values from 0.5 to 1.5
- query_weight: bfloat16 [2048, 4096], P(('fsdp', 'ctx'), 'tp'), may hold values from -0.125 to 0.125
- key_matrix: bfloat16 [2048, 512], P(('fsdp', 'ctx'), 'tp'), may hold values from -0.125 to 0.125
- value_matrix: bfloat16 [2048, 512], P(('fsdp', 'ctx'), 'tp'), may hold values from -0.125 to 0.125
- out_weight: bfloat16 [2048, 4096], P(('fsdp', 'ctx'), 'tp'), may hold values from -0.5 to 0.5
- query_gain: bfloat16 [128], P(('fsdp', 'ctx')), may hold values from 0.099609375 to 1.8984375
- key_gain: bfloat16 [128], P(('fsdp', 'ctx')), may hold values from 0.099609375 to 1.8984375
- moe_gain: bfloat16 [2048], P(('fsdp', 'ctx')), may hold values from 0.5 to 1.5
- expert_gate: bfloat16 [64, 2048, 768], P(('fsdp', 'ctx'), None, 'tp'), may hold values from -0.125 to 0.125
- expert_up: bfloat16 [64, 2048, 768], P(('fsdp', 'ctx'), None, 'tp'), may hold values from -0.125 to 0.125
- expert_down: bfloat16 [64, 768, 2048], P(('fsdp', 'ctx'), 'tp'), may hold values from -0.875 to 0.875
Outputs:
- output_prompt: bfloat16 [2, 8, 448, 2048], P(None, 'fsdp', 'ctx')
- output_cont: bfloat16 [2, 8, 512, 2048], P(None, 'fsdp', 'ctx')
- grad_prompt: bfloat16 [2, 8, 448, 2048], P(None, 'fsdp', 'ctx')
- grad_cont: bfloat16 [2, 8, 512, 2048], P(None, 'fsdp', 'ctx')
- grad_norm_gain: float32 [2048], P(('fsdp', 'ctx'))
- grad_query_weight: float32 [2048, 4096], P(('fsdp', 'ctx'), 'tp')
- grad_key_weight: float32 [2048, 512], P(('fsdp', 'ctx'), 'tp')
- grad_value_weight: float32 [2048, 512], P(('fsdp', 'ctx'), 'tp')
- grad_out_weight: float32 [2048, 4096], P(('fsdp', 'ctx'), 'tp')
- grad_query_gain: float32 [128], P(('fsdp', 'ctx'))
- grad_key_gain: float32 [128], P(('fsdp', 'ctx'))
- grad_moe_gain: float32 [2048], P(('fsdp', 'ctx'))
- grad_expert_gate: float32 [64, 2048, 768], P(('fsdp', 'ctx'), None, 'tp')
- grad_expert_up: float32 [64, 2048, 768], P(('fsdp', 'ctx'), None, 'tp')
- grad_expert_down: float32 [64, 768, 2048], P(('fsdp', 'ctx'), 'tp')
Inputs may be any that keep to these rules, and one draw needn't show every extreme that they name: `ids_prompt`: each row names 8 different experts; in every aligned block of 56 rows (the prompt rows of one group and micro-batch on one index of ctx) every expert is named by exactly 7 rows. `ids_cont`: each row names 8 different experts; in every aligned block of 64 rows every expert is named by exactly 8 rows. `gates_prompt`: each row's 8 gates are positive and sum to one. `gates_cont`: each row's 8 gates are positive and sum to one.
All inputs are finite; a program needn't handle non-finite values.
Results may differ from a plain program's by a relative error of at most 0.035.
Values may be sent and summed in bfloat16 or wider, within the bound.
A program may use at most 256 MiB of HBM per device.

v0:
```python
import jax
import jax.numpy as jnp
from jax import lax
from jax.sharding import PartitionSpec as P

HEAD_SIZE = 128
TOPK = 8
PROMPT = 448
CL = 128


EPS = 1e-06
THETA = 1000000.0
NEG = -1e30


def shifted(value, axis, steps):
    count = lax.axis_size(axis)
    initial, last = (max(0, -steps), min(count, count - steps))
    return lax.ppermute(value, axis, [(source, source + steps) for source in range(initial, last)])


def rounded(value_rows):
    return lax.optimization_barrier(value_rows.astype(jnp.bfloat16)).astype(jnp.float32)


def normalize(value_rows, gain_vector):
    scaling = lax.rsqrt(jnp.mean(value_rows * value_rows, axis=-1, keepdims=True) + EPS)
    return (value_rows * scaling * gain_vector, scaling)


def normalize_back(value_rows, scaling, gain_vector, upstream):
    normed_input = value_rows * scaling
    gain_grad = jnp.sum((upstream * normed_input).reshape(-1, value_rows.shape[-1]), axis=0)
    scaled = upstream * gain_vector
    inner_mean = jnp.mean(scaled * normed_input, axis=-1, keepdims=True)
    return (scaling * (scaled - normed_input * inner_mean), gain_grad)


def rotate(value_rows, cosine, sine):
    half_width = value_rows.shape[-1] // 2
    first_half = value_rows[..., :half_width]
    second_half = value_rows[..., half_width:]
    return jnp.concatenate(
        [first_half * cosine - second_half * sine, second_half * cosine + first_half * sine],
        axis=-1,
    )


def rotate_back(upstream, cosine, sine):
    half_width = upstream.shape[-1] // 2
    first_half = upstream[..., :half_width]
    second_half = upstream[..., half_width:]
    return jnp.concatenate(
        [first_half * cosine + second_half * sine, second_half * cosine - first_half * sine],
        axis=-1,
    )


def reduce_grads(grad_parts):
    return (
        lax.psum_scatter(grad_parts[0], ("fsdp", "ctx"), scatter_dimension=0, tiled=True),
        lax.psum_scatter(grad_parts[1], ("fsdp", "ctx"), scatter_dimension=0, tiled=True),
        lax.psum_scatter(grad_parts[2], ("fsdp", "ctx"), scatter_dimension=0, tiled=True),
        lax.psum_scatter(grad_parts[3], ("fsdp", "ctx"), scatter_dimension=0, tiled=True),
        lax.psum_scatter(grad_parts[4], ("fsdp", "ctx"), scatter_dimension=0, tiled=True),
        lax.psum_scatter(grad_parts[5], ("fsdp", "ctx"), scatter_dimension=0, tiled=True),
        lax.psum_scatter(grad_parts[6], ("fsdp", "ctx"), scatter_dimension=0, tiled=True),
        lax.psum_scatter(grad_parts[7], ("fsdp", "ctx"), scatter_dimension=0, tiled=True),
    )


def send_back(partial_rows):
    slot_piece = partial_rows.shape[2]
    summed = lax.psum(partial_rows, "tp").astype(jnp.bfloat16)
    summed = summed.reshape(-1, slot_piece, summed.shape[3])
    return lax.all_to_all(summed, ("fsdp", "ctx"), split_axis=0, concat_axis=0, tiled=True)


def local(
    x_prompt,
    x_cont,
    cot_prompt,
    cot_cont,
    ids_prompt,
    ids_cont,
    gates_prompt,
    gates_cont,
    norm_gain,
    query_weight,
    key_matrix,
    value_matrix,
    out_weight,
    query_gain,
    key_gain,
    moe_gain,
    expert_gate,
    expert_up,
    expert_down,
):
    micro_count = x_prompt.shape[0]
    groups = x_prompt.shape[1]
    prompt_rows = x_prompt.shape[2]
    cont_rows = x_cont.shape[2]
    row_count = prompt_rows + cont_rows
    width = x_prompt.shape[3]
    ctx_index = lax.axis_index("ctx")
    local_experts = expert_gate.shape[0]
    experts = lax.axis_size(("fsdp", "ctx")) * local_experts
    pair_count = groups * row_count * TOPK
    slot_count = pair_count // experts
    token_total = groups * row_count
    inv_scale = HEAD_SIZE ** (-0.5)
    offsets = jnp.arange(row_count, dtype=jnp.int32)
    is_prompt = offsets < prompt_rows
    prompt_pos = ctx_index * prompt_rows + offsets
    cont_pos = ctx_index * cont_rows + offsets - prompt_rows
    rot_place = jnp.where(is_prompt, prompt_pos, PROMPT + cont_pos % CL).astype(jnp.float32)
    steps_freq = jnp.arange(HEAD_SIZE // 2, dtype=jnp.float32) * (2.0 / HEAD_SIZE)
    angles = rot_place[:, None] * jnp.power(THETA, -steps_freq)[None, :]
    cosine = jnp.cos(angles)[:, None, :]
    sine = jnp.sin(angles)[:, None, :]
    key_index = jnp.arange(PROMPT + 2 * cont_rows, dtype=jnp.int32)
    key_prompt = key_index < PROMPT
    key_cont = (ctx_index - 1) * cont_rows + key_index - PROMPT
    not_prompt = jnp.logical_not(is_prompt)[:, None]
    visible = jnp.where(
        key_prompt[None, :],
        jnp.logical_or(not_prompt, key_index[None, :] <= prompt_pos[:, None]),
        jnp.logical_and(
            not_prompt,
            jnp.logical_and(
                key_cont[None, :] // CL == cont_pos[:, None] // CL,
                key_cont[None, :] <= cont_pos[:, None],
            ),
        ),
    )
    gate_total = jnp.zeros(expert_gate.shape, jnp.float32)
    up_total = jnp.zeros(expert_up.shape, jnp.float32)
    down_total = jnp.zeros(expert_down.shape, jnp.float32)
    grad_total = None
    out_first = []
    out_second = []
    grad_first = []
    grad_second = []
    for step_index in range(micro_count):
        gathered = (
            lax.all_gather(norm_gain, ("fsdp", "ctx"), axis=0, tiled=True),
            lax.all_gather(query_weight, ("fsdp", "ctx"), axis=0, tiled=True),
            lax.all_gather(key_matrix, ("fsdp", "ctx"), axis=0, tiled=True),
            lax.all_gather(value_matrix, ("fsdp", "ctx"), axis=0, tiled=True),
            lax.all_gather(out_weight, ("fsdp", "ctx"), axis=0, tiled=True),
            lax.all_gather(query_gain, ("fsdp", "ctx"), axis=0, tiled=True),
            lax.all_gather(key_gain, ("fsdp", "ctx"), axis=0, tiled=True),
            lax.all_gather(moe_gain, ("fsdp", "ctx"), axis=0, tiled=True),
        )
        gain_in = gathered[0].astype(jnp.float32)
        gain_query = gathered[5].astype(jnp.float32)
        gain_key = gathered[6].astype(jnp.float32)
        gain_moe = gathered[7].astype(jnp.float32)
        head_count = gathered[1].shape[1] // HEAD_SIZE
        kv_heads = gathered[2].shape[1] // HEAD_SIZE
        repeat_factor = head_count // kv_heads
        tokens = jnp.concatenate([x_prompt[step_index], x_cont[step_index]], axis=1).astype(
            jnp.float32
        )
        normed_input, scale_in = normalize(tokens, gain_in)
        normed_low = normed_input.astype(jnp.bfloat16)
        query_rows = jnp.einsum(
            "grd,dj->grj", normed_low, gathered[1], preferred_element_type=jnp.float32
        ).reshape(groups, row_count, head_count, HEAD_SIZE)
        keys_unnormed = jnp.einsum(
            "grd,dj->grj", normed_low, gathered[2], preferred_element_type=jnp.float32
        ).reshape(groups, row_count, kv_heads, HEAD_SIZE)
        values_low = (
            jnp.einsum("grd,dj->grj", normed_low, gathered[3], preferred_element_type=jnp.float32)
            .astype(jnp.bfloat16)
            .reshape(groups, row_count, kv_heads, HEAD_SIZE)
        )
        query_normed, query_scale = normalize(query_rows, gain_query)
        query_low = rotate(query_normed, cosine, sine).astype(jnp.bfloat16)
        key_normed, key_scale = normalize(keys_unnormed, gain_key)
        key_low = rotate(key_normed, cosine, sine).astype(jnp.bfloat16)
        prompt_pieces = (
            lax.all_gather(key_low[:, :prompt_rows], "ctx", axis=1, tiled=True),
            lax.all_gather(values_low[:, :prompt_rows], "ctx", axis=1, tiled=True),
        )
        earlier_pieces = shifted((key_low[:, prompt_rows:], values_low[:, prompt_rows:]), "ctx", 1)
        keys_all = jnp.concatenate(
            [prompt_pieces[0], earlier_pieces[0], key_low[:, prompt_rows:]], axis=1
        )
        values_all = jnp.concatenate(
            [prompt_pieces[1], earlier_pieces[1], values_low[:, prompt_rows:]], axis=1
        )
        grouped_heads = query_low.reshape(groups, row_count, kv_heads, repeat_factor, HEAD_SIZE)
        scores = (
            jnp.einsum(
                "grhed,gkhd->gherk", grouped_heads, keys_all, preferred_element_type=jnp.float32
            )
            * inv_scale
        )
        scores = jnp.where(visible, scores, NEG)
        row_peak = jnp.max(scores, axis=-1, keepdims=True)
        exp_scores = jnp.exp(scores - row_peak)
        sum_exp = jnp.sum(exp_scores, axis=-1, keepdims=True)
        log_total = row_peak + jnp.log(sum_exp)
        probs_low = (exp_scores / sum_exp).astype(jnp.bfloat16)
        attended = jnp.einsum(
            "gherk,gkhd->grhed", probs_low, values_all, preferred_element_type=jnp.float32
        )
        attended = attended.astype(jnp.bfloat16).reshape(groups, row_count, head_count * HEAD_SIZE)
        branch_part = jnp.einsum(
            "grj,dj->grd", attended, gathered[4], preferred_element_type=jnp.float32
        )
        branch = lax.psum(branch_part, "tp")
        middle = tokens + branch
        moe_normed, moe_scale = normalize(middle, gain_moe)
        moe_low = moe_normed.astype(jnp.bfloat16).reshape(token_total, width)
        routing = jnp.concatenate([ids_prompt[step_index], ids_cont[step_index]], axis=1).reshape(
            -1
        )
        mixing = jnp.concatenate(
            [gates_prompt[step_index], gates_cont[step_index]], axis=1
        ).reshape(token_total, TOPK)
        sort_order = jnp.argsort(routing, stable=True)
        inverse = jnp.argsort(sort_order)
        owner_rows = sort_order // TOPK
        send_rows = moe_low[owner_rows].reshape(experts, slot_count, width)

        def combine(returned_rows, weights):
            per_pair = (
                returned_rows.reshape(pair_count, -1)[inverse]
                .reshape(token_total, TOPK, -1)
                .astype(jnp.float32)
            )
            mixed = jnp.sum(per_pair * weights[:, :, None], axis=1)
            return mixed

        received = lax.all_to_all(
            send_rows, ("fsdp", "ctx"), split_axis=0, concat_axis=0, tiled=True
        )
        slot_piece = received.shape[1]
        blocks = received.reshape(-1, local_experts, slot_piece, width)
        gate_pre = jnp.einsum(
            "nesd,edf->nesf", blocks, expert_gate, preferred_element_type=jnp.float32
        )
        up_pre = jnp.einsum("nesd,edf->nesf", blocks, expert_up, preferred_element_type=jnp.float32)
        hidden = (gate_pre * jax.nn.sigmoid(gate_pre) * up_pre).astype(jnp.bfloat16)
        out_part = jnp.einsum(
            "nesf,efd->nesd", hidden, expert_down, preferred_element_type=jnp.float32
        )
        returned = send_back(out_part)
        hidden_width = gate_pre.shape[-1]
        returned, received, gate_keep, up_keep = (
            returned,
            received,
            gate_pre.reshape(-1, slot_piece, hidden_width),
            up_pre.reshape(-1, slot_piece, hidden_width),
        )
        moe_out = combine(returned, mixing).reshape(groups, row_count, width)
        result = (middle + moe_out).astype(jnp.bfloat16)
        out_first.append(result[:, :prompt_rows])
        out_second.append(result[:, prompt_rows:])
        upstream = jnp.concatenate([cot_prompt[step_index], cot_cont[step_index]], axis=1).astype(
            jnp.float32
        )
        pair_grad = (
            (upstream.reshape(token_total, 1, width) * mixing[:, :, None])
            .astype(jnp.bfloat16)
            .reshape(pair_count, width)
        )
        grad_send = pair_grad[sort_order].reshape(experts, slot_count, width)
        grad_received = lax.all_to_all(
            grad_send, ("fsdp", "ctx"), split_axis=0, concat_axis=0, tiled=True
        )
        hidden_width = gate_keep.shape[-1]
        grad_blocks = grad_received.reshape(-1, local_experts, slot_count, width)
        row_blocks = received.reshape(-1, local_experts, slot_count, width)
        gate_blocks = gate_keep.reshape(-1, local_experts, slot_count, hidden_width)
        up_blocks = up_keep.reshape(-1, local_experts, slot_count, hidden_width)
        sigmoid_gate = jax.nn.sigmoid(gate_blocks)
        activated = gate_blocks * sigmoid_gate
        hidden = (activated * up_blocks).astype(jnp.bfloat16)
        hidden_grad = jnp.einsum(
            "nesd,efd->nesf", grad_blocks, expert_down, preferred_element_type=jnp.float32
        )
        down_total = down_total + jnp.einsum(
            "nesf,nesd->efd", hidden, grad_blocks, preferred_element_type=jnp.float32
        )
        up_grad_low = (hidden_grad * activated).astype(jnp.bfloat16)
        gate_grad_low = (
            hidden_grad * up_blocks * sigmoid_gate * (1.0 + gate_blocks * (1.0 - sigmoid_gate))
        ).astype(jnp.bfloat16)
        gate_total = gate_total + jnp.einsum(
            "nesd,nesf->edf", row_blocks, gate_grad_low, preferred_element_type=jnp.float32
        )
        up_total = up_total + jnp.einsum(
            "nesd,nesf->edf", row_blocks, up_grad_low, preferred_element_type=jnp.float32
        )
        row_grad_part = jnp.einsum(
            "nesf,edf->nesd", gate_grad_low, expert_gate, preferred_element_type=jnp.float32
        ) + jnp.einsum("nesf,edf->nesd", up_grad_low, expert_up, preferred_element_type=jnp.float32)
        grad_back = send_back(row_grad_part)
        unit_weights = jnp.ones((token_total, TOPK), jnp.float32)
        moe_in_grad = combine(grad_back, unit_weights)
        middle_from, moe_gain_grad = normalize_back(
            middle, moe_scale, gain_moe, moe_in_grad.reshape(groups, row_count, width)
        )
        middle_grad = upstream + middle_from
        branch_grad = middle_grad.astype(jnp.bfloat16)
        out_w_grad = jnp.einsum(
            "grd,grj->dj", branch_grad, attended, preferred_element_type=jnp.float32
        )
        attended_grad = jnp.einsum(
            "grd,dj->grj", branch_grad, gathered[4], preferred_element_type=jnp.float32
        )
        attended_grad = attended_grad.astype(jnp.bfloat16).reshape(
            groups, row_count, kv_heads, repeat_factor, HEAD_SIZE
        )
        again = (
            jnp.einsum(
                "grhed,gkhd->gherk", grouped_heads, keys_all, preferred_element_type=jnp.float32
            )
            * inv_scale
        )
        probs = jnp.exp(jnp.where(visible, again, NEG) - log_total)
        probs_again = probs.astype(jnp.bfloat16)
        prob_grad = jnp.einsum(
            "grhed,gkhd->gherk", attended_grad, values_all, preferred_element_type=jnp.float32
        )
        values_grad = jnp.einsum(
            "gherk,grhed->gkhd", probs_again, attended_grad, preferred_element_type=jnp.float32
        )
        inner_sum = jnp.sum(prob_grad * probs, axis=-1, keepdims=True)
        score_low = (probs * (prob_grad - inner_sum)).astype(jnp.bfloat16)
        query_grad = (
            jnp.einsum("gherk,gkhd->grhed", score_low, keys_all, preferred_element_type=jnp.float32)
            * inv_scale
        )
        keys_grad = (
            jnp.einsum(
                "gherk,grhed->gkhd", score_low, grouped_heads, preferred_element_type=jnp.float32
            )
            * inv_scale
        )
        prompt_grads = (
            lax.psum_scatter(keys_grad[:, :PROMPT], "ctx", scatter_dimension=1, tiled=True),
            lax.psum_scatter(values_grad[:, :PROMPT], "ctx", scatter_dimension=1, tiled=True),
        )
        later_grads = shifted(
            (
                keys_grad[:, PROMPT : PROMPT + cont_rows],
                values_grad[:, PROMPT : PROMPT + cont_rows],
            ),
            "ctx",
            -1,
        )
        key_rows_grad = jnp.concatenate(
            [prompt_grads[0], keys_grad[:, PROMPT + cont_rows :] + later_grads[0]], axis=1
        )
        value_rows_grad = jnp.concatenate(
            [prompt_grads[1], values_grad[:, PROMPT + cont_rows :] + later_grads[1]], axis=1
        )
        query_grad = rounded(query_grad.reshape(groups, row_count, head_count, HEAD_SIZE))
        query_pre, query_gain_part = normalize_back(
            query_rows, query_scale, gain_query, rotate_back(query_grad, cosine, sine)
        )
        key_pre, key_gain_part = normalize_back(
            keys_unnormed, key_scale, gain_key, rotate_back(rounded(key_rows_grad), cosine, sine)
        )
        query_low_grad = query_pre.astype(jnp.bfloat16).reshape(
            groups, row_count, head_count * HEAD_SIZE
        )
        key_low_grad = key_pre.astype(jnp.bfloat16).reshape(groups, row_count, kv_heads * HEAD_SIZE)
        value_low_grad = value_rows_grad.astype(jnp.bfloat16).reshape(
            groups, row_count, kv_heads * HEAD_SIZE
        )
        input_part = (
            jnp.einsum(
                "grj,dj->grd", query_low_grad, gathered[1], preferred_element_type=jnp.float32
            )
            + jnp.einsum(
                "grj,dj->grd", key_low_grad, gathered[2], preferred_element_type=jnp.float32
            )
            + jnp.einsum(
                "grj,dj->grd", value_low_grad, gathered[3], preferred_element_type=jnp.float32
            )
        )
        input_grad, query_gain_grad, key_gain_grad = lax.psum(
            (input_part, query_gain_part, key_gain_part), "tp"
        )
        token_from, norm_gain_grad = normalize_back(tokens, scale_in, gain_in, input_grad)
        token_grad = (middle_grad + token_from).astype(jnp.bfloat16)
        grad_first.append(token_grad[:, :prompt_rows])
        grad_second.append(token_grad[:, prompt_rows:])
        query_w_grad = jnp.einsum(
            "grd,grj->dj", normed_low, query_low_grad, preferred_element_type=jnp.float32
        )
        key_w_grad = jnp.einsum(
            "grd,grj->dj", normed_low, key_low_grad, preferred_element_type=jnp.float32
        )
        value_w_grad = jnp.einsum(
            "grd,grj->dj", normed_low, value_low_grad, preferred_element_type=jnp.float32
        )
        grad_parts = (
            norm_gain_grad,
            query_w_grad,
            key_w_grad,
            value_w_grad,
            out_w_grad,
            query_gain_grad,
            key_gain_grad,
            moe_gain_grad,
        )
        shares = reduce_grads(grad_parts)
        if grad_total is None:
            grad_total = shares
        else:
            grad_total = tuple(
                (first_item + second_item for first_item, second_item in zip(grad_total, shares))
            )
    return (
        jnp.stack(out_first, axis=0),
        jnp.stack(out_second, axis=0),
        jnp.stack(grad_first, axis=0),
        jnp.stack(grad_second, axis=0),
        grad_total[0],
        grad_total[1],
        grad_total[2],
        grad_total[3],
        grad_total[4],
        grad_total[5],
        grad_total[6],
        grad_total[7],
        gate_total,
        up_total,
        down_total,
    )


def solution(mesh):
    in_specs = (
        P(None, "fsdp", "ctx", None),
        P(None, "fsdp", "ctx", None),
        P(None, "fsdp", "ctx", None),
        P(None, "fsdp", "ctx", None),
        P(None, "fsdp", "ctx", None),
        P(None, "fsdp", "ctx", None),
        P(None, "fsdp", "ctx", None),
        P(None, "fsdp", "ctx", None),
        P(("fsdp", "ctx")),
        P(("fsdp", "ctx"), "tp"),
        P(("fsdp", "ctx"), "tp"),
        P(("fsdp", "ctx"), "tp"),
        P(("fsdp", "ctx"), "tp"),
        P(("fsdp", "ctx")),
        P(("fsdp", "ctx")),
        P(("fsdp", "ctx")),
        P(("fsdp", "ctx"), None, "tp"),
        P(("fsdp", "ctx"), None, "tp"),
        P(("fsdp", "ctx"), "tp", None),
    )
    out_specs = (
        P(None, "fsdp", "ctx", None),
        P(None, "fsdp", "ctx", None),
        P(None, "fsdp", "ctx", None),
        P(None, "fsdp", "ctx", None),
        P(("fsdp", "ctx")),
        P(("fsdp", "ctx"), "tp"),
        P(("fsdp", "ctx"), "tp"),
        P(("fsdp", "ctx"), "tp"),
        P(("fsdp", "ctx"), "tp"),
        P(("fsdp", "ctx")),
        P(("fsdp", "ctx")),
        P(("fsdp", "ctx")),
        P(("fsdp", "ctx"), None, "tp"),
        P(("fsdp", "ctx"), None, "tp"),
        P(("fsdp", "ctx"), "tp", None),
    )
    return jax.shard_map(local, mesh=mesh, in_specs=in_specs, out_specs=out_specs, check_vma=False)
```

profile of v0, /device:TPU:0, one launch (start us, length us, event | category | flops | bytes accessed | tf_op | source)
XLA Modules:
  0.0 3220.3 jit_solution(7064115923695095204)
XLA Ops:
  24.7 11.4 gather_fusion.4
  41.2 10.4 all-to-all-start.4
  54.5 190.1 %all-reduce.13 = (bf16[2048]{0:T(1024)(128)(2,1)S(1)}, bf16[128]{0:T(256)(128)(2,1)S(1)}, bf16[128]{0:T(256)(128)(2,1)S(1)}, bf16[2048]{0:T(1024)(128)(2,1)}) all-reduce(bf16[2048]{0:T(1024)(128)(2,1)S(1)} %dynamic-update-slice, bf16[128]{0:T(256)(128)(2,1)S(1)} %dynamic-update-slice.1, ...), channel_id=1, replica_groups=mesh['fsdp'=8,'ctx'=8,'tp'=2] {'fsdp','ctx'}, use_global_device_ids=true, to_apply=%add | all-reduce | flops 4352 | bytes 17408
  253.0 11.3 gather_fusion.6
  275.8 71.3 %all-gather.7.cloned.1.call-done = bf16[2048,256]{1,0:T(8,128)(2,1)} async-done(((bf16[32,256]{1,0:T(8,128)(2,1)}), bf16[2048,256]{1,0:T(8,128)(2,1)}) %all-gather.7.cloned.1.call-update) | async-done | bytes 1048592 | tf_op jit(solution)/shard_map/all_gather | solution.py:150
  367.6 30.9 all_gather.49
  398.4 29.1 all_gather.46
  427.6 30.8 all_gather.55
  458.4 31.3 all_gather.54
  489.7 29.4 all-gather.9.cloned.1.call-done
  543.4 145.4 %all-gather.11.cloned.1.call-done = bf16[2048,2048]{1,0:T(8,128)(2,1)} async-done(((bf16[32,2048]{1,0:T(8,128)(2,1)}), bf16[2048,2048]{1,0:T(8,128)(2,1)}) %all-gather.11.cloned.1.call-update) | async-done | bytes 8388624 | tf_op jit(solution)/shard_map/all_gather | solution.py:152
  688.8 7.2 convolution_bitcast_fusion.3
  696.0 8.4 all-to-all-start.6
  704.5 7.2 convolution_bitcast_fusion.2
  712.4 90.0 %all-reduce.21.cloned.1.call-done = (f32[1,120,2048]{2,1,0:T(8,128)}, f32[1,120,2048]{2,1,0:T(8,128)}) async-done(((f32[1,120,2048]{2,1,0:T(8,128)}, f32[1,120,2048]{2,1,0:T(8,128)}), (f32[1,120,2048]{2,1,0:T(8,128)}, f32[1,120,2048]{2,1,0:T(8,128)})) %all-reduce.21.cloned.1.call-update) | async-done | bytes 1966096 | tf_op jit(solution)/shard_map/psum | solution.py:215
  818.4 8.2 all-to-all-start
  837.7 41.1 %all-to-all-done = bf16[64,15,2048]{2,1,0:T(8,128)(2,1)} async-done(((bf16[64,15,2048]{2,1,0:T(8,128)(2,1)}), bf16[64,15,2048]{2,1,0:T(8,128)(2,1)}, u32[]{:S(2)}, u32[]{:S(2)}) %all-to-all-start) | async-done | bytes 3932192 | tf_op jit(solution)/shard_map/all_to_all | solution.py:239
  878.8 6.5 all-to-all-start.2
  901.6 6.5 fusion.140
  916.2 21.1 all-to-all-done.2
  942.7 6.4 fusion.142
  956.8 362.5 %all-reduce.22 = (bf16[64,1,15,2048]{3,0,2,1:T(8,128)(2,1)}, bf16[64,1,15,2048]{3,0,2,1:T(8,128)(2,1)}) all-reduce(f32[64,1,15,2048]{3,0,2,1:T(8,128)} %add_bitcast_fusion, f32[64,1,15,2048]{3,0,2,1:T(8,128)} %add_bitcast_fusion.1), channel_id=1, replica_groups=mesh['fsdp'=8,'ctx'=8,'tp'=2] {'tp'}, use_global_device_ids=true, to_apply=%region_32.33 | all-reduce | flops 3932160 | bytes 23592960 | tf_op jit(solution)/shard_map/psum | solution.py:75
  1325.6 6.7 all-to-all-start.5
  1338.8 45.8 %all-to-all-done.5 = bf16[64,15,2048]{2,1,0:T(8,128)(2,1)} async-done(((bf16[64,15,2048]{2,1,0:T(8,128)(2,1)}), bf16[64,15,2048]{2,1,0:T(8,128)(2,1)}, u32[]{:S(2)}, u32[]{:S(2)}) %all-to-all-start.5) | async-done | bytes 3932192 | tf_op jit(solution)/shard_map/all_to_all | solution.py:77
  1407.7 11.3 gather_fusion.5
  1424.2 18.8 all-to-all-done.7
  1448.2 11.6 gather_fusion.7
  1542.9 7.6 fusion.216
  1559.0 9.9 reduce-scatter.11.cloned.1.call-done
  1569.7 38.8 %reduce-scatter.13.cloned.1.call-done = f32[1,56,2,128]{3,1,2,0:T(8,128)} async-done(((f32[1,448,2,128]{3,1,2,0:T(8,128)}), f32[1,56,2,128]{3,1,2,0:T(8,128)}) %reduce-scatter.13.cloned.1.call-update) | async-done | bytes 57360 | tf_op jit(solution)/shard_map/reduce_scatter | solution.py:347
  1610.6 37.6 %reduce-scatter.9.cloned.1.call-done = f32[1,56,2,128]{3,1,2,0:T(8,128)} async-done(((f32[1,448,2,128]{3,1,2,0:T(8,128)}), f32[1,56,2,128]{3,1,2,0:T(8,128)}) %reduce-scatter.9.cloned.1.call-update) | async-done | bytes 57360 | tf_op jit(solution)/shard_map/reduce_scatter | solution.py:347
  1674.1 8.2 convolution_add_fusion
  1686.3 8.4 convolution_add_fusion.1
  1705.8 7.2 convolution_bitcast_fusion.1
  1720.4 8.4 all-reduce.19.cloned.1.call-done
  1733.4 281.8 %all-reduce.8 = (f32[2048]{0:T(1024)S(1)}, f32[128]{0:T(128)S(1)}, f32[128]{0:T(128)S(1)}, f32[2048]{0:T(1024)S(1)}) all-reduce(f32[2048]{0:T(1024)S(1)} %add.505, f32[128]{0:T(128)S(1)} %add.510, f32[128]{0:T(128)S(1)} %add.511, f32[2048]{0:T(1024)S(1)} %add.512), channel_id=14, replica_groups=mesh['fsdp'=8,'ctx'=8,'tp'=2] {'fsdp','ctx'}, use_global_device_ids=true, to_apply=%region_43.44.clone | all-reduce | flops 4352 | bytes 34816
  2015.4 471.3 %all-reduce.23 = (bf16[64,1,15,2048]{3,0,2,1:T(8,128)(2,1)}, bf16[64,1,15,2048]{3,0,2,1:T(8,128)(2,1)}, f32[2]{0:T(128)}, f32[2]{0:T(128)}) all-reduce(f32[64,1,15,2048]{3,0,2,1:T(8,128)} %convolution_bitcast_fusion, f32[64,1,15,2048]{3,0,2,1:T(8,128)} %convolution_bitcast_fusion.1, ...), channel_id=1, replica_groups=mesh['fsdp'=8,'ctx'=8,'tp'=2] {'tp'}, use_global_device_ids=true, to_apply=%region_19.20 | all-reduce | flops 3932164 | bytes 23592992 | tf_op jit(solution)/shard_map/psum | solution.py:75
  2510.9 9.1 fusion.14
  2520.0 8.1 fusion.23
  2528.1 7.9 fusion.24
  2540.3 54.9 %all-to-all-done.1 = bf16[64,15,2048]{2,1,0:T(8,128)(2,1)} async-done(((bf16[64,15,2048]{2,1,0:T(8,128)(2,1)}), bf16[64,15,2048]{2,1,0:T(8,128)(2,1)}, u32[]{:S(2)}, u32[]{:S(2)}) %all-to-all-start.1) | async-done | bytes 3932192 | tf_op jit(solution)/shard_map/all_to_all | solution.py:77
  2595.1 8.4 all-to-all-start.3
  2603.5 10.2 fusion.22
  2622.1 11.4 gather_fusion.1
  2633.5 66.6 %all-to-all-done.3 = bf16[64,15,2048]{2,1,0:T(8,128)(2,1)} async-done(((bf16[64,15,2048]{2,1,0:T(8,128)(2,1)}), bf16[64,15,2048]{2,1,0:T(8,128)(2,1)}, u32[]{:S(2)}, u32[]{:S(2)}) %all-to-all-start.3) | async-done | bytes 3932192 | tf_op jit(solution)/shard_map/all_to_all | solution.py:77
  2705.2 11.5 gather_fusion.3
  2729.2 115.8 %reduce-scatter.23.cloned.1.call-done = f32[32,2048]{1,0:T(8,128)} async-done(((f32[2048,2048]{1,0:T(8,128)}), f32[32,2048]{1,0:T(8,128)}) %reduce-scatter.23.cloned.1.call-update) | async-done | bytes 262160 | tf_op jit(solution)/shard_map/reduce_scatter | solution.py:66
  2845.0 368.6 %reduce-scatter.17.cloned.1.call-done = f32[32,2048]{1,0:T(8,128)} async-done(((f32[2048,2048]{1,0:T(8,128)}), f32[32,2048]{1,0:T(8,128)}) %reduce-scatter.17.cloned.1.call-update) | async-done | bytes 262160 | tf_op jit(solution)/shard_map/reduce_scatter | solution.py:63
  (720 shorter events, 398.2 us)
Async XLA Ops:
  7.2 894.4 %copy-start = (bf16[1,2048,384]{2,1,0:T(8,128)(2,1)S(1)}, bf16[1,2048,384]{2,1,0:T(8,128)(2,1)}, u32[]{:S(2)}) copy-start(bf16[1,2048,384]{2,1,0:T(8,128)(2,1)} %param.35) | copy-start | bytes 4718596
  7.2 265.3 %all-gather.5.cloned.1.call-start = ((), (), s32[]{:S(2)}) async-start(), calls=%async_computation.16 | async-start | bytes 1064960 | tf_op jit(solution)/shard_map/all_gather | solution.py:151
  7.9 339.2 %all-gather.7.cloned.1.call-start = ((), (), s32[]{:S(2)}) async-start(), calls=%async_computation.17 | async-start | bytes 1064960 | tf_op jit(solution)/shard_map/all_gather | solution.py:150
  8.7 510.4 %all-gather.9.cloned.1.call-start = ((), (), s32[]{:S(2)}) async-start(), calls=%async_computation.18 | async-start | bytes 8519680 | tf_op jit(solution)/shard_map/all_gather | solution.py:149
  9.4 679.4 %all-gather.11.cloned.1.call-start = ((), (), s32[]{:S(2)}) async-start(), calls=%async_computation.19 | async-start | bytes 8519680 | tf_op jit(solution)/shard_map/all_gather | solution.py:152
  13.2 232.1 %copy-start.134 = (f32[1,120,8]{1,2,0:T(8,128)}, f32[1,120,8]{1,2,0:T(8,128)S(1)}, u32[]{:S(2)}) copy-start(f32[1,120,8]{1,2,0:T(8,128)S(1)} %get-tuple-element.154) | copy-start | bytes 11524
  41.2 654.8 %all-to-all-start.4 = ((bf16[64,15,2048]{2,1,0:T(8,128)(2,1)}), bf16[64,15,2048]{2,1,0:T(8,128)(2,1)}, u32[]{:S(2)}, u32[]{:S(2)}) async-start(bf16[64,15,2048]{2,1,0:T(8,128)(2,1)} %reshape.2125), calls=%async_computation.4 | async-start | bytes 8388608 | tf_op jit(solution)/shard_map/all_to_all | solution.py:273
  244.6 280.5 %copy-start.61 = (f32[2048]{0:T(1024)}, f32[2048]{0:T(1024)S(1)}, u32[]{:S(2)}) copy-start(f32[2048]{0:T(1024)S(1)} %convert_element_type.429) | copy-start | bytes 24580
  269.7 249.4 %copy-start.39 = (bf16[56,2048]{1,0:T(8,128)(2,1)}, bf16[56,2048]{1,0:T(8,128)(2,1)S(1)}, u32[]{:S(2)}) copy-start(bf16[56,2048]{1,0:T(8,128)(2,1)S(1)} %get-tuple-element.93) | copy-start | bytes 688132
  269.7 255.4 %copy-start.37 = (bf16[56,2048]{1,0:T(8,128)(2,1)}, bf16[56,2048]{1,0:T(8,128)(2,1)S(1)}, u32[]{:S(2)}) copy-start(bf16[56,2048]{1,0:T(8,128)(2,1)S(1)} %get-tuple-element.92) | copy-start | bytes 688132
  269.8 249.2 %copy-start.26 = (bf16[64,2048]{1,0:T(8,128)(2,1)}, bf16[64,2048]{1,0:T(8,128)(2,1)S(1)}, u32[]{:S(2)}) copy-start(bf16[64,2048]{1,0:T(8,128)(2,1)S(1)} %get-tuple-element.85) | copy-start | bytes 786436
  269.9 255.3 %copy-start.28 = (bf16[64,2048]{1,0:T(8,128)(2,1)}, bf16[64,2048]{1,0:T(8,128)(2,1)S(1)}, u32[]{:S(2)}) copy-start(bf16[64,2048]{1,0:T(8,128)(2,1)S(1)} %get-tuple-element.84) | copy-start | bytes 786436
  269.9 532.6 %copy-start.30 = (bf16[1,64,2048]{2,1,0:T(8,128)(2,1)}, bf16[1,64,2048]{2,1,0:T(8,128)(2,1)S(1)}, u32[]{:S(2)}) copy-start(bf16[1,64,2048]{2,1,0:T(8,128)(2,1)S(1)} %get-tuple-element.83) | copy-start | bytes 786436
  271.1 247.9 %copy-start.148 = (f32[120]{0:T(128)}, f32[120]{0:T(128)S(1)}, u32[]{:S(2)}) copy-start(f32[120]{0:T(128)S(1)} %add_rsqrt_fusion.5) | copy-start | bytes 1444
  271.2 254.0 %copy-start.146 = (f32[120]{0:T(128)}, f32[120]{0:T(128)S(1)}, u32[]{:S(2)}) copy-start(f32[120]{0:T(128)S(1)} %add_rsqrt_fusion.7) | copy-start | bytes 1444
  272.4 255.8 %copy-start.81 = (f32[120,64]{1,0:T(8,128)}, f32[120,64]{1,0:T(8,128)S(1)}, u32[]{:S(2)}) copy-start(f32[120,64]{1,0:T(8,128)S(1)} %get-tuple-element.131) | copy-start | bytes 92164
  272.4 255.8 %copy-start.83 = (f32[120,64]{1,0:T(8,128)}, f32[120,64]{1,0:T(8,128)S(1)}, u32[]{:S(2)}) copy-start(f32[120,64]{1,0:T(8,128)S(1)} %get-tuple-element.132) | copy-start | bytes 92164
  348.8 175.2 %copy-start.72 = (f32[1,120,2,128]{3,2,1,0:T(2,128)}, f32[1,120,2,128]{3,2,1,0:T(2,128)S(1)}, u32[]{:S(2)}) copy-start(f32[1,120,2,128]{3,2,1,0:T(2,128)S(1)} %reshape.2113) | copy-start | bytes 368644
  351.0 173.0 %copy-start.87 = (f32[120,256]{1,0:T(8,128)}, f32[120,256]{1,0:T(8,128)S(1)}, u32[]{:S(2)}) copy-start(f32[120,256]{1,0:T(8,128)S(1)} %fusion.201) | copy-start | bytes 368644
  351.0 173.0 %copy-start.74 = (f32[1,120,2,128]{3,2,1,0:T(2,128)}, f32[1,120,2,128]{3,2,1,0:T(2,128)S(1)}, u32[]{:S(2)}) copy-start(f32[1,120,2,128]{3,2,1,0:T(2,128)S(1)} %reshape.2096) | copy-start | bytes 368644
  352.3 177.0 %collective-permute-start.1 = (bf16[1,64,2,128]{3,1,2,0:T(8,128)(2,1)}, bf16[1,64,2,128]{3,1,2,0:T(8,128)(2,1)}, u32[]{:S(2)}, u32[]{:S(2)}) collective-permute-start(bf16[1,64,2,128]{3,1,2,0:T(8,128)(2,1)} %pad_maximum_fusion.19), channel_id=1, source_target_pairs={{0,2},{2,4},{4,6},{6,8},{8,10},{10,12},{12,14},{1,3},{3,5},{5,7},{... | collective-permute-start | bytes 98312 | tf_op jit(solution)/shard_map/ppermute | solution.py:20
  357.5 178.3 %collective-permute-start = (bf16[1,64,2,128]{3,1,2,0:T(8,128)(2,1)}, bf16[1,64,2,128]{3,1,2,0:T(8,128)(2,1)}, u32[]{:S(2)}, u32[]{:S(2)}) collective-permute-start(bf16[1,64,2,128]{3,1,2,0:T(8,128)(2,1)} %copy.278), channel_id=1, source_target_pairs={{0,2},{2,4},{4,6},{6,8},{8,10},{10,12},{12,14},{1,3},{3,5},{5,7},{... | collective-permute-start | bytes 98312 | tf_op jit(solution)/shard_map/ppermute | solution.py:20
  361.6 170.4 %collective-permute-start.3 = (bf16[1,64,2,128]{3,1,2,0:T(8,128)(2,1)}, bf16[1,64,2,128]{3,1,2,0:T(8,128)(2,1)}, u32[]{:S(2)}, u32[]{:S(2)}) collective-permute-start(bf16[1,64,2,128]{3,1,2,0:T(8,128)(2,1)} %pad_maximum_fusion.18), channel_id=1, source_target_pairs={{0,2},{2,4},{4,6},{6,8},{8,10},{10,12},{12,14},{1,3},{3,5},{5,7},{... | collective-permute-start | bytes 98312 | tf_op jit(solution)/shard_map/ppermute | solution.py:20
  365.4 173.7 %collective-permute-start.2 = (bf16[1,64,2,128]{3,1,2,0:T(8,128)(2,1)}, bf16[1,64,2,128]{3,1,2,0:T(8,128)(2,1)}, u32[]{:S(2)}, u32[]{:S(2)}) collective-permute-start(bf16[1,64,2,128]{3,1,2,0:T(8,128)(2,1)} %copy.280), channel_id=1, source_target_pairs={{0,2},{2,4},{4,6},{6,8},{8,10},{10,12},{12,14},{1,3},{3,5},{5,7},{... | collective-permute-start | bytes 98312 | tf_op jit(solution)/shard_map/ppermute | solution.py:20
  543.4 161.1 %copy-start.46 = (bf16[120,2048]{1,0:T(8,128)(2,1)}, bf16[120,2048]{1,0:T(8,128)(2,1)S(1)}, u32[]{:S(2)}) copy-start(bf16[120,2048]{1,0:T(8,128)(2,1)S(1)} %reshape.2117) | copy-start | bytes 1474564
  696.0 122.4 %all-to-all-start.6 = ((bf16[64,15,2048]{2,1,0:T(8,128)(2,1)}), bf16[64,15,2048]{2,1,0:T(8,128)(2,1)}, u32[]{:S(2)}, u32[]{:S(2)}) async-start(bf16[64,15,2048]{2,1,0:T(8,128)(2,1)} %reshape.2134), calls=%async_computation.8 | async-start | bytes 8388608 | tf_op jit(solution)/shard_map/all_to_all | solution.py:273
  704.5 98.0 %all-reduce.21.cloned.1.call-start = ((), (), s32[]{:S(2)}) async-start(), calls=%async_computation.29 | async-start | bytes 3932160 | tf_op jit(solution)/shard_map/psum | solution.py:215
  803.9 660.9 %copy-start.5 = (f32[1,120,2048]{2,1,0:T(8,128)}, f32[1,120,2048]{2,1,0:T(8,128)S(1)}, u32[]{:S(2)}) copy-start(f32[1,120,2048]{2,1,0:T(8,128)S(1)} %get-tuple-element.58) | copy-start | bytes 2949124
  818.4 60.4 %all-to-all-start = ((bf16[64,15,2048]{2,1,0:T(8,128)(2,1)}), bf16[64,15,2048]{2,1,0:T(8,128)(2,1)}, u32[]{:S(2)}, u32[]{:S(2)}) async-start(bf16[64,15,2048]{2,1,0:T(8,128)(2,1)} %reshape.2103), calls=%async_computation | async-start | bytes 8388608 | tf_op jit(solution)/shard_map/all_to_all | solution.py:239
  878.8 58.5 %all-to-all-start.2 = ((bf16[64,15,2048]{2,1,0:T(8,128)(2,1)}), bf16[64,15,2048]{2,1,0:T(8,128)(2,1)}, u32[]{:S(2)}, u32[]{:S(2)}) async-start(bf16[64,15,2048]{2,1,0:T(8,128)(2,1)} %reshape.2120), calls=%async_computation.2 | async-start | bytes 8388608 | tf_op jit(solution)/shard_map/all_to_all | solution.py:239
  1325.6 58.9 %all-to-all-start.5 = ((bf16[64,15,2048]{2,1,0:T(8,128)(2,1)}), bf16[64,15,2048]{2,1,0:T(8,128)(2,1)}, u32[]{:S(2)}, u32[]{:S(2)}) async-start(bf16[64,15,2048]{2,1,0:T(8,128)(2,1)} %copy.239), calls=%async_computation.5 | async-start | bytes 8388608 | tf_op jit(solution)/shard_map/all_to_all | solution.py:77
  1384.5 58.5 %all-to-all-start.7 = ((bf16[64,15,2048]{2,1,0:T(8,128)(2,1)}), bf16[64,15,2048]{2,1,0:T(8,128)(2,1)}, u32[]{:S(2)}, u32[]{:S(2)}) async-start(bf16[64,15,2048]{2,1,0:T(8,128)(2,1)} %copy.250), calls=%async_computation.9 | async-start | bytes 8388608 | tf_op jit(solution)/shard_map/all_to_all | solution.py:77
  1390.8 167.3 %reduce-scatter.15.cloned.1.call-start = ((), (), s32[]{:S(2)}) async-start(), calls=%async_computation.23 | async-start | bytes 516096 | tf_op jit(solution)/shard_map/reduce_scatter | solution.py:348
  1487.1 81.8 %reduce-scatter.11.cloned.1.call-start = ((), (), s32[]{:S(2)}) async-start(), calls=%async_computation.21 | async-start | bytes 516096 | tf_op jit(solution)/shard_map/reduce_scatter | solution.py:348
  1518.5 35.9 %collective-permute-start.7 = (f32[1,64,2,128]{3,1,2,0:T(8,128)}, f32[1,64,2,128]{3,1,2,0:T(8,128)}, u32[]{:S(2)}, u32[]{:S(2)}) collective-permute-start(f32[1,64,2,128]{3,1,2,0:T(8,128)} %slice.296), channel_id=1, source_target_pairs={{2,0},{4,2},{6,4},{8,6},{10,8},{12,10},{14,12},{3,1},{5,3},{7,5},{... | collective-permute-start | bytes 196616 | tf_op jit(solution)/shard_map/ppermute | solution.py:20
  1519.8 35.5 %collective-permute-start.5 = (f32[1,64,2,128]{3,1,2,0:T(8,128)}, f32[1,64,2,128]{3,1,2,0:T(8,128)}, u32[]{:S(2)}, u32[]{:S(2)}) collective-permute-start(f32[1,64,2,128]{3,1,2,0:T(8,128)} %slice.285), channel_id=1, source_target_pairs={{2,0},{4,2},{6,4},{8,6},{10,8},{12,10},{14,12},{3,1},{5,3},{7,5},{... | collective-permute-start | bytes 196616 | tf_op jit(solution)/shard_map/ppermute | solution.py:20
  1521.1 35.1 %collective-permute-start.6 = (f32[1,64,2,128]{3,1,2,0:T(8,128)}, f32[1,64,2,128]{3,1,2,0:T(8,128)}, u32[]{:S(2)}, u32[]{:S(2)}) collective-permute-start(f32[1,64,2,128]{3,1,2,0:T(8,128)} %slice.291), channel_id=1, source_target_pairs={{2,0},{4,2},{6,4},{8,6},{10,8},{12,10},{14,12},{3,1},{5,3},{7,5},{... | collective-permute-start | bytes 196616 | tf_op jit(solution)/shard_map/ppermute | solution.py:20
  1522.4 34.8 %collective-permute-start.4 = (f32[1,64,2,128]{3,1,2,0:T(8,128)}, f32[1,64,2,128]{3,1,2,0:T(8,128)}, u32[]{:S(2)}, u32[]{:S(2)}) collective-permute-start(f32[1,64,2,128]{3,1,2,0:T(8,128)} %slice.280), channel_id=1, source_target_pairs={{2,0},{4,2},{6,4},{8,6},{10,8},{12,10},{14,12},{3,1},{5,3},{7,5},{... | collective-permute-start | bytes 196616 | tf_op jit(solution)/shard_map/ppermute | solution.py:20
  1523.7 84.8 %reduce-scatter.13.cloned.1.call-start = ((), (), s32[]{:S(2)}) async-start(), calls=%async_computation.22 | async-start | bytes 516096 | tf_op jit(solution)/shard_map/reduce_scatter | solution.py:347
  1531.6 116.6 %reduce-scatter.9.cloned.1.call-start = ((), (), s32[]{:S(2)}) async-start(), calls=%async_computation.20 | async-start | bytes 516096 | tf_op jit(solution)/shard_map/reduce_scatter | solution.py:347
  1537.6 191.3 %all-reduce.19.cloned.1.call-start = ((), (), s32[]{:S(2)}) async-start(), calls=%async_computation.28 | async-start | bytes 3932160 | tf_op jit(solution)/shard_map/psum | solution.py:389
  1662.0 1067.2 %reduce-scatter.21.cloned.1.call-start = ((), (), s32[]{:S(2)}) async-start(), calls=%async_computation.26 | async-start | bytes 2129920 | tf_op jit(solution)/shard_map/reduce_scatter | solution.py:65
  1666.4 1062.9 %reduce-scatter.19.cloned.1.call-start = ((), (), s32[]{:S(2)}) async-start(), calls=%async_computation.25 | async-start | bytes 2129920 | tf_op jit(solution)/shard_map/reduce_scatter | solution.py:64
  1670.6 1174.4 %reduce-scatter.23.cloned.1.call-start = ((), (), s32[]{:S(2)}) async-start(), calls=%async_computation.27 | async-start | bytes 17039360 | tf_op jit(solution)/shard_map/reduce_scatter | solution.py:66
  1682.3 1531.3 %reduce-scatter.17.cloned.1.call-start = ((), (), s32[]{:S(2)}) async-start(), calls=%async_computation.24 | async-start | bytes 17039360 | tf_op jit(solution)/shard_map/reduce_scatter | solution.py:63
  2493.0 102.1 %all-to-all-start.1 = ((bf16[64,15,2048]{2,1,0:T(8,128)(2,1)}), bf16[64,15,2048]{2,1,0:T(8,128)(2,1)}, u32[]{:S(2)}, u32[]{:S(2)}) async-start(bf16[64,15,2048]{2,1,0:T(8,128)(2,1)} %copy.223), calls=%async_computation.1 | async-start | bytes 8388608 | tf_op jit(solution)/shard_map/all_to_all | solution.py:77
  2595.1 105.0 %all-to-all-start.3 = ((bf16[64,15,2048]{2,1,0:T(8,128)(2,1)}), bf16[64,15,2048]{2,1,0:T(8,128)(2,1)}, u32[]{:S(2)}, u32[]{:S(2)}) async-start(bf16[64,15,2048]{2,1,0:T(8,128)(2,1)} %copy.235), calls=%async_computation.3 | async-start | bytes 8388608 | tf_op jit(solution)/shard_map/all_to_all | solution.py:77
  2723.2 490.4 %copy-start.1 = (bf16[1,2048,384]{2,1,0:T(8,128)(2,1)S(1)}, bf16[1,2048,384]{2,1,0:T(8,128)(2,1)}, u32[]{:S(2)}) copy-start(bf16[1,2048,384]{2,1,0:T(8,128)(2,1)} %param.35) | copy-start | bytes 4718596
  (172 other events, 2665.7 us)
Sparse Core Ops, SparseCore 0:
  9.7 187.0 all-gather.4
  198.5 148.5 all-gather.6
  348.8 170.2 all-gather.8
  520.6 168.1 all-gather.10
  711.9 90.4 all-reduce.20
  1487.2 36.4 reduce-scatter.14
  1526.1 42.7 reduce-scatter.10
  1571.9 36.5 reduce-scatter.12
  1611.4 36.6 reduce-scatter.8
  1662.1 66.7 all-reduce.18
  1731.8 288.3 reduce-scatter.20
  2023.1 300.8 reduce-scatter.18
  2327.0 517.9 reduce-scatter.22
  2847.8 365.7 reduce-scatter.16
where the time goes:
time: 3230 us; the launch traced here: 3220 us
  blocking collectives  1430 us (44%)
  waiting for transfers between devices  1170 us (36%)
  matrix products  229 us (7%)
  local copies, waits for them, and re-layouts  200 us (6%)
  other arithmetic  96.1 us (3%)
  starting transfers between devices  80.9 us (3%)
    psum x2, blocking collectives, send_back(): summed = lax.psum(partial_rows, 'tp').astype(jnp.bfloat16)  834 us
    unnamed x2, blocking collectives  472 us
    reduce_scatter x1, waiting for transfers between devices, reduce_grads(): lax.psum_scatter(grad_parts[1], ('fsdp', 'ctx'), scatter_dimension=0, til...  369 us
    all_to_all x4, waiting for transfers between devices, send_back(): lax.all_to_all(summed, ('fsdp', 'ctx'), split_axis=0, concat_axis=0, tile...  186 us
    all_gather x1, waiting for transfers between devices, local(): lax.all_gather(out_weight, ('fsdp', 'ctx'), axis=0, tiled=True)  145 us
    reduce_scatter x1, waiting for transfers between devices, reduce_grads(): lax.psum_scatter(grad_parts[4], ('fsdp', 'ctx'), scatter_dimension=0, til...  116 us
    psum x1, waiting for transfers between devices, local(): branch = lax.psum(branch_part, 'tp')  90 us
    reduce_scatter x2, waiting for transfers between devices, local(): lax.psum_scatter(keys_grad[:, :PROMPT], 'ctx', scatter_dimension=1, tiled...  76.4 us
  transfers between devices with their start and end apart: 30, of which 16 were waited for; matrix products, arithmetic and copies ran while one was open for 14% of the time, Pallas kernels for 0%

commit v1 on v0

v1 whole, which is shorter than its diff:
```python
import functools

import jax
import jax.numpy as jnp
from jax import lax
from jax.experimental import pallas as pl
from jax.experimental.pallas import tpu as pltpu
from jax.sharding import PartitionSpec as P

HEAD_SIZE = 128
TOPK = 8
PROMPT = 448
CL = 128
EPS = 1e-06
THETA = 1000000.0
NEG = -1e30
F32 = jnp.float32
BF16 = jnp.bfloat16
ALL = ("fsdp", "ctx")
MESH = pl.DeviceIdType.MESH
RING = 4
VMEM_LIMIT = 48 * 1024 * 1024


def place():
    f, c = lax.axis_index("fsdp"), lax.axis_index("ctx")
    return f // 2, f % 2, c // 2, c % 2


def device(y, core, z, x):
    return {"fsdp": y * 2 + core, "ctx": z * 2 + x}


def greet(partners):
    barrier = pltpu.get_barrier_semaphore()
    for partner in partners:
        pl.semaphore_signal(barrier, inc=1, device_id=partner, device_id_type=MESH)
    pl.semaphore_wait(barrier, len(partners))


def neighbours():
    y, core, z, x = place()
    up, down = (lambda v: lax.rem(v + 1, RING)), (lambda v: lax.rem(v + RING - 1, RING))
    return [
        device(y, core, z, 1 - x),
        device(y, 1 - core, z, x),
        device(up(y), core, z, x),
        device(down(y), core, z, x),
        device(y, core, up(z), x),
        device(y, core, down(z), x),
    ]


def other_tp():
    return {"tp": 1 - lax.axis_index("tp")}


def swap_halves(src, dst, send_sem, recv_sem):
    return pltpu.make_async_remote_copy(
        src_ref=src, dst_ref=dst, send_sem=send_sem, recv_sem=recv_sem, device_id=other_tp(),
        device_id_type=MESH,
    )


def gather_kernel(
    a_ref, b_ref, gate_ref, up_ref, a_all, b_all, wide_all,
    local_sem, send_sem, recv_sem, away_sem, home_sem, keep_sem, give_sem, take_sem,
):
    y, core, z, x = place()
    greet(neighbours() + [other_tp()])
    hidden = gate_ref.shape[1]
    wide = []
    for n, ref in enumerate((gate_ref, up_ref)):
        own_cols = wide_all.at[:, pl.ds(n * hidden, hidden)]
        far_cols = wide_all.at[:, pl.ds((2 + n) * hidden, hidden)]
        wide.append(pltpu.make_async_copy(ref, own_cols, keep_sem.at[n]))
        wide.append(swap_halves(ref, far_cols, give_sem.at[n], take_sem.at[n]))
    for copy in wide:
        copy.start()
    refs, own = (a_all, b_all), (a_ref, b_ref)
    started = []
    count = [0, 0]

    def chunk(n, i, j):
        return refs[n].at[j, core, i] if n == 0 else refs[n].at[i, core, j]

    def to(n, first, second):
        return device(second, core, first, x) if n == 0 else device(first, core, second, x)

    def send(n, ref, where, slot):
        copy = pltpu.make_async_remote_copy(
            src_ref=ref, dst_ref=ref, send_sem=send_sem.at[n, slot], recv_sem=recv_sem.at[n, slot],
            device_id=where, device_id_type=MESH,
        )
        copy.start()
        started.append(copy)

    def arrived(n, ref, slot):
        pltpu.make_async_remote_copy(
            src_ref=ref, dst_ref=ref, send_sem=send_sem.at[n, slot], recv_sem=recv_sem.at[n, slot],
            device_id=device(y, core, z, x), device_id_type=MESH,
        ).wait_recv()

    homes = []

    def across(n, i, j):
        slot = count[n]
        count[n] += 1
        ref = chunk(n, i, j)
        copy = pltpu.make_async_remote_copy(
            src_ref=ref, dst_ref=ref, send_sem=away_sem.at[n, slot], recv_sem=home_sem.at[n, slot],
            device_id=device(y, 1 - core, z, x), device_id_type=MESH,
        )
        copy.start()
        homes.append(copy)

    def second(n, i, j, k):
        base = 5 + 4 * k
        send(n, chunk(n, i, j), to(n, me[n][0], up(j)), base)
        send(n, chunk(n, i, j), to(n, me[n][0], down(j)), base + 1)
        across(n, i, j)

    up, down = (lambda v: lax.rem(v + 1, RING)), (lambda v: lax.rem(v + RING - 1, RING))
    me = ((z, y), (y, z))
    locals_ = []
    for n in (0, 1):
        i, j = me[n]
        keep = pltpu.make_async_copy(own[n], chunk(n, i, j).at[x], local_sem.at[n])
        keep.start()
        locals_.append(keep)
        copy = pltpu.make_async_remote_copy(
            src_ref=own[n], dst_ref=chunk(n, i, j).at[x], send_sem=send_sem.at[n, 0],
            recv_sem=recv_sem.at[n, 0], device_id=device(y, core, z, 1 - x), device_id_type=MESH,
        )
        copy.start()
        started.append(copy)
    for n in (0, 1):
        i, j = me[n]
        locals_[n].wait()
        arrived(n, chunk(n, i, j).at[1 - x], 0)
        send(n, chunk(n, i, j), to(n, up(i), j), 1)
        send(n, chunk(n, i, j), to(n, down(i), j), 2)
    for n in (0, 1):
        i, j = me[n]
        second(n, i, j, 0)
    for n in (0, 1):
        i, j = me[n]
        arrived(n, chunk(n, down(i), j), 1)
        send(n, chunk(n, down(i), j).at[0], to(n, up(i), j), 3)
        second(n, down(i), j, 1)
    for n in (0, 1):
        i, j = me[n]
        arrived(n, chunk(n, up(i), j), 2)
        send(n, chunk(n, up(i), j).at[1], to(n, down(i), j), 4)
        second(n, up(i), j, 2)
    for n in (0, 1):
        i, j = me[n]
        far = lax.rem(i + 2, RING)
        arrived(n, chunk(n, far, j).at[0], 3)
        arrived(n, chunk(n, far, j).at[1], 4)
        second(n, far, j, 3)
    for k in range(4):
        for n in (0, 1):
            i, j = me[n]
            it = (i, down(i), up(i), lax.rem(i + 2, RING))[k]
            base = 5 + 4 * k
            arrived(n, chunk(n, it, down(j)), base)
            send(n, chunk(n, it, down(j)).at[0], to(n, i, up(j)), base + 2)
            across(n, it, down(j))
            arrived(n, chunk(n, it, up(j)), base + 1)
            send(n, chunk(n, it, up(j)).at[1], to(n, i, down(j)), base + 3)
            across(n, it, up(j))
    for k in range(4):
        for n in (0, 1):
            i, j = me[n]
            it = (i, down(i), up(i), lax.rem(i + 2, RING))[k]
            base = 5 + 4 * k
            far = lax.rem(j + 2, RING)
            arrived(n, chunk(n, it, far).at[0], base + 2)
            arrived(n, chunk(n, it, far).at[1], base + 3)
            across(n, it, far)
    for copy in homes:
        copy.wait()
    for copy in started:
        copy.wait_send()
    for copy in wide:
        copy.wait()


def gather_weights(a, b, gate, up):
    rows = a.shape[0]
    shape = (RING, 2, RING, 2, rows)
    any_space = pl.BlockSpec(memory_space=pl.ANY)
    a_all, b_all, wide = pl.pallas_call(
        gather_kernel,
        in_specs=[any_space] * 4,
        out_specs=[any_space] * 3,
        out_shape=[jax.ShapeDtypeStruct(shape + (v.shape[1],), v.dtype) for v in (a, b)]
        + [jax.ShapeDtypeStruct((gate.shape[0], 4 * gate.shape[1]), gate.dtype)],
        scratch_shapes=[
            pltpu.SemaphoreType.DMA((2,)),
            pltpu.SemaphoreType.DMA((2, 21)),
            pltpu.SemaphoreType.DMA((2, 21)),
            pltpu.SemaphoreType.DMA((2, 16)),
            pltpu.SemaphoreType.DMA((2, 16)),
            pltpu.SemaphoreType.DMA((2,)),
            pltpu.SemaphoreType.DMA((2,)),
            pltpu.SemaphoreType.DMA((2,)),
        ],
        compiler_params=pltpu.CompilerParams(collective_id=0, has_side_effects=True),
        cost_estimate=pl.CostEstimate(flops=0, bytes_accessed=250_000_000, transcendentals=0),
        name="gather_weights",
    )(a, b, gate, up)
    return a_all.reshape(-1, a.shape[1]), b_all.reshape(-1, b.shape[1]), wide


ORDER = (2, 1, 3, 0)
SLICE = 16


def up(v):
    return lax.rem(v + 1, RING)


def down(v):
    return lax.rem(v + RING - 1, RING)


def add_into(target, *terms):
    flat = [target.shape[0]] if len(target.shape) == 3 else []
    for lead in range(flat[0]) if flat else (None,):
        for start in range(0, target.shape[-2], SLICE):
            at = (pl.ds(start, SLICE), slice(None))
            at = at if lead is None else (lead,) + at
            total = terms[0][at].astype(F32)
            for term in terms[1:]:
                total = total + term[at].astype(F32)
            target[at] = total.astype(target.dtype)


def scatter_kernel(
    a_ref, b_ref, extra_ref, wide_ref, a_out, b_out, wide_out, a_mine, b_mine, a_theirs, b_theirs, a_one, b_one, a_two, b_two,
    a_first, b_first, a_last, b_last, a_x, b_x, load_sem, send_sem, recv_sem,
    extra_load_sem, extra_send_sem, extra_recv_sem, give_sem, take_sem,
):
    y, core, z, x = place()
    greet(neighbours() + [other_tp()])
    wide = swap_halves(wide_ref, wide_out, give_sem, take_sem)
    wide.start()
    grads, outs = (a_ref, b_ref), (a_out, b_out)
    mine, theirs = (a_mine, b_mine), (a_theirs, b_theirs)
    one, two = (a_one, b_one), (a_two, b_two)
    first, last, side = (a_first, b_first), (a_last, b_last), (a_x, b_x)
    me = ((z, y), (y, z))
    sent = []

    def chunk(n, i, j, c):
        return grads[n].at[j, c, i] if n == 0 else grads[n].at[i, c, j]

    def to(n, i, j):
        return device(j, core, i, x) if n == 0 else device(i, core, j, x)

    def copy_of(n, src, dst, slot, where):
        return pltpu.make_async_remote_copy(
            src_ref=src, dst_ref=dst, send_sem=send_sem.at[n, slot], recv_sem=recv_sem.at[n, slot],
            device_id=where, device_id_type=MESH,
        )

    def send(n, src, dst, slot, where):
        copy = copy_of(n, src, dst, slot, where)
        copy.start()
        sent.append(copy)

    def arrived(n, dst, slot):
        copy_of(n, dst, dst, slot, device(y, core, z, x)).wait_recv()

    cols = b_ref.shape[-1]

    def columns(ref, start, count):
        return ref.at[:, :, pl.ds(start, count)]

    def extra_copy(slot):
        ref = columns(theirs[1].at[slot], cols, extra_ref.shape[-1])
        far = extra_ref.at[lax.rem(y + slot // RING, RING), 1 - core, lax.rem(z + slot % RING, RING)]
        return pltpu.make_async_remote_copy(
            src_ref=far, dst_ref=ref, send_sem=extra_send_sem.at[slot],
            recv_sem=extra_recv_sem.at[slot], device_id=device(y, 1 - core, z, x),
            device_id_type=MESH,
        )

    def extra_load(slot):
        near = extra_ref.at[lax.rem(y + slot // RING, RING), core, lax.rem(z + slot % RING, RING)]
        return pltpu.make_async_copy(
            near, columns(mine[1].at[slot], cols, extra_ref.shape[-1]), extra_load_sem.at[slot]
        )

    def load(n, di, dj):
        i, j = me[n]
        slot = di * RING + dj
        target = mine[n].at[slot] if n == 0 else columns(mine[n].at[slot], 0, cols)
        return pltpu.make_async_copy(
            chunk(n, lax.rem(i + di, RING), lax.rem(j + dj, RING), core), target,
            load_sem.at[n, slot],
        )

    for dj in ORDER:
        for di in ORDER:
            for n in (0, 1):
                i, j = me[n]
                slot = di * RING + dj
                there = chunk(n, lax.rem(i + di, RING), lax.rem(j + dj, RING), 1 - core)
                target = theirs[n].at[slot] if n == 0 else columns(theirs[n].at[slot], 0, cols)
                send(n, there, target, slot, device(y, 1 - core, z, x))
                load(n, di, dj).start()
                if n == 1:
                    extra_copy(slot).start()
                    extra_load(slot).start()

    def ready(n, di, dj):
        slot = di * RING + dj
        load(n, di, dj).wait()
        if n == 0:
            arrived(n, theirs[n].at[slot], slot)
        else:
            arrived(n, columns(theirs[n].at[slot], 0, cols), slot)
            extra_load(slot).wait()
            extra_copy(slot).wait_recv()
        return slot

    for di in ORDER:
        for n in (0, 1):
            i, j = me[n]
            slot = ready(n, di, 2)
            add_into(mine[n].at[slot], mine[n].at[slot], theirs[n].at[slot])
            for half in (0, 1):
                send(
                    n, mine[n].at[slot, half], one[n].at[di, half], 16 + di * 2 + half,
                    to(n, i, up(j) if half == 0 else down(j)),
                )
    for di in ORDER:
        for n in (0, 1):
            i, j = me[n]
            for half, dj in ((0, 1), (1, 3)):
                slot = ready(n, di, dj)
                arrived(n, one[n].at[di, half], 16 + di * 2 + half)
                add_into(
                    mine[n].at[slot, half], mine[n].at[slot, half], theirs[n].at[slot, half],
                    one[n].at[di, half],
                )
                add_into(
                    mine[n].at[slot, 1 - half], mine[n].at[slot, 1 - half],
                    theirs[n].at[slot, 1 - half],
                )
                send(
                    n, mine[n].at[slot], two[n].at[di, half], 24 + di * 2 + half,
                    to(n, i, up(j) if half == 0 else down(j)),
                )
    for di in ORDER:
        for n in (0, 1):
            i, j = me[n]
            slot = ready(n, di, 0)
            for half in (0, 1):
                arrived(n, two[n].at[di, half], 24 + di * 2 + half)
            add_into(
                mine[n].at[slot], mine[n].at[slot], theirs[n].at[slot], two[n].at[di, 0],
                two[n].at[di, 1],
            )
            if di == 2:
                for half in (0, 1):
                    send(
                        n, mine[n].at[slot, half], first[n].at[half], 32 + half,
                        to(n, up(i) if half == 0 else down(i), j),
                    )
            elif di != 0:
                half = 0 if di == 1 else 1
                arrived(n, first[n].at[half], 32 + half)
                add_into(mine[n].at[slot, half], mine[n].at[slot, half], first[n].at[half])
                send(
                    n, mine[n].at[slot], last[n].at[half], 34 + half,
                    to(n, up(i) if half == 0 else down(i), j),
                )
    for n in (0, 1):
        for half in (0, 1):
            arrived(n, last[n].at[half], 34 + half)
        add_into(mine[n].at[0], mine[n].at[0], last[n].at[0], last[n].at[1])
        send(n, mine[n].at[0, 1 - x], side[n], 36, device(y, core, z, 1 - x))
    for n in (0, 1):
        arrived(n, side[n], 36)
        add_into(outs[n], mine[n].at[0, x], side[n])
    for copy in sent:
        copy.wait_send()
    for slot in range(RING * RING):
        extra_copy(slot).wait_send()
    wide.wait()


def scatter_grads(a, b, extra, wide):
    peers = RING * RING * 4
    rows = a.shape[0] // peers
    shape = (RING, 2, RING, 2, rows)
    cols = (a.shape[1], b.shape[1] + extra.shape[1])
    buffers = []
    for lead in ((16, 2), (16, 2), (4, 2), (4, 2, 2), (2,), (2, 2), ()):
        buffers += [pltpu.VMEM(lead + (rows, c), a.dtype) for c in cols]
    any_space = pl.BlockSpec(memory_space=pl.ANY)
    return pl.pallas_call(
        scatter_kernel,
        in_specs=[any_space] * 4,
        out_specs=[pl.BlockSpec(memory_space=pltpu.VMEM)] * 2 + [any_space],
        out_shape=[jax.ShapeDtypeStruct((rows, c), F32) for c in cols]
        + [jax.ShapeDtypeStruct(wide.shape, wide.dtype)],
        scratch_shapes=buffers + [
            pltpu.SemaphoreType.DMA((2, 16)),
            pltpu.SemaphoreType.DMA((2, 37)),
            pltpu.SemaphoreType.DMA((2, 37)),
            pltpu.SemaphoreType.DMA((16,)),
            pltpu.SemaphoreType.DMA((16,)),
            pltpu.SemaphoreType.DMA((16,)),
            pltpu.SemaphoreType.DMA,
            pltpu.SemaphoreType.DMA,
        ],
        compiler_params=pltpu.CompilerParams(
            collective_id=1, has_side_effects=True, vmem_limit_bytes=44 * 1024 * 1024
        ),
        cost_estimate=pl.CostEstimate(flops=0, bytes_accessed=250_000_000, transcendentals=0),
        name="scatter_grads",
    )(*(v.reshape(shape + (v.shape[1],)) for v in (a, b, extra)), wide)


BLOCK = 64
CTX = 8


def dot(a, b, dims):
    return lax.dot_general(a, b, (dims, ((), ())), preferred_element_type=F32)


def rotated(u, gain, cosine, sine):
    scaling = lax.rsqrt(jnp.mean(u * u, axis=-1, keepdims=True) + EPS)
    normed = u * scaling
    n = normed * gain
    rot = n * cosine + pltpu.roll(n, HEAD_SIZE // 2, 1) * sine
    return rot.astype(BF16), normed, scaling


def rotated_back(e, normed, scaling, gain, cosine, sine):
    back = e * cosine + pltpu.roll(e * sine, HEAD_SIZE // 2, 1)
    scaled = back * gain
    inner = jnp.mean(scaled * normed, axis=-1, keepdims=True)
    return scaling * (scaled - normed * inner), jnp.sum(back * normed, axis=0, keepdims=True)


def ctx_peer(step):
    return {"ctx": lax.rem(lax.axis_index("ctx") + step, CTX)}


def beside():
    c = lax.axis_index("ctx")
    return {"ctx": c + 1 - 2 * lax.rem(c, 2)}


def remote(src, dst, send_sem, recv_sem, where):
    return pltpu.make_async_remote_copy(
        src_ref=src, dst_ref=dst, send_sem=send_sem, recv_sem=recv_sem, device_id=where,
        device_id_type=MESH,
    )


def softmax_parts(q_low, k, bias):
    s = dot(q_low, k, ((1,), (1,))) * (HEAD_SIZE ** -0.5) + bias
    e = jnp.exp(s - jnp.max(s, axis=-1, keepdims=True))
    return e / jnp.sum(e, axis=-1, keepdims=True)


def attention_kernel(
    kv, heads, qkv_ref, cos_ref, sin_ref, gq_ref, gk_ref, bias_ref, down_ref, o_ref, kv_ref, tall_ref,
    held, send_sem, recv_sem, keep_sem, give_sem, take_sem,
):
    c = lax.axis_index("ctx")
    greet([ctx_peer(step) for step in range(1, CTX)] + [other_tp()])
    half = down_ref.shape[0]
    keep = pltpu.make_async_copy(down_ref, tall_ref.at[pl.ds(0, half)], keep_sem)
    tall = swap_halves(down_ref, tall_ref.at[pl.ds(half, half)], give_sem, take_sem)
    micro, rows = held.shape[0], 2 * BLOCK
    q_cols = kv * heads * HEAD_SIZE
    cosine, sine, gq, gk = cos_ref[...], sin_ref[...], gq_ref[...], gk_ref[...]
    mine = pl.ds(pl.multiple_of(c * BLOCK, BLOCK), BLOCK)
    earlier, own = pl.ds(CTX * BLOCK, BLOCK), pl.ds((CTX + 1) * BLOCK, BLOCK)
    copies = []
    for m in range(micro):
        span = slice(m * rows, (m + 1) * rows)
        for h in range(2 * kv):
            cols = slice(h * HEAD_SIZE, (h + 1) * HEAD_SIZE)
            u = qkv_ref[span, q_cols + h * HEAD_SIZE : q_cols + (h + 1) * HEAD_SIZE]
            low = rotated(u, gk, cosine, sine)[0] if h < kv else u.astype(BF16)
            held[m, mine, cols] = low[:BLOCK]
            held[m, own, cols] = low[BLOCK:]
        for step in range(1, CTX):
            part = held.at[m, mine]
            copies.append(
                remote(part, part, send_sem.at[step, m], recv_sem.at[step, m], ctx_peer(step))
            )
        copies.append(
            remote(
                held.at[m, own], held.at[m, earlier], send_sem.at[0, m], recv_sem.at[0, m], beside()
            )
        )
        for copy in copies[-CTX:]:
            copy.start()
    keep.start()
    tall.start()

    def group(m, h, carry):
        span = slice(m * rows, (m + 1) * rows)
        k = held[m, :, pl.ds(pl.multiple_of(h * HEAD_SIZE, HEAD_SIZE), HEAD_SIZE)]
        v = held[m, :, pl.ds(pl.multiple_of((kv + h) * HEAD_SIZE, HEAD_SIZE), HEAD_SIZE)]
        for e in range(heads):
            cols = pl.ds(pl.multiple_of((h * heads + e) * HEAD_SIZE, HEAD_SIZE), HEAD_SIZE)
            q_low = rotated(qkv_ref[span, cols], gq, cosine, sine)[0]
            p = softmax_parts(q_low, k, bias_ref[...]).astype(BF16)
            o_ref[span, cols] = dot(p, v, ((1,), (0,))).astype(BF16)
        return carry

    for m in range(micro):
        for step in range(1, CTX):
            source = lax.rem(c + CTX - step, CTX)
            part = held.at[m, pl.ds(pl.multiple_of(source * BLOCK, BLOCK), BLOCK)]
            remote(
                part, part, send_sem.at[step, m], recv_sem.at[step, m], ctx_peer(step)
            ).wait_recv()
        copies[(m + 1) * CTX - 1].wait_recv()
        lax.fori_loop(0, kv, functools.partial(group, m), 0)
    kv_ref[...] = held[...]
    for copy in copies:
        copy.wait_send()
    keep.wait()
    tall.wait()


def attention_back_kernel(
    kv, heads, qkv_ref, cos_ref, sin_ref, gq_ref, gk_ref, bias_ref, kv_ref, do_ref, tall_ref,
    dqkv_ref, gains_ref, tall_out, grads, given, given_side, p_all, ds_all, q_all, do_all,
    send_sem, recv_sem, give_sem, take_sem,
):
    c = lax.axis_index("ctx")
    greet([ctx_peer(step) for step in range(1, CTX)] + [other_tp()])
    tall = swap_halves(tall_ref, tall_out, give_sem, take_sem)
    tall.start()
    micro, rows = grads.shape[0], 2 * BLOCK
    q_cols = kv * heads * HEAD_SIZE
    scale = HEAD_SIZE ** -0.5
    cosine, sine, gq, gk = cos_ref[...], sin_ref[...], gq_ref[...], gk_ref[...]
    mine = pl.ds(pl.multiple_of(c * BLOCK, BLOCK), BLOCK)
    earlier, own = pl.ds(CTX * BLOCK, BLOCK), pl.ds((CTX + 1) * BLOCK, BLOCK)

    def group(m, h, total):
        span = slice(m * rows, (m + 1) * rows)
        k_cols = pl.ds(pl.multiple_of(h * HEAD_SIZE, HEAD_SIZE), HEAD_SIZE)
        v_cols = pl.ds(pl.multiple_of((kv + h) * HEAD_SIZE, HEAD_SIZE), HEAD_SIZE)
        k, v = kv_ref[m, :, k_cols], kv_ref[m, :, v_cols]
        for e in range(heads):
            cols = pl.ds(pl.multiple_of((h * heads + e) * HEAD_SIZE, HEAD_SIZE), HEAD_SIZE)
            stack = slice(e * rows, (e + 1) * rows)
            q_low, normed, scaling = rotated(qkv_ref[span, cols], gq, cosine, sine)
            q_all[stack, :] = q_low
            p = softmax_parts(q_low, k, bias_ref[...])
            p_all[stack, :] = p.astype(BF16)
            do = do_ref[span, cols]
            do_all[stack, :] = do
            dp = dot(do, v, ((1,), (1,)))
            ds = (p * (dp - jnp.sum(dp * p, axis=-1, keepdims=True))).astype(BF16)
            ds_all[stack, :] = ds
            dqr = (dot(ds, k, ((1,), (0,))) * scale).astype(BF16).astype(F32)
            dq, part = rotated_back(dqr, normed, scaling, gq, cosine, sine)
            dqkv_ref[span, cols] = dq.astype(BF16)
            total = total + part
        grads[m, :, v_cols] = dot(p_all[...], do_all[...], ((0,), (0,))).astype(BF16)
        grads[m, :, k_cols] = (dot(ds_all[...], q_all[...], ((0,), (0,))) * scale).astype(BF16)
        return total

    total = jnp.zeros((1, HEAD_SIZE), F32)
    copies = []
    for m in range(micro):
        total = lax.fori_loop(0, kv, functools.partial(group, m), total)
        for step in range(1, CTX):
            peer = lax.rem(c + step, CTX)
            part = grads.at[m, pl.ds(pl.multiple_of(peer * BLOCK, BLOCK), BLOCK)]
            copies.append(
                remote(
                    part, given.at[step - 1, m], send_sem.at[step, m], recv_sem.at[step, m],
                    ctx_peer(step),
                )
            )
        copies.append(
            remote(
                grads.at[m, earlier], given_side.at[m], send_sem.at[0, m], recv_sem.at[0, m],
                beside(),
            )
        )
        for copy in copies[-CTX:]:
            copy.start()
    k_total = jnp.zeros((1, HEAD_SIZE), F32)
    for m in range(micro):
        for copy in copies[m * CTX : (m + 1) * CTX]:
            copy.wait_recv()
        for h in range(2 * kv):
            cols = slice(h * HEAD_SIZE, (h + 1) * HEAD_SIZE)
            at = slice(q_cols + h * HEAD_SIZE, q_cols + (h + 1) * HEAD_SIZE)
            prompt = grads[m, mine, cols].astype(F32)
            for step in range(CTX - 1):
                prompt = prompt + given[step, m, :, cols].astype(F32)
            cont = grads[m, own, cols].astype(F32) + given_side[m, :, cols].astype(F32)
            e = jnp.concatenate([prompt, cont], axis=0).astype(BF16)
            span = slice(m * rows, (m + 1) * rows)
            if h < kv:
                _, normed, scaling = rotated(qkv_ref[span, at], gk, cosine, sine)
                d, part = rotated_back(e.astype(F32), normed, scaling, gk, cosine, sine)
                k_total = k_total + part
                dqkv_ref[span, at] = d.astype(BF16)
            else:
                dqkv_ref[span, at] = e
    gains_ref[0:1, :] = total
    gains_ref[1:2, :] = k_total
    for copy in copies:
        copy.wait_send()
    tall.wait()


def attention(qkv, cosine, sine, gain_query, gain_key, bias, down, kv, micro):
    heads = qkv.shape[1] // HEAD_SIZE // kv - 2
    rows, keys = bias.shape
    vmem, any_space = (pl.BlockSpec(memory_space=space) for space in (pltpu.VMEM, pl.ANY))
    return pl.pallas_call(
        functools.partial(attention_kernel, kv, heads),
        in_specs=[vmem] * 6 + [any_space],
        out_specs=[vmem] * 2 + [any_space],
        out_shape=[
            jax.ShapeDtypeStruct((qkv.shape[0], kv * heads * HEAD_SIZE), BF16),
            jax.ShapeDtypeStruct((micro, keys, 2 * kv * HEAD_SIZE), BF16),
            jax.ShapeDtypeStruct((2 * down.shape[0], down.shape[1]), BF16),
        ],
        scratch_shapes=[
            pltpu.VMEM((micro, keys, 2 * kv * HEAD_SIZE), BF16),
            pltpu.SemaphoreType.DMA((CTX, micro)),
            pltpu.SemaphoreType.DMA((CTX, micro)),
            pltpu.SemaphoreType.DMA,
            pltpu.SemaphoreType.DMA,
            pltpu.SemaphoreType.DMA,
        ],
        compiler_params=pltpu.CompilerParams(
            collective_id=2, has_side_effects=True, vmem_limit_bytes=VMEM_LIMIT
        ),
        cost_estimate=pl.CostEstimate(flops=0, bytes_accessed=120_000_000, transcendentals=0),
        name="attention_forward",
    )(qkv, cosine, sine, gain_query, gain_key, bias, down)


def attention_back(qkv, cosine, sine, gain_query, gain_key, bias, kv_all, d_out, tall, kv):
    heads = qkv.shape[1] // HEAD_SIZE // kv - 2
    rows, keys = bias.shape
    micro, _, kv_cols = kv_all.shape
    vmem, any_space = (pl.BlockSpec(memory_space=space) for space in (pltpu.VMEM, pl.ANY))
    return pl.pallas_call(
        functools.partial(attention_back_kernel, kv, heads),
        in_specs=[vmem] * 8 + [any_space],
        out_specs=[vmem] * 2 + [any_space],
        out_shape=[
            jax.ShapeDtypeStruct(qkv.shape, BF16),
            jax.ShapeDtypeStruct((2, HEAD_SIZE), F32),
            jax.ShapeDtypeStruct(tall.shape, tall.dtype),
        ],
        scratch_shapes=[
            pltpu.VMEM((micro, keys, kv_cols), BF16),
            pltpu.VMEM((CTX - 1, micro, BLOCK, kv_cols), BF16),
            pltpu.VMEM((micro, BLOCK, kv_cols), BF16),
            pltpu.VMEM((heads * rows, keys), BF16),
            pltpu.VMEM((heads * rows, keys), BF16),
            pltpu.VMEM((heads * rows, HEAD_SIZE), BF16),
            pltpu.VMEM((heads * rows, HEAD_SIZE), BF16),
            pltpu.SemaphoreType.DMA((CTX, micro)),
            pltpu.SemaphoreType.DMA((CTX, micro)),
            pltpu.SemaphoreType.DMA,
            pltpu.SemaphoreType.DMA,
        ],
        compiler_params=pltpu.CompilerParams(
            collective_id=3, has_side_effects=True, vmem_limit_bytes=VMEM_LIMIT
        ),
        cost_estimate=pl.CostEstimate(flops=0, bytes_accessed=120_000_000, transcendentals=0),
        name="attention_backward",
    )(qkv, cosine, sine, gain_query, gain_key, bias, kv_all, d_out, tall)


def normalize(rows, gain):
    scaling = lax.rsqrt(jnp.mean(rows * rows, axis=-1, keepdims=True) + EPS)
    return rows * scaling * gain, scaling


def normalize_back(rows, scaling, gain, upstream):
    normed = rows * scaling
    gain_grad = jnp.sum((upstream * normed).reshape(-1, rows.shape[-1]), axis=0)
    scaled = upstream * gain
    inner = jnp.mean(scaled * normed, axis=-1, keepdims=True)
    return scaling * (scaled - normed * inner), gain_grad


def swap_tp(value):
    return lax.ppermute(value, "tp", [(0, 1), (1, 0)])


def local(
    x_prompt, x_cont, cot_prompt, cot_cont, ids_prompt, ids_cont, gates_prompt, gates_cont,
    norm_gain, query_weight, key_matrix, value_matrix, out_weight, query_gain, key_gain, moe_gain,
    expert_gate, expert_up, expert_down,
):
    micro = x_prompt.shape[0]
    prompt_rows, cont_rows, width = x_prompt.shape[2], x_cont.shape[2], x_prompt.shape[3]
    block = cont_rows
    rows = 2 * block
    s = lax.axis_index("ctx")
    ctx = lax.axis_size("ctx")
    first = lax.axis_index("tp") == 0
    peers = lax.axis_size(ALL)
    q_cols, kv_cols = query_weight.shape[1], key_matrix.shape[1]
    kv = kv_cols // HEAD_SIZE
    qkv_cols = q_cols + 2 * kv_cols
    shard_rows = query_weight.shape[0]
    hidden = expert_gate.shape[2]
    slots = cont_rows * TOPK // peers

    def exchange(rows_of):
        return lax.all_to_all(rows_of, ALL, split_axis=0, concat_axis=0, tiled=True)

    def pad(v):
        return jnp.pad(v[:, 0], ((0, 0), (0, block - prompt_rows), (0, 0)))

    x_first, x_second = pad(x_prompt), x_cont[:, 0]
    own_tokens = jnp.where(first, x_second, x_first).astype(F32)
    own_cot = jnp.where(first, cot_cont[:, 0], pad(cot_prompt)).astype(F32)
    ids_pad = jnp.pad(
        ids_prompt[:, 0], ((0, 0), (0, block - prompt_rows), (0, 0)), constant_values=-1
    )
    own_ids = jnp.where(first, ids_cont[:, 0], ids_pad)
    own_gates = jnp.where(first, gates_cont[:, 0], pad(gates_prompt))

    named = own_ids[:, :, :, None] == jnp.arange(peers, dtype=jnp.int32)
    chosen = jnp.any(named, axis=2)
    weight = jnp.sum(jnp.where(named, own_gates[:, :, :, None], 0.0), axis=2)
    lower = jnp.tril(jnp.ones((block, block), BF16), -1)
    rank = jnp.einsum("ts,mse->mte", lower, chosen.astype(BF16), preferred_element_type=F32)
    place = jnp.where(chosen, rank, -1.0)
    placed = place[:, :, :, None] == jnp.arange(slots, dtype=F32)
    flat = (micro, block, peers * slots)
    select = placed.astype(BF16).reshape(flat)
    mixing = jnp.where(placed, weight[:, :, :, None], 0.0).reshape(flat)
    mixing_high = mixing.astype(BF16)
    mixing_low = (mixing - mixing_high.astype(F32)).astype(BF16)
    slot_gate = jnp.sum(mixing, axis=1)

    extra = jnp.concatenate(
        [
            norm_gain[:, None],
            moe_gain[:, None],
            jnp.pad(query_gain, (0, shard_rows - query_gain.shape[0]))[:, None],
            jnp.pad(key_gain, (0, shard_rows - key_gain.shape[0]))[:, None],
            jnp.zeros((shard_rows, 124), BF16),
        ],
        axis=1,
    )
    w_qkv, w_out_extra, gu_all = gather_weights(
        jnp.concatenate([query_weight, key_matrix, value_matrix], axis=1),
        jnp.concatenate([out_weight, extra], axis=1),
        expert_gate[0],
        expert_up[0],
    )
    w_out = w_out_extra[:, :q_cols]
    gains = w_out_extra[:, q_cols:].astype(F32)
    gain_in, gain_moe = gains[:, 0], gains[:, 1]
    head_gains = gains[:, 2:4].reshape(peers, shard_rows, 2)[:, : query_gain.shape[0]]
    head_gains = head_gains.reshape(HEAD_SIZE, 2)
    gain_query, gain_key = head_gains[:, 0], head_gains[:, 1]

    cot_low, w_qkv = lax.optimization_barrier((own_cot.astype(BF16), w_qkv))
    spread = [
        (dot(select[m], cot_low[m], ((0,), (0,))) * slot_gate[m][:, None]).astype(BF16)
        for m in range(micro)
    ]
    d_eo_rows = exchange(jnp.stack(spread).reshape(micro, peers, slots, width).swapaxes(0, 1))

    offsets = jnp.arange(rows, dtype=jnp.int32)
    is_prompt = offsets < block
    prompt_pos = s * prompt_rows + offsets
    cont_pos = s * cont_rows + offsets - block
    rot_place = jnp.where(is_prompt, prompt_pos, PROMPT + cont_pos % CL).astype(F32)
    steps_freq = jnp.arange(HEAD_SIZE // 2, dtype=F32) * (2.0 / HEAD_SIZE)
    angles = rot_place[:, None] * jnp.power(THETA, -steps_freq)[None, :]
    cosine, sine = jnp.cos(angles), jnp.sin(angles)
    cosine = jnp.concatenate([cosine, cosine], axis=1)
    sine = jnp.concatenate([-sine, sine], axis=1)
    keys = (ctx + 2) * block
    key_index = jnp.arange(keys, dtype=jnp.int32)[None, :]
    key_off = key_index % block
    key_prompt_pos = key_index // block * prompt_rows + key_off
    key_cont = (s - 1) * cont_rows + key_index - ctx * block
    is_cont = jnp.logical_not(is_prompt)[:, None]
    visible = jnp.where(
        key_index < ctx * block,
        jnp.logical_and(
            key_off < prompt_rows,
            jnp.logical_or(is_cont, key_prompt_pos <= prompt_pos[:, None]),
        ),
        jnp.logical_and(
            is_cont,
            jnp.logical_and(
                key_cont // CL == cont_pos[:, None] // CL, key_cont <= cont_pos[:, None]
            ),
        ),
    )
    bias = jnp.where(visible, 0.0, NEG).astype(F32)

    def share_rows(own):
        other = swap_tp(own)
        return jnp.where(first, other, own), jnp.where(first, own, other)

    def sum_own(part):
        part = part.reshape(micro, rows, width)
        given = jnp.where(first, part[:, :block], part[:, block:]).astype(BF16)
        kept = jnp.where(first, part[:, block:], part[:, :block])
        return kept + swap_tp(given).astype(F32)

    tokens = jnp.concatenate([x_first, x_second], axis=1).astype(F32).reshape(-1, width)
    a = normalize(tokens, gain_in)[0].astype(BF16)
    qkv = dot(a, w_qkv, ((1,), (0,)))
    heads_in = (cosine, sine, gain_query[None], gain_key[None], bias)
    o, kv_all, down_all = attention(qkv, *heads_in, expert_down[0], kv, micro)
    middle = own_tokens + sum_own(dot(o, w_out, ((1,), (1,))))
    b_normed, b_scale = normalize(middle, gain_moe)
    b_low = b_normed.astype(BF16)

    got_rows, z_rows, d_gu_rows, backs = [], [], [], []
    for m in range(micro):
        got = exchange(dot(select[m], b_low[m], ((0,), (0,))).astype(BF16))
        d_eo = d_eo_rows[:, m].reshape(-1, width)
        pre = dot(got, gu_all, ((1,), (0,)))
        d_z = dot(d_eo, down_all, ((1,), (1,)))
        acts, d_gu = [], []
        for part in range(2):
            at = 2 * part * hidden
            g, u = pre[:, at : at + hidden], pre[:, at + hidden : at + 2 * hidden]
            dz = d_z[:, part * hidden : (part + 1) * hidden]
            sig = jax.nn.sigmoid(g)
            act = g * sig
            acts.append((act * u).astype(BF16))
            d_gu.append((dz * u * sig * (1.0 + g * (1.0 - sig))).astype(BF16))
            d_gu.append((dz * act).astype(BF16))
        d_gu = jnp.concatenate(d_gu, axis=1)
        backs.append(exchange(dot(d_gu, gu_all, ((1,), (1,))).astype(BF16)))
        got_rows.append(got)
        z_rows.append(jnp.concatenate(acts, axis=1))
        d_gu_rows.append(d_gu)

    rows_all = jnp.concatenate(got_rows, axis=0)
    d_eo_all = d_eo_rows.swapaxes(0, 1).reshape(-1, width)
    z_all = jnp.concatenate(z_rows, axis=0)
    d_gu_all = jnp.concatenate(d_gu_rows, axis=0)
    wide_other = dot(rows_all, d_gu_all[:, 2 * hidden :], ((0,), (0,))).astype(BF16)
    tall_other = dot(z_all[:, hidden:], d_eo_all, ((0,), (0,))).astype(BF16)
    grad_down = dot(z_all[:, :hidden], d_eo_all, ((0,), (0,)))

    d_b = jnp.stack([dot(select[m], backs[m], ((1,), (0,))) for m in range(micro)])
    middle_from, moe_total = normalize_back(middle, b_scale, gain_moe, d_b)
    d_h = own_cot + middle_from
    d_attn = jnp.concatenate(share_rows(d_h.astype(BF16)), axis=1).reshape(-1, width)

    z_late, d_attn = lax.optimization_barrier((z_all, d_attn))
    eo = dot(z_late, down_all, ((1,), (0,))).astype(BF16)
    eo_back = exchange(eo.reshape(micro, peers, slots, width).swapaxes(0, 1))
    moe_out = []
    for m in range(micro):
        term = eo_back[:, m].reshape(-1, width)
        moe_out.append(
            dot(mixing_high[m], term, ((1,), (0,))) + dot(mixing_low[m], term, ((1,), (0,)))
        )
    out_first, out_second = share_rows((middle + jnp.stack(moe_out)).astype(BF16))

    d_o = dot(d_attn, w_out, ((1,), (0,))).astype(BF16)
    grad_out = dot(d_attn, o, ((0,), (0,))).astype(BF16)
    d_qkv, head_totals, tall_there = attention_back(qkv, *heads_in, kv_all, d_o, tall_other, kv)
    input_grad = sum_own(dot(d_qkv, w_qkv, ((1,), (1,))))
    grad_qkv = dot(a, d_qkv, ((0,), (0,))).astype(BF16)
    scale_in = lax.rsqrt(jnp.mean(own_tokens * own_tokens, axis=-1, keepdims=True) + EPS)
    token_from, norm_total = normalize_back(own_tokens, scale_in, gain_in, input_grad)
    grad_first, grad_second = share_rows((d_h + token_from).astype(BF16))

    head_grads = head_totals.T.reshape(peers, -1, 2)
    head_grads = jnp.pad(head_grads, ((0, 0), (0, shard_rows - head_grads.shape[1]), (0, 0)))
    extra_grads = jnp.concatenate(
        [
            norm_total[:, None],
            moe_total[:, None],
            head_grads.reshape(-1, 2),
            jnp.zeros((peers * shard_rows, 124), F32),
        ],
        axis=1,
    ).astype(BF16)
    share, share_out, wide_there = scatter_grads(grad_qkv, grad_out, extra_grads, wide_other)
    late = lax.optimization_barrier((rows_all, d_gu_all, wide_there))
    grad_wide = [
        dot(late[0], late[1][:, n * hidden : (n + 1) * hidden], ((0,), (0,)))
        + late[2][:, n * hidden : (n + 1) * hidden].astype(F32)
        for n in range(2)
    ]
    gain_share = share_out[:, q_cols:]
    gain_share = gain_share + swap_tp(gain_share)
    head_rows = query_gain.shape[0]

    return (
        out_first[:, None, :prompt_rows],
        out_second[:, None],
        grad_first[:, None, :prompt_rows],
        grad_second[:, None],
        gain_share[:, 0],
        share[:, :q_cols],
        share[:, q_cols : q_cols + kv_cols],
        share[:, q_cols + kv_cols : qkv_cols],
        share_out[:, :q_cols],
        gain_share[:head_rows, 2],
        gain_share[:head_rows, 3],
        gain_share[:, 1],
        grad_wide[0][None],
        grad_wide[1][None],
        (grad_down + tall_there.astype(F32))[None],
    )


def solution(mesh):
    rows = P(None, "fsdp", "ctx", None)
    vector = P(("fsdp", "ctx"))
    matrix = P(("fsdp", "ctx"), "tp")
    wide = P(("fsdp", "ctx"), None, "tp")
    tall = P(("fsdp", "ctx"), "tp", None)
    in_specs = (rows,) * 8 + (vector,) + (matrix,) * 4 + (vector,) * 3 + (wide, wide, tall)
    out_specs = (rows,) * 4 + (vector,) + (matrix,) * 4 + (vector,) * 3 + (wide, wide, tall)
    return jax.shard_map(local, mesh=mesh, in_specs=in_specs, out_specs=out_specs, check_vma=False)
```

time: 3230 us -> 762 us (0.24)
  blocking collectives: 1430 us -> 0 us
  waiting for transfers between devices: 1170 us -> 108 us
  Pallas kernels: 0 us -> 378 us
  local copies, waits for them, and re-layouts: 200 us -> 31.6 us
  matrix products: 229 us -> 119 us
  starting transfers between devices: 80.9 us -> 47.9 us
  other arithmetic: 96.1 us -> 63.3 us
    psum x2 -> x0, blocking collectives: 834 us -> none  [send_back(): summed = lax.psum(partial_rows, 'tp').astype(jnp.bfloat16)]
    reduce_scatter x8 -> x0, waiting for transfers between devices: 571 us -> none  [the longest x1 369 us: reduce_grads(): lax.psum_scatter(grad_parts[1], ('fsdp', 'ctx'), scatter_dimension=0, til...]
    unnamed x2 -> x0, blocking collectives: 472 us -> none
    pallas_call x0 -> x4, Pallas kernels: none -> 378 us  [the longest x1 168 us: gather_weights(): pl.pallas_call(gather_kernel, in_specs=[any_space] * 4, out_specs=[any_sp...]
    all_gather x4 -> x0, waiting for transfers between devices: 246 us -> none  [the longest x1 145 us: local(): lax.all_gather(out_weight, ('fsdp', 'ctx'), axis=0, tiled=True)]
    all_to_all x8 -> x6, waiting for transfers between devices: 248 us -> 79.5 us  [exchange(): return lax.all_to_all(rows_of, ALL, split_axis=0, concat_axis=0, tiled=True)]
    all_gather x4 -> x0, blocking collectives: 122 us -> none  [the longest x2 61.6 us: local(): lax.all_gather(key_low[:, :prompt_rows], 'ctx', axis=1, tiled=True)]
    dot_general x54 -> x29, matrix products: 229 us -> 119 us  [the longest x28 118 us: dot(): return lax.dot_general(a, b, (dims, ((), ())), preferred_element_type=F32)]
  transfers between devices with their start and end apart: 30 -> 12, of which waited for: 16 -> 8; matrix products, arithmetic and copies ran while one was open for 14% -> 21% of each run, Pallas kernels for 0% -> 13%
where the time goes in v1:
time: 762 us; the launch traced here: 751 us
  Pallas kernels  378 us (50%)
  matrix products  119 us (16%)
  waiting for transfers between devices  108 us (14%)
  other arithmetic  63.3 us (8%)
  starting transfers between devices  47.9 us (6%)
  local copies, waits for them, and re-layouts  31.6 us (4%)
    pallas_call x1, Pallas kernels, gather_weights(): pl.pallas_call(gather_kernel, in_specs=[any_space] * 4, out_specs=[any_sp...  168 us
    dot_general x28, matrix products, dot(): return lax.dot_general(a, b, (dims, ((), ())), preferred_element_type=F32)  118 us
    pallas_call x1, Pallas kernels, scatter_grads(): pl.pallas_call(scatter_kernel, in_specs=[any_space] * 4, out_specs=[pl.Bl...  98.7 us
    all_to_all x6, waiting for transfers between devices, exchange(): return lax.all_to_all(rows_of, ALL, split_axis=0, concat_axis=0, tiled=True)  79.5 us
    pallas_call x1, Pallas kernels, attention(): pl.pallas_call(functools.partial(attention_kernel, kv, heads), in_specs=[...  56.3 us
    pallas_call x1, Pallas kernels, attention_back(): pl.pallas_call(functools.partial(attention_back_kernel, kv, heads), in_sp...  54.9 us
    all_to_all x6, starting transfers between devices, exchange(): return lax.all_to_all(rows_of, ALL, split_axis=0, concat_axis=0, tiled=True)  34.9 us
    ppermute x6, waiting for transfers between devices, swap_tp(): return lax.ppermute(value, 'tp', [(0, 1), (1, 0)])  28.9 us
  transfers between devices with their start and end apart: 12, of which 8 were waited for; matrix products, arithmetic and copies ran while one was open for 21% of the time, Pallas kernels for 13%

profile of v1, /device:TPU:0, one launch (start us, length us, event | category | flops | bytes accessed | tf_op | source)
XLA Modules:
  0.0 750.7 jit_solution(10239087556484346428)
XLA Ops:
  5.9 168.0 %gather_weights.1 = (bf16[4,2,4,2,32,2560]{5,4,3,2,1,0:T(8,128)(2,1)}, bf16[4,2,4,2,32,2176]{5,4,3,2,1,0:T(8,128)(2,1)}, bf16[2048,1536]{1,0:T(8,128)(2,1)}) custom-call(bf16[32,2560]{1,0:T(8,128)(2,1)} %pad_maximum_fusion.3.a_ref, bf16[32,2176]{1,0:T(8,128)(2,1)} %concatenate.53.b_ref, bf16[2048,384]{1,0:T(8,128)(2,1)} %bitcast.234, bf16[2048,384]{1,0:T(8,128)(2,1)} %bitcast.235), custom_call_target="tpu_custom_call" | custom-call | bytes 250000000 | tf_op jit(solution)/shard_map/gather_weights/pallas_call | solution.py:194
  179.6 9.0 %fusion.101.qkv_ref = f32[256,2560]{1,0:T(8,128)} fusion(bf16[256,2048]{1,0:T(8,128)(2,1)S(1)} %fusion.20, bf16[2048,2560]{1,0:T(8,128)(2,1)} %bitcast.255), kind=kOutput, calls=%fused_computation.229 | convolution fusion | flops 2684354560 | bytes 14155776 | tf_op jit(solution)/shard_map/dot_general | solution.py:435
  189.3 56.3 %attention_forward.1 = (bf16[256,2048]{1,0:T(8,128)(2,1)S(1)}, bf16[2,640,512]{2,1,0:T(8,128)(2,1)S(1)}, bf16[768,2048]{1,0:T(8,128)(2,1)}) custom-call(f32[256,2560]{1,0:T(8,128)} %fusion.101.qkv_ref, f32[128,128]{1,0:T(8,128)S(1)} %get-tuple-element.185.cos_ref, f32[128,128]{1,0:T(8,128)S(1)} %get-tuple-element.186.sin_ref, ...), custom_call_target="tpu_custom_call" | custom-call | bytes 120000000 | tf_op jit(solution)/shard_map/attention_forward/pallas_call | solution.py:633
  245.7 2.4 fusion.2
  258.2 6.5 collective-permute-done
  269.2 5.4 all-to-all-start.1
  288.4 2.3 maximum_bitcast_fusion
  290.7 12.6 %all-to-all-done.1 = bf16[64,8,2048]{2,1,0:T(8,128)(2,1)S(1)} async-done(((bf16[64,8,2048]{2,1,0:T(8,128)(2,1)}), bf16[64,8,2048]{2,1,0:T(8,128)(2,1)S(1)}, u32[]{:S(2)}, u32[]{:S(2)}) %all-to-all-start.1) | async-done | bytes 2097184 | tf_op jit(solution)/shard_map/all_to_all | solution.py:731
  303.3 5.7 all-to-all-start.2
  312.8 48.3 %all-to-all-done.2 = bf16[64,2,8,2048]{3,2,1,0:T(8,128)(2,1)} async-done(((bf16[64,2,8,2048]{3,2,1,0:T(8,128)(2,1)}), bf16[64,2,8,2048]{3,2,1,0:T(8,128)(2,1)}, u32[]{:S(2)}, u32[]{:S(2)}) %all-to-all-start.2) | async-done | bytes 4194336 | tf_op jit(solution)/shard_map/all_to_all | solution.py:731
  361.2 5.9 all-to-all-start
  367.1 5.7 fusion.91
  372.9 3.4 fusion.15
  378.1 7.7 %fusion.7 = bf16[64,8,2048]{2,1,0:T(8,128)(2,1)} fusion(bf16[2048,1536]{1,0:T(8,128)(2,1)} %get-tuple-element.38, bf16[512,384]{1,0:T(8,128)(2,1)S(1)} %get-tuple-element.162, bf16[512,384]{1,0:T(8,128)(2,1)S(1)} %get-tuple-element.163, bf16[512,384]{1,0:T(8,128)(2,1)S(1)} %get-tuple-element.161, bf16[512,384]{1,0:T(8,128)(2,1)S(1)} %get-tuple-element.160), kind=kOutput, calls=%fused_computation.25 | convolution fusion | flops 3228565504 | bytes 9961472 | tf_op jit(solution)/shard_map/dot_general | solution.py:435
  385.8 10.0 %all-to-all-done = bf16[64,8,2048]{2,1,0:T(8,128)(2,1)} async-done(((bf16[64,8,2048]{2,1,0:T(8,128)(2,1)}), bf16[64,8,2048]{2,1,0:T(8,128)(2,1)}, u32[]{:S(2)}, u32[]{:S(2)}) %all-to-all-start) | async-done | bytes 2097184 | tf_op jit(solution)/shard_map/all_to_all | solution.py:731
  395.7 4.7 all-to-all-start.4
  400.4 6.3 fusion.93
  406.8 3.4 fusion.16
  413.2 7.4 fusion.6
  420.6 8.6 %all-to-all-done.4 = bf16[64,8,2048]{2,1,0:T(8,128)(2,1)S(1)} async-done(((bf16[64,8,2048]{2,1,0:T(8,128)(2,1)}), bf16[64,8,2048]{2,1,0:T(8,128)(2,1)S(1)}, u32[]{:S(2)}, u32[]{:S(2)}) %all-to-all-start.4) | async-done | bytes 2097184 | tf_op jit(solution)/shard_map/all_to_all | solution.py:731
  429.2 5.8 all-to-all-start.3
  436.2 4.9 pad_maximum_fusion
  441.2 19.4 %maximum_maximum_fusion = bf16[1024,1536]{1,0:T(8,128)(2,1)S(1)} fusion(bf16[512,384]{1,0:T(8,128)(2,1)S(1)} %copy-done.49, bf16[512,384]{1,0:T(8,128)(2,1)S(1)} %copy-done.51, bf16[512,384]{1,0:T(8,128)(2,1)S(1)} %get-tuple-element.161, bf16[512,384]{1,0:T(8,128)(2,1)S(1)} %get-tuple-element.160, bf16[512,384]{1,0:T(8,128)(2,1)S(1)} %copy-done.57, ...), kind=kLoop, calls=%fused_computation.13 | loop fusion | flops 25165824 | bytes 6291456 | tf_op jit(solution)/shard_map/concatenate | solution.py:864
  460.7 6.3 convolution_convert_fusion.3.wide_ref
  468.3 2.3 convolution_bitcast_fusion.1
  474.8 2.4 collective-permute-start.1
  477.3 3.1 copy.123
  480.4 3.0 convolution_convert_fusion.8.tall_ref
  485.2 5.2 collective-permute-done.1
  491.8 6.1 fusion.10.do_ref
  498.0 54.9 %attention_backward.1 = (bf16[256,2560]{1,0:T(8,128)(2,1)S(1)}, f32[2,128]{1,0:T(2,128)S(1)}, bf16[384,2048]{1,0:T(8,128)(2,1)S(1)}) custom-call(f32[256,2560]{1,0:T(8,128)} %fusion.101.qkv_ref, f32[128,128]{1,0:T(8,128)S(1)} %get-tuple-element.185.cos_ref, f32[128,128]{1,0:T(8,128)S(1)} %copy-done.8, f32[1,128]{1,0:T(1,128)S(1)} %get-tuple-element.179.gq_ref, ...), custom_call_target="tpu_custom_call" | custom-call | bytes 120000000 | tf_op jit(solution)/shard_map/attention_backward/pallas_call | solution.py:663
  552.9 6.7 fusion.102
  560.6 2.4 collective-permute-start.3
  563.0 3.8 convolution_convert_fusion.2
  566.9 2.3 copy.136
  569.1 7.4 all-to-all-start.5
  576.6 6.6 add_bitcast_fusion
  583.1 5.6 convolution_convert_fusion
  589.8 7.3 convolution_convert_fusion.1
  597.1 2.4 fusion.47
  603.3 98.7 %scatter_grads.1 = (f32[32,2560]{1,0:T(8,128)S(1)}, f32[32,2176]{1,0:T(8,128)S(1)}, bf16[2048,768]{1,0:T(8,128)(2,1)S(1)}) custom-call(bf16[4,2,4,2,32,2560]{5,4,3,2,1,0:T(8,128)(2,1)} %bitcast.215, bf16[4,2,4,2,32,2048]{5,4,3,2,1,0:T(8,128)(2,1)} %bitcast.216, bf16[4,2,4,2,32,128]{5,4,3,2,1,0:T(8,128)(2,1)S(1)} %maximum_maximum_fusion.2.extra_ref, ...), custom_call_target="tpu_custom_call" | custom-call | bytes 250000000 | tf_op jit(solution)/shard_map/scatter_grads/pallas_call | solution.py:406
  702.0 2.7 collective-permute-start.5
  704.7 4.1 add_bitcast_fusion.2
  708.9 4.2 add_bitcast_fusion.1
  717.4 2.3 fusion.14
  727.3 2.4 collective-permute-start.4
  729.7 9.3 %collective-permute-done.2 = bf16[2,64,2048]{2,1,0:T(8,128)(2,1)S(1)} collective-permute-done((bf16[2,64,2048]{2,1,0:T(8,128)(2,1)S(1)}, bf16[2,64,2048]{2,1,0:T(8,128)(2,1)S(1)}, u32[]{:S(2)}, u32[]{:S(2)}) %collective-permute-start.2) | collective-permute-done | bytes 524320 | tf_op jit(solution)/shard_map/ppermute | solution.py:707
  740.7 7.9 %collective-permute-done.4 = bf16[2,64,2048]{2,1,0:T(8,128)(2,1)S(1)} collective-permute-done((bf16[2,64,2048]{2,1,0:T(8,128)(2,1)S(1)}, bf16[2,64,2048]{2,1,0:T(8,128)(2,1)S(1)}, u32[]{:S(2)}, u32[]{:S(2)}) %collective-permute-start.4) | collective-permute-done | bytes 524320 | tf_op jit(solution)/shard_map/ppermute | solution.py:707
  (293 shorter events, 79.1 us)
Async XLA Ops:
  176.8 11.8 %copy-start.67 = (f32[2048,1]{0,1:T(1,128)}, f32[2048,1]{0,1:T(1,128)S(1)}, u32[]{:S(2)}) copy-start(f32[2048,1]{0,1:T(1,128)S(1)} %get-tuple-element.173) | copy-start | bytes 24580
  176.8 296.1 %copy-start.65 = (f32[2048,1]{0,1:T(1,128)}, f32[2048,1]{0,1:T(1,128)S(1)}, u32[]{:S(2)}) copy-start(f32[2048,1]{0,1:T(1,128)S(1)} %get-tuple-element.172) | copy-start | bytes 24580
  179.1 107.8 %copy-start.26 = (bf16[2,64,2048]{2,1,0:T(8,128)(2,1)}, bf16[2,64,2048]{2,1,0:T(8,128)(2,1)S(1)}, u32[]{:S(2)}) copy-start(bf16[2,64,2048]{2,1,0:T(8,128)(2,1)S(1)} %bitcast_select_fusion.1) | copy-start | bytes 1572868
  179.3 66.3 %slice-start = ((s8[8912896]{0:T(1024)(128)(4,1)}), s8[4194304]{0:T(1024)(128)(4,1)S(1)}, s32[]{:S(2)}) async-start(s8[8912896]{0:T(1024)(128)(4,1)} %bitcast.248), calls=%async_computation.6 | async-start | bytes 8388608
  179.6 9.0 %copy-start.30 = (bf16[256,2048]{1,0:T(8,128)(2,1)}, bf16[256,2048]{1,0:T(8,128)(2,1)S(1)}, u32[]{:S(2)}) copy-start(bf16[256,2048]{1,0:T(8,128)(2,1)S(1)} %fusion.20) | copy-start | bytes 3145732
  179.6 9.0 %copy-start.84 = (f32[64]{0:T(128)S(1)}, f32[64]{0:T(128)}, u32[]{:S(2)}) copy-start(f32[64]{0:T(128)} %negate_power_fusion) | copy-start | bytes 772
  179.6 9.7 %copy-start = (bf16[1,384,2048]{2,1,0:T(8,128)(2,1)S(1)}, bf16[1,384,2048]{2,1,0:T(8,128)(2,1)}, u32[]{:S(2)}) copy-start(bf16[1,384,2048]{2,1,0:T(8,128)(2,1)} %param.37) | copy-start | bytes 4718596
  179.6 66.0 %slice-start.1 = ((s8[8912896]{0:T(1024)(128)(4,1)}), s8[4194304]{0:T(1024)(128)(4,1)S(1)}, s32[]{:S(2)}) async-start(s8[8912896]{0:T(1024)(128)(4,1)} %bitcast.248), calls=%async_computation.7 | async-start | bytes 8388608
  179.6 66.0 %slice-start.2 = ((s8[8912896]{0:T(1024)(128)(4,1)}), s8[524288]{0:T(1024)(128)(4,1)S(1)}, s32[]{:S(2)}) async-start(s8[8912896]{0:T(1024)(128)(4,1)} %bitcast.248), calls=%async_computation.8 | async-start | bytes 1048576
  189.0 59.0 %copy-start.7 = (f32[128,128]{1,0:T(8,128)}, f32[128,128]{1,0:T(8,128)S(1)}, u32[]{:S(2)}) copy-start(f32[128,128]{1,0:T(8,128)S(1)} %get-tuple-element.186.sin_ref) | copy-start | bytes 196612
  249.0 15.7 %collective-permute-start = (bf16[2,64,2048]{2,1,0:T(8,128)(2,1)}, bf16[2,64,2048]{2,1,0:T(8,128)(2,1)}, u32[]{:S(2)}, u32[]{:S(2)}) collective-permute-start(bf16[2,64,2048]{2,1,0:T(8,128)(2,1)} %select_convert_fusion.1), channel_id=1, source_target_pairs={{0,1},{1,0},{2,3},{3,2},{4,5},{5,4},{6,7},{7,6},{8,9},{9,8},{10,11... | collective-permute-start | bytes 1572872 | tf_op jit(solution)/shard_map/ppermute | solution.py:707
  256.2 11.0 %copy-start.41 = (pred[2,64,64,8]{1,3,2,0:T(8,128)(4,1)}, pred[2,64,64,8]{1,3,2,0:T(8,128)(4,1)S(1)}, u32[]{:S(2)}) copy-start(pred[2,64,64,8]{1,3,2,0:T(8,128)(4,1)S(1)} %iota_compare_fusion) | copy-start | bytes 196612
  258.2 9.0 %copy-start.17 = (bf16[2,64,2048]{2,1,0:T(8,128)(2,1)}, bf16[2,64,2048]{2,1,0:T(8,128)(2,1)S(1)}, u32[]{:S(2)}) copy-start(bf16[2,64,2048]{2,1,0:T(8,128)(2,1)S(1)} %get-tuple-element.153) | copy-start | bytes 1572868
  269.2 34.1 %all-to-all-start.1 = ((bf16[64,8,2048]{2,1,0:T(8,128)(2,1)}), bf16[64,8,2048]{2,1,0:T(8,128)(2,1)S(1)}, u32[]{:S(2)}, u32[]{:S(2)}) async-start(bf16[64,8,2048]{2,1,0:T(8,128)(2,1)} %fusion.5), calls=%async_computation.1 | async-start | bytes 4194304 | tf_op jit(solution)/shard_map/all_to_all | solution.py:731
  290.7 18.4 %copy-start.62 = (f32[2,64,64]{1,2,0:T(8,128)S(1)}, f32[2,64,64]{1,2,0:T(8,128)}, u32[]{:S(2)}) copy-start(f32[2,64,64]{1,2,0:T(8,128)} %copy-done.61) | copy-start | bytes 98308
  290.7 18.4 %copy-start.63 = (f32[2,64,64]{1,2,0:T(8,128)S(1)}, f32[2,64,64]{1,2,0:T(8,128)}, u32[]{:S(2)}) copy-start(f32[2,64,64]{1,2,0:T(8,128)} %copy.119) | copy-start | bytes 98308
  290.7 20.1 %copy-start.42 = (pred[2,64,64,8]{1,3,2,0:T(8,128)(4,1)S(1)}, pred[2,64,64,8]{1,3,2,0:T(8,128)(4,1)}, u32[]{:S(2)}) copy-start(pred[2,64,64,8]{1,3,2,0:T(8,128)(4,1)} %copy-done.41) | copy-start | bytes 196612
  303.3 63.8 %copy-start.20 = (bf16[64,8,2048]{2,1,0:T(8,128)(2,1)}, bf16[64,8,2048]{2,1,0:T(8,128)(2,1)S(1)}, u32[]{:S(2)}) copy-start(bf16[64,8,2048]{2,1,0:T(8,128)(2,1)S(1)} %all-to-all-done.1) | copy-start | bytes 6291460
  303.3 57.8 %all-to-all-start.2 = ((bf16[64,2,8,2048]{3,2,1,0:T(8,128)(2,1)}), bf16[64,2,8,2048]{3,2,1,0:T(8,128)(2,1)}, u32[]{:S(2)}, u32[]{:S(2)}) async-start(bf16[64,2,8,2048]{3,2,1,0:T(8,128)(2,1)} %maximum_bitcast_fusion), calls=%async_computation.2 | async-start | bytes 8388608 | tf_op jit(solution)/shard_map/all_to_all | solution.py:731
  361.2 34.6 %all-to-all-start = ((bf16[64,8,2048]{2,1,0:T(8,128)(2,1)}), bf16[64,8,2048]{2,1,0:T(8,128)(2,1)}, u32[]{:S(2)}, u32[]{:S(2)}) async-start(bf16[64,8,2048]{2,1,0:T(8,128)(2,1)} %fusion.4), calls=%async_computation | async-start | bytes 4194304 | tf_op jit(solution)/shard_map/all_to_all | solution.py:731
  378.1 7.7 %copy-start.48 = (bf16[512,384]{1,0:T(8,128)(2,1)}, bf16[512,384]{1,0:T(8,128)(2,1)S(1)}, u32[]{:S(2)}) copy-start(bf16[512,384]{1,0:T(8,128)(2,1)S(1)} %get-tuple-element.162) | copy-start | bytes 1179652
  378.1 7.7 %copy-start.50 = (bf16[512,384]{1,0:T(8,128)(2,1)}, bf16[512,384]{1,0:T(8,128)(2,1)S(1)}, u32[]{:S(2)}) copy-start(bf16[512,384]{1,0:T(8,128)(2,1)S(1)} %get-tuple-element.163) | copy-start | bytes 1179652
  395.7 33.5 %all-to-all-start.4 = ((bf16[64,8,2048]{2,1,0:T(8,128)(2,1)}), bf16[64,8,2048]{2,1,0:T(8,128)(2,1)S(1)}, u32[]{:S(2)}, u32[]{:S(2)}) async-start(bf16[64,8,2048]{2,1,0:T(8,128)(2,1)} %fusion.7), calls=%async_computation.4 | async-start | bytes 4194304 | tf_op jit(solution)/shard_map/all_to_all | solution.py:731
  420.6 14.4 %copy-start.82 = (f32[2,64]{1,0:T(2,128)S(1)}, f32[2,64]{1,0:T(2,128)}, u32[]{:S(2)}) copy-start(f32[2,64]{1,0:T(2,128)} %get-tuple-element.152) | copy-start | bytes 1540
  429.2 11.9 %copy-start.15 = (bf16[64,8,2048]{2,1,0:T(8,128)(2,1)}, bf16[64,8,2048]{2,1,0:T(8,128)(2,1)S(1)}, u32[]{:S(2)}) copy-start(bf16[64,8,2048]{2,1,0:T(8,128)(2,1)S(1)} %all-to-all-done.4) | copy-start | bytes 6291460
  429.2 39.1 %all-to-all-start.3 = ((bf16[64,8,2048]{2,1,0:T(8,128)(2,1)}), bf16[64,8,2048]{2,1,0:T(8,128)(2,1)}, u32[]{:S(2)}, u32[]{:S(2)}) async-start(bf16[64,8,2048]{2,1,0:T(8,128)(2,1)} %fusion.6), calls=%async_computation.3 | async-start | bytes 4194304 | tf_op jit(solution)/shard_map/all_to_all | solution.py:731
  441.2 19.5 %copy-start.21 = (bf16[64,8,2048]{2,1,0:T(8,128)(2,1)S(1)}, bf16[64,8,2048]{2,1,0:T(8,128)(2,1)}, u32[]{:S(2)}) copy-start(bf16[64,8,2048]{2,1,0:T(8,128)(2,1)} %copy-done.20) | copy-start | bytes 6291460
  470.7 6.5 copy-start.44
  474.8 15.6 %collective-permute-start.1 = (bf16[2,64,2048]{2,1,0:T(8,128)(2,1)}, bf16[2,64,2048]{2,1,0:T(8,128)(2,1)}, u32[]{:S(2)}, u32[]{:S(2)}) collective-permute-start(bf16[2,64,2048]{2,1,0:T(8,128)(2,1)} %fusion.97), channel_id=1, source_target_pairs={{0,1},{1,0},{2,3},{3,2},{4,5},{5,4},{6,7},{7,6},{8,9},{9,8},{10,11... | collective-permute-start | bytes 1572872 | tf_op jit(solution)/shard_map/ppermute | solution.py:707
  552.9 6.7 copy-start.1
  552.9 6.7 copy-start.4
  552.9 10.1 %copy-start.33 = (bf16[1024,768]{1,0:T(8,128)(2,1)S(1)}, bf16[1024,768]{1,0:T(8,128)(2,1)}, u32[]{:S(2)}) copy-start(bf16[1024,768]{1,0:T(8,128)(2,1)} %copy-done.32) | copy-start | bytes 4718596
  552.9 10.1 %copy-start.89 = (bf16[768,2048]{1,0:T(8,128)(2,1)S(1)}, bf16[768,2048]{1,0:T(8,128)(2,1)}, u32[]{:S(2)}) copy-start(bf16[768,2048]{1,0:T(8,128)(2,1)} %get-tuple-element.40) | copy-start | bytes 9437188
  559.6 7.2 copy-start.34
  560.6 36.4 %collective-permute-start.3 = (bf16[2,64,2048]{2,1,0:T(8,128)(2,1)}, bf16[2,64,2048]{2,1,0:T(8,128)(2,1)}, u32[]{:S(2)}, u32[]{:S(2)}) collective-permute-start(bf16[2,64,2048]{2,1,0:T(8,128)(2,1)} %select_convert_fusion), channel_id=1, source_target_pairs={{0,1},{1,0},{2,3},{3,2},{4,5},{5,4},{6,7},{7,6},{8,9},{9,8},{10,11... | collective-permute-start | bytes 1572872 | tf_op jit(solution)/shard_map/ppermute | solution.py:707
  569.1 143.9 %all-to-all-start.5 = ((bf16[64,2,8,2048]{3,2,1,0:T(8,128)(2,1)}), bf16[64,2,8,2048]{3,2,1,0:T(8,128)(2,1)}, u32[]{:S(2)}, u32[]{:S(2)}) async-start(bf16[64,2,8,2048]{3,2,1,0:T(8,128)(2,1)} %bitcast.219), calls=%async_computation.5 | async-start | bytes 8388608 | tf_op jit(solution)/shard_map/all_to_all | solution.py:731
  576.6 6.6 copy-start.5
  576.6 6.6 copy-start.31
  589.8 7.3 copy-start.18
  589.8 7.3 copy-start.35
  589.8 7.3 copy-start.68
  589.8 7.3 copy-start.76
  603.2 101.5 %copy-start.37 = (bf16[1024,2048]{1,0:T(8,128)(2,1)S(1)}, bf16[1024,2048]{1,0:T(8,128)(2,1)}, u32[]{:S(2)}) copy-start(bf16[1024,2048]{1,0:T(8,128)(2,1)} %pad_maximum_fusion) | copy-start | bytes 12582916
  603.2 101.5 %copy-start.40 = (bf16[1024,1536]{1,0:T(8,128)(2,1)S(1)}, bf16[1024,1536]{1,0:T(8,128)(2,1)}, u32[]{:S(2)}) copy-start(bf16[1024,1536]{1,0:T(8,128)(2,1)} %copy-done.39) | copy-start | bytes 9437188
  702.0 6.9 copy-start.9
  702.0 23.9 %collective-permute-start.5 = (f32[32,128]{1,0:T(8,128)S(1)}, f32[32,128]{1,0:T(8,128)S(1)}, u32[]{:S(2)}, u32[]{:S(2)}) collective-permute-start(f32[32,128]{1,0:T(8,128)S(1)} %slice.230), channel_id=1, source_target_pairs={{0,1},{1,0},{2,3},{3,2},{4,5},{5,4},{6,7},{7,6},{8,9},{9,8},{10,11... | collective-permute-start | bytes 49160 | tf_op jit(solution)/shard_map/ppermute | solution.py:707
  722.6 16.4 %collective-permute-start.2 = (bf16[2,64,2048]{2,1,0:T(8,128)(2,1)S(1)}, bf16[2,64,2048]{2,1,0:T(8,128)(2,1)S(1)}, u32[]{:S(2)}, u32[]{:S(2)}) collective-permute-start(bf16[2,64,2048]{2,1,0:T(8,128)(2,1)S(1)} %get-tuple-element.169), channel_id=1, source_target_pairs={{0,1},{1,0},{2,3},{3,2},{4,5},{5,4},{6,7},{7,6},{8,9},{9,8},{10,11... | collective-permute-start | bytes 1572872 | tf_op jit(solution)/shard_map/ppermute | solution.py:707
  727.3 21.3 %collective-permute-start.4 = (bf16[2,64,2048]{2,1,0:T(8,128)(2,1)S(1)}, bf16[2,64,2048]{2,1,0:T(8,128)(2,1)S(1)}, u32[]{:S(2)}, u32[]{:S(2)}) collective-permute-start(bf16[2,64,2048]{2,1,0:T(8,128)(2,1)S(1)} %get-tuple-element.168), channel_id=1, source_target_pairs={{0,1},{1,0},{2,3},{3,2},{4,5},{5,4},{6,7},{7,6},{8,9},{9,8},{10,11... | collective-permute-start | bytes 1572872 | tf_op jit(solution)/shard_map/ppermute | solution.py:707
  (59 other events, 245.4 us)

commit v2 on v1

--- a/solution.py
+++ b/solution.py
@@ -55,28 +55,38 @@
     return {"tp": 1 - lax.axis_index("tp")}
 
 
-def swap_halves(src, dst, send_sem, recv_sem):
+def opposite():
+    f = lax.axis_index("fsdp")
+    return {"fsdp": f + 1 - 2 * (f % 2), "tp": 1 - lax.axis_index("tp")}
+
+
+def native():
+    return lax.axis_index("fsdp") % 2 == lax.axis_index("tp")
+
+
+def swap_opposite(src, dst, send_sem, recv_sem):
     return pltpu.make_async_remote_copy(
-        src_ref=src, dst_ref=dst, send_sem=send_sem, recv_sem=recv_sem, device_id=other_tp(),
+        src_ref=src, dst_ref=dst, send_sem=send_sem, recv_sem=recv_sem, device_id=opposite(),
         device_id_type=MESH,
     )
 
 
 def gather_kernel(
-    a_ref, b_ref, gate_ref, up_ref, a_all, b_all, wide_all,
+    a_ref, b_ref, gate_ref, up_ref, down_ref, a_all, b_all, wide_all, tall_all,
     local_sem, send_sem, recv_sem, away_sem, home_sem, keep_sem, give_sem, take_sem,
 ):
     y, core, z, x = place()
-    greet(neighbours() + [other_tp()])
+    greet(neighbours() + [opposite()])
     hidden = gate_ref.shape[1]
-    wide = []
-    for n, ref in enumerate((gate_ref, up_ref)):
-        own_cols = wide_all.at[:, pl.ds(n * hidden, hidden)]
-        far_cols = wide_all.at[:, pl.ds((2 + n) * hidden, hidden)]
-        wide.append(pltpu.make_async_copy(ref, own_cols, keep_sem.at[n]))
-        wide.append(swap_halves(ref, far_cols, give_sem.at[n], take_sem.at[n]))
-    for copy in wide:
-        copy.start()
+    shards = (
+        (gate_ref, wide_all.at[:, pl.ds(0, hidden)]),
+        (up_ref, wide_all.at[:, pl.ds(hidden, hidden)]),
+        (down_ref, tall_all),
+    )
+    kept = [pltpu.make_async_copy(p, q, keep_sem.at[n]) for n, (p, q) in enumerate(shards)]
+    moved = [
+        swap_opposite(p, q, give_sem.at[n], take_sem.at[n]) for n, (p, q) in enumerate(shards)
+    ]
     refs, own = (a_all, b_all), (a_ref, b_ref)
     started = []
     count = [0, 0]
@@ -143,6 +153,17 @@
     for n in (0, 1):
         i, j = me[n]
         second(n, i, j, 0)
+
+    @pl.when(native())
+    def _():
+        for copy in kept:
+            copy.start()
+
+    @pl.when(jnp.logical_not(native()))
+    def _():
+        for copy in moved:
+            copy.start()
+
     for n in (0, 1):
         i, j = me[n]
         arrived(n, chunk(n, down(i), j), 1)
@@ -183,35 +204,46 @@
         copy.wait()
     for copy in started:
         copy.wait_send()
-    for copy in wide:
-        copy.wait()
-
-
-def gather_weights(a, b, gate, up):
+
+    @pl.when(native())
+    def _():
+        for copy in kept:
+            copy.wait()
+
+    @pl.when(jnp.logical_not(native()))
+    def _():
+        for copy in moved:
+            copy.wait()
+
+
+def gather_weights(a, b, gate, up, down):
     rows = a.shape[0]
     shape = (RING, 2, RING, 2, rows)
     any_space = pl.BlockSpec(memory_space=pl.ANY)
-    a_all, b_all, wide = pl.pallas_call(
+    a_all, b_all, wide, tall = pl.pallas_call(
         gather_kernel,
-        in_specs=[any_space] * 4,
-        out_specs=[any_space] * 3,
+        in_specs=[any_space] * 5,
+        out_specs=[any_space] * 4,
         out_shape=[jax.ShapeDtypeStruct(shape + (v.shape[1],), v.dtype) for v in (a, b)]
-        + [jax.ShapeDtypeStruct((gate.shape[0], 4 * gate.shape[1]), gate.dtype)],
+        + [
+            jax.ShapeDtypeStruct((gate.shape[0], 2 * gate.shape[1]), gate.dtype),
+            jax.ShapeDtypeStruct(down.shape, down.dtype),
+        ],
         scratch_shapes=[
             pltpu.SemaphoreType.DMA((2,)),
             pltpu.SemaphoreType.DMA((2, 21)),
             pltpu.SemaphoreType.DMA((2, 21)),
             pltpu.SemaphoreType.DMA((2, 16)),
             pltpu.SemaphoreType.DMA((2, 16)),
-            pltpu.SemaphoreType.DMA((2,)),
-            pltpu.SemaphoreType.DMA((2,)),
-            pltpu.SemaphoreType.DMA((2,)),
+            pltpu.SemaphoreType.DMA((3,)),
+            pltpu.SemaphoreType.DMA((3,)),
+            pltpu.SemaphoreType.DMA((3,)),
         ],
         compiler_params=pltpu.CompilerParams(collective_id=0, has_side_effects=True),
         cost_estimate=pl.CostEstimate(flops=0, bytes_accessed=250_000_000, transcendentals=0),
         name="gather_weights",
-    )(a, b, gate, up)
-    return a_all.reshape(-1, a.shape[1]), b_all.reshape(-1, b.shape[1]), wide
+    )(a, b, gate, up, down)
+    return a_all.reshape(-1, a.shape[1]), b_all.reshape(-1, b.shape[1]), wide, tall
 
 
 ORDER = (2, 1, 3, 0)
@@ -239,14 +271,23 @@
 
 
 def scatter_kernel(
-    a_ref, b_ref, extra_ref, wide_ref, a_out, b_out, wide_out, a_mine, b_mine, a_theirs, b_theirs, a_one, b_one, a_two, b_two,
+    a_ref, b_ref, extra_ref, wide_ref, tall_ref, a_out, b_out, wide_out, tall_out, a_mine, b_mine, a_theirs, b_theirs, a_one, b_one, a_two, b_two,
     a_first, b_first, a_last, b_last, a_x, b_x, load_sem, send_sem, recv_sem,
-    extra_load_sem, extra_send_sem, extra_recv_sem, give_sem, take_sem,
+    gains_here, gains_there,
+    extra_load_sem, extra_send_sem, extra_recv_sem, give_sem, take_sem, gains_sem,
 ):
     y, core, z, x = place()
-    greet(neighbours() + [other_tp()])
-    wide = swap_halves(wide_ref, wide_out, give_sem, take_sem)
-    wide.start()
+    greet(neighbours() + [other_tp(), opposite()])
+    moved = [
+        swap_opposite(wide_ref, wide_out, give_sem.at[0], take_sem.at[0]),
+        swap_opposite(tall_ref, tall_out, give_sem.at[1], take_sem.at[1]),
+    ]
+
+    @pl.when(jnp.logical_not(native()))
+    def _():
+        for copy in moved:
+            copy.start()
+
     grads, outs = (a_ref, b_ref), (a_out, b_out)
     mine, theirs = (a_mine, b_mine), (a_theirs, b_theirs)
     one, two = (a_one, b_one), (a_two, b_two)
@@ -387,14 +428,26 @@
     for n in (0, 1):
         arrived(n, side[n], 36)
         add_into(outs[n], mine[n].at[0, x], side[n])
+    gains_here[...] = b_out[:, cols:]
+    gains = pltpu.make_async_remote_copy(
+        src_ref=gains_here, dst_ref=gains_there, send_sem=gains_sem.at[0],
+        recv_sem=gains_sem.at[1], device_id=other_tp(), device_id_type=MESH,
+    )
+    gains.start()
     for copy in sent:
         copy.wait_send()
     for slot in range(RING * RING):
         extra_copy(slot).wait_send()
-    wide.wait()
-
-
-def scatter_grads(a, b, extra, wide):
+    gains.wait()
+    b_out[:, cols:] = gains_here[...] + gains_there[...]
+
+    @pl.when(jnp.logical_not(native()))
+    def _():
+        for copy in moved:
+            copy.wait()
+
+
+def scatter_grads(a, b, extra, wide, tall):
     peers = RING * RING * 4
     rows = a.shape[0] // peers
     shape = (RING, 2, RING, 2, rows)
@@ -405,26 +458,29 @@
     any_space = pl.BlockSpec(memory_space=pl.ANY)
     return pl.pallas_call(
         scatter_kernel,
-        in_specs=[any_space] * 4,
-        out_specs=[pl.BlockSpec(memory_space=pltpu.VMEM)] * 2 + [any_space],
+        in_specs=[any_space] * 5,
+        out_specs=[pl.BlockSpec(memory_space=pltpu.VMEM)] * 2 + [any_space] * 2,
         out_shape=[jax.ShapeDtypeStruct((rows, c), F32) for c in cols]
-        + [jax.ShapeDtypeStruct(wide.shape, wide.dtype)],
+        + [jax.ShapeDtypeStruct(v.shape, v.dtype) for v in (wide, tall)],
         scratch_shapes=buffers + [
             pltpu.SemaphoreType.DMA((2, 16)),
             pltpu.SemaphoreType.DMA((2, 37)),
             pltpu.SemaphoreType.DMA((2, 37)),
+            pltpu.VMEM((rows, extra.shape[1]), F32),
+            pltpu.VMEM((rows, extra.shape[1]), F32),
             pltpu.SemaphoreType.DMA((16,)),
             pltpu.SemaphoreType.DMA((16,)),
             pltpu.SemaphoreType.DMA((16,)),
-            pltpu.SemaphoreType.DMA,
-            pltpu.SemaphoreType.DMA,
+            pltpu.SemaphoreType.DMA((2,)),
+            pltpu.SemaphoreType.DMA((2,)),
+            pltpu.SemaphoreType.DMA((2,)),
         ],
         compiler_params=pltpu.CompilerParams(
             collective_id=1, has_side_effects=True, vmem_limit_bytes=44 * 1024 * 1024
         ),
         cost_estimate=pl.CostEstimate(flops=0, bytes_accessed=250_000_000, transcendentals=0),
         name="scatter_grads",
-    )(*(v.reshape(shape + (v.shape[1],)) for v in (a, b, extra)), wide)
+    )(*(v.reshape(shape + (v.shape[1],)) for v in (a, b, extra)), wide, tall)
 
 
 BLOCK = 64
@@ -473,14 +529,11 @@
 
 
 def attention_kernel(
-    kv, heads, qkv_ref, cos_ref, sin_ref, gq_ref, gk_ref, bias_ref, down_ref, o_ref, kv_ref, tall_ref,
-    held, send_sem, recv_sem, keep_sem, give_sem, take_sem,
+    kv, heads, qkv_ref, cos_ref, sin_ref, gq_ref, gk_ref, bias_ref, o_ref, kv_ref, held,
+    send_sem, recv_sem,
 ):
     c = lax.axis_index("ctx")
-    greet([ctx_peer(step) for step in range(1, CTX)] + [other_tp()])
-    half = down_ref.shape[0]
-    keep = pltpu.make_async_copy(down_ref, tall_ref.at[pl.ds(0, half)], keep_sem)
-    tall = swap_halves(down_ref, tall_ref.at[pl.ds(half, half)], give_sem, take_sem)
+    greet([ctx_peer(step) for step in range(1, CTX)])
     micro, rows = held.shape[0], 2 * BLOCK
     q_cols = kv * heads * HEAD_SIZE
     cosine, sine, gq, gk = cos_ref[...], sin_ref[...], gq_ref[...], gk_ref[...]
@@ -507,8 +560,6 @@
         )
         for copy in copies[-CTX:]:
             copy.start()
-    keep.start()
-    tall.start()
 
     def group(m, h, carry):
         span = slice(m * rows, (m + 1) * rows)
@@ -533,19 +584,15 @@
     kv_ref[...] = held[...]
     for copy in copies:
         copy.wait_send()
-    keep.wait()
-    tall.wait()
 
 
 def attention_back_kernel(
-    kv, heads, qkv_ref, cos_ref, sin_ref, gq_ref, gk_ref, bias_ref, kv_ref, do_ref, tall_ref,
-    dqkv_ref, gains_ref, tall_out, grads, given, given_side, p_all, ds_all, q_all, do_all,
-    send_sem, recv_sem, give_sem, take_sem,
+    kv, heads, qkv_ref, cos_ref, sin_ref, gq_ref, gk_ref, bias_ref, kv_ref, do_ref,
+    dqkv_ref, gains_ref, grads, given, given_side, p_all, ds_all, q_all, do_all,
+    send_sem, recv_sem,
 ):
     c = lax.axis_index("ctx")
-    greet([ctx_peer(step) for step in range(1, CTX)] + [other_tp()])
-    tall = swap_halves(tall_ref, tall_out, give_sem, take_sem)
-    tall.start()
+    greet([ctx_peer(step) for step in range(1, CTX)])
     micro, rows = grads.shape[0], 2 * BLOCK
     q_cols = kv * heads * HEAD_SIZE
     scale = HEAD_SIZE ** -0.5
@@ -623,51 +670,39 @@
     gains_ref[1:2, :] = k_total
     for copy in copies:
         copy.wait_send()
-    tall.wait()
-
-
-def attention(qkv, cosine, sine, gain_query, gain_key, bias, down, kv, micro):
+
+
+def attention(qkv, cosine, sine, gain_query, gain_key, bias, kv, micro):
     heads = qkv.shape[1] // HEAD_SIZE // kv - 2
     rows, keys = bias.shape
-    vmem, any_space = (pl.BlockSpec(memory_space=space) for space in (pltpu.VMEM, pl.ANY))
     return pl.pallas_call(
         functools.partial(attention_kernel, kv, heads),
-        in_specs=[vmem] * 6 + [any_space],
-        out_specs=[vmem] * 2 + [any_space],
         out_shape=[
             jax.ShapeDtypeStruct((qkv.shape[0], kv * heads * HEAD_SIZE), BF16),
             jax.ShapeDtypeStruct((micro, keys, 2 * kv * HEAD_SIZE), BF16),
-            jax.ShapeDtypeStruct((2 * down.shape[0], down.shape[1]), BF16),
         ],
         scratch_shapes=[
             pltpu.VMEM((micro, keys, 2 * kv * HEAD_SIZE), BF16),
             pltpu.SemaphoreType.DMA((CTX, micro)),
             pltpu.SemaphoreType.DMA((CTX, micro)),
-            pltpu.SemaphoreType.DMA,
-            pltpu.SemaphoreType.DMA,
-            pltpu.SemaphoreType.DMA,
         ],
         compiler_params=pltpu.CompilerParams(
             collective_id=2, has_side_effects=True, vmem_limit_bytes=VMEM_LIMIT
         ),
         cost_estimate=pl.CostEstimate(flops=0, bytes_accessed=120_000_000, transcendentals=0),
         name="attention_forward",
-    )(qkv, cosine, sine, gain_query, gain_key, bias, down)
-
-
-def attention_back(qkv, cosine, sine, gain_query, gain_key, bias, kv_all, d_out, tall, kv):
+    )(qkv, cosine, sine, gain_query, gain_key, bias)
+
+
+def attention_back(qkv, cosine, sine, gain_query, gain_key, bias, kv_all, d_out, kv):
     heads = qkv.shape[1] // HEAD_SIZE // kv - 2
     rows, keys = bias.shape
     micro, _, kv_cols = kv_all.shape
-    vmem, any_space = (pl.BlockSpec(memory_space=space) for space in (pltpu.VMEM, pl.ANY))
     return pl.pallas_call(
         functools.partial(attention_back_kernel, kv, heads),
-        in_specs=[vmem] * 8 + [any_space],
-        out_specs=[vmem] * 2 + [any_space],
         out_shape=[
             jax.ShapeDtypeStruct(qkv.shape, BF16),
             jax.ShapeDtypeStruct((2, HEAD_SIZE), F32),
-            jax.ShapeDtypeStruct(tall.shape, tall.dtype),
         ],
         scratch_shapes=[
             pltpu.VMEM((micro, keys, kv_cols), BF16),
@@ -679,15 +714,151 @@
             pltpu.VMEM((heads * rows, HEAD_SIZE), BF16),
             pltpu.SemaphoreType.DMA((CTX, micro)),
             pltpu.SemaphoreType.DMA((CTX, micro)),
-            pltpu.SemaphoreType.DMA,
-            pltpu.SemaphoreType.DMA,
         ],
         compiler_params=pltpu.CompilerParams(
             collective_id=3, has_side_effects=True, vmem_limit_bytes=VMEM_LIMIT
         ),
         cost_estimate=pl.CostEstimate(flops=0, bytes_accessed=120_000_000, transcendentals=0),
         name="attention_backward",
-    )(qkv, cosine, sine, gain_query, gain_key, bias, kv_all, d_out, tall)
+    )(qkv, cosine, sine, gain_query, gain_key, bias, kv_all, d_out)
+
+
+PART = 256
+
+
+def other_core():
+    f = lax.axis_index("fsdp")
+    return {"fsdp": f + 1 - 2 * (f % 2)}
+
+
+def expert_kernel(
+    got_ref, deo_ref, gu_ref, down_ref, back_ref, eo_ref, rows_ref, deos_ref, z_ref, dgu_ref,
+    rows, deos, gu, down, own, give, take, load_sem, send_sem, recv_sem, save_sem,
+):
+    greet([other_core()])
+    count, hidden = got_ref.shape[0], down_ref.shape[0]
+    parts = count // PART
+    near, far = pl.ds(0, count), pl.ds(count, count)
+    swaps = [
+        remote(got_ref, rows.at[far], send_sem.at[0], recv_sem.at[0], other_core()),
+        remote(deo_ref, deos.at[far], send_sem.at[1], recv_sem.at[1], other_core()),
+    ]
+    loads = [
+        pltpu.make_async_copy(src, dst, load_sem.at[n])
+        for n, (src, dst) in enumerate(
+            ((got_ref, rows.at[near]), (gu_ref, gu), (deo_ref, deos.at[near]), (down_ref, down))
+        )
+    ]
+    saves = [
+        pltpu.make_async_copy(rows, rows_ref, save_sem.at[0]),
+        pltpu.make_async_copy(deos, deos_ref, save_sem.at[1]),
+    ]
+    for copy in loads + swaps:
+        copy.start()
+
+    def span(i):
+        return pl.ds(pl.multiple_of(i * PART, PART), PART)
+
+    def returned(kind, i):
+        slot = kind * parts + i
+        return remote(
+            give.at[kind, span(i)], take.at[kind, span(i)], send_sem.at[2 + slot],
+            recv_sem.at[2 + slot], other_core(),
+        )
+
+    def through(i):
+        pre = dot(rows[span(i), :], gu[...], ((1,), (0,)))
+        dz = dot(deos[span(i), :], down[...], ((1,), (1,)))
+        g, u = pre[:, :hidden], pre[:, hidden:]
+        sig = 1.0 / (1.0 + jnp.exp(-g))
+        act = g * sig
+        z_ref[span(i), :] = (act * u).astype(BF16)
+        dgu_ref[span(i), :hidden] = (dz * u * sig * (1.0 + g * (1.0 - sig))).astype(BF16)
+        dgu_ref[span(i), hidden:] = (dz * act).astype(BF16)
+
+    def to_rows(i):
+        return dot(dgu_ref[span(i), :], gu[...], ((1,), (1,)))
+
+    def to_outputs(i):
+        return dot(z_ref[span(i), :], down[...], ((1,), (0,)))
+
+    def each(body):
+        def step(i, carry):
+            body(i)
+            return carry
+
+        lax.fori_loop(0, parts, step, 0)
+
+    def give_rows(i):
+        through(parts + i)
+        give[0, span(i), :] = to_rows(parts + i).astype(BF16)
+        returned(0, i).start()
+
+    def keep_rows(i):
+        own[span(i), :] = to_rows(i)
+
+    def give_outputs(i):
+        give[1, span(i), :] = to_outputs(parts + i).astype(BF16)
+        returned(1, i).start()
+
+    def end_rows(i):
+        returned(0, i).wait()
+        back_ref[span(i), :] = (own[span(i), :] + take[0, span(i), :].astype(F32)).astype(BF16)
+
+    def end_outputs(i):
+        total = to_outputs(i)
+        returned(1, i).wait()
+        eo_ref[span(i), :] = (total + take[1, span(i), :].astype(F32)).astype(BF16)
+
+    for copy in loads:
+        copy.wait()
+    each(through)
+    for copy in swaps:
+        copy.wait_recv()
+    for copy in saves:
+        copy.start()
+    each(give_rows)
+    each(give_outputs)
+    each(keep_rows)
+    each(end_rows)
+    each(end_outputs)
+    for copy in swaps:
+        copy.wait_send()
+    for copy in saves:
+        copy.wait()
+
+
+def expert(got, d_eo, gu, down, collective):
+    count, width = got.shape
+    hidden = down.shape[0]
+    parts = count // PART
+    vmem, any_space = (pl.BlockSpec(memory_space=space) for space in (pltpu.VMEM, pl.ANY))
+    shapes = [(count, width), (count, width), (2 * count, width), (2 * count, width)]
+    shapes += [(2 * count, hidden), (2 * count, 2 * hidden)]
+    return pl.pallas_call(
+        expert_kernel,
+        in_specs=[any_space] * 4,
+        out_specs=[vmem] * 2 + [any_space] * 2 + [vmem] * 2,
+        out_shape=[jax.ShapeDtypeStruct(shape, BF16) for shape in shapes],
+        scratch_shapes=[
+            pltpu.VMEM((2 * count, width), BF16),
+            pltpu.VMEM((2 * count, width), BF16),
+            pltpu.VMEM(gu.shape, BF16),
+            pltpu.VMEM(down.shape, BF16),
+            pltpu.VMEM((count, width), F32),
+            pltpu.VMEM((2, count, width), BF16),
+            pltpu.VMEM((2, count, width), BF16),
+            pltpu.SemaphoreType.DMA((4,)),
+            pltpu.SemaphoreType.DMA((2 + 2 * parts,)),
+            pltpu.SemaphoreType.DMA((2 + 2 * parts,)),
+            pltpu.SemaphoreType.DMA((2,)),
+        ],
+        compiler_params=pltpu.CompilerParams(
+            collective_id=collective, has_side_effects=True, vmem_limit_bytes=VMEM_LIMIT
+        ),
+        cost_estimate=pl.CostEstimate(flops=0, bytes_accessed=80_000_000, transcendentals=0),
+        name="expert_both_ways",
+    )(got, d_eo, gu, down)
 
 
 def normalize(rows, gain):
@@ -727,8 +898,16 @@
     hidden = expert_gate.shape[2]
     slots = cont_rows * TOPK // peers
 
+    fsdp, tp = lax.axis_size("fsdp"), lax.axis_size("tp")
+    chips = [(2 * y, c, t) for y in range(fsdp // 2) for c in range(ctx) for t in range(tp)]
+    groups = [[((f + core) * ctx + c) * tp + t for f, c, t in chips] for core in range(2)]
+    expert_of = jnp.array([(f + t) * ctx + c for f, c, t in chips], jnp.int32)
+
     def exchange(rows_of):
-        return lax.all_to_all(rows_of, ALL, split_axis=0, concat_axis=0, tiled=True)
+        return lax.all_to_all(
+            rows_of, ("fsdp", "ctx", "tp"), split_axis=0, concat_axis=0, tiled=True,
+            axis_index_groups=groups,
+        )
 
     def pad(v):
         return jnp.pad(v[:, 0], ((0, 0), (0, block - prompt_rows), (0, 0)))
@@ -742,19 +921,22 @@
     own_ids = jnp.where(first, ids_cont[:, 0], ids_pad)
     own_gates = jnp.where(first, gates_cont[:, 0], pad(gates_prompt))
 
-    named = own_ids[:, :, :, None] == jnp.arange(peers, dtype=jnp.int32)
+    named = own_ids[:, :, :, None] == expert_of
     chosen = jnp.any(named, axis=2)
     weight = jnp.sum(jnp.where(named, own_gates[:, :, :, None], 0.0), axis=2)
     lower = jnp.tril(jnp.ones((block, block), BF16), -1)
     rank = jnp.einsum("ts,mse->mte", lower, chosen.astype(BF16), preferred_element_type=F32)
     place = jnp.where(chosen, rank, -1.0)
     placed = place[:, :, :, None] == jnp.arange(slots, dtype=F32)
-    flat = (micro, block, peers * slots)
-    select = placed.astype(BF16).reshape(flat)
-    mixing = jnp.where(placed, weight[:, :, :, None], 0.0).reshape(flat)
+    select = placed.astype(BF16).reshape(micro, block, peers * slots)
+    same = jnp.arange(micro)[:, None] == jnp.arange(micro)[None, :]
+    both = jnp.logical_and(placed[:, :, :, None, :], same[:, None, None, :, None])
+    flat = (micro * block, peers * micro * slots)
+    select_both = both.astype(BF16).reshape(flat)
+    mixing = jnp.where(both, weight[:, :, :, None, None], 0.0).reshape(flat)
     mixing_high = mixing.astype(BF16)
     mixing_low = (mixing - mixing_high.astype(F32)).astype(BF16)
-    slot_gate = jnp.sum(mixing, axis=1)
+    slot_gate = jnp.sum(mixing, axis=0)
 
     extra = jnp.concatenate(
         [
@@ -766,11 +948,12 @@
         ],
         axis=1,
     )
-    w_qkv, w_out_extra, gu_all = gather_weights(
+    w_qkv, w_out_extra, gu, down = gather_weights(
         jnp.concatenate([query_weight, key_matrix, value_matrix], axis=1),
         jnp.concatenate([out_weight, extra], axis=1),
         expert_gate[0],
         expert_up[0],
+        expert_down[0],
     )
     w_out = w_out_extra[:, :q_cols]
     gains = w_out_extra[:, q_cols:].astype(F32)
@@ -780,11 +963,8 @@
     gain_query, gain_key = head_gains[:, 0], head_gains[:, 1]
 
     cot_low, w_qkv = lax.optimization_barrier((own_cot.astype(BF16), w_qkv))
-    spread = [
-        (dot(select[m], cot_low[m], ((0,), (0,))) * slot_gate[m][:, None]).astype(BF16)
-        for m in range(micro)
-    ]
-    d_eo_rows = exchange(jnp.stack(spread).reshape(micro, peers, slots, width).swapaxes(0, 1))
+    spread = dot(select_both, cot_low.reshape(-1, width), ((0,), (0,))) * slot_gate[:, None]
+    d_eo_rows = exchange(spread.astype(BF16))
 
     offsets = jnp.arange(rows, dtype=jnp.int32)
     is_prompt = offsets < block
@@ -831,60 +1011,43 @@
     a = normalize(tokens, gain_in)[0].astype(BF16)
     qkv = dot(a, w_qkv, ((1,), (0,)))
     heads_in = (cosine, sine, gain_query[None], gain_key[None], bias)
-    o, kv_all, down_all = attention(qkv, *heads_in, expert_down[0], kv, micro)
+    o, kv_all = attention(qkv, *heads_in, kv, micro)
     middle = own_tokens + sum_own(dot(o, w_out, ((1,), (1,))))
     b_normed, b_scale = normalize(middle, gain_moe)
     b_low = b_normed.astype(BF16)
 
-    got_rows, z_rows, d_gu_rows, backs = [], [], [], []
+    b_low, d_eo_rows = lax.optimization_barrier((b_low, d_eo_rows))
+    d_eo_rows = d_eo_rows.reshape(peers, micro, slots, width)
+    backs, outputs, wide_terms, tall_terms = [], [], [], []
     for m in range(micro):
         got = exchange(dot(select[m], b_low[m], ((0,), (0,))).astype(BF16))
-        d_eo = d_eo_rows[:, m].reshape(-1, width)
-        pre = dot(got, gu_all, ((1,), (0,)))
-        d_z = dot(d_eo, down_all, ((1,), (1,)))
-        acts, d_gu = [], []
-        for part in range(2):
-            at = 2 * part * hidden
-            g, u = pre[:, at : at + hidden], pre[:, at + hidden : at + 2 * hidden]
-            dz = d_z[:, part * hidden : (part + 1) * hidden]
-            sig = jax.nn.sigmoid(g)
-            act = g * sig
-            acts.append((act * u).astype(BF16))
-            d_gu.append((dz * u * sig * (1.0 + g * (1.0 - sig))).astype(BF16))
-            d_gu.append((dz * act).astype(BF16))
-        d_gu = jnp.concatenate(d_gu, axis=1)
-        backs.append(exchange(dot(d_gu, gu_all, ((1,), (1,))).astype(BF16)))
-        got_rows.append(got)
-        z_rows.append(jnp.concatenate(acts, axis=1))
-        d_gu_rows.append(d_gu)
-
-    rows_all = jnp.concatenate(got_rows, axis=0)
-    d_eo_all = d_eo_rows.swapaxes(0, 1).reshape(-1, width)
-    z_all = jnp.concatenate(z_rows, axis=0)
-    d_gu_all = jnp.concatenate(d_gu_rows, axis=0)
-    wide_other = dot(rows_all, d_gu_all[:, 2 * hidden :], ((0,), (0,))).astype(BF16)
-    tall_other = dot(z_all[:, hidden:], d_eo_all, ((0,), (0,))).astype(BF16)
-    grad_down = dot(z_all[:, :hidden], d_eo_all, ((0,), (0,)))
+        back, eo, rows_m, d_eo_m, z_m, d_gu_m = expert(
+            got, d_eo_rows[:, m].reshape(-1, width), gu, down, 4 + m
+        )
+        backs.append(exchange(back))
+        outputs.append(eo.reshape(peers, slots, width))
+        wide_terms.append((rows_m, d_gu_m))
+        tall_terms.append((z_m, d_eo_m))
+
+    def over_rows(terms):
+        return sum(dot(left, right, ((0,), (0,))) for left, right in terms).astype(BF16)
+
+    wide_here, tall_here = over_rows(wide_terms), over_rows(tall_terms)
 
     d_b = jnp.stack([dot(select[m], backs[m], ((1,), (0,))) for m in range(micro)])
     middle_from, moe_total = normalize_back(middle, b_scale, gain_moe, d_b)
     d_h = own_cot + middle_from
     d_attn = jnp.concatenate(share_rows(d_h.astype(BF16)), axis=1).reshape(-1, width)
 
-    z_late, d_attn = lax.optimization_barrier((z_all, d_attn))
-    eo = dot(z_late, down_all, ((1,), (0,))).astype(BF16)
-    eo_back = exchange(eo.reshape(micro, peers, slots, width).swapaxes(0, 1))
-    moe_out = []
-    for m in range(micro):
-        term = eo_back[:, m].reshape(-1, width)
-        moe_out.append(
-            dot(mixing_high[m], term, ((1,), (0,))) + dot(mixing_low[m], term, ((1,), (0,)))
-        )
-    out_first, out_second = share_rows((middle + jnp.stack(moe_out)).astype(BF16))
+    late = lax.optimization_barrier((*outputs, backs[-1]))
+    eo_back = exchange(jnp.stack(late[:micro], axis=1).reshape(-1, width))
 
     d_o = dot(d_attn, w_out, ((1,), (0,))).astype(BF16)
     grad_out = dot(d_attn, o, ((0,), (0,))).astype(BF16)
-    d_qkv, head_totals, tall_there = attention_back(qkv, *heads_in, kv_all, d_o, tall_other, kv)
+    d_qkv, head_totals = attention_back(qkv, *heads_in, kv_all, d_o, kv)
+    d_qkv, eo_back = lax.optimization_barrier((d_qkv, eo_back))
+    moe_out = dot(mixing_high, eo_back, ((1,), (0,))) + dot(mixing_low, eo_back, ((1,), (0,)))
+    out_first, out_second = share_rows((middle + moe_out.reshape(middle.shape)).astype(BF16))
     input_grad = sum_own(dot(d_qkv, w_qkv, ((1,), (1,))))
     grad_qkv = dot(a, d_qkv, ((0,), (0,))).astype(BF16)
     scale_in = lax.rsqrt(jnp.mean(own_tokens * own_tokens, axis=-1, keepdims=True) + EPS)
@@ -902,15 +1065,13 @@
         ],
         axis=1,
     ).astype(BF16)
-    share, share_out, wide_there = scatter_grads(grad_qkv, grad_out, extra_grads, wide_other)
-    late = lax.optimization_barrier((rows_all, d_gu_all, wide_there))
-    grad_wide = [
-        dot(late[0], late[1][:, n * hidden : (n + 1) * hidden], ((0,), (0,)))
-        + late[2][:, n * hidden : (n + 1) * hidden].astype(F32)
-        for n in range(2)
-    ]
+    grad_qkv, out_first, out_second = lax.optimization_barrier((grad_qkv, out_first, out_second))
+    share, share_out, wide_there, tall_there = scatter_grads(
+        grad_qkv, grad_out, extra_grads, wide_here, tall_here
+    )
+    grad_wide = jnp.where(native(), wide_here, wide_there).astype(F32)
+    grad_down = jnp.where(native(), tall_here, tall_there).astype(F32)
     gain_share = share_out[:, q_cols:]
-    gain_share = gain_share + swap_tp(gain_share)
     head_rows = query_gain.shape[0]
 
     return (
@@ -926,9 +1087,9 @@
         gain_share[:head_rows, 2],
         gain_share[:head_rows, 3],
         gain_share[:, 1],
-        grad_wide[0][None],
-        grad_wide[1][None],
-        (grad_down + tall_there.astype(F32))[None],
+        grad_wide[None, :, :hidden],
+        grad_wide[None, :, hidden:],
+        grad_down[None],
     )
 
 

time: 762 us -> 707 us (0.928)
  matrix products: 119 us -> 71 us
  other arithmetic: 63.3 us -> 32.4 us
  starting transfers between devices: 47.9 us -> 69.4 us
    dot_general x28 -> x17, matrix products: 118 us -> 70.8 us  [dot(): return lax.dot_general(a, b, (dims, ((), ())), preferred_element_type=F32)]
    ppermute x6 -> x5, waiting for transfers between devices: 28.9 us -> 67.6 us  [swap_tp(): return lax.ppermute(value, 'tp', [(0, 1), (1, 0)])]
    all_to_all x6, waiting for transfers between devices: 79.5 us -> 44.9 us  [exchange(): lax.all_to_all(rows_of, ('fsdp', 'ctx', 'tp'), split_axis=0, concat_axis=...]
    concatenate x3 -> x1, other arithmetic: 24.5 us -> 0.08 us  [local(): sine = jnp.concatenate([-sine, sine], axis=1)]
    all_to_all x6, starting transfers between devices: 34.9 us -> 57.2 us  [exchange(): lax.all_to_all(rows_of, ('fsdp', 'ctx', 'tp'), split_axis=0, concat_axis=...]
    pallas_call x4 -> x6, Pallas kernels: 378 us -> 380 us  [the longest x1 160 us: gather_weights(): pl.pallas_call(gather_kernel, in_specs=[any_space] * 5, out_specs=[any_sp...]
  transfers between devices with their start and end apart: 12 -> 11, of which waited for: 8 -> 8; matrix products, arithmetic and copies ran while one was open for 21% -> 15% of each run, Pallas kernels for 13% -> 31%
where the time goes in v2:
time: 707 us; the launch traced here: 699 us
  Pallas kernels  380 us (54%)
  waiting for transfers between devices  113 us (16%)
  matrix products  71 us (10%)
  starting transfers between devices  69.4 us (10%)
  other arithmetic  32.4 us (5%)
  local copies, waits for them, and re-layouts  31.7 us (4%)
    pallas_call x1, Pallas kernels, gather_weights(): pl.pallas_call(gather_kernel, in_specs=[any_space] * 5, out_specs=[any_sp...  160 us
    pallas_call x1, Pallas kernels, scatter_grads(): pl.pallas_call(scatter_kernel, in_specs=[any_space] * 5, out_specs=[pl.Bl...  73.9 us
    dot_general x17, matrix products, dot(): return lax.dot_general(a, b, (dims, ((), ())), preferred_element_type=F32)  70.8 us
    ppermute x5, waiting for transfers between devices, swap_tp(): return lax.ppermute(value, 'tp', [(0, 1), (1, 0)])  67.6 us
    pallas_call x1, Pallas kernels, attention(): pl.pallas_call(functools.partial(attention_kernel, kv, heads), out_shape=...  65.9 us
    all_to_all x6, starting transfers between devices, exchange(): lax.all_to_all(rows_of, ('fsdp', 'ctx', 'tp'), split_axis=0, concat_axis=...  57.2 us
    all_to_all x6, waiting for transfers between devices, exchange(): lax.all_to_all(rows_of, ('fsdp', 'ctx', 'tp'), split_axis=0, concat_axis=...  44.9 us
    pallas_call x2, Pallas kernels, expert(): pl.pallas_call(expert_kernel, in_specs=[any_space] * 4, out_specs=[vmem]...  41 us
  transfers between devices with their start and end apart: 11, of which 8 were waited for; matrix products, arithmetic and copies ran while one was open for 15% of the time, Pallas kernels for 31%

profile of v2, /device:TPU:0, one launch (start us, length us, event | category | flops | bytes accessed | tf_op | source)
XLA Modules:
  0.0 698.7 jit_solution(12867821423754562601)
XLA Ops:
  6.0 2.0 broadcast_select_fusion
  8.0 2.4 fusion.56
  13.1 159.9 %gather_weights.1 = (bf16[4,2,4,2,32,2560]{5,4,3,2,1,0:T(8,128)(2,1)}, bf16[4,2,4,2,32,2176]{5,4,3,2,1,0:T(8,128)(2,1)}, bf16[2048,768]{1,0:T(8,128)(2,1)}, bf16[384,2048]{1,0:T(8,128)(2,1)}) custom-call(bf16[32,2560]{1,0:T(8,128)(2,1)} %pad_maximum_fusion.2.a_ref, bf16[32,2176]{1,0:T(8,128)(2,1)} %concatenate.31.b_ref, bf16[2048,384]{1,0:T(8,128)(2,1)} %bitcast.176, ...), custom_call_target="tpu_custom_call" | custom-call | bytes 250000000 | tf_op jit(solution)/shard_map/gather_weights/pallas_call | solution.py:223
  172.9 3.3 multiply_convert_fusion
  176.2 8.0 %all-to-all-start = ((bf16[64,16,2048]{2,1,0:T(8,128)(2,1)}), bf16[64,16,2048]{2,1,0:T(8,128)(2,1)}, u32[]{:S(2)}, u32[]{:S(2)}) async-start(bf16[64,16,2048]{2,1,0:T(8,128)(2,1)} %bitcast.159), calls=%async_computation | async-start | bytes 8388608 | tf_op jit(solution)/shard_map/all_to_all | solution.py:907
  192.3 6.0 fusion.60.qkv_ref
  198.3 65.9 %attention_forward.1 = (bf16[256,2048]{1,0:T(8,128)(2,1)S(1)}, bf16[2,640,512]{2,1,0:T(8,128)(2,1)S(1)}) custom-call(f32[256,2560]{1,0:T(8,128)S(1)} %fusion.60.qkv_ref, f32[128,128]{1,0:T(8,128)S(1)} %pad_maximum_fusion.3.cos_ref, f32[128,128]{1,0:T(8,128)S(1)} %pad_maximum_fusion.4.sin_ref, f32[1,128]{1,0:T(1,128)S(1)} %get-tuple-element.175.gq_ref, ...), custom_call_target="tpu_custom_call" | custom-call | bytes 120000000 | tf_op jit(solution)/shard_map/attention_forward/pallas_call | solution.py:678
  264.2 6.6 fusion.2
  271.0 5.3 collective-permute-start
  277.1 11.3 %collective-permute-done = bf16[2,64,2048]{2,1,0:T(8,128)(2,1)S(1)} collective-permute-done((bf16[2,64,2048]{2,1,0:T(8,128)(2,1)S(1)}, bf16[2,64,2048]{2,1,0:T(8,128)(2,1)S(1)}, u32[]{:S(2)}, u32[]{:S(2)}) %collective-permute-start) | collective-permute-done | bytes 524320 | tf_op jit(solution)/shard_map/ppermute | solution.py:878
  289.0 2.0 fusion.4
  291.0 17.5 %all-to-all-start.1 = ((bf16[64,8,2048]{2,1,0:T(8,128)(2,1)}), bf16[64,8,2048]{2,1,0:T(8,128)(2,1)S(1)}, u32[]{:S(2)}, u32[]{:S(2)}) async-start(bf16[64,8,2048]{2,1,0:T(8,128)(2,1)} %fusion.4), calls=%async_computation.1 | async-start | bytes 4194304 | tf_op jit(solution)/shard_map/all_to_all | solution.py:907
  308.5 3.0 fusion.5
  311.5 26.6 %all-to-all-done.1 = bf16[64,8,2048]{2,1,0:T(8,128)(2,1)S(1)} async-done(((bf16[64,8,2048]{2,1,0:T(8,128)(2,1)}), bf16[64,8,2048]{2,1,0:T(8,128)(2,1)S(1)}, u32[]{:S(2)}, u32[]{:S(2)}) %all-to-all-start.1) | async-done | bytes 2097184 | tf_op jit(solution)/shard_map/all_to_all | solution.py:907
  338.1 5.6 all-to-all-start.3
  343.7 5.0 slice_bitcast_fusion.3
  348.6 20.5 %expert_both_ways.2 = (bf16[512,2048]{1,0:T(8,128)(2,1)S(1)}, bf16[512,2048]{1,0:T(8,128)(2,1)}, bf16[1024,2048]{1,0:T(8,128)(2,1)}, bf16[1024,2048]{1,0:T(8,128...) custom-call(bf16[512,2048]{1,0:T(8,128)(2,1)} %bitcast.160, ...), custom_call_target="tpu_custom_call" | custom-call | bytes 80000000 | tf_op jit(solution)/shard_map/expert_both_ways/pallas_call | solution.py:838
  372.9 9.9 %all-to-all-start.2 = ((bf16[64,8,2048]{2,1,0:T(8,128)(2,1)}), bf16[64,8,2048]{2,1,0:T(8,128)(2,1)}, u32[]{:S(2)}, u32[]{:S(2)}) async-start(bf16[64,8,2048]{2,1,0:T(8,128)(2,1)} %bitcast.155), calls=%async_computation.2 | async-start | bytes 4194304 | tf_op jit(solution)/shard_map/all_to_all | solution.py:907
  382.8 2.6 select_n.206
  386.6 20.5 %expert_both_ways.3 = (bf16[512,2048]{1,0:T(8,128)(2,1)S(1)}, bf16[512,2048]{1,0:T(8,128)(2,1)}, bf16[1024,2048]{1,0:T(8,128)(2,1)}, bf16[1024,2048]{1,0:T(8,128...) custom-call(bf16[512,2048]{1,0:T(8,128)(2,1)} %bitcast.41.got_ref, ...), custom_call_target="tpu_custom_call" | custom-call | bytes 80000000 | tf_op jit(solution)/shard_map/expert_both_ways/pallas_call | solution.py:838
  409.6 3.5 fusion.63
  413.3 10.6 %all-to-all-start.4 = ((bf16[64,8,2048]{2,1,0:T(8,128)(2,1)}), bf16[64,8,2048]{2,1,0:T(8,128)(2,1)}, u32[]{:S(2)}, u32[]{:S(2)}) async-start(bf16[64,8,2048]{2,1,0:T(8,128)(2,1)} %bitcast.156), calls=%async_computation.4 | async-start | bytes 4194304 | tf_op jit(solution)/shard_map/all_to_all | solution.py:907
  424.0 4.7 maximum_bitcast_fusion
  428.7 3.7 fusion.62
  432.5 5.2 add_convert_fusion.wide_ref
  437.7 16.9 %all-to-all-done.4 = bf16[64,8,2048]{2,1,0:T(8,128)(2,1)} async-done(((bf16[64,8,2048]{2,1,0:T(8,128)(2,1)}), bf16[64,8,2048]{2,1,0:T(8,128)(2,1)}, u32[]{:S(2)}, u32[]{:S(2)}) %all-to-all-start.4) | async-done | bytes 2097184 | tf_op jit(solution)/shard_map/all_to_all | solution.py:907
  454.5 5.7 all-to-all-start.5
  460.2 2.2 convolution_bitcast_fusion.1
  462.5 2.3 convolution_bitcast_fusion
  466.4 2.9 collective-permute-start.1
  469.3 2.0 add_convert_fusion.1.tall_ref
  471.3 1.8 concatenate.40
  473.1 46.0 %collective-permute-done.1 = bf16[2,64,2048]{2,1,0:T(8,128)(2,1)} collective-permute-done((bf16[2,64,2048]{2,1,0:T(8,128)(2,1)}, bf16[2,64,2048]{2,1,0:T(8,128)(2,1)}, u32[]{:S(2)}, u32[]{:S(2)}) %collective-permute-start.1) | collective-permute-done | bytes 524320 | tf_op jit(solution)/shard_map/ppermute | solution.py:878
  520.5 6.1 fusion.6.do_ref
  526.6 39.0 %attention_backward.1 = (bf16[256,2560]{1,0:T(8,128)(2,1)S(1)}, f32[2,128]{1,0:T(2,128)S(1)}) custom-call(f32[256,2560]{1,0:T(8,128)} %copy-done, f32[128,128]{1,0:T(8,128)S(1)} %copy-done.8, f32[128,128]{1,0:T(8,128)S(1)} %pad_maximum_fusion.4.sin_ref, f32[1,128]{1,0:T(1,128)S(1)} %get-tuple-element.175.gq_ref, f32[1,128]{1,0:T(1,128)S(1)} %get-tuple-element.174.gk_ref, ...), custom_call_target="tpu_custom_call" | custom-call | bytes 120000000 | tf_op jit(solution)/shard_map/attention_backward/pallas_call | solution.py:701
  566.6 7.2 %convolution_convert_fusion.1 = bf16[2048,2048]{1,0:T(8,128)(2,1)} fusion(bf16[256,2048]{1,0:T(8,128)(2,1)} %bitcast.163, bf16[256,2048]{1,0:T(8,128)(2,1)} %copy-done.6), kind=kOutput, calls=%fused_computation.2 | convolution fusion | flops 2151677952 | bytes 10485760 | tf_op jit(solution)/shard_map/dot_general | solution.py:491
  573.8 6.0 fusion.61
  580.2 2.9 fusion.30
  583.2 3.0 convolution_add_fusion
  586.3 6.5 collective-permute-done.3
  595.3 5.8 convolution_convert_fusion
  602.1 3.5 collective-permute-start.4
  605.6 1.7 maximum_maximum_fusion.extra_ref
  607.3 3.9 collective-permute-done.2
  611.1 2.1 broadcast_select_fusion.1
  613.2 73.9 %scatter_grads.1 = (f32[32,2560]{1,0:T(8,128)S(1)}, f32[32,2176]{1,0:T(8,128)S(1)}, bf16[2048,768]{1,0:T(8,128)(2,1)S(1)}, bf16[384,2048]{1,0:T(8,128)(2,1)S(1)}) custom-call(bf16[4,2,4,2,32,2560]{5,4,3,2,1,0:T(8,128)(2,1)} %bitcast.157, bf16[4,2,4,2,32,2048]{5,4,3,2,1,0:T(8,128)(2,1)} %bitcast.158, ...), custom_call_target="tpu_custom_call" | custom-call | bytes 250000000 | tf_op jit(solution)/shard_map/scatter_grads/pallas_call | solution.py:459
  687.5 1.9 bitcast_convert_fusion
  689.4 3.1 slice_bitcast_fusion
  (213 shorter events, 39.0 us)
Async XLA Ops:
  0.6 10.2 %copy-start.62 = (bf16[2]{0:T(256)(128)(2,1)S(1)}, bf16[2]{0:T(256)(128)(2,1)}, u32[]{:S(2)}) copy-start(bf16[2]{0:T(256)(128)(2,1)} %param.33) | copy-start | bytes 16
  0.7 10.2 %copy-start.63 = (bf16[2]{0:T(256)(128)(2,1)S(1)}, bf16[2]{0:T(256)(128)(2,1)}, u32[]{:S(2)}) copy-start(bf16[2]{0:T(256)(128)(2,1)} %param.34) | copy-start | bytes 16
  0.7 10.4 %copy-start.58 = (bf16[32]{0:T(256)(128)(2,1)S(1)}, bf16[32]{0:T(256)(128)(2,1)}, u32[]{:S(2)}) copy-start(bf16[32]{0:T(256)(128)(2,1)} %param.28) | copy-start | bytes 196
  0.7 10.5 %copy-start.59 = (bf16[32]{0:T(256)(128)(2,1)S(1)}, bf16[32]{0:T(256)(128)(2,1)}, u32[]{:S(2)}) copy-start(bf16[32]{0:T(256)(128)(2,1)} %param.35) | copy-start | bytes 196
  0.7 10.7 %copy-start.42 = (bf16[2,1,64,2048]{3,2,1,0:T(8,128)(2,1)S(1)}, bf16[2,1,64,2048]{3,2,1,0:T(8,128)(2,1)}, u32[]{:S(2)}) copy-start(bf16[2,1,64,2048]{3,2,1,0:T(8,128)(2,1)} %param.23) | copy-start | bytes 1572868
  0.7 10.7 %copy-start.43 = (bf16[2,1,56,2048]{3,2,1,0:T(8,128)(2,1)S(1)}, bf16[2,1,56,2048]{3,2,1,0:T(8,128)(2,1)}, u32[]{:S(2)}) copy-start(bf16[2,1,56,2048]{3,2,1,0:T(8,128)(2,1)} %param.22) | copy-start | bytes 1376260
  0.7 10.8 %copy-start.51 = (bf16[32,256]{1,0:T(8,128)(2,1)S(1)}, bf16[32,256]{1,0:T(8,128)(2,1)}, u32[]{:S(2)}) copy-start(bf16[32,256]{1,0:T(8,128)(2,1)} %param.31) | copy-start | bytes 49156
  0.7 10.8 %copy-start.52 = (bf16[32,256]{1,0:T(8,128)(2,1)S(1)}, bf16[32,256]{1,0:T(8,128)(2,1)}, u32[]{:S(2)}) copy-start(bf16[32,256]{1,0:T(8,128)(2,1)} %param.30) | copy-start | bytes 49156
  0.7 10.8 %copy-start.46 = (bf16[32,2048]{1,0:T(8,128)(2,1)S(1)}, bf16[32,2048]{1,0:T(8,128)(2,1)}, u32[]{:S(2)}) copy-start(bf16[32,2048]{1,0:T(8,128)(2,1)} %param.29) | copy-start | bytes 393220
  2.7 9.6 %copy-start.47 = (bf16[32,2048]{1,0:T(8,128)(2,1)S(1)}, bf16[32,2048]{1,0:T(8,128)(2,1)}, u32[]{:S(2)}) copy-start(bf16[32,2048]{1,0:T(8,128)(2,1)} %param.32) | copy-start | bytes 393220
  11.6 164.6 %copy-start.27 = (bf16[2,64,2048]{2,1,0:T(8,128)(2,1)}, bf16[2,64,2048]{2,1,0:T(8,128)(2,1)S(1)}, u32[]{:S(2)}) copy-start(bf16[2,64,2048]{2,1,0:T(8,128)(2,1)S(1)} %bitcast_select_fusion) | copy-start | bytes 1572868
  176.2 9.7 %copy-start.40 = (bf16[2,1,56,2048]{3,2,1,0:T(8,128)(2,1)S(1)}, bf16[2,1,56,2048]{3,2,1,0:T(8,128)(2,1)}, u32[]{:S(2)}) copy-start(bf16[2,1,56,2048]{3,2,1,0:T(8,128)(2,1)} %param.20) | copy-start | bytes 1376260
  176.2 9.7 %copy-start.33 = (bf16[2,1,64,2048]{3,2,1,0:T(8,128)(2,1)S(1)}, bf16[2,1,64,2048]{3,2,1,0:T(8,128)(2,1)}, u32[]{:S(2)}) copy-start(bf16[2,1,64,2048]{3,2,1,0:T(8,128)(2,1)} %param.21) | copy-start | bytes 1572868
  176.2 112.7 %all-to-all-start = ((bf16[64,16,2048]{2,1,0:T(8,128)(2,1)}), bf16[64,16,2048]{2,1,0:T(8,128)(2,1)}, u32[]{:S(2)}, u32[]{:S(2)}) async-start(bf16[64,16,2048]{2,1,0:T(8,128)(2,1)} %bitcast.159), calls=%async_computation | async-start | bytes 8388608 | tf_op jit(solution)/shard_map/all_to_all | solution.py:907
  190.2 8.0 %copy-start.44 = (f32[2048,1]{0,1:T(1,128)}, f32[2048,1]{0,1:T(1,128)S(1)}, u32[]{:S(2)}) copy-start(f32[2048,1]{0,1:T(1,128)S(1)} %get-tuple-element.171) | copy-start | bytes 24580
  190.7 7.6 %copy-start.7 = (f32[128,128]{1,0:T(8,128)}, f32[128,128]{1,0:T(8,128)S(1)}, u32[]{:S(2)}) copy-start(f32[128,128]{1,0:T(8,128)S(1)} %pad_maximum_fusion.3.cos_ref) | copy-start | bytes 196612
  198.3 72.6 %copy-start = (f32[256,2560]{1,0:T(8,128)}, f32[256,2560]{1,0:T(8,128)S(1)}, u32[]{:S(2)}) copy-start(f32[256,2560]{1,0:T(8,128)S(1)} %fusion.60.qkv_ref) | copy-start | bytes 7864324
  264.2 6.7 copy-start.4
  264.2 12.9 %copy-start.6 = (bf16[256,2048]{1,0:T(8,128)(2,1)}, bf16[256,2048]{1,0:T(8,128)(2,1)S(1)}, u32[]{:S(2)}) copy-start(bf16[256,2048]{1,0:T(8,128)(2,1)S(1)} %get-tuple-element.54) | copy-start | bytes 3145732
  264.2 12.1 %copy-start.41 = (bf16[2,1,56,2048]{3,2,1,0:T(8,128)(2,1)S(1)}, bf16[2,1,56,2048]{3,2,1,0:T(8,128)(2,1)}, u32[]{:S(2)}) copy-start(bf16[2,1,56,2048]{3,2,1,0:T(8,128)(2,1)} %param.20) | copy-start | bytes 1376260
  271.0 17.4 %collective-permute-start = (bf16[2,64,2048]{2,1,0:T(8,128)(2,1)S(1)}, bf16[2,64,2048]{2,1,0:T(8,128)(2,1)S(1)}, u32[]{:S(2)}, u32[]{:S(2)}) collective-permute-start(bf16[2,64,2048]{2,1,0:T(8,128)(2,1)S(1)} %select_convert_fusion.2), channel_id=1, source_target_pairs={{0,1},{1,0},{2,3},{3,2},{4,5},{5,4},{6,7},{7,6},{8,9},{9,8},{10,11... | collective-permute-start | bytes 1572872 | tf_op jit(solution)/shard_map/ppermute | solution.py:878
  277.1 13.9 %copy-start.21 = (bf16[2,64,2048]{2,1,0:T(8,128)(2,1)}, bf16[2,64,2048]{2,1,0:T(8,128)(2,1)S(1)}, u32[]{:S(2)}) copy-start(bf16[2,64,2048]{2,1,0:T(8,128)(2,1)S(1)} %get-tuple-element.155) | copy-start | bytes 1572868
  277.1 11.8 %copy-start.38 = (pred[2,64,64,8]{1,3,2,0:T(8,128)(4,1)S(1)}, pred[2,64,64,8]{1,3,2,0:T(8,128)(4,1)}, u32[]{:S(2)}) copy-start(pred[2,64,64,8]{1,3,2,0:T(8,128)(4,1)} %copy-done.37) | copy-start | bytes 196612
  291.0 47.1 %all-to-all-start.1 = ((bf16[64,8,2048]{2,1,0:T(8,128)(2,1)}), bf16[64,8,2048]{2,1,0:T(8,128)(2,1)S(1)}, u32[]{:S(2)}, u32[]{:S(2)}) async-start(bf16[64,8,2048]{2,1,0:T(8,128)(2,1)} %fusion.4), calls=%async_computation.1 | async-start | bytes 4194304 | tf_op jit(solution)/shard_map/all_to_all | solution.py:907
  338.1 34.8 %all-to-all-start.3 = ((bf16[64,8,2048]{2,1,0:T(8,128)(2,1)}), bf16[64,8,2048]{2,1,0:T(8,128)(2,1)}, u32[]{:S(2)}, u32[]{:S(2)}) async-start(bf16[64,8,2048]{2,1,0:T(8,128)(2,1)} %fusion.5), calls=%async_computation.3 | async-start | bytes 4194304 | tf_op jit(solution)/shard_map/all_to_all | solution.py:907
  371.7 14.3 %copy-start.56 = (f32[2,64]{1,0:T(2,128)S(1)}, f32[2,64]{1,0:T(2,128)}, u32[]{:S(2)}) copy-start(f32[2,64]{1,0:T(2,128)} %get-tuple-element.154) | copy-start | bytes 1540
  372.9 40.5 %all-to-all-start.2 = ((bf16[64,8,2048]{2,1,0:T(8,128)(2,1)}), bf16[64,8,2048]{2,1,0:T(8,128)(2,1)}, u32[]{:S(2)}, u32[]{:S(2)}) async-start(bf16[64,8,2048]{2,1,0:T(8,128)(2,1)} %bitcast.155), calls=%async_computation.2 | async-start | bytes 4194304 | tf_op jit(solution)/shard_map/all_to_all | solution.py:907
  386.6 23.0 %copy-start.19 = (bf16[1024,2048]{1,0:T(8,128)(2,1)S(1)}, bf16[1024,2048]{1,0:T(8,128)(2,1)}, u32[]{:S(2)}) copy-start(bf16[1024,2048]{1,0:T(8,128)(2,1)} %get-tuple-element.78) | copy-start | bytes 12582916
  413.3 41.2 %all-to-all-start.4 = ((bf16[64,8,2048]{2,1,0:T(8,128)(2,1)}), bf16[64,8,2048]{2,1,0:T(8,128)(2,1)}, u32[]{:S(2)}, u32[]{:S(2)}) async-start(bf16[64,8,2048]{2,1,0:T(8,128)(2,1)} %bitcast.156), calls=%async_computation.4 | async-start | bytes 4194304 | tf_op jit(solution)/shard_map/all_to_all | solution.py:907
  437.7 22.5 %copy-start.39 = (pred[2,64,64,8]{1,3,2,0:T(8,128)(4,1)S(1)}, pred[2,64,64,8]{1,3,2,0:T(8,128)(4,1)}, u32[]{:S(2)}) copy-start(pred[2,64,64,8]{1,3,2,0:T(8,128)(4,1)} %copy-done.37) | copy-start | bytes 196612
  454.5 119.3 %all-to-all-start.5 = ((bf16[64,16,2048]{2,1,0:T(8,128)(2,1)}), bf16[64,16,2048]{2,1,0:T(8,128)(2,1)}, u32[]{:S(2)}, u32[]{:S(2)}) async-start(bf16[64,16,2048]{2,1,0:T(8,128)(2,1)} %maximum_bitcast_fusion), calls=%async_computation.5 | async-start | bytes 8388608 | tf_op jit(solution)/shard_map/all_to_all | solution.py:907
  462.5 6.8 copy-start.18
  466.4 52.7 %collective-permute-start.1 = (bf16[2,64,2048]{2,1,0:T(8,128)(2,1)}, bf16[2,64,2048]{2,1,0:T(8,128)(2,1)}, u32[]{:S(2)}, u32[]{:S(2)}) collective-permute-start(bf16[2,64,2048]{2,1,0:T(8,128)(2,1)} %fusion.57), channel_id=1, source_target_pairs={{0,1},{1,0},{2,3},{3,2},{4,5},{5,4},{6,7},{7,6},{8,9},{9,8},{10,11... | collective-permute-start | bytes 1572872 | tf_op jit(solution)/shard_map/ppermute | solution.py:878
  580.0 12.8 %collective-permute-start.3 = (bf16[2,64,2048]{2,1,0:T(8,128)(2,1)S(1)}, bf16[2,64,2048]{2,1,0:T(8,128)(2,1)S(1)}, u32[]{:S(2)}, u32[]{:S(2)}) collective-permute-start(bf16[2,64,2048]{2,1,0:T(8,128)(2,1)S(1)} %select_convert_fusion.1), channel_id=1, source_target_pairs={{0,1},{1,0},{2,3},{3,2},{4,5},{5,4},{6,7},{7,6},{8,9},{9,8},{10,11... | collective-permute-start | bytes 1572872 | tf_op jit(solution)/shard_map/ppermute | solution.py:878
  583.2 9.6 %copy-start.22 = (bf16[2,64,2048]{2,1,0:T(8,128)(2,1)S(1)}, bf16[2,64,2048]{2,1,0:T(8,128)(2,1)}, u32[]{:S(2)}) copy-start(bf16[2,64,2048]{2,1,0:T(8,128)(2,1)} %copy-done.21) | copy-start | bytes 1572868
  583.2 9.6 %copy-start.45 = (f32[2048,1]{0,1:T(1,128)S(1)}, f32[2048,1]{0,1:T(1,128)}, u32[]{:S(2)}) copy-start(f32[2048,1]{0,1:T(1,128)} %copy-done.44) | copy-start | bytes 24580
  583.2 9.6 %copy-start.53 = (f32[2,64]{1,0:T(2,128)S(1)}, f32[2,64]{1,0:T(2,128)}, u32[]{:S(2)}) copy-start(f32[2,64]{1,0:T(2,128)} %add_rsqrt_fusion) | copy-start | bytes 1540
  586.2 7.2 %copy-start.15 = (f32[2,64,2048]{2,1,0:T(8,128)S(1)}, f32[2,64,2048]{2,1,0:T(8,128)}, u32[]{:S(2)}) copy-start(f32[2,64,2048]{2,1,0:T(8,128)} %copy-done.13) | copy-start | bytes 3145732
  586.2 7.2 %copy-start.24 = (f32[1,64,2048]{2,1,0:T(8,128)S(1)}, f32[1,64,2048]{2,1,0:T(8,128)}, u32[]{:S(2)}) copy-start(f32[1,64,2048]{2,1,0:T(8,128)} %copy-done.23) | copy-start | bytes 1572868
  586.2 7.2 %copy-start.26 = (f32[1,64,2048]{2,1,0:T(8,128)S(1)}, f32[1,64,2048]{2,1,0:T(8,128)}, u32[]{:S(2)}) copy-start(f32[1,64,2048]{2,1,0:T(8,128)} %copy-done.25) | copy-start | bytes 1572868
  586.2 7.2 %copy-start.29 = (bf16[2,64,2048]{2,1,0:T(8,128)(2,1)S(1)}, bf16[2,64,2048]{2,1,0:T(8,128)(2,1)}, u32[]{:S(2)}) copy-start(bf16[2,64,2048]{2,1,0:T(8,128)(2,1)} %copy-done.27) | copy-start | bytes 1572868
  586.2 7.2 %copy-start.50 = (f32[2,64]{1,0:T(2,128)S(1)}, f32[2,64]{1,0:T(2,128)}, u32[]{:S(2)}) copy-start(f32[2,64]{1,0:T(2,128)} %copy-done.48) | copy-start | bytes 1540
  586.2 7.2 %copy-start.55 = (f32[2,64]{1,0:T(2,128)S(1)}, f32[2,64]{1,0:T(2,128)}, u32[]{:S(2)}) copy-start(f32[2,64]{1,0:T(2,128)} %copy-done.54) | copy-start | bytes 1540
  595.0 10.6 %copy-start.57 = (bf16[128]{0:T(256)(128)(2,1)S(1)}, bf16[128]{0:T(256)(128)(2,1)}, u32[]{:S(2)}) copy-start(bf16[128]{0:T(256)(128)(2,1)} %pad.37.clone) | copy-start | bytes 772
  595.0 16.1 %collective-permute-start.2 = (bf16[2,64,2048]{2,1,0:T(8,128)(2,1)}, bf16[2,64,2048]{2,1,0:T(8,128)(2,1)}, u32[]{:S(2)}, u32[]{:S(2)}) collective-permute-start(bf16[2,64,2048]{2,1,0:T(8,128)(2,1)} %get-tuple-element.165), channel_id=1, source_target_pairs={{0,1},{1,0},{2,3},{3,2},{4,5},{5,4},{6,7},{7,6},{8,9},{9,8},{10,11... | collective-permute-start | bytes 1572872 | tf_op jit(solution)/shard_map/ppermute | solution.py:878
  602.1 94.7 %collective-permute-start.4 = (bf16[2,64,2048]{2,1,0:T(8,128)(2,1)}, bf16[2,64,2048]{2,1,0:T(8,128)(2,1)S(1)}, u32[]{:S(2)}, u32[]{:S(2)}) collective-permute-start(bf16[2,64,2048]{2,1,0:T(8,128)(2,1)} %get-tuple-element.164), channel_id=1, source_target_pairs={{0,1},{1,0},{2,3},{3,2},{4,5},{5,4},{6,7},{7,6},{8,9},{9,8},{10,11... | collective-permute-start | bytes 1572872 | tf_op jit(solution)/shard_map/ppermute | solution.py:878
  613.2 73.9 %copy-start.17 = (bf16[2048,768]{1,0:T(8,128)(2,1)S(1)}, bf16[2048,768]{1,0:T(8,128)(2,1)}, u32[]{:S(2)}) copy-start(bf16[2048,768]{1,0:T(8,128)(2,1)} %add_convert_fusion.wide_ref) | copy-start | bytes 9437188
  689.4 7.4 %copy-start.35 = (bf16[2,64,2048]{2,1,0:T(8,128)(2,1)S(1)}, bf16[2,64,2048]{2,1,0:T(8,128)(2,1)}, u32[]{:S(2)}) copy-start(bf16[2,64,2048]{2,1,0:T(8,128)(2,1)} %get-tuple-element.164) | copy-start | bytes 1572868
  (27 other events, 107.4 us)

commit v3 on v2

--- a/solution.py
+++ b/solution.py
@@ -72,18 +72,12 @@
 
 
 def gather_kernel(
-    a_ref, b_ref, gate_ref, up_ref, down_ref, a_all, b_all, wide_all, tall_all,
-    local_sem, send_sem, recv_sem, away_sem, home_sem, keep_sem, give_sem, take_sem,
+    a_ref, b_ref, gate_ref, up_ref, down_ref, a_all, b_all, gate_all, up_all, down_all,
+    local_sem, send_sem, recv_sem, away_sem, home_sem, give_sem, take_sem,
 ):
     y, core, z, x = place()
     greet(neighbours() + [opposite()])
-    hidden = gate_ref.shape[1]
-    shards = (
-        (gate_ref, wide_all.at[:, pl.ds(0, hidden)]),
-        (up_ref, wide_all.at[:, pl.ds(hidden, hidden)]),
-        (down_ref, tall_all),
-    )
-    kept = [pltpu.make_async_copy(p, q, keep_sem.at[n]) for n, (p, q) in enumerate(shards)]
+    shards = ((gate_ref, gate_all), (up_ref, up_all), (down_ref, down_all))
     moved = [
         swap_opposite(p, q, give_sem.at[n], take_sem.at[n]) for n, (p, q) in enumerate(shards)
     ]
@@ -153,11 +147,6 @@
     for n in (0, 1):
         i, j = me[n]
         second(n, i, j, 0)
-
-    @pl.when(native())
-    def _():
-        for copy in kept:
-            copy.start()
 
     @pl.when(jnp.logical_not(native()))
     def _():
@@ -205,11 +194,6 @@
     for copy in started:
         copy.wait_send()
 
-    @pl.when(native())
-    def _():
-        for copy in kept:
-            copy.wait()
-
     @pl.when(jnp.logical_not(native()))
     def _():
         for copy in moved:
@@ -220,15 +204,12 @@
     rows = a.shape[0]
     shape = (RING, 2, RING, 2, rows)
     any_space = pl.BlockSpec(memory_space=pl.ANY)
-    a_all, b_all, wide, tall = pl.pallas_call(
+    a_all, b_all, *experts = pl.pallas_call(
         gather_kernel,
-        in_specs=[any_space] * 5,
-        out_specs=[any_space] * 4,
+        in_specs=[pl.BlockSpec(memory_space=pltpu.VMEM)] * 2 + [any_space] * 3,
+        out_specs=[any_space] * 5,
         out_shape=[jax.ShapeDtypeStruct(shape + (v.shape[1],), v.dtype) for v in (a, b)]
-        + [
-            jax.ShapeDtypeStruct((gate.shape[0], 2 * gate.shape[1]), gate.dtype),
-            jax.ShapeDtypeStruct(down.shape, down.dtype),
-        ],
+        + [jax.ShapeDtypeStruct(v.shape, v.dtype) for v in (gate, up, down)],
         scratch_shapes=[
             pltpu.SemaphoreType.DMA((2,)),
             pltpu.SemaphoreType.DMA((2, 21)),
@@ -237,13 +218,12 @@
             pltpu.SemaphoreType.DMA((2, 16)),
             pltpu.SemaphoreType.DMA((3,)),
             pltpu.SemaphoreType.DMA((3,)),
-            pltpu.SemaphoreType.DMA((3,)),
         ],
         compiler_params=pltpu.CompilerParams(collective_id=0, has_side_effects=True),
         cost_estimate=pl.CostEstimate(flops=0, bytes_accessed=250_000_000, transcendentals=0),
         name="gather_weights",
     )(a, b, gate, up, down)
-    return a_all.reshape(-1, a.shape[1]), b_all.reshape(-1, b.shape[1]), wide, tall
+    return a_all.reshape(-1, a.shape[1]), b_all.reshape(-1, b.shape[1]), *experts
 
 
 ORDER = (2, 1, 3, 0)
@@ -528,15 +508,11 @@
     return e / jnp.sum(e, axis=-1, keepdims=True)
 
 
-def attention_kernel(
-    kv, heads, qkv_ref, cos_ref, sin_ref, gq_ref, gk_ref, bias_ref, o_ref, kv_ref, held,
-    send_sem, recv_sem,
-):
+def share_kernel(kv, rows_ref, cos_ref, sin_ref, gk_ref, kv_ref, held, send_sem, recv_sem):
     c = lax.axis_index("ctx")
     greet([ctx_peer(step) for step in range(1, CTX)])
     micro, rows = held.shape[0], 2 * BLOCK
-    q_cols = kv * heads * HEAD_SIZE
-    cosine, sine, gq, gk = cos_ref[...], sin_ref[...], gq_ref[...], gk_ref[...]
+    cosine, sine, gk = cos_ref[...], sin_ref[...], gk_ref[...]
     mine = pl.ds(pl.multiple_of(c * BLOCK, BLOCK), BLOCK)
     earlier, own = pl.ds(CTX * BLOCK, BLOCK), pl.ds((CTX + 1) * BLOCK, BLOCK)
     copies = []
@@ -544,7 +520,7 @@
         span = slice(m * rows, (m + 1) * rows)
         for h in range(2 * kv):
             cols = slice(h * HEAD_SIZE, (h + 1) * HEAD_SIZE)
-            u = qkv_ref[span, q_cols + h * HEAD_SIZE : q_cols + (h + 1) * HEAD_SIZE]
+            u = rows_ref[span, cols]
             low = rotated(u, gk, cosine, sine)[0] if h < kv else u.astype(BF16)
             held[m, mine, cols] = low[:BLOCK]
             held[m, own, cols] = low[BLOCK:]
@@ -560,18 +536,6 @@
         )
         for copy in copies[-CTX:]:
             copy.start()
-
-    def group(m, h, carry):
-        span = slice(m * rows, (m + 1) * rows)
-        k = held[m, :, pl.ds(pl.multiple_of(h * HEAD_SIZE, HEAD_SIZE), HEAD_SIZE)]
-        v = held[m, :, pl.ds(pl.multiple_of((kv + h) * HEAD_SIZE, HEAD_SIZE), HEAD_SIZE)]
-        for e in range(heads):
-            cols = pl.ds(pl.multiple_of((h * heads + e) * HEAD_SIZE, HEAD_SIZE), HEAD_SIZE)
-            q_low = rotated(qkv_ref[span, cols], gq, cosine, sine)[0]
-            p = softmax_parts(q_low, k, bias_ref[...]).astype(BF16)
-            o_ref[span, cols] = dot(p, v, ((1,), (0,))).astype(BF16)
-        return carry
-
     for m in range(micro):
         for step in range(1, CTX):
             source = lax.rem(c + CTX - step, CTX)
@@ -580,10 +544,18 @@
                 part, part, send_sem.at[step, m], recv_sem.at[step, m], ctx_peer(step)
             ).wait_recv()
         copies[(m + 1) * CTX - 1].wait_recv()
-        lax.fori_loop(0, kv, functools.partial(group, m), 0)
-    kv_ref[...] = held[...]
+        kv_ref[m] = held[m]
     for copy in copies:
         copy.wait_send()
+
+
+def attention_kernel(heads, q_ref, cos_ref, sin_ref, gq_ref, bias_ref, k_ref, v_ref, o_ref):
+    cosine, sine, gq = cos_ref[...], sin_ref[...], gq_ref[...]
+    for e in range(heads):
+        cols = slice(e * HEAD_SIZE, (e + 1) * HEAD_SIZE)
+        q_low = rotated(q_ref[:, cols], gq, cosine, sine)[0]
+        p = softmax_parts(q_low, k_ref[...], bias_ref[...]).astype(BF16)
+        o_ref[:, cols] = dot(p, v_ref[...], ((1,), (0,))).astype(BF16)
 
 
 def attention_back_kernel(
@@ -672,26 +644,57 @@
         copy.wait_send()
 
 
-def attention(qkv, cosine, sine, gain_query, gain_key, bias, kv, micro):
-    heads = qkv.shape[1] // HEAD_SIZE // kv - 2
-    rows, keys = bias.shape
+def share_keys(qkv, cosine, sine, gain_key, kv, keys, micro):
+    rows, cols = qkv.shape[0], 2 * kv * HEAD_SIZE
+    last = qkv.shape[1] // cols - 1
+
+    def whole(shape):
+        return pl.BlockSpec(shape, lambda i: (0,) * len(shape))
+
     return pl.pallas_call(
-        functools.partial(attention_kernel, kv, heads),
-        out_shape=[
-            jax.ShapeDtypeStruct((qkv.shape[0], kv * heads * HEAD_SIZE), BF16),
-            jax.ShapeDtypeStruct((micro, keys, 2 * kv * HEAD_SIZE), BF16),
-        ],
+        functools.partial(share_kernel, kv),
+        grid=(1,),
+        in_specs=[pl.BlockSpec((rows, cols), lambda i: (0, last)), whole(cosine.shape)]
+        + [whole(sine.shape), whole(gain_key.shape)],
+        out_specs=whole((micro, keys, cols)),
+        out_shape=jax.ShapeDtypeStruct((micro, keys, cols), BF16),
         scratch_shapes=[
-            pltpu.VMEM((micro, keys, 2 * kv * HEAD_SIZE), BF16),
+            pltpu.VMEM((micro, keys, cols), BF16),
             pltpu.SemaphoreType.DMA((CTX, micro)),
             pltpu.SemaphoreType.DMA((CTX, micro)),
         ],
         compiler_params=pltpu.CompilerParams(
             collective_id=2, has_side_effects=True, vmem_limit_bytes=VMEM_LIMIT
         ),
-        cost_estimate=pl.CostEstimate(flops=0, bytes_accessed=120_000_000, transcendentals=0),
+        cost_estimate=pl.CostEstimate(flops=0, bytes_accessed=50_000_000, transcendentals=0),
+        name="share_keys",
+    )(qkv, cosine, sine, gain_key)
+
+
+def attention(qkv, cosine, sine, gain_query, bias, kv_all, kv):
+    micro, keys, cols = kv_all.shape
+    rows = bias.shape[0]
+    heads = qkv.shape[1] // HEAD_SIZE // kv - 2
+    width = heads * HEAD_SIZE
+
+    def whole(v):
+        return pl.BlockSpec(v.shape, lambda m, g: (0,) * v.ndim)
+
+    return pl.pallas_call(
+        functools.partial(attention_kernel, heads),
+        grid=(micro, kv),
+        in_specs=[pl.BlockSpec((rows, width), lambda m, g: (m, g))]
+        + [whole(v) for v in (cosine, sine, gain_query, bias)]
+        + [
+            pl.BlockSpec((None, keys, HEAD_SIZE), lambda m, g: (m, 0, g)),
+            pl.BlockSpec((None, keys, HEAD_SIZE), lambda m, g: (m, 0, kv + g)),
+        ],
+        out_specs=pl.BlockSpec((rows, width), lambda m, g: (m, g)),
+        out_shape=jax.ShapeDtypeStruct((micro * rows, kv * width), BF16),
+        compiler_params=pltpu.CompilerParams(vmem_limit_bytes=VMEM_LIMIT),
+        cost_estimate=pl.CostEstimate(flops=0, bytes_accessed=60_000_000, transcendentals=0),
         name="attention_forward",
-    )(qkv, cosine, sine, gain_query, gain_key, bias)
+    )(qkv, cosine, sine, gain_query, bias, kv_all, kv_all)
 
 
 def attention_back(qkv, cosine, sine, gain_query, gain_key, bias, kv_all, d_out, kv):
@@ -732,7 +735,7 @@
 
 
 def expert_kernel(
-    got_ref, deo_ref, gu_ref, down_ref, back_ref, eo_ref, rows_ref, deos_ref, z_ref, dgu_ref,
+    got_ref, deo_ref, gate_ref, up_ref, down_ref, gate_far, up_far, down_far, back_ref, eo_ref, rows_ref, deos_ref, z_ref, dgu_ref,
     rows, deos, gu, down, own, give, take, load_sem, send_sem, recv_sem, save_sem,
 ):
     greet([other_core()])
@@ -744,17 +747,32 @@
         remote(deo_ref, deos.at[far], send_sem.at[1], recv_sem.at[1], other_core()),
     ]
     loads = [
-        pltpu.make_async_copy(src, dst, load_sem.at[n])
-        for n, (src, dst) in enumerate(
-            ((got_ref, rows.at[near]), (gu_ref, gu), (deo_ref, deos.at[near]), (down_ref, down))
-        )
+        pltpu.make_async_copy(got_ref, rows.at[near], load_sem.at[0]),
+        pltpu.make_async_copy(deo_ref, deos.at[near], load_sem.at[1]),
     ]
+    places = (gu.at[:, pl.ds(0, hidden)], gu.at[:, pl.ds(hidden, hidden)], down)
+    weights = [
+        [pltpu.make_async_copy(src, dst, load_sem.at[2 + n]) for n, (src, dst) in enumerate(pairs)]
+        for pairs in (
+            zip((gate_ref, up_ref, down_ref), places), zip((gate_far, up_far, down_far), places)
+        )
+    ]
+
+    def on_weights(act):
+        for condition, copies in zip((native(), jnp.logical_not(native())), weights):
+
+            @pl.when(condition)
+            def _(copies=copies):
+                for copy in copies:
+                    act(copy)
+
     saves = [
         pltpu.make_async_copy(rows, rows_ref, save_sem.at[0]),
         pltpu.make_async_copy(deos, deos_ref, save_sem.at[1]),
     ]
     for copy in loads + swaps:
         copy.start()
+    on_weights(lambda copy: copy.start())
 
     def span(i):
         return pl.ds(pl.multiple_of(i * PART, PART), PART)
@@ -812,6 +830,7 @@
 
     for copy in loads:
         copy.wait()
+    on_weights(lambda copy: copy.wait())
     each(through)
     for copy in swaps:
         copy.wait_recv()
@@ -828,27 +847,27 @@
         copy.wait()
 
 
-def expert(got, d_eo, gu, down, collective):
+def expert(got, d_eo, own, far, collective):
     count, width = got.shape
-    hidden = down.shape[0]
+    hidden = own[2].shape[0]
     parts = count // PART
     vmem, any_space = (pl.BlockSpec(memory_space=space) for space in (pltpu.VMEM, pl.ANY))
     shapes = [(count, width), (count, width), (2 * count, width), (2 * count, width)]
     shapes += [(2 * count, hidden), (2 * count, 2 * hidden)]
     return pl.pallas_call(
         expert_kernel,
-        in_specs=[any_space] * 4,
+        in_specs=[any_space] * 8,
         out_specs=[vmem] * 2 + [any_space] * 2 + [vmem] * 2,
         out_shape=[jax.ShapeDtypeStruct(shape, BF16) for shape in shapes],
         scratch_shapes=[
             pltpu.VMEM((2 * count, width), BF16),
             pltpu.VMEM((2 * count, width), BF16),
-            pltpu.VMEM(gu.shape, BF16),
-            pltpu.VMEM(down.shape, BF16),
+            pltpu.VMEM((width, 2 * hidden), BF16),
+            pltpu.VMEM((hidden, width), BF16),
             pltpu.VMEM((count, width), F32),
             pltpu.VMEM((2, count, width), BF16),
             pltpu.VMEM((2, count, width), BF16),
-            pltpu.SemaphoreType.DMA((4,)),
+            pltpu.SemaphoreType.DMA((5,)),
             pltpu.SemaphoreType.DMA((2 + 2 * parts,)),
             pltpu.SemaphoreType.DMA((2 + 2 * parts,)),
             pltpu.SemaphoreType.DMA((2,)),
@@ -858,7 +877,7 @@
         ),
         cost_estimate=pl.CostEstimate(flops=0, bytes_accessed=80_000_000, transcendentals=0),
         name="expert_both_ways",
-    )(got, d_eo, gu, down)
+    )(got, d_eo, *own, *far)
 
 
 def normalize(rows, gain):
@@ -933,10 +952,10 @@
     both = jnp.logical_and(placed[:, :, :, None, :], same[:, None, None, :, None])
     flat = (micro * block, peers * micro * slots)
     select_both = both.astype(BF16).reshape(flat)
-    mixing = jnp.where(both, weight[:, :, :, None, None], 0.0).reshape(flat)
+    mixing = jnp.where(placed, weight[:, :, :, None], 0.0).reshape(select.shape)
     mixing_high = mixing.astype(BF16)
     mixing_low = (mixing - mixing_high.astype(F32)).astype(BF16)
-    slot_gate = jnp.sum(mixing, axis=0)
+    slot_gate = jnp.sum(mixing, axis=1).reshape(micro, peers, slots).swapaxes(0, 1).reshape(-1)
 
     extra = jnp.concatenate(
         [
@@ -948,7 +967,7 @@
         ],
         axis=1,
     )
-    w_qkv, w_out_extra, gu, down = gather_weights(
+    w_qkv, w_out_extra, *far_experts = gather_weights(
         jnp.concatenate([query_weight, key_matrix, value_matrix], axis=1),
         jnp.concatenate([out_weight, extra], axis=1),
         expert_gate[0],
@@ -961,10 +980,6 @@
     head_gains = gains[:, 2:4].reshape(peers, shard_rows, 2)[:, : query_gain.shape[0]]
     head_gains = head_gains.reshape(HEAD_SIZE, 2)
     gain_query, gain_key = head_gains[:, 0], head_gains[:, 1]
-
-    cot_low, w_qkv = lax.optimization_barrier((own_cot.astype(BF16), w_qkv))
-    spread = dot(select_both, cot_low.reshape(-1, width), ((0,), (0,))) * slot_gate[:, None]
-    d_eo_rows = exchange(spread.astype(BF16))
 
     offsets = jnp.arange(rows, dtype=jnp.int32)
     is_prompt = offsets < block
@@ -1011,7 +1026,13 @@
     a = normalize(tokens, gain_in)[0].astype(BF16)
     qkv = dot(a, w_qkv, ((1,), (0,)))
     heads_in = (cosine, sine, gain_query[None], gain_key[None], bias)
-    o, kv_all = attention(qkv, *heads_in, kv, micro)
+    kv_all = share_keys(qkv, cosine, sine, gain_key[None], kv, keys, micro)
+
+    spread = dot(select_both, own_cot.astype(BF16).reshape(-1, width), ((0,), (0,)))
+    spread = (spread * slot_gate[:, None]).astype(BF16)
+    spread, kv_all = lax.optimization_barrier((spread, kv_all))
+    d_eo_rows = exchange(spread)
+    o = attention(qkv, cosine, sine, gain_query[None], bias, kv_all, kv)
     middle = own_tokens + sum_own(dot(o, w_out, ((1,), (1,))))
     b_normed, b_scale = normalize(middle, gain_moe)
     b_low = b_normed.astype(BF16)
@@ -1022,10 +1043,11 @@
     for m in range(micro):
         got = exchange(dot(select[m], b_low[m], ((0,), (0,))).astype(BF16))
         back, eo, rows_m, d_eo_m, z_m, d_gu_m = expert(
-            got, d_eo_rows[:, m].reshape(-1, width), gu, down, 4 + m
+            got, d_eo_rows[:, m].reshape(-1, width), (expert_gate[0], expert_up[0], expert_down[0]),
+            far_experts, 4 + m,
         )
         backs.append(exchange(back))
-        outputs.append(eo.reshape(peers, slots, width))
+        outputs.append(eo)
         wide_terms.append((rows_m, d_gu_m))
         tall_terms.append((z_m, d_eo_m))
 
@@ -1039,15 +1061,20 @@
     d_h = own_cot + middle_from
     d_attn = jnp.concatenate(share_rows(d_h.astype(BF16)), axis=1).reshape(-1, width)
 
-    late = lax.optimization_barrier((*outputs, backs[-1]))
-    eo_back = exchange(jnp.stack(late[:micro], axis=1).reshape(-1, width))
+    late, d_attn = lax.optimization_barrier((outputs[0], d_attn))
+    eo_back = [exchange(late)]
 
     d_o = dot(d_attn, w_out, ((1,), (0,))).astype(BF16)
     grad_out = dot(d_attn, o, ((0,), (0,))).astype(BF16)
     d_qkv, head_totals = attention_back(qkv, *heads_in, kv_all, d_o, kv)
-    d_qkv, eo_back = lax.optimization_barrier((d_qkv, eo_back))
-    moe_out = dot(mixing_high, eo_back, ((1,), (0,))) + dot(mixing_low, eo_back, ((1,), (0,)))
-    out_first, out_second = share_rows((middle + moe_out.reshape(middle.shape)).astype(BF16))
+    for m in range(1, micro):
+        late, d_qkv, eo_back[m - 1] = lax.optimization_barrier((outputs[m], d_qkv, eo_back[m - 1]))
+        eo_back.append(exchange(late))
+    moe_out = [
+        dot(high, eo, ((1,), (0,))) + dot(low, eo, ((1,), (0,)))
+        for high, low, eo in zip(mixing_high, mixing_low, eo_back)
+    ]
+    out_first, out_second = share_rows((middle + jnp.stack(moe_out)).astype(BF16))
     input_grad = sum_own(dot(d_qkv, w_qkv, ((1,), (1,))))
     grad_qkv = dot(a, d_qkv, ((0,), (0,))).astype(BF16)
     scale_in = lax.rsqrt(jnp.mean(own_tokens * own_tokens, axis=-1, keepdims=True) + EPS)

time: 707 us -> 590 us (0.83)
  Pallas kernels: 380 us -> 261 us
  waiting for transfers between devices: 113 us -> 103 us
  matrix products: 71 us -> 78.6 us
  local copies, waits for them, and re-layouts: 31.7 us -> 38.8 us
    pallas_call x4 -> x5, Pallas kernels: 267 us -> 150 us  [the longest x1 71.3 us: gather_weights(): pl.pallas_call(gather_kernel, in_specs=[pl.BlockSpec(memory_space=pltpu.V...]
    ppermute x5, waiting for transfers between devices: 67.6 us -> 56.9 us  [swap_tp(): return lax.ppermute(value, 'tp', [(0, 1), (1, 0)])]
    dot_general x17 -> x19, matrix products: 70.8 us -> 78.4 us  [dot(): return lax.dot_general(a, b, (dims, ((), ())), preferred_element_type=F32)]
    all_to_all x6 -> x7, starting transfers between devices: 57.2 us -> 58.4 us  [exchange(): lax.all_to_all(rows_of, ('fsdp', 'ctx', 'tp'), split_axis=0, concat_axis=...]
    all_to_all x6 -> x7, waiting for transfers between devices: 44.9 us -> 46.1 us  [exchange(): lax.all_to_all(rows_of, ('fsdp', 'ctx', 'tp'), split_axis=0, concat_axis=...]
  transfers between devices with their start and end apart: 11 -> 12, of which waited for: 8 -> 8; matrix products, arithmetic and copies ran while one was open for 15% -> 17% of each run, Pallas kernels for 31% -> 29%
where the time goes in v3:
time: 590 us; the launch traced here: 582 us
  Pallas kernels  261 us (44%)
  waiting for transfers between devices  103 us (17%)
  matrix products  78.6 us (13%)
  starting transfers between devices  70.3 us (12%)
  local copies, waits for them, and re-layouts  38.8 us (7%)
  other arithmetic  27.7 us (5%)
    dot_general x19, matrix products, dot(): return lax.dot_general(a, b, (dims, ((), ())), preferred_element_type=F32)  78.4 us
    pallas_call x1, Pallas kernels, scatter_grads(): pl.pallas_call(scatter_kernel, in_specs=[any_space] * 5, out_specs=[pl.Bl...  75 us
    pallas_call x1, Pallas kernels, gather_weights(): pl.pallas_call(gather_kernel, in_specs=[pl.BlockSpec(memory_space=pltpu.V...  71.3 us
    all_to_all x7, starting transfers between devices, exchange(): lax.all_to_all(rows_of, ('fsdp', 'ctx', 'tp'), split_axis=0, concat_axis=...  58.4 us
    ppermute x5, waiting for transfers between devices, swap_tp(): return lax.ppermute(value, 'tp', [(0, 1), (1, 0)])  56.9 us
    all_to_all x7, waiting for transfers between devices, exchange(): lax.all_to_all(rows_of, ('fsdp', 'ctx', 'tp'), split_axis=0, concat_axis=...  46.1 us
    pallas_call x2, Pallas kernels, expert(): pl.pallas_call(expert_kernel, in_specs=[any_space] * 8, out_specs=[vmem]...  42.2 us
    pallas_call x1, Pallas kernels, attention_back(): pl.pallas_call(functools.partial(attention_back_kernel, kv, heads), out_s...  36.5 us
  transfers between devices with their start and end apart: 12, of which 8 were waited for; matrix products, arithmetic and copies ran while one was open for 17% of the time, Pallas kernels for 29%

profile of v3, /device:TPU:0, one launch (start us, length us, event | category | flops | bytes accessed | tf_op | source)
XLA Modules:
  0.0 581.6 jit_solution(4357107476391267783)
XLA Ops:
  7.0 71.3 %gather_weights.1 = (bf16[4,2,4,2,32,2560]{5,4,3,2,1,0:T(8,128)(2,1)}, bf16[4,2,4,2,32,2176]{5,4,3,2,1,0:T(8,128)(2,1)}, bf16[2048,384]{1,0:T(8,128)(2,1)}, bf16[2048,384]{1,0:T(8,128)(2,1)}, bf16[384,2048]{1,0:T(8,128)(2,1)}) custom-call(bf16[32,2560]{1,0:T(8,128)(2,1)} %pad_maximum_fusion.2.a_ref, bf16[32,2176]{1,0:T(8,128)(2,1)} %concatenate.31.b_ref, ...), custom_call_target="tpu_custom_call" | custom-call | bytes 250000000 | tf_op jit(solution)/shard_map/gather_weights/pallas_call | solution.py:207
  85.3 5.6 fusion.67.rows_ref.q_ref.qkv_ref
  91.0 3.2 multiply_convert_fusion
  94.3 21.0 %share_keys.1.k_ref.v_ref.kv_ref = bf16[2,640,512]{2,1,0:T(8,128)(2,1)S(1)} custom-call(f32[256,2560]{1,0:T(8,128)S(1)} %fusion.67.rows_ref.q_ref.qkv_ref, f32[128,128]{1,0:T(8,128)S(1)} %pad_maximum_fusion.3.cos_ref, f32[128,128]{1,0:T(8,128)S(1)} %pad_maximum_fusion.4.sin_ref, f32[1,128]{1,0:T(1,128)S(1)} %get-tuple-element.187.gk_ref), custom_call_target="tpu_custom_call" | custom-call | bytes 50000000 | tf_op jit(solution)/shard_map/share_keys/pallas_call | solution.py:654
  116.3 6.6 %all-to-all-start = ((bf16[64,16,2048]{2,1,0:T(8,128)(2,1)}), bf16[64,16,2048]{2,1,0:T(8,128)(2,1)}, u32[]{:S(2)}, u32[]{:S(2)}) async-start(bf16[64,16,2048]{2,1,0:T(8,128)(2,1)} %bitcast.200), calls=%async_computation | async-start | bytes 8388608 | tf_op jit(solution)/shard_map/all_to_all | solution.py:926
  124.6 15.1 %attention_forward.1 = bf16[256,2048]{1,0:T(8,128)(2,1)S(1)} custom-call(f32[256,2560]{1,0:T(8,128)S(1)} %fusion.67.rows_ref.q_ref.qkv_ref, f32[128,128]{1,0:T(8,128)S(1)} %pad_maximum_fusion.3.cos_ref, f32[128,128]{1,0:T(8,128)S(1)} %pad_maximum_fusion.4.sin_ref, f32[1,128]{1,0:T(1,128)S(1)} %get-tuple-element.188.gq_ref, ...), custom_call_target="tpu_custom_call" | custom-call | bytes 60000000 | tf_op jit(solution)/shard_map/attention_forward/pallas_call | solution.py:683
  139.7 6.1 %fusion.2 = f32[256,2048]{1,0:T(8,128)S(1)} fusion(bf16[256,2048]{1,0:T(8,128)(2,1)S(1)} %attention_forward.1, bf16[2048,2176]{1,0:T(8,128)(2,1)} %bitcast.235), kind=kOutput, calls=%fused_computation.5 | convolution fusion | flops 2147483648 | bytes 11534336 | tf_op jit(solution)/shard_map/dot_general | solution.py:471
  145.9 3.3 collective-permute-start
  150.0 32.8 %collective-permute-done = bf16[2,64,2048]{2,1,0:T(8,128)(2,1)S(1)} collective-permute-done((bf16[2,64,2048]{2,1,0:T(8,128)(2,1)S(1)}, bf16[2,64,2048]{2,1,0:T(8,128)(2,1)S(1)}, u32[]{:S(2)}, u32[]{:S(2)}) %collective-permute-start) | collective-permute-done | bytes 524320 | tf_op jit(solution)/shard_map/ppermute | solution.py:897
  184.5 2.0 fusion.5
  186.5 13.3 %all-to-all-start.2 = ((bf16[64,8,2048]{2,1,0:T(8,128)(2,1)}), bf16[64,8,2048]{2,1,0:T(8,128)(2,1)S(1)}, u32[]{:S(2)}, u32[]{:S(2)}) async-start(bf16[64,8,2048]{2,1,0:T(8,128)(2,1)} %fusion.5), calls=%async_computation.2 | async-start | bytes 4194304 | tf_op jit(solution)/shard_map/all_to_all | solution.py:926
  199.8 2.0 fusion.4
  201.8 26.7 %all-to-all-done.2 = bf16[64,8,2048]{2,1,0:T(8,128)(2,1)S(1)} async-done(((bf16[64,8,2048]{2,1,0:T(8,128)(2,1)}), bf16[64,8,2048]{2,1,0:T(8,128)(2,1)S(1)}, u32[]{:S(2)}, u32[]{:S(2)}) %all-to-all-start.2) | async-done | bytes 2097184 | tf_op jit(solution)/shard_map/all_to_all | solution.py:926
  229.8 5.6 all-to-all-start.1
  235.4 5.0 slice_bitcast_fusion.2
  240.4 21.1 %expert_both_ways.3 = (bf16[512,2048]{1,0:T(8,128)(2,1)}, bf16[512,2048]{1,0:T(8,128)(2,1)}, bf16[1024,2048]{1,0:T(8,128)(2,1)}, bf16[1024,2048]{1,0:T(8,128)(2,...) custom-call(bf16[512,2048]{1,0:T(8,128)(2,1)} %bitcast.207, ...), custom_call_target="tpu_custom_call" | custom-call | bytes 80000000 | tf_op jit(solution)/shard_map/expert_both_ways/pallas_call | solution.py:857
  263.8 10.3 %all-to-all-start.3 = ((bf16[64,8,2048]{2,1,0:T(8,128)(2,1)}), bf16[64,8,2048]{2,1,0:T(8,128)(2,1)}, u32[]{:S(2)}, u32[]{:S(2)}) async-start(bf16[64,8,2048]{2,1,0:T(8,128)(2,1)} %bitcast.217), calls=%async_computation.3 | async-start | bytes 4194304 | tf_op jit(solution)/shard_map/all_to_all | solution.py:926
  277.9 21.1 %expert_both_ways.2 = (bf16[512,2048]{1,0:T(8,128)(2,1)}, bf16[512,2048]{1,0:T(8,128)(2,1)}, bf16[1024,2048]{1,0:T(8,128)(2,1)}, bf16[1024,2048]{1,0:T(8,128)(2,...) custom-call(bf16[512,2048]{1,0:T(8,128)(2,1)} %bitcast.34.got_ref, ...), custom_call_target="tpu_custom_call" | custom-call | bytes 80000000 | tf_op jit(solution)/shard_map/expert_both_ways/pallas_call | solution.py:857
  301.0 3.7 all-to-all-done.3
  304.7 7.2 %all-to-all-start.4 = ((bf16[64,8,2048]{2,1,0:T(8,128)(2,1)}), bf16[64,8,2048]{2,1,0:T(8,128)(2,1)S(1)}, u32[]{:S(2)}, u32[]{:S(2)}) async-start(bf16[64,8,2048]{2,1,0:T(8,128)(2,1)} %bitcast.216), calls=%async_computation.4 | async-start | bytes 4194304 | tf_op jit(solution)/shard_map/all_to_all | solution.py:926
  315.7 2.0 fusion.17
  318.6 5.5 fusion.69
  324.1 3.0 convolution_bitcast_fusion.1
  327.1 15.5 %all-to-all-done.4 = bf16[64,8,2048]{2,1,0:T(8,128)(2,1)S(1)} async-done(((bf16[64,8,2048]{2,1,0:T(8,128)(2,1)}), bf16[64,8,2048]{2,1,0:T(8,128)(2,1)S(1)}, u32[]{:S(2)}, u32[]{:S(2)}) %all-to-all-start.4) | async-done | bytes 2097184 | tf_op jit(solution)/shard_map/all_to_all | solution.py:926
  344.2 1.7 multiply_reduce_fusion.1
  347.7 6.9 %add_convert_fusion.wide_ref = bf16[2048,768]{1,0:T(8,128)(2,1)} fusion(f32[2048,768]{1,0:T(8,128)} %fusion.69, bf16[1024,2048]{1,0:T(8,128)(2,1)S(1)} %copy-done.72, bf16[1024,768]{1,0:T(8,128)(2,1)S(1)} %copy-done.19), kind=kOutput, calls=%fused_computation.7 | convolution fusion | flops 3224371200 | bytes 15204352 | tf_op jit(solution)/shard_map/dot_general | solution.py:471
  354.6 3.5 fusion.70
  358.1 2.6 collective-permute-done.1
  361.9 6.1 %all-to-all-start.5 = ((bf16[64,8,2048]{2,1,0:T(8,128)(2,1)}), bf16[64,8,2048]{2,1,0:T(8,128)(2,1)}, u32[]{:S(2)}, u32[]{:S(2)}) async-start(bf16[64,8,2048]{2,1,0:T(8,128)(2,1)} %bitcast.215), calls=%async_computation.5 | async-start | bytes 4194304 | tf_op jit(solution)/shard_map/all_to_all | solution.py:926
  368.0 5.0 add_convert_fusion.1.tall_ref
  373.1 1.8 concatenate.40
  374.9 6.1 %fusion.6.do_ref = bf16[256,2048]{1,0:T(8,128)(2,1)S(1)} fusion(bf16[256,2048]{1,0:T(8,128)(2,1)} %bitcast.209, bf16[2048,2176]{1,0:T(8,128)(2,1)} %bitcast.236), kind=kOutput, calls=%fused_computation.16 | convolution fusion | flops 2148007936 | bytes 10485760 | tf_op jit(solution)/shard_map/dot_general | solution.py:471
  381.1 36.5 %attention_backward.1 = (bf16[256,2560]{1,0:T(8,128)(2,1)S(1)}, f32[2,128]{1,0:T(2,128)S(1)}) custom-call(f32[256,2560]{1,0:T(8,128)} %copy-done, f32[128,128]{1,0:T(8,128)S(1)} %copy-done.15, f32[128,128]{1,0:T(8,128)S(1)} %pad_maximum_fusion.4.sin_ref, f32[1,128]{1,0:T(1,128)S(1)} %get-tuple-element.188.gq_ref, f32[1,128]{1,0:T(1,128)S(1)} %get-tuple-element.187.gk_ref, ...), custom_call_target="tpu_custom_call" | custom-call | bytes 120000000 | tf_op jit(solution)/shard_map/attention_backward/pallas_call | solution.py:704
  419.7 6.9 %convolution_convert_fusion.1 = bf16[2048,2048]{1,0:T(8,128)(2,1)} fusion(bf16[256,2048]{1,0:T(8,128)(2,1)} %bitcast.210, bf16[256,2048]{1,0:T(8,128)(2,1)S(1)} %copy-done.7), kind=kOutput, calls=%fused_computation.2 | convolution fusion | flops 2151677952 | bytes 10485760 | tf_op jit(solution)/shard_map/dot_general | solution.py:471
  426.6 9.3 %all-to-all-start.6 = ((bf16[64,8,2048]{2,1,0:T(8,128)(2,1)}), bf16[64,8,2048]{2,1,0:T(8,128)(2,1)}, u32[]{:S(2)}, u32[]{:S(2)}) async-start(bf16[64,8,2048]{2,1,0:T(8,128)(2,1)} %bitcast.214), calls=%async_computation.6 | async-start | bytes 4194304 | tf_op jit(solution)/shard_map/all_to_all | solution.py:926
  436.0 5.7 fusion.68
  441.8 3.3 collective-permute-start.3
  445.1 2.1 fusion.39
  447.2 2.9 fusion.9
  450.2 19.9 %collective-permute-done.3 = bf16[2,64,2048]{2,1,0:T(8,128)(2,1)S(1)} collective-permute-done((bf16[2,64,2048]{2,1,0:T(8,128)(2,1)S(1)}, bf16[2,64,2048]{2,1,0:T(8,128)(2,1)S(1)}, u32[]{:S(2)}, u32[]{:S(2)}) %collective-permute-start.3) | collective-permute-done | bytes 524320 | tf_op jit(solution)/shard_map/ppermute | solution.py:897
  471.5 2.2 fusion.12
  473.8 2.3 fusion.10
  478.2 5.7 convolution_convert_fusion
  486.7 3.3 collective-permute-start.4
  491.6 2.1 broadcast_select_fusion
  493.7 75.0 %scatter_grads.1 = (f32[32,2560]{1,0:T(8,128)S(1)}, f32[32,2176]{1,0:T(8,128)S(1)}, bf16[2048,768]{1,0:T(8,128)(2,1)S(1)}, bf16[384,2048]{1,0:T(8,128)(2,1)S(1)}) custom-call(bf16[4,2,4,2,32,2560]{5,4,3,2,1,0:T(8,128)(2,1)} %bitcast.198, bf16[4,2,4,2,32,2048]{5,4,3,2,1,0:T(8,128)(2,1)} %bitcast.199, ...), custom_call_target="tpu_custom_call" | custom-call | bytes 250000000 | tf_op jit(solution)/shard_map/scatter_grads/pallas_call | solution.py:439
  568.6 1.9 bitcast_convert_fusion
  572.1 3.1 slice_bitcast_fusion
  (240 shorter events, 54.2 us)
Async XLA Ops:
  79.4 3.7 copy-start.47
  79.7 5.2 copy-start.55
  79.7 3.5 copy-start.25
  81.2 118.6 %copy-start.45 = (pred[2,64,64,8]{1,3,2,0:T(8,128)(4,1)}, pred[2,64,64,8]{1,3,2,0:T(8,128)(4,1)S(1)}, u32[]{:S(2)}) copy-start(pred[2,64,64,8]{1,3,2,0:T(8,128)(4,1)S(1)} %iota_compare_fusion) | copy-start | bytes 196612
  84.8 38.5 %copy-start.14 = (f32[128,128]{1,0:T(8,128)}, f32[128,128]{1,0:T(8,128)S(1)}, u32[]{:S(2)}) copy-start(f32[128,128]{1,0:T(8,128)S(1)} %pad_maximum_fusion.3.cos_ref) | copy-start | bytes 196612
  84.9 6.1 %copy-start.38 = (bf16[2,64,2048]{2,1,0:T(8,128)(2,1)}, bf16[2,64,2048]{2,1,0:T(8,128)(2,1)S(1)}, u32[]{:S(2)}) copy-start(bf16[2,64,2048]{2,1,0:T(8,128)(2,1)S(1)} %bitcast_select_fusion.1) | copy-start | bytes 1572868
  90.9 32.3 %copy-start = (f32[256,2560]{1,0:T(8,128)}, f32[256,2560]{1,0:T(8,128)S(1)}, u32[]{:S(2)}) copy-start(f32[256,2560]{1,0:T(8,128)S(1)} %fusion.67.rows_ref.q_ref.qkv_ref) | copy-start | bytes 7864324
  116.3 68.2 %all-to-all-start = ((bf16[64,16,2048]{2,1,0:T(8,128)(2,1)}), bf16[64,16,2048]{2,1,0:T(8,128)(2,1)}, u32[]{:S(2)}, u32[]{:S(2)}) async-start(bf16[64,16,2048]{2,1,0:T(8,128)(2,1)} %bitcast.200), calls=%async_computation | async-start | bytes 8388608 | tf_op jit(solution)/shard_map/all_to_all | solution.py:926
  139.6 6.2 %copy-start.6 = (bf16[256,2048]{1,0:T(8,128)(2,1)}, bf16[256,2048]{1,0:T(8,128)(2,1)S(1)}, u32[]{:S(2)}) copy-start(bf16[256,2048]{1,0:T(8,128)(2,1)S(1)} %attention_forward.1) | copy-start | bytes 3145732
  139.6 9.6 %copy-start.26 = (bf16[2,1,64,2048]{3,2,1,0:T(8,128)(2,1)S(1)}, bf16[2,1,64,2048]{3,2,1,0:T(8,128)(2,1)}, u32[]{:S(2)}) copy-start(bf16[2,1,64,2048]{3,2,1,0:T(8,128)(2,1)} %param.21) | copy-start | bytes 1572868
  139.7 9.5 %copy-start.48 = (bf16[2,1,56,2048]{3,2,1,0:T(8,128)(2,1)S(1)}, bf16[2,1,56,2048]{3,2,1,0:T(8,128)(2,1)}, u32[]{:S(2)}) copy-start(bf16[2,1,56,2048]{3,2,1,0:T(8,128)(2,1)} %param.20) | copy-start | bytes 1376260
  145.9 36.9 %collective-permute-start = (bf16[2,64,2048]{2,1,0:T(8,128)(2,1)S(1)}, bf16[2,64,2048]{2,1,0:T(8,128)(2,1)S(1)}, u32[]{:S(2)}, u32[]{:S(2)}) collective-permute-start(bf16[2,64,2048]{2,1,0:T(8,128)(2,1)S(1)} %select_convert_fusion.2), channel_id=1, source_target_pairs={{0,1},{1,0},{2,3},{3,2},{4,5},{5,4},{6,7},{7,6},{8,9},{9,8},{10,11... | collective-permute-start | bytes 1572872 | tf_op jit(solution)/shard_map/ppermute | solution.py:897
  150.0 33.2 %copy-start.28 = (bf16[2,64,2048]{2,1,0:T(8,128)(2,1)}, bf16[2,64,2048]{2,1,0:T(8,128)(2,1)S(1)}, u32[]{:S(2)}) copy-start(bf16[2,64,2048]{2,1,0:T(8,128)(2,1)S(1)} %get-tuple-element.170) | copy-start | bytes 1572868
  186.5 42.0 %all-to-all-start.2 = ((bf16[64,8,2048]{2,1,0:T(8,128)(2,1)}), bf16[64,8,2048]{2,1,0:T(8,128)(2,1)S(1)}, u32[]{:S(2)}, u32[]{:S(2)}) async-start(bf16[64,8,2048]{2,1,0:T(8,128)(2,1)} %fusion.5), calls=%async_computation.2 | async-start | bytes 4194304 | tf_op jit(solution)/shard_map/all_to_all | solution.py:926
  229.8 33.9 %all-to-all-start.1 = ((bf16[64,8,2048]{2,1,0:T(8,128)(2,1)}), bf16[64,8,2048]{2,1,0:T(8,128)(2,1)}, u32[]{:S(2)}, u32[]{:S(2)}) async-start(bf16[64,8,2048]{2,1,0:T(8,128)(2,1)} %fusion.4), calls=%async_computation.1 | async-start | bytes 4194304 | tf_op jit(solution)/shard_map/all_to_all | solution.py:926
  235.4 5.0 copy-start.4
  235.4 5.0 copy-start.5
  263.8 40.9 %all-to-all-start.3 = ((bf16[64,8,2048]{2,1,0:T(8,128)(2,1)}), bf16[64,8,2048]{2,1,0:T(8,128)(2,1)}, u32[]{:S(2)}, u32[]{:S(2)}) async-start(bf16[64,8,2048]{2,1,0:T(8,128)(2,1)} %bitcast.217), calls=%async_computation.3 | async-start | bytes 4194304 | tf_op jit(solution)/shard_map/all_to_all | solution.py:926
  304.7 10.8 %copy-start.27 = (bf16[2,1,64,2048]{3,2,1,0:T(8,128)(2,1)S(1)}, bf16[2,1,64,2048]{3,2,1,0:T(8,128)(2,1)}, u32[]{:S(2)}) copy-start(bf16[2,1,64,2048]{3,2,1,0:T(8,128)(2,1)} %param.21) | copy-start | bytes 1572868
  304.7 10.8 %copy-start.32 = (bf16[2,64,2048]{2,1,0:T(8,128)(2,1)S(1)}, bf16[2,64,2048]{2,1,0:T(8,128)(2,1)}, u32[]{:S(2)}) copy-start(bf16[2,64,2048]{2,1,0:T(8,128)(2,1)} %copy-done.31) | copy-start | bytes 1572868
  304.7 37.9 %all-to-all-start.4 = ((bf16[64,8,2048]{2,1,0:T(8,128)(2,1)}), bf16[64,8,2048]{2,1,0:T(8,128)(2,1)S(1)}, u32[]{:S(2)}, u32[]{:S(2)}) async-start(bf16[64,8,2048]{2,1,0:T(8,128)(2,1)} %bitcast.216), calls=%async_computation.4 | async-start | bytes 4194304 | tf_op jit(solution)/shard_map/all_to_all | solution.py:926
  318.6 5.5 copy-start.46
  324.1 20.1 %copy-start.21 = (f32[2,64,2048]{2,1,0:T(8,128)S(1)}, f32[2,64,2048]{2,1,0:T(8,128)}, u32[]{:S(2)}) copy-start(f32[2,64,2048]{2,1,0:T(8,128)} %copy-done.20) | copy-start | bytes 3145732
  342.6 3.3 copy-start.59
  342.6 5.1 copy-start.72
  345.9 8.7 %copy-start.63 = (f32[2,64]{1,0:T(2,128)}, f32[2,64]{1,0:T(2,128)S(1)}, u32[]{:S(2)}) copy-start(f32[2,64]{1,0:T(2,128)S(1)} %broadcast_multiply_fusion.1) | copy-start | bytes 1540
  346.3 14.4 %collective-permute-start.1 = (bf16[2,64,2048]{2,1,0:T(8,128)(2,1)S(1)}, bf16[2,64,2048]{2,1,0:T(8,128)(2,1)S(1)}, u32[]{:S(2)}, u32[]{:S(2)}) collective-permute-start(bf16[2,64,2048]{2,1,0:T(8,128)(2,1)S(1)} %fusion.64), channel_id=1, source_target_pairs={{0,1},{1,0},{2,3},{3,2},{4,5},{5,4},{6,7},{7,6},{8,9},{9,8},{10,11... | collective-permute-start | bytes 1572872 | tf_op jit(solution)/shard_map/ppermute | solution.py:897
  347.7 6.9 %copy-start.11 = (bf16[1024,384]{1,0:T(8,128)(2,1)S(1)}, bf16[1024,384]{1,0:T(8,128)(2,1)}, u32[]{:S(2)}) copy-start(bf16[1024,384]{1,0:T(8,128)(2,1)} %copy-done.10) | copy-start | bytes 2359300
  347.7 7.0 %copy-start.24 = (bf16[1024,2048]{1,0:T(8,128)(2,1)S(1)}, bf16[1024,2048]{1,0:T(8,128)(2,1)}, u32[]{:S(2)}) copy-start(bf16[1024,2048]{1,0:T(8,128)(2,1)} %get-tuple-element.78) | copy-start | bytes 12582916
  361.9 6.1 %copy-start.9 = (bf16[1024,384]{1,0:T(8,128)(2,1)S(1)}, bf16[1024,384]{1,0:T(8,128)(2,1)}, u32[]{:S(2)}) copy-start(bf16[1024,384]{1,0:T(8,128)(2,1)} %copy-done.8) | copy-start | bytes 2359300
  361.9 64.7 %all-to-all-start.5 = ((bf16[64,8,2048]{2,1,0:T(8,128)(2,1)}), bf16[64,8,2048]{2,1,0:T(8,128)(2,1)}, u32[]{:S(2)}, u32[]{:S(2)}) async-start(bf16[64,8,2048]{2,1,0:T(8,128)(2,1)} %bitcast.215), calls=%async_computation.5 | async-start | bytes 4194304 | tf_op jit(solution)/shard_map/all_to_all | solution.py:926
  368.0 5.0 copy-start.61
  374.9 6.1 %copy-start.3 = (bf16[2,640,512]{2,1,0:T(8,128)(2,1)S(1)}, bf16[2,640,512]{2,1,0:T(8,128)(2,1)}, u32[]{:S(2)}) copy-start(bf16[2,640,512]{2,1,0:T(8,128)(2,1)} %copy-done.1) | copy-start | bytes 3932164
  374.9 6.2 %copy-start.15 = (f32[128,128]{1,0:T(8,128)S(1)}, f32[128,128]{1,0:T(8,128)}, u32[]{:S(2)}) copy-start(f32[128,128]{1,0:T(8,128)} %copy-done.14) | copy-start | bytes 196612
  381.1 38.6 %copy-start.7 = (bf16[256,2048]{1,0:T(8,128)(2,1)S(1)}, bf16[256,2048]{1,0:T(8,128)(2,1)}, u32[]{:S(2)}) copy-start(bf16[256,2048]{1,0:T(8,128)(2,1)} %copy-done.6) | copy-start | bytes 3145732
  426.6 9.3 %copy-start.13 = (bf16[256,2560]{1,0:T(8,128)(2,1)S(1)}, bf16[256,2560]{1,0:T(8,128)(2,1)}, u32[]{:S(2)}) copy-start(bf16[256,2560]{1,0:T(8,128)(2,1)} %copy-done.12) | copy-start | bytes 3932164
  426.6 44.9 %all-to-all-start.6 = ((bf16[64,8,2048]{2,1,0:T(8,128)(2,1)}), bf16[64,8,2048]{2,1,0:T(8,128)(2,1)}, u32[]{:S(2)}, u32[]{:S(2)}) async-start(bf16[64,8,2048]{2,1,0:T(8,128)(2,1)} %bitcast.214), calls=%async_computation.6 | async-start | bytes 4194304 | tf_op jit(solution)/shard_map/all_to_all | solution.py:926
  435.9 9.1 %copy-start.52 = (bf16[2,64,512]{1,2,0:T(8,128)(2,1)S(1)}, bf16[2,64,512]{1,2,0:T(8,128)(2,1)}, u32[]{:S(2)}) copy-start(bf16[2,64,512]{1,2,0:T(8,128)(2,1)} %fusion.32) | copy-start | bytes 393220
  441.6 5.5 copy-start.49
  441.8 28.4 %collective-permute-start.3 = (bf16[2,64,2048]{2,1,0:T(8,128)(2,1)S(1)}, bf16[2,64,2048]{2,1,0:T(8,128)(2,1)S(1)}, u32[]{:S(2)}, u32[]{:S(2)}) collective-permute-start(bf16[2,64,2048]{2,1,0:T(8,128)(2,1)S(1)} %select_convert_fusion.1), channel_id=1, source_target_pairs={{0,1},{1,0},{2,3},{3,2},{4,5},{5,4},{6,7},{7,6},{8,9},{9,8},{10,11... | collective-permute-start | bytes 1572872 | tf_op jit(solution)/shard_map/ppermute | solution.py:897
  447.2 22.9 %copy-start.29 = (bf16[2,64,2048]{2,1,0:T(8,128)(2,1)S(1)}, bf16[2,64,2048]{2,1,0:T(8,128)(2,1)}, u32[]{:S(2)}) copy-start(bf16[2,64,2048]{2,1,0:T(8,128)(2,1)} %copy-done.28) | copy-start | bytes 1572868
  447.2 22.9 %copy-start.57 = (f32[2048,1]{0,1:T(1,128)S(1)}, f32[2048,1]{0,1:T(1,128)}, u32[]{:S(2)}) copy-start(f32[2048,1]{0,1:T(1,128)} %copy-done.55) | copy-start | bytes 24580
  447.2 22.9 %copy-start.62 = (f32[2,64]{1,0:T(2,128)S(1)}, f32[2,64]{1,0:T(2,128)}, u32[]{:S(2)}) copy-start(f32[2,64]{1,0:T(2,128)} %add_rsqrt_fusion) | copy-start | bytes 1540
  471.5 4.6 copy-start.43
  471.5 4.6 copy-start.44
  477.7 7.3 %copy-start.70 = (bf16[128]{0:T(256)(128)(2,1)S(1)}, bf16[128]{0:T(256)(128)(2,1)}, u32[]{:S(2)}) copy-start(bf16[128]{0:T(256)(128)(2,1)} %pad.37.clone) | copy-start | bytes 772
  477.7 13.9 %collective-permute-start.2 = (bf16[2,64,2048]{2,1,0:T(8,128)(2,1)}, bf16[2,64,2048]{2,1,0:T(8,128)(2,1)}, u32[]{:S(2)}, u32[]{:S(2)}) collective-permute-start(bf16[2,64,2048]{2,1,0:T(8,128)(2,1)} %get-tuple-element.178), channel_id=1, source_target_pairs={{0,1},{1,0},{2,3},{3,2},{4,5},{5,4},{6,7},{7,6},{8,9},{9,8},{10,11... | collective-permute-start | bytes 1572872 | tf_op jit(solution)/shard_map/ppermute | solution.py:897
  486.7 92.7 %collective-permute-start.4 = (bf16[2,64,2048]{2,1,0:T(8,128)(2,1)S(1)}, bf16[2,64,2048]{2,1,0:T(8,128)(2,1)S(1)}, u32[]{:S(2)}, u32[]{:S(2)}) collective-permute-start(bf16[2,64,2048]{2,1,0:T(8,128)(2,1)S(1)} %copy-done.42), channel_id=1, source_target_pairs={{0,1},{1,0},{2,3},{3,2},{4,5},{5,4},{6,7},{7,6},{8,9},{9,8},{10,11... | collective-permute-start | bytes 1572872 | tf_op jit(solution)/shard_map/ppermute | solution.py:897
  (37 other events, 72.2 us)

commit v4 on v3

--- a/solution.py
+++ b/solution.py
@@ -72,16 +72,21 @@
 
 
 def gather_kernel(
-    a_ref, b_ref, gate_ref, up_ref, down_ref, a_all, b_all, gate_all, up_all, down_all,
-    local_sem, send_sem, recv_sem, away_sem, home_sem, give_sem, take_sem,
+    query_ref, key_ref, value_ref, out_ref, extra_ref, gate_ref, up_ref, down_ref,
+    a_all, b_all, gate_all, up_all, down_all, a_own, b_own, local_sem, send_sem, recv_sem, away_sem, home_sem, give_sem, take_sem,
 ):
     y, core, z, x = place()
+    for own, refs in ((a_own, (query_ref, key_ref, value_ref)), (b_own, (out_ref, extra_ref))):
+        at = 0
+        for ref in refs:
+            own[:, at : at + ref.shape[1]] = ref[...]
+            at += ref.shape[1]
     greet(neighbours() + [opposite()])
     shards = ((gate_ref, gate_all), (up_ref, up_all), (down_ref, down_all))
     moved = [
         swap_opposite(p, q, give_sem.at[n], take_sem.at[n]) for n, (p, q) in enumerate(shards)
     ]
-    refs, own = (a_all, b_all), (a_ref, b_ref)
+    refs, own = (a_all, b_all), (a_own, b_own)
     started = []
     count = [0, 0]
 
@@ -200,17 +205,18 @@
             copy.wait()
 
 
-def gather_weights(a, b, gate, up, down):
-    rows = a.shape[0]
+def gather_weights(query, key, value, out, extra, gate, up, down):
+    rows = query.shape[0]
+    cols = (query.shape[1] + key.shape[1] + value.shape[1], out.shape[1] + extra.shape[1])
     shape = (RING, 2, RING, 2, rows)
     any_space = pl.BlockSpec(memory_space=pl.ANY)
     a_all, b_all, *experts = pl.pallas_call(
         gather_kernel,
-        in_specs=[pl.BlockSpec(memory_space=pltpu.VMEM)] * 2 + [any_space] * 3,
+        in_specs=[pl.BlockSpec(memory_space=pltpu.VMEM)] * 5 + [any_space] * 3,
         out_specs=[any_space] * 5,
-        out_shape=[jax.ShapeDtypeStruct(shape + (v.shape[1],), v.dtype) for v in (a, b)]
+        out_shape=[jax.ShapeDtypeStruct(shape + (c,), query.dtype) for c in cols]
         + [jax.ShapeDtypeStruct(v.shape, v.dtype) for v in (gate, up, down)],
-        scratch_shapes=[
+        scratch_shapes=[pltpu.VMEM((rows, c), query.dtype) for c in cols] + [
             pltpu.SemaphoreType.DMA((2,)),
             pltpu.SemaphoreType.DMA((2, 21)),
             pltpu.SemaphoreType.DMA((2, 21)),
@@ -222,8 +228,8 @@
         compiler_params=pltpu.CompilerParams(collective_id=0, has_side_effects=True),
         cost_estimate=pl.CostEstimate(flops=0, bytes_accessed=250_000_000, transcendentals=0),
         name="gather_weights",
-    )(a, b, gate, up, down)
-    return a_all.reshape(-1, a.shape[1]), b_all.reshape(-1, b.shape[1]), *experts
+    )(query, key, value, out, extra, gate, up, down)
+    return a_all.reshape(-1, cols[0]), b_all.reshape(-1, cols[1]), *experts
 
 
 ORDER = (2, 1, 3, 0)
@@ -572,15 +578,16 @@
     mine = pl.ds(pl.multiple_of(c * BLOCK, BLOCK), BLOCK)
     earlier, own = pl.ds(CTX * BLOCK, BLOCK), pl.ds((CTX + 1) * BLOCK, BLOCK)
 
-    def group(m, h, total):
+    def head_cols(h):
+        return pl.ds(pl.multiple_of(h * HEAD_SIZE, HEAD_SIZE), HEAD_SIZE)
+
+    def keys_back(m, h, carry):
         span = slice(m * rows, (m + 1) * rows)
-        k_cols = pl.ds(pl.multiple_of(h * HEAD_SIZE, HEAD_SIZE), HEAD_SIZE)
-        v_cols = pl.ds(pl.multiple_of((kv + h) * HEAD_SIZE, HEAD_SIZE), HEAD_SIZE)
-        k, v = kv_ref[m, :, k_cols], kv_ref[m, :, v_cols]
+        k, v = kv_ref[m, :, head_cols(h)], kv_ref[m, :, head_cols(kv + h)]
         for e in range(heads):
-            cols = pl.ds(pl.multiple_of((h * heads + e) * HEAD_SIZE, HEAD_SIZE), HEAD_SIZE)
+            cols = head_cols(h * heads + e)
             stack = slice(e * rows, (e + 1) * rows)
-            q_low, normed, scaling = rotated(qkv_ref[span, cols], gq, cosine, sine)
+            q_low = rotated(qkv_ref[span, cols], gq, cosine, sine)[0]
             q_all[stack, :] = q_low
             p = softmax_parts(q_low, k, bias_ref[...])
             p_all[stack, :] = p.astype(BF16)
@@ -588,19 +595,29 @@
             do_all[stack, :] = do
             dp = dot(do, v, ((1,), (1,)))
             ds = (p * (dp - jnp.sum(dp * p, axis=-1, keepdims=True))).astype(BF16)
-            ds_all[stack, :] = ds
+            ds_all[m * kv + h, stack, :] = ds
+        grads[m, :, head_cols(kv + h)] = dot(p_all[...], do_all[...], ((0,), (0,))).astype(BF16)
+        d_k = dot(ds_all[m * kv + h], q_all[...], ((0,), (0,))) * scale
+        grads[m, :, head_cols(h)] = d_k.astype(BF16)
+        return carry
+
+    def queries_back(m, h, total):
+        span = slice(m * rows, (m + 1) * rows)
+        k = kv_ref[m, :, head_cols(h)]
+        for e in range(heads):
+            cols = head_cols(h * heads + e)
+            ds = ds_all[m * kv + h, e * rows : (e + 1) * rows, :]
             dqr = (dot(ds, k, ((1,), (0,))) * scale).astype(BF16).astype(F32)
-            dq, part = rotated_back(dqr, normed, scaling, gq, cosine, sine)
+            u = qkv_ref[span, cols]
+            scaling = lax.rsqrt(jnp.mean(u * u, axis=-1, keepdims=True) + EPS)
+            dq, part = rotated_back(dqr, u * scaling, scaling, gq, cosine, sine)
             dqkv_ref[span, cols] = dq.astype(BF16)
             total = total + part
-        grads[m, :, v_cols] = dot(p_all[...], do_all[...], ((0,), (0,))).astype(BF16)
-        grads[m, :, k_cols] = (dot(ds_all[...], q_all[...], ((0,), (0,))) * scale).astype(BF16)
         return total
 
-    total = jnp.zeros((1, HEAD_SIZE), F32)
     copies = []
     for m in range(micro):
-        total = lax.fori_loop(0, kv, functools.partial(group, m), total)
+        lax.fori_loop(0, kv, functools.partial(keys_back, m), 0)
         for step in range(1, CTX):
             peer = lax.rem(c + step, CTX)
             part = grads.at[m, pl.ds(pl.multiple_of(peer * BLOCK, BLOCK), BLOCK)]
@@ -618,6 +635,9 @@
         )
         for copy in copies[-CTX:]:
             copy.start()
+    total = jnp.zeros((1, HEAD_SIZE), F32)
+    for m in range(micro):
+        total = lax.fori_loop(0, kv, functools.partial(queries_back, m), total)
     k_total = jnp.zeros((1, HEAD_SIZE), F32)
     for m in range(micro):
         for copy in copies[m * CTX : (m + 1) * CTX]:
@@ -712,7 +732,7 @@
             pltpu.VMEM((CTX - 1, micro, BLOCK, kv_cols), BF16),
             pltpu.VMEM((micro, BLOCK, kv_cols), BF16),
             pltpu.VMEM((heads * rows, keys), BF16),
-            pltpu.VMEM((heads * rows, keys), BF16),
+            pltpu.VMEM((micro * kv, heads * rows, keys), BF16),
             pltpu.VMEM((heads * rows, HEAD_SIZE), BF16),
             pltpu.VMEM((heads * rows, HEAD_SIZE), BF16),
             pltpu.SemaphoreType.DMA((CTX, micro)),
@@ -726,7 +746,29 @@
     )(qkv, cosine, sine, gain_query, gain_key, bias, kv_all, d_out)
 
 
-PART = 256
+CHIPS = RING * RING * RING
+GROUP = 16
+MIX = 27
+
+
+def chip_at(slot, sign):
+    f, c, t = lax.axis_index("fsdp"), lax.axis_index("ctx"), lax.axis_index("tp")
+    k = slot * MIX % CHIPS
+    turn = RING * sign
+    y = (f // 2 + turn + sign * (k // (RING * RING))) % RING
+    z = (c // 2 + turn + sign * (k // RING % RING)) % RING
+    x = (t * 2 + c % 2 + turn + sign * (k % RING)) % RING
+    return y, z, x
+
+
+def device_at(slot, sign):
+    y, z, x = chip_at(slot, sign)
+    return {"fsdp": y * 2 + lax.axis_index("fsdp") % 2, "ctx": z * 2 + x % 2, "tp": x // 2}
+
+
+def chip_number(slot, sign):
+    y, z, x = chip_at(slot, sign)
+    return (y * 2 * RING + z * 2 + x % 2) * 2 + x // 2
 
 
 def other_core():
@@ -734,25 +776,90 @@
     return {"fsdp": f + 1 - 2 * (f % 2)}
 
 
-def expert_kernel(
-    got_ref, deo_ref, gate_ref, up_ref, down_ref, gate_far, up_far, down_far, back_ref, eo_ref, rows_ref, deos_ref, z_ref, dgu_ref,
-    rows, deos, gu, down, own, give, take, load_sem, send_sem, recv_sem, save_sem,
+def moe_kernel(
+    send_ref, deo_ref, gate_ref, up_ref, down_ref, gate_far, up_far, down_far,
+    back_ref, eo_ref, rows_ref, deos_ref, z_ref, dgu_ref,
+    rows, deos, gu, down, give, take,
+    go_sem, come_sem, load_sem, weight_sem, share_send, share_recv, part_send, part_recv,
+    save_sem, back_send, back_recv, eo_sem,
 ):
-    greet([other_core()])
-    count, hidden = got_ref.shape[0], down_ref.shape[0]
-    parts = count // PART
-    near, far = pl.ds(0, count), pl.ds(count, count)
-    swaps = [
-        remote(got_ref, rows.at[far], send_sem.at[0], recv_sem.at[0], other_core()),
-        remote(deo_ref, deos.at[far], send_sem.at[1], recv_sem.at[1], other_core()),
-    ]
-    loads = [
-        pltpu.make_async_copy(got_ref, rows.at[near], load_sem.at[0]),
-        pltpu.make_async_copy(deo_ref, deos.at[near], load_sem.at[1]),
-    ]
+    size, hidden = send_ref.shape[1], down_ref.shape[0]
+    count = GROUP * size
+    groups = CHIPS // GROUP
+    total = CHIPS * size
+
+    def each(body, low, high):
+        def step(i, carry):
+            body(i)
+            return carry
+
+        lax.fori_loop(low, high, step, 0)
+
+    barrier = pltpu.get_barrier_semaphore()
+    each(
+        lambda s: pl.semaphore_signal(
+            barrier, inc=1, device_id=device_at(s, 1), device_id_type=MESH
+        ),
+        1, CHIPS,
+    )
+    pl.semaphore_signal(barrier, inc=1, device_id=other_core(), device_id_type=MESH)
+    pl.semaphore_wait(barrier, CHIPS)
+
+    def slot_rows(s):
+        return pl.ds(pl.multiple_of(s * size, size), size)
+
+    def group_rows(g):
+        return pl.ds(pl.multiple_of(g * count, count), count)
+
+    def go(s):
+        return remote(
+            send_ref.at[s], rows.at[0, slot_rows(s)], go_sem.at[s], come_sem.at[s], device_at(s, 1)
+        )
+
+    def stay(s):
+        return pltpu.make_async_copy(send_ref.at[s], rows.at[0, slot_rows(s)], come_sem.at[s])
+
+    def load(s):
+        return pltpu.make_async_copy(
+            deo_ref.at[chip_number(s, -1)], deos.at[0, slot_rows(s)], load_sem.at[s]
+        )
+
+    def back(s):
+        return remote(
+            rows.at[0, slot_rows(s)], back_ref.at[s], back_send.at[s], back_recv.at[s],
+            device_at(s, -1),
+        )
+
+    def back_stay():
+        return pltpu.make_async_copy(rows.at[0, slot_rows(0)], back_ref.at[0], back_recv.at[0])
+
+    def out(s):
+        return pltpu.make_async_copy(
+            deos.at[0, slot_rows(s)], eo_ref.at[chip_number(s, -1)], eo_sem.at[s]
+        )
+
+    def share(n, g):
+        ref = (rows, deos)[n]
+        return remote(
+            ref.at[0, group_rows(g)], ref.at[1, group_rows(g)], share_send.at[n, g],
+            share_recv.at[n, g], other_core(),
+        )
+
+    def part(n, g):
+        return remote(
+            give.at[n, group_rows(g)], take.at[n, group_rows(g)], part_send.at[n, g],
+            part_recv.at[n, g], other_core(),
+        )
+
+    def save(n, side, g):
+        ref, to = ((rows, rows_ref), (deos, deos_ref))[n]
+        return pltpu.make_async_copy(
+            ref.at[side, group_rows(g)], to.at[side, group_rows(g)], save_sem.at[n, side, g]
+        )
+
     places = (gu.at[:, pl.ds(0, hidden)], gu.at[:, pl.ds(hidden, hidden)], down)
     weights = [
-        [pltpu.make_async_copy(src, dst, load_sem.at[2 + n]) for n, (src, dst) in enumerate(pairs)]
+        [pltpu.make_async_copy(src, dst, weight_sem.at[n]) for n, (src, dst) in enumerate(pairs)]
         for pairs in (
             zip((gate_ref, up_ref, down_ref), places), zip((gate_far, up_far, down_far), places)
         )
@@ -766,118 +873,117 @@
                 for copy in copies:
                     act(copy)
 
-    saves = [
-        pltpu.make_async_copy(rows, rows_ref, save_sem.at[0]),
-        pltpu.make_async_copy(deos, deos_ref, save_sem.at[1]),
-    ]
-    for copy in loads + swaps:
-        copy.start()
+    stay(0).start()
+    each(lambda s: go(s).start(), 1, CHIPS)
+    each(lambda s: load(s).start(), 0, CHIPS)
     on_weights(lambda copy: copy.start())
 
-    def span(i):
-        return pl.ds(pl.multiple_of(i * PART, PART), PART)
-
-    def returned(kind, i):
-        slot = kind * parts + i
-        return remote(
-            give.at[kind, span(i)], take.at[kind, span(i)], send_sem.at[2 + slot],
-            recv_sem.at[2 + slot], other_core(),
-        )
-
-    def through(i):
-        pre = dot(rows[span(i), :], gu[...], ((1,), (0,)))
-        dz = dot(deos[span(i), :], down[...], ((1,), (1,)))
-        g, u = pre[:, :hidden], pre[:, hidden:]
-        sig = 1.0 / (1.0 + jnp.exp(-g))
-        act = g * sig
-        z_ref[span(i), :] = (act * u).astype(BF16)
-        dgu_ref[span(i), :hidden] = (dz * u * sig * (1.0 + g * (1.0 - sig))).astype(BF16)
-        dgu_ref[span(i), hidden:] = (dz * act).astype(BF16)
-
-    def to_rows(i):
-        return dot(dgu_ref[span(i), :], gu[...], ((1,), (1,)))
-
-    def to_outputs(i):
-        return dot(z_ref[span(i), :], down[...], ((1,), (0,)))
-
-    def each(body):
-        def step(i, carry):
-            body(i)
-            return carry
-
-        lax.fori_loop(0, parts, step, 0)
-
-    def give_rows(i):
-        through(parts + i)
-        give[0, span(i), :] = to_rows(parts + i).astype(BF16)
-        returned(0, i).start()
-
-    def keep_rows(i):
-        own[span(i), :] = to_rows(i)
-
-    def give_outputs(i):
-        give[1, span(i), :] = to_outputs(parts + i).astype(BF16)
-        returned(1, i).start()
-
-    def end_rows(i):
-        returned(0, i).wait()
-        back_ref[span(i), :] = (own[span(i), :] + take[0, span(i), :].astype(F32)).astype(BF16)
-
-    def end_outputs(i):
-        total = to_outputs(i)
-        returned(1, i).wait()
-        eo_ref[span(i), :] = (total + take[1, span(i), :].astype(F32)).astype(BF16)
-
-    for copy in loads:
-        copy.wait()
+    def through(side, g):
+        at = group_rows(g)
+        kept = pl.ds(pl.multiple_of(side * total + g * count, count), count)
+        pre = dot(rows[side, at, :], gu[...], ((1,), (0,)))
+        dz = dot(deos[side, at, :], down[...], ((1,), (1,)))
+        gate, u = pre[:, :hidden], pre[:, hidden:]
+        sig = 1.0 / (1.0 + jnp.exp(-gate))
+        act = gate * sig
+        z_ref[kept, :] = (act * u).astype(BF16)
+        dgu_ref[kept, :hidden] = (dz * u * sig * (1.0 + gate * (1.0 - sig))).astype(BF16)
+        dgu_ref[kept, hidden:] = (dz * act).astype(BF16)
+
+    def to_rows(side, g):
+        kept = pl.ds(pl.multiple_of(side * total + g * count, count), count)
+        return dot(dgu_ref[kept, :], gu[...], ((1,), (1,)))
+
+    def to_outputs(side, g):
+        kept = pl.ds(pl.multiple_of(side * total + g * count, count), count)
+        return dot(z_ref[kept, :], down[...], ((1,), (0,)))
+
     on_weights(lambda copy: copy.wait())
-    each(through)
-    for copy in swaps:
-        copy.wait_recv()
-    for copy in saves:
-        copy.start()
-    each(give_rows)
-    each(give_outputs)
-    each(keep_rows)
-    each(end_rows)
-    each(end_outputs)
-    for copy in swaps:
-        copy.wait_send()
-    for copy in saves:
-        copy.wait()
-
-
-def expert(got, d_eo, own, far, collective):
-    count, width = got.shape
+
+    def group(g):
+        first, last = g * GROUP, (g + 1) * GROUP
+
+        @pl.when(g == 0)
+        def _():
+            stay(0).wait()
+
+        each(lambda s: go(s).wait_recv(), lax.max(first, 1), last)
+        each(lambda s: load(s).wait(), first, last)
+        for n in (0, 1):
+            share(n, g).start()
+            save(n, 0, g).start()
+        through(0, g)
+        for n in (0, 1):
+            share(n, g).wait_recv()
+            save(n, 1, g).start()
+        through(1, g)
+        give[0, group_rows(g), :] = to_rows(1, g).astype(BF16)
+        part(0, g).start()
+        give[1, group_rows(g), :] = to_outputs(1, g).astype(BF16)
+        part(1, g).start()
+        own = to_rows(0, g)
+        part(0, g).wait_recv()
+        share(0, g).wait_send()
+        save(0, 0, g).wait()
+        at = group_rows(g)
+        rows[0, at, :] = (own + take[0, at, :].astype(F32)).astype(BF16)
+
+        @pl.when(g == 0)
+        def _():
+            back_stay().start()
+
+        each(lambda s: back(s).start(), lax.max(first, 1), last)
+        own = to_outputs(0, g)
+        part(1, g).wait_recv()
+        share(1, g).wait_send()
+        save(1, 0, g).wait()
+        deos[0, at, :] = (own + take[1, at, :].astype(F32)).astype(BF16)
+        each(lambda s: out(s).start(), first, last)
+
+    each(group, 0, groups)
+
+    def finish(g):
+        for n in (0, 1):
+            part(n, g).wait_send()
+            save(n, 1, g).wait()
+
+    each(finish, 0, groups)
+    each(lambda s: out(s).wait(), 0, CHIPS)
+    back_stay().wait()
+    each(lambda s: go(s).wait_send(), 1, CHIPS)
+    each(lambda s: back(s).wait(), 1, CHIPS)
+
+
+def moe(send, d_eo, own, far):
+    chips, size, width = send.shape
     hidden = own[2].shape[0]
-    parts = count // PART
+    total, groups = chips * size, chips // GROUP
     vmem, any_space = (pl.BlockSpec(memory_space=space) for space in (pltpu.VMEM, pl.ANY))
-    shapes = [(count, width), (count, width), (2 * count, width), (2 * count, width)]
-    shapes += [(2 * count, hidden), (2 * count, 2 * hidden)]
+    shapes = [send.shape, send.shape, (2, total, width), (2, total, width)]
+    shapes += [(2 * total, hidden), (2 * total, 2 * hidden)]
+    dma = pltpu.SemaphoreType.DMA
     return pl.pallas_call(
-        expert_kernel,
+        moe_kernel,
         in_specs=[any_space] * 8,
-        out_specs=[vmem] * 2 + [any_space] * 2 + [vmem] * 2,
+        out_specs=[any_space] * 4 + [vmem] * 2,
         out_shape=[jax.ShapeDtypeStruct(shape, BF16) for shape in shapes],
         scratch_shapes=[
-            pltpu.VMEM((2 * count, width), BF16),
-            pltpu.VMEM((2 * count, width), BF16),
+            pltpu.VMEM((2, total, width), BF16),
+            pltpu.VMEM((2, total, width), BF16),
             pltpu.VMEM((width, 2 * hidden), BF16),
             pltpu.VMEM((hidden, width), BF16),
-            pltpu.VMEM((count, width), F32),
-            pltpu.VMEM((2, count, width), BF16),
-            pltpu.VMEM((2, count, width), BF16),
-            pltpu.SemaphoreType.DMA((5,)),
-            pltpu.SemaphoreType.DMA((2 + 2 * parts,)),
-            pltpu.SemaphoreType.DMA((2 + 2 * parts,)),
-            pltpu.SemaphoreType.DMA((2,)),
+            pltpu.VMEM((2, total, width), BF16),
+            pltpu.VMEM((2, total, width), BF16),
+            dma((chips,)), dma((chips,)), dma((chips,)), dma((3,)),
+            dma((2, groups)), dma((2, groups)), dma((2, groups)), dma((2, groups)),
+            dma((2, 2, groups)), dma((chips,)), dma((chips,)), dma((chips,)),
         ],
         compiler_params=pltpu.CompilerParams(
-            collective_id=collective, has_side_effects=True, vmem_limit_bytes=VMEM_LIMIT
+            collective_id=4, has_side_effects=True, vmem_limit_bytes=56 * 1024 * 1024
         ),
-        cost_estimate=pl.CostEstimate(flops=0, bytes_accessed=80_000_000, transcendentals=0),
-        name="expert_both_ways",
-    )(got, d_eo, *own, *far)
+        cost_estimate=pl.CostEstimate(flops=0, bytes_accessed=400_000_000, transcendentals=0),
+        name="experts",
+    )(send, d_eo, *own, *far)
 
 
 def normalize(rows, gain):
@@ -940,46 +1046,43 @@
     own_ids = jnp.where(first, ids_cont[:, 0], ids_pad)
     own_gates = jnp.where(first, gates_cont[:, 0], pad(gates_prompt))
 
-    named = own_ids[:, :, :, None] == expert_of
-    chosen = jnp.any(named, axis=2)
-    weight = jnp.sum(jnp.where(named, own_gates[:, :, :, None], 0.0), axis=2)
     lower = jnp.tril(jnp.ones((block, block), BF16), -1)
-    rank = jnp.einsum("ts,mse->mte", lower, chosen.astype(BF16), preferred_element_type=F32)
-    place = jnp.where(chosen, rank, -1.0)
-    placed = place[:, :, :, None] == jnp.arange(slots, dtype=F32)
-    select = placed.astype(BF16).reshape(micro, block, peers * slots)
     same = jnp.arange(micro)[:, None] == jnp.arange(micro)[None, :]
-    both = jnp.logical_and(placed[:, :, :, None, :], same[:, None, None, :, None])
     flat = (micro * block, peers * micro * slots)
-    select_both = both.astype(BF16).reshape(flat)
-    mixing = jnp.where(placed, weight[:, :, :, None], 0.0).reshape(select.shape)
+
+    def routing(experts):
+        named = own_ids[:, :, :, None] == experts
+        chosen = jnp.any(named, axis=2)
+        weight = jnp.sum(jnp.where(named, own_gates[:, :, :, None], 0.0), axis=2)
+        rank = jnp.einsum("ts,mse->mte", lower, chosen.astype(BF16), preferred_element_type=F32)
+        place = jnp.where(chosen, rank, -1.0)
+        placed = place[:, :, :, None] == jnp.arange(slots, dtype=F32)
+        both = jnp.logical_and(placed[:, :, :, None, :], same[:, None, None, :, None])
+        return both, weight[:, :, :, None, None]
+
+    placed, weight = routing(expert_of)
+    select = placed.astype(BF16).reshape(flat)
+    mixing = jnp.where(placed, weight, 0.0).reshape(flat)
     mixing_high = mixing.astype(BF16)
     mixing_low = (mixing - mixing_high.astype(F32)).astype(BF16)
-    slot_gate = jnp.sum(mixing, axis=1).reshape(micro, peers, slots).swapaxes(0, 1).reshape(-1)
-
-    extra = jnp.concatenate(
-        [
-            norm_gain[:, None],
-            moe_gain[:, None],
-            jnp.pad(query_gain, (0, shard_rows - query_gain.shape[0]))[:, None],
-            jnp.pad(key_gain, (0, shard_rows - key_gain.shape[0]))[:, None],
-            jnp.zeros((shard_rows, 124), BF16),
-        ],
-        axis=1,
-    )
+    slot_gate = jnp.sum(mixing, axis=0)
+    y, z, x = chip_at(jnp.arange(peers, dtype=jnp.int32), 1)
+    select_near = routing((2 * y + x // 2) * ctx + 2 * z + x % 2)[0].astype(BF16).reshape(flat)
+
+    def lanes(v):
+        return jnp.pad(v, [(0, 0)] * (v.ndim - 1) + [(0, HEAD_SIZE - v.shape[-1])])
+
+    extra = jnp.stack([lanes(v) for v in (norm_gain, moe_gain, query_gain, key_gain)])
+    extra = jnp.pad(extra, ((0, shard_rows - extra.shape[0]), (0, 0)))
+    own_experts = (expert_gate[0], expert_up[0], expert_down[0])
     w_qkv, w_out_extra, *far_experts = gather_weights(
-        jnp.concatenate([query_weight, key_matrix, value_matrix], axis=1),
-        jnp.concatenate([out_weight, extra], axis=1),
-        expert_gate[0],
-        expert_up[0],
-        expert_down[0],
+        query_weight, key_matrix, value_matrix, out_weight, extra, *own_experts
     )
     w_out = w_out_extra[:, :q_cols]
-    gains = w_out_extra[:, q_cols:].astype(F32)
-    gain_in, gain_moe = gains[:, 0], gains[:, 1]
-    head_gains = gains[:, 2:4].reshape(peers, shard_rows, 2)[:, : query_gain.shape[0]]
-    head_gains = head_gains.reshape(HEAD_SIZE, 2)
-    gain_query, gain_key = head_gains[:, 0], head_gains[:, 1]
+    gains = w_out_extra[:, q_cols:].reshape(peers, shard_rows, HEAD_SIZE)[:, :4].astype(F32)
+    gain_in, gain_moe = (gains[:, n, :shard_rows].reshape(-1) for n in (0, 1))
+    head_rows = query_gain.shape[0]
+    gain_query, gain_key = (gains[:, n, :head_rows].reshape(-1) for n in (2, 3))
 
     offsets = jnp.arange(rows, dtype=jnp.int32)
     is_prompt = offsets < block
@@ -1028,70 +1131,50 @@
     heads_in = (cosine, sine, gain_query[None], gain_key[None], bias)
     kv_all = share_keys(qkv, cosine, sine, gain_key[None], kv, keys, micro)
 
-    spread = dot(select_both, own_cot.astype(BF16).reshape(-1, width), ((0,), (0,)))
+    spread = dot(select, own_cot.astype(BF16).reshape(-1, width), ((0,), (0,)))
     spread = (spread * slot_gate[:, None]).astype(BF16)
     spread, kv_all = lax.optimization_barrier((spread, kv_all))
-    d_eo_rows = exchange(spread)
+    d_eo_rows = exchange(spread).reshape(peers, micro * slots, width)
     o = attention(qkv, cosine, sine, gain_query[None], bias, kv_all, kv)
     middle = own_tokens + sum_own(dot(o, w_out, ((1,), (1,))))
     b_normed, b_scale = normalize(middle, gain_moe)
     b_low = b_normed.astype(BF16)
 
-    b_low, d_eo_rows = lax.optimization_barrier((b_low, d_eo_rows))
-    d_eo_rows = d_eo_rows.reshape(peers, micro, slots, width)
-    backs, outputs, wide_terms, tall_terms = [], [], [], []
-    for m in range(micro):
-        got = exchange(dot(select[m], b_low[m], ((0,), (0,))).astype(BF16))
-        back, eo, rows_m, d_eo_m, z_m, d_gu_m = expert(
-            got, d_eo_rows[:, m].reshape(-1, width), (expert_gate[0], expert_up[0], expert_down[0]),
-            far_experts, 4 + m,
-        )
-        backs.append(exchange(back))
-        outputs.append(eo)
-        wide_terms.append((rows_m, d_gu_m))
-        tall_terms.append((z_m, d_eo_m))
-
-    def over_rows(terms):
-        return sum(dot(left, right, ((0,), (0,))) for left, right in terms).astype(BF16)
-
-    wide_here, tall_here = over_rows(wide_terms), over_rows(tall_terms)
-
-    d_b = jnp.stack([dot(select[m], backs[m], ((1,), (0,))) for m in range(micro)])
+    send = dot(select_near, b_low.reshape(-1, width), ((0,), (0,))).astype(BF16)
+    back, eo, rows_in, d_eo_in, z, d_gu = moe(
+        send.reshape(d_eo_rows.shape), d_eo_rows, own_experts, far_experts
+    )
+    wide_here = dot(rows_in.reshape(-1, width), d_gu, ((0,), (0,))).astype(BF16)
+    tall_here = dot(z, d_eo_in.reshape(-1, width), ((0,), (0,))).astype(BF16)
+    d_b = dot(select_near, back.reshape(-1, width), ((1,), (0,))).reshape(middle.shape)
     middle_from, moe_total = normalize_back(middle, b_scale, gain_moe, d_b)
     d_h = own_cot + middle_from
     d_attn = jnp.concatenate(share_rows(d_h.astype(BF16)), axis=1).reshape(-1, width)
 
-    late, d_attn = lax.optimization_barrier((outputs[0], d_attn))
-    eo_back = [exchange(late)]
+    late, d_attn = lax.optimization_barrier((eo, d_attn))
+    eo_back = exchange(late.reshape(-1, width))
 
     d_o = dot(d_attn, w_out, ((1,), (0,))).astype(BF16)
     grad_out = dot(d_attn, o, ((0,), (0,))).astype(BF16)
     d_qkv, head_totals = attention_back(qkv, *heads_in, kv_all, d_o, kv)
-    for m in range(1, micro):
-        late, d_qkv, eo_back[m - 1] = lax.optimization_barrier((outputs[m], d_qkv, eo_back[m - 1]))
-        eo_back.append(exchange(late))
-    moe_out = [
-        dot(high, eo, ((1,), (0,))) + dot(low, eo, ((1,), (0,)))
-        for high, low, eo in zip(mixing_high, mixing_low, eo_back)
-    ]
-    out_first, out_second = share_rows((middle + jnp.stack(moe_out)).astype(BF16))
+    d_qkv, eo_back = lax.optimization_barrier((d_qkv, eo_back))
+    moe_out = dot(mixing_high, eo_back, ((1,), (0,))) + dot(mixing_low, eo_back, ((1,), (0,)))
+    out_first, out_second = share_rows((middle + moe_out.reshape(middle.shape)).astype(BF16))
     input_grad = sum_own(dot(d_qkv, w_qkv, ((1,), (1,))))
     grad_qkv = dot(a, d_qkv, ((0,), (0,))).astype(BF16)
     scale_in = lax.rsqrt(jnp.mean(own_tokens * own_tokens, axis=-1, keepdims=True) + EPS)
     token_from, norm_total = normalize_back(own_tokens, scale_in, gain_in, input_grad)
     grad_first, grad_second = share_rows((d_h + token_from).astype(BF16))
 
-    head_grads = head_totals.T.reshape(peers, -1, 2)
-    head_grads = jnp.pad(head_grads, ((0, 0), (0, shard_rows - head_grads.shape[1]), (0, 0)))
-    extra_grads = jnp.concatenate(
+    extra_grads = jnp.stack(
         [
-            norm_total[:, None],
-            moe_total[:, None],
-            head_grads.reshape(-1, 2),
-            jnp.zeros((peers * shard_rows, 124), F32),
+            lanes(v.reshape(peers, -1))
+            for v in (norm_total, moe_total, head_totals[0], head_totals[1])
         ],
         axis=1,
-    ).astype(BF16)
+    )
+    extra_grads = jnp.pad(extra_grads, ((0, 0), (0, shard_rows - extra_grads.shape[1]), (0, 0)))
+    extra_grads = extra_grads.reshape(-1, HEAD_SIZE).astype(BF16)
     grad_qkv, out_first, out_second = lax.optimization_barrier((grad_qkv, out_first, out_second))
     share, share_out, wide_there, tall_there = scatter_grads(
         grad_qkv, grad_out, extra_grads, wide_here, tall_here
@@ -1099,21 +1182,19 @@
     grad_wide = jnp.where(native(), wide_here, wide_there).astype(F32)
     grad_down = jnp.where(native(), tall_here, tall_there).astype(F32)
     gain_share = share_out[:, q_cols:]
-    head_rows = query_gain.shape[0]
-
     return (
         out_first[:, None, :prompt_rows],
         out_second[:, None],
         grad_first[:, None, :prompt_rows],
         grad_second[:, None],
-        gain_share[:, 0],
+        gain_share[0, :shard_rows],
         share[:, :q_cols],
         share[:, q_cols : q_cols + kv_cols],
         share[:, q_cols + kv_cols : qkv_cols],
         share_out[:, :q_cols],
-        gain_share[:head_rows, 2],
-        gain_share[:head_rows, 3],
-        gain_share[:, 1],
+        gain_share[2, :head_rows],
+        gain_share[3, :head_rows],
+        gain_share[1, :shard_rows],
         grad_wide[None, :, :hidden],
         grad_wide[None, :, hidden:],
         grad_down[None],

time: 590 us -> 570 us (0.966)
  Pallas kernels: 261 us -> 365 us
  waiting for transfers between devices: 103 us -> 42.4 us
  starting transfers between devices: 70.3 us -> 23.9 us
  local copies, waits for them, and re-layouts: 38.8 us -> 23 us
  matrix products: 78.6 us -> 71 us
    pallas_call x2 -> x1, Pallas kernels: 42.2 us -> 150 us  [moe(): pl.pallas_call(moe_kernel, in_specs=[any_space] * 8, out_specs=[any_space...]
    all_to_all x7 -> x2, waiting for transfers between devices: 46.1 us -> 0.01 us  [exchange(): lax.all_to_all(rows_of, ('fsdp', 'ctx', 'tp'), split_axis=0, concat_axis=...]
    all_to_all x7 -> x2, starting transfers between devices: 58.4 us -> 12.4 us  [exchange(): lax.all_to_all(rows_of, ('fsdp', 'ctx', 'tp'), split_axis=0, concat_axis=...]
    ppermute x5, waiting for transfers between devices: 56.9 us -> 42.4 us  [swap_tp(): return lax.ppermute(value, 'tp', [(0, 1), (1, 0)])]
    dot_general x19 -> x13, matrix products: 78.4 us -> 70.6 us  [dot(): return lax.dot_general(a, b, (dims, ((), ())), preferred_element_type=F32)]
    unnamed x149 -> x94, local copies, waits for them, and re-layouts: 13.5 us -> 5.96 us
  transfers between devices with their start and end apart: 12 -> 7, of which waited for: 8 -> 4; matrix products, arithmetic and copies ran while one was open for 17% -> 15% of each run, Pallas kernels for 29% -> 22%
where the time goes in v4:
time: 570 us; the launch traced here: 559 us
  Pallas kernels  365 us (64%)
  matrix products  71 us (12%)
  waiting for transfers between devices  42.4 us (7%)
  other arithmetic  32 us (6%)
  starting transfers between devices  23.9 us (4%)
  local copies, waits for them, and re-layouts  23 us (4%)
    pallas_call x1, Pallas kernels, moe(): pl.pallas_call(moe_kernel, in_specs=[any_space] * 8, out_specs=[any_space...  150 us
    pallas_call x1, Pallas kernels, scatter_grads(): pl.pallas_call(scatter_kernel, in_specs=[any_space] * 5, out_specs=[pl.Bl...  73.2 us
    pallas_call x1, Pallas kernels, gather_weights(): pl.pallas_call(gather_kernel, in_specs=[pl.BlockSpec(memory_space=pltpu.V...  71.4 us
    dot_general x13, matrix products, dot(): return lax.dot_general(a, b, (dims, ((), ())), preferred_element_type=F32)  70.6 us
    ppermute x5, waiting for transfers between devices, swap_tp(): return lax.ppermute(value, 'tp', [(0, 1), (1, 0)])  42.4 us
    pallas_call x1, Pallas kernels, attention_back(): pl.pallas_call(functools.partial(attention_back_kernel, kv, heads), out_s...  34.4 us
    pallas_call x1, Pallas kernels, share_keys(): pl.pallas_call(functools.partial(share_kernel, kv), grid=(1,), in_specs=[...  21 us
    pallas_call x1, Pallas kernels, attention(): pl.pallas_call(functools.partial(attention_kernel, heads), grid=(micro, k...  15.1 us
  transfers between devices with their start and end apart: 7, of which 4 were waited for; matrix products, arithmetic and copies ran while one was open for 15% of the time, Pallas kernels for 22%

profile of v4, /device:TPU:0, one launch (start us, length us, event | category | flops | bytes accessed | tf_op | source)
XLA Modules:
  0.0 559.2 jit_solution(5807109498677990687)
XLA Ops:
  1.7 1.7 compare_reduce_fusion.1
  4.5 1.0 fusion.23
  5.9 2.0 broadcast_select_fusion
  7.9 2.4 fusion.78
  10.3 1.1 and.305
  12.1 71.4 %gather_weights.1 = (bf16[4,2,4,2,32,2560]{5,4,3,2,1,0:T(8,128)(2,1)}, bf16[4,2,4,2,32,2176]{5,4,3,2,1,0:T(8,128)(2,1)}, bf16[2048,384]{1,0:T(8,128)(2,1)}, bf16[2048,384]{1,0:T(8,128)(2,1)}, bf16[384,2048]{1,0:T(8,128)(2,1)}) custom-call(bf16[32,2048]{1,0:T(8,128)(2,1)} %query_ref.1, bf16[32,256]{1,0:T(8,128)(2,1)} %key_ref.1, bf16[32,256]{1,0:T(8,128)(2,1)} %value_ref.1, ...), custom_call_target="tpu_custom_call" | custom-call | bytes 250000000 | tf_op jit(solution)/shard_map/gather_weights/pallas_call | solution.py:213
  83.6 1.2 slice.111
  89.7 5.6 %fusion.81.rows_ref.q_ref.qkv_ref = f32[256,2560]{1,0:T(8,128)S(1)} fusion(bf16[256,2048]{1,0:T(8,128)(2,1)S(1)} %bitcast.159, bf16[2048,2560]{1,0:T(8,128)(2,1)} %bitcast.168), kind=kOutput, calls=%fused_computation.211 | convolution fusion | flops 2684354560 | bytes 14155776 | tf_op jit(solution)/shard_map/dot_general | solution.py:477
  95.4 3.3 multiply_convert_fusion
  98.7 21.0 %share_keys.1.k_ref.v_ref.kv_ref = bf16[2,640,512]{2,1,0:T(8,128)(2,1)S(1)} custom-call(f32[256,2560]{1,0:T(8,128)S(1)} %fusion.81.rows_ref.q_ref.qkv_ref, f32[128,128]{1,0:T(8,128)S(1)} %pad_maximum_fusion.1.cos_ref, f32[128,128]{1,0:T(8,128)S(1)} %pad_maximum_fusion.2.sin_ref, f32[1,128]{1,0:T(1,128)S(1)} %broadcast_in_dim_reshape_squeeze.5.gk_ref), custom_call_target="tpu_custom_call" | custom-call | bytes 50000000 | tf_op jit(solution)/shard_map/share_keys/pallas_call | solution.py:674
  119.7 1.1 copy-done.1
  120.8 6.5 %all-to-all-start = ((bf16[64,16,2048]{2,1,0:T(8,128)(2,1)}), bf16[64,16,2048]{2,1,0:T(8,128)(2,1)}, u32[]{:S(2)}, u32[]{:S(2)}) async-start(bf16[64,16,2048]{2,1,0:T(8,128)(2,1)} %bitcast.138), calls=%async_computation | async-start | bytes 8388608 | tf_op jit(solution)/shard_map/all_to_all | solution.py:1032
  130.2 1.0 select_select_fusion.bias_ref
  131.3 1.3 copy-done.2
  132.6 15.1 %attention_forward.1 = bf16[256,2048]{1,0:T(8,128)(2,1)S(1)} custom-call(f32[256,2560]{1,0:T(8,128)S(1)} %fusion.81.rows_ref.q_ref.qkv_ref, f32[128,128]{1,0:T(8,128)S(1)} %pad_maximum_fusion.1.cos_ref, f32[128,128]{1,0:T(8,128)S(1)} %pad_maximum_fusion.2.sin_ref, f32[1,128]{1,0:T(1,128)S(1)} %broadcast_in_dim_reshape_squeeze.4.gq_ref, ...), custom_call_target="tpu_custom_call" | custom-call | bytes 60000000 | tf_op jit(solution)/shard_map/attention_forward/pallas_call | solution.py:703
  147.7 6.1 %fusion.2 = f32[256,2048]{1,0:T(8,128)S(1)} fusion(bf16[256,2048]{1,0:T(8,128)(2,1)S(1)} %attention_forward.1, bf16[2048,2176]{1,0:T(8,128)(2,1)} %bitcast.164), kind=kOutput, calls=%fused_computation.5 | convolution fusion | flops 2147483648 | bytes 11534336 | tf_op jit(solution)/shard_map/dot_general | solution.py:477
  154.8 3.0 collective-permute-start
  158.5 1.4 broadcast_and_fusion
  160.7 2.6 and.321
  163.3 1.4 select_n.321
  166.4 1.6 maximum_convert_fusion
  167.9 19.6 %collective-permute-done = bf16[2,64,2048]{2,1,0:T(8,128)(2,1)} collective-permute-done((bf16[2,64,2048]{2,1,0:T(8,128)(2,1)}, bf16[2,64,2048]{2,1,0:T(8,128)(2,1)}, u32[]{:S(2)}, u32[]{:S(2)}) %collective-permute-start) | collective-permute-done | bytes 524320 | tf_op jit(solution)/shard_map/ppermute | solution.py:1003
  187.5 1.4 multiply_reduce_fusion.3
  189.1 3.2 convolution_convert_fusion.2
  192.3 149.7 %experts.1 = (bf16[64,16,2048]{2,1,0:T(8,128)(2,1)}, bf16[64,16,2048]{2,1,0:T(8,128)(2,1)}, bf16[2,1024,2048]{2,1,0:T(8,128)(2,1)}, bf16[2,1024,2048]{2,1,0:T(8,...) custom-call(bf16[64,16,2048]{2,1,0:T(8,128)(2,1)} %bitcast.137, ...), custom_call_target="tpu_custom_call" | custom-call | bytes 400000000 | tf_op jit(solution)/shard_map/experts/pallas_call | solution.py:965
  342.1 3.2 multiply_reduce_fusion.1
  345.8 1.5 copy-done.13
  347.3 1.2 fusion.8
  348.5 10.5 %collective-permute-done.1 = bf16[2,64,2048]{2,1,0:T(8,128)(2,1)S(1)} collective-permute-done((bf16[2,64,2048]{2,1,0:T(8,128)(2,1)S(1)}, bf16[2,64,2048]{2,1,0:T(8,128)(2,1)S(1)}, u32[]{:S(2)}, u32[]{:S(2)}) %collective-permute-start.1) | collective-permute-done | bytes 524320 | tf_op jit(solution)/shard_map/ppermute | solution.py:1003
  359.2 5.9 %all-to-all-start.1 = ((bf16[64,16,2048]{2,1,0:T(8,128)(2,1)}), bf16[64,16,2048]{2,1,0:T(8,128)(2,1)}, u32[]{:S(2)}, u32[]{:S(2)}) async-start(bf16[64,16,2048]{2,1,0:T(8,128)(2,1)} %get-tuple-element.52), calls=%async_computation.1 | async-start | bytes 8388608 | tf_op jit(solution)/shard_map/all_to_all | solution.py:1032
  365.1 7.3 %convolution_convert_fusion.4.tall_ref = bf16[384,2048]{1,0:T(8,128)(2,1)S(1)} fusion(bf16[2048,384]{1,0:T(8,128)(2,1)} %get-tuple-element.61, bf16[2048,2048]{1,0:T(8,128)(2,1)} %bitcast.171), kind=kOutput, calls=%fused_computation.12 | convolution fusion | flops 3222011904 | bytes 11534336 | tf_op jit(solution)/shard_map/dot_general | solution.py:477
  372.5 11.4 %convolution_convert_fusion.3.wide_ref = bf16[2048,768]{1,0:T(8,128)(2,1)} fusion(bf16[2048,2048]{1,0:T(8,128)(2,1)} %bitcast.170, bf16[2048,768]{1,0:T(8,128)(2,1)} %get-tuple-element.60), kind=kOutput, calls=%fused_computation.8 | convolution fusion | flops 6444023808 | bytes 14680064 | tf_op jit(solution)/shard_map/dot_general | solution.py:477
  383.9 5.8 %fusion.4.do_ref = bf16[256,2048]{1,0:T(8,128)(2,1)S(1)} fusion(bf16[256,2048]{1,0:T(8,128)(2,1)S(1)} %bitcast.150, bf16[2048,2176]{1,0:T(8,128)(2,1)} %bitcast.165), kind=kOutput, calls=%fused_computation.13 | convolution fusion | flops 2148007936 | bytes 10485760 | tf_op jit(solution)/shard_map/dot_general | solution.py:477
  389.7 34.4 %attention_backward.1 = (bf16[256,2560]{1,0:T(8,128)(2,1)S(1)}, f32[2,128]{1,0:T(2,128)S(1)}) custom-call(f32[256,2560]{1,0:T(8,128)} %copy-done, f32[128,128]{1,0:T(8,128)S(1)} %pad_maximum_fusion.1.cos_ref, f32[128,128]{1,0:T(8,128)S(1)} %pad_maximum_fusion.2.sin_ref, f32[1,128]{1,0:T(1,128)S(1)} %broadcast_in_dim_reshape_squeeze.4.gq_ref, ...), custom_call_target="tpu_custom_call" | custom-call | bytes 120000000 | tf_op jit(solution)/shard_map/attention_backward/pallas_call | solution.py:724
  424.2 1.0 copy-done.6
  425.6 6.9 %convolution_convert_fusion.1 = bf16[2048,2048]{1,0:T(8,128)(2,1)} fusion(bf16[256,2048]{1,0:T(8,128)(2,1)} %bitcast.151, bf16[256,2048]{1,0:T(8,128)(2,1)S(1)} %copy-done.5), kind=kOutput, calls=%fused_computation.2 | convolution fusion | flops 2151677952 | bytes 10485760 | tf_op jit(solution)/shard_map/dot_general | solution.py:477
  432.5 6.1 %fusion.82 = f32[2,128,2048]{2,1,0:T(8,128)S(1)} fusion(bf16[2,128,2560]{2,1,0:T(8,128)(2,1)} %bitcast.134, bf16[2048,2560,1]{1,0,2:T(8,128)(2,1)} %bitcast.169), kind=kOutput, calls=%fused_computation.212 | convolution fusion | flops 2684354560 | bytes 13893632 | tf_op jit(solution)/shard_map/dot_general | solution.py:477
  438.7 4.2 collective-permute-start.3
  442.9 2.9 fusion.26
  445.8 3.0 convolution_add_fusion
  448.8 5.7 %collective-permute-done.3 = bf16[2,64,2048]{2,1,0:T(8,128)(2,1)S(1)} collective-permute-done((bf16[2,64,2048]{2,1,0:T(8,128)(2,1)S(1)}, bf16[2,64,2048]{2,1,0:T(8,128)(2,1)S(1)}, u32[]{:S(2)}, u32[]{:S(2)}) %collective-permute-start.3) | collective-permute-done | bytes 524320 | tf_op jit(solution)/shard_map/ppermute | solution.py:1003
  455.8 3.6 collective-permute-start.2
  459.4 5.6 %convolution_convert_fusion = bf16[2048,2560]{1,0:T(8,128)(2,1)} fusion(bf16[256,2048]{1,0:T(8,128)(2,1)S(1)} %copy-done.24, bf16[256,2560]{1,0:T(8,128)(2,1)S(1)} %copy-done.7), kind=kOutput, calls=%fused_computation | convolution fusion | flops 2689597440 | bytes 12845056 | tf_op jit(solution)/shard_map/dot_general | solution.py:477
  465.9 6.7 %collective-permute-done.2 = bf16[2,64,2048]{2,1,0:T(8,128)(2,1)} collective-permute-done((bf16[2,64,2048]{2,1,0:T(8,128)(2,1)S(1)}, bf16[2,64,2048]{2,1,0:T(8,128)(2,1)}, u32[]{:S(2)}, u32[]{:S(2)}) %collective-permute-start.2) | collective-permute-done | bytes 524320 | tf_op jit(solution)/shard_map/ppermute | solution.py:1003
  472.6 1.9 broadcast_select_fusion.1
  474.5 73.2 %scatter_grads.1 = (f32[32,2560]{1,0:T(8,128)S(1)}, f32[32,2176]{1,0:T(8,128)S(1)}, bf16[2048,768]{1,0:T(8,128)(2,1)S(1)}, bf16[384,2048]{1,0:T(8,128)(2,1)S(1)}) custom-call(bf16[4,2,4,2,32,2560]{5,4,3,2,1,0:T(8,128)(2,1)} %bitcast.135, bf16[4,2,4,2,32,2048]{5,4,3,2,1,0:T(8,128)(2,1)} %bitcast.136, bf16[4,2,4,2,32,128]{5,4,3,2,1,0:T(8,128)(2,1)S(1)} %bitcast.133, ...), custom_call_target="tpu_custom_call" | custom-call | bytes 250000000 | tf_op jit(solution)/shard_map/scatter_grads/pallas_call | solution.py:445
  548.2 1.9 bitcast_convert_fusion
  550.1 3.1 slice_bitcast_fusion
  (170 shorter events, 24.5 us)
Async XLA Ops:
  0.6 10.8 %copy-start.40 = (bf16[32]{0:T(256)(128)(2,1)S(1)}, bf16[32]{0:T(256)(128)(2,1)}, u32[]{:S(2)}) copy-start(bf16[32]{0:T(256)(128)(2,1)} %param.35) | copy-start | bytes 196
  0.7 10.7 %copy-start.41 = (bf16[32]{0:T(256)(128)(2,1)S(1)}, bf16[32]{0:T(256)(128)(2,1)}, u32[]{:S(2)}) copy-start(bf16[32]{0:T(256)(128)(2,1)} %param.28) | copy-start | bytes 196
  0.7 10.7 %copy-start.42 = (bf16[2]{0:T(256)(128)(2,1)S(1)}, bf16[2]{0:T(256)(128)(2,1)}, u32[]{:S(2)}) copy-start(bf16[2]{0:T(256)(128)(2,1)} %param.34) | copy-start | bytes 16
  0.7 10.7 %copy-start.43 = (bf16[2]{0:T(256)(128)(2,1)S(1)}, bf16[2]{0:T(256)(128)(2,1)}, u32[]{:S(2)}) copy-start(bf16[2]{0:T(256)(128)(2,1)} %param.33) | copy-start | bytes 16
  0.7 82.8 %copy-start.44 = (s32[64]{0:T(128)}, s32[64]{0:T(128)S(1)}, u32[]{:S(2)}) copy-start(s32[64]{0:T(128)S(1)} %iota_add_fusion) | copy-start | bytes 772
  0.7 11.3 %copy-start.38 = (pred[2,2]{0,1:T(4,128)(4,1)}, pred[2,2]{0,1:T(4,128)(4,1)S(1)}, u32[]{:S(2)}) copy-start(pred[2,2]{0,1:T(4,128)(4,1)S(1)} %iota_compare_fusion.5) | copy-start | bytes 16
  12.1 75.1 %copy-start.30 = (bf16[2,1,56,2048]{3,2,1,0:T(8,128)(2,1)S(1)}, bf16[2,1,56,2048]{3,2,1,0:T(8,128)(2,1)}, u32[]{:S(2)}) copy-start(bf16[2,1,56,2048]{3,2,1,0:T(8,128)(2,1)} %param.20) | copy-start | bytes 1376260
  12.1 75.2 %copy-start.14 = (bf16[2,1,64,2048]{3,2,1,0:T(8,128)(2,1)S(1)}, bf16[2,1,64,2048]{3,2,1,0:T(8,128)(2,1)}, u32[]{:S(2)}) copy-start(bf16[2,1,64,2048]{3,2,1,0:T(8,128)(2,1)} %param.21) | copy-start | bytes 1572868
  83.5 5.7 %copy-start.32 = (bf16[2,1,64,2048]{3,2,1,0:T(8,128)(2,1)S(1)}, bf16[2,1,64,2048]{3,2,1,0:T(8,128)(2,1)}, u32[]{:S(2)}) copy-start(bf16[2,1,64,2048]{3,2,1,0:T(8,128)(2,1)} %param.23) | copy-start | bytes 1572868
  83.5 5.7 %copy-start.33 = (bf16[2,1,56,2048]{3,2,1,0:T(8,128)(2,1)S(1)}, bf16[2,1,56,2048]{3,2,1,0:T(8,128)(2,1)}, u32[]{:S(2)}) copy-start(bf16[2,1,56,2048]{3,2,1,0:T(8,128)(2,1)} %param.22) | copy-start | bytes 1376260
  87.3 2.4 copy-start.18
  89.4 6.0 %copy-start.20 = (bf16[2,64,2048]{2,1,0:T(8,128)(2,1)}, bf16[2,64,2048]{2,1,0:T(8,128)(2,1)S(1)}, u32[]{:S(2)}) copy-start(bf16[2,64,2048]{2,1,0:T(8,128)(2,1)S(1)} %bitcast_select_fusion) | copy-start | bytes 1572868
  89.7 5.7 %copy-start.31 = (pred[128,1024]{0,1:T(32,128)(4,1)S(1)}, pred[128,1024]{0,1:T(32,128)(4,1)}, u32[]{:S(2)}) copy-start(pred[128,1024]{0,1:T(32,128)(4,1)} %and.305) | copy-start | bytes 393220
  89.7 5.7 %copy-start.36 = (f32[1024]{0:T(1024)S(1)}, f32[1024]{0:T(1024)}, u32[]{:S(2)}) copy-start(f32[1024]{0:T(1024)} %mul.244) | copy-start | bytes 12292
  95.4 35.9 %copy-start = (f32[256,2560]{1,0:T(8,128)}, f32[256,2560]{1,0:T(8,128)S(1)}, u32[]{:S(2)}) copy-start(f32[256,2560]{1,0:T(8,128)S(1)} %fusion.81.rows_ref.q_ref.qkv_ref) | copy-start | bytes 7864324
  120.7 9.4 %copy-start.34 = (f32[64,2]{1,0:T(8,128)S(1)}, f32[64,2]{1,0:T(8,128)}, u32[]{:S(2)}) copy-start(f32[64,2]{1,0:T(8,128)} %get-tuple-element.119) | copy-start | bytes 1540
  120.8 71.6 %all-to-all-start = ((bf16[64,16,2048]{2,1,0:T(8,128)(2,1)}), bf16[64,16,2048]{2,1,0:T(8,128)(2,1)}, u32[]{:S(2)}, u32[]{:S(2)}) async-start(bf16[64,16,2048]{2,1,0:T(8,128)(2,1)} %bitcast.138), calls=%async_computation | async-start | bytes 8388608 | tf_op jit(solution)/shard_map/all_to_all | solution.py:1032
  147.7 6.2 %copy-start.4 = (bf16[256,2048]{1,0:T(8,128)(2,1)}, bf16[256,2048]{1,0:T(8,128)(2,1)S(1)}, u32[]{:S(2)}) copy-start(bf16[256,2048]{1,0:T(8,128)(2,1)S(1)} %attention_forward.1) | copy-start | bytes 3145732
  147.7 10.1 %copy-start.35 = (pred[2,64,64]{2,1,0:T(8,128)(4,1)S(1)}, pred[2,64,64]{2,1,0:T(8,128)(4,1)}, u32[]{:S(2)}) copy-start(pred[2,64,64]{2,1,0:T(8,128)(4,1)} %get-tuple-element.120) | copy-start | bytes 24580
  147.7 10.2 %copy-start.45 = (s32[64]{0:T(128)S(1)}, s32[64]{0:T(128)}, u32[]{:S(2)}) copy-start(s32[64]{0:T(128)} %copy-done.44) | copy-start | bytes 772
  147.7 10.8 %copy-start.39 = (pred[2,2]{0,1:T(4,128)(4,1)S(1)}, pred[2,2]{0,1:T(4,128)(4,1)}, u32[]{:S(2)}) copy-start(pred[2,2]{0,1:T(4,128)(4,1)} %copy-done.38) | copy-start | bytes 16
  153.8 4.6 copy-start.25
  153.9 6.0 %copy-start.15 = (bf16[2,1,64,2048]{3,2,1,0:T(8,128)(2,1)S(1)}, bf16[2,1,64,2048]{3,2,1,0:T(8,128)(2,1)}, u32[]{:S(2)}) copy-start(bf16[2,1,64,2048]{3,2,1,0:T(8,128)(2,1)} %param.21) | copy-start | bytes 1572868
  153.9 9.4 %copy-start.28 = (f32[2,64,64,2,8]{1,0,4,3,2:T(2,128)S(1)}, f32[2,64,64,2,8]{1,0,4,3,2:T(2,128)}, u32[]{:S(2)}) copy-start(f32[2,64,64,2,8]{1,0,4,3,2:T(2,128)} %get-tuple-element.127) | copy-start | bytes 1572868
  153.9 12.5 %copy-start.19 = (bf16[2,64,2048]{2,1,0:T(8,128)(2,1)S(1)}, bf16[2,64,2048]{2,1,0:T(8,128)(2,1)}, u32[]{:S(2)}) copy-start(bf16[2,64,2048]{2,1,0:T(8,128)(2,1)} %copy-done.18) | copy-start | bytes 1572868
  154.8 32.7 %collective-permute-start = (bf16[2,64,2048]{2,1,0:T(8,128)(2,1)}, bf16[2,64,2048]{2,1,0:T(8,128)(2,1)}, u32[]{:S(2)}, u32[]{:S(2)}) collective-permute-start(bf16[2,64,2048]{2,1,0:T(8,128)(2,1)} %select_convert_fusion.2), channel_id=1, source_target_pairs={{0,1},{1,0},{2,3},{3,2},{4,5},{5,4},{6,7},{7,6},{8,9},{9,8},{10,11... | collective-permute-start | bytes 1572872 | tf_op jit(solution)/shard_map/ppermute | solution.py:1003
  160.7 28.2 %copy-start.16 = (bf16[2,64,2048]{2,1,0:T(8,128)(2,1)}, bf16[2,64,2048]{2,1,0:T(8,128)(2,1)S(1)}, u32[]{:S(2)}) copy-start(bf16[2,64,2048]{2,1,0:T(8,128)(2,1)S(1)} %get-tuple-element.126) | copy-start | bytes 1572868
  165.5 22.0 %copy-start.26 = (f32[256,2048]{1,0:T(8,128)S(1)}, f32[256,2048]{1,0:T(8,128)}, u32[]{:S(2)}) copy-start(f32[256,2048]{1,0:T(8,128)} %copy-done.25) | copy-start | bytes 6291460
  188.9 156.5 %copy-start.8 = (f32[2,64,2048]{2,1,0:T(8,128)}, f32[2,64,2048]{2,1,0:T(8,128)S(1)}, u32[]{:S(2)}) copy-start(f32[2,64,2048]{2,1,0:T(8,128)S(1)} %get-tuple-element.130) | copy-start | bytes 3145732
  192.3 149.7 %copy-start.29 = (pred[2,64,64,2,8]{1,0,4,3,2:T(4,128)(4,1)S(1)}, pred[2,64,64,2,8]{1,0,4,3,2:T(4,128)(4,1)}, u32[]{:S(2)}) copy-start(pred[2,64,64,2,8]{1,0,4,3,2:T(4,128)(4,1)} %broadcast_and_fusion) | copy-start | bytes 393220
  342.0 3.3 copy-start.21
  345.3 3.2 copy-start.11
  345.7 13.3 %collective-permute-start.1 = (bf16[2,64,2048]{2,1,0:T(8,128)(2,1)S(1)}, bf16[2,64,2048]{2,1,0:T(8,128)(2,1)S(1)}, u32[]{:S(2)}, u32[]{:S(2)}) collective-permute-start(bf16[2,64,2048]{2,1,0:T(8,128)(2,1)S(1)} %fusion.79), channel_id=1, source_target_pairs={{0,1},{1,0},{2,3},{3,2},{4,5},{5,4},{6,7},{7,6},{8,9},{9,8},{10,11... | collective-permute-start | bytes 1572872 | tf_op jit(solution)/shard_map/ppermute | solution.py:1003
  359.2 24.7 %copy-start.23 = (bf16[2,128,2048]{2,1,0:T(8,128)(2,1)}, bf16[2,128,2048]{2,1,0:T(8,128)(2,1)S(1)}, u32[]{:S(2)}) copy-start(bf16[2,128,2048]{2,1,0:T(8,128)(2,1)S(1)} %pad_maximum_fusion) | copy-start | bytes 3145732
  359.2 73.3 %all-to-all-start.1 = ((bf16[64,16,2048]{2,1,0:T(8,128)(2,1)}), bf16[64,16,2048]{2,1,0:T(8,128)(2,1)}, u32[]{:S(2)}, u32[]{:S(2)}) async-start(bf16[64,16,2048]{2,1,0:T(8,128)(2,1)} %get-tuple-element.52), calls=%async_computation.1 | async-start | bytes 8388608 | tf_op jit(solution)/shard_map/all_to_all | solution.py:1032
  383.9 5.8 %copy-start.3 = (bf16[2,640,512]{2,1,0:T(8,128)(2,1)S(1)}, bf16[2,640,512]{2,1,0:T(8,128)(2,1)}, u32[]{:S(2)}) copy-start(bf16[2,640,512]{2,1,0:T(8,128)(2,1)} %copy-done.1) | copy-start | bytes 3932164
  389.7 35.9 %copy-start.5 = (bf16[256,2048]{1,0:T(8,128)(2,1)S(1)}, bf16[256,2048]{1,0:T(8,128)(2,1)}, u32[]{:S(2)}) copy-start(bf16[256,2048]{1,0:T(8,128)(2,1)} %copy-done.4) | copy-start | bytes 3145732
  432.5 10.3 %copy-start.27 = (f32[128,1024]{0,1:T(8,128)S(1)}, f32[128,1024]{0,1:T(8,128)}, u32[]{:S(2)}) copy-start(f32[128,1024]{0,1:T(8,128)} %select_n.321) | copy-start | bytes 1572868
  438.7 15.8 %collective-permute-start.3 = (bf16[2,64,2048]{2,1,0:T(8,128)(2,1)S(1)}, bf16[2,64,2048]{2,1,0:T(8,128)(2,1)S(1)}, u32[]{:S(2)}, u32[]{:S(2)}) collective-permute-start(bf16[2,64,2048]{2,1,0:T(8,128)(2,1)S(1)} %select_convert_fusion.1), channel_id=1, source_target_pairs={{0,1},{1,0},{2,3},{3,2},{4,5},{5,4},{6,7},{7,6},{8,9},{9,8},{10,11... | collective-permute-start | bytes 1572872 | tf_op jit(solution)/shard_map/ppermute | solution.py:1003
  445.8 8.7 %copy-start.17 = (bf16[2,64,2048]{2,1,0:T(8,128)(2,1)S(1)}, bf16[2,64,2048]{2,1,0:T(8,128)(2,1)}, u32[]{:S(2)}) copy-start(bf16[2,64,2048]{2,1,0:T(8,128)(2,1)} %copy-done.16) | copy-start | bytes 1572868
  448.8 6.3 %copy-start.9 = (f32[2,64,2048]{2,1,0:T(8,128)S(1)}, f32[2,64,2048]{2,1,0:T(8,128)}, u32[]{:S(2)}) copy-start(f32[2,64,2048]{2,1,0:T(8,128)} %copy-done.8) | copy-start | bytes 3145732
  448.8 6.3 %copy-start.12 = (f32[2,64,2048]{2,1,0:T(8,128)S(1)}, f32[2,64,2048]{2,1,0:T(8,128)}, u32[]{:S(2)}) copy-start(f32[2,64,2048]{2,1,0:T(8,128)} %copy-done.11) | copy-start | bytes 3145732
  448.8 6.3 %copy-start.22 = (bf16[2,64,2048]{2,1,0:T(8,128)(2,1)S(1)}, bf16[2,64,2048]{2,1,0:T(8,128)(2,1)}, u32[]{:S(2)}) copy-start(bf16[2,64,2048]{2,1,0:T(8,128)(2,1)} %copy-done.20) | copy-start | bytes 1572868
  455.1 4.3 copy-start.7
  455.1 4.2 copy-start.24
  455.8 16.8 %collective-permute-start.2 = (bf16[2,64,2048]{2,1,0:T(8,128)(2,1)S(1)}, bf16[2,64,2048]{2,1,0:T(8,128)(2,1)}, u32[]{:S(2)}, u32[]{:S(2)}) collective-permute-start(bf16[2,64,2048]{2,1,0:T(8,128)(2,1)S(1)} %get-tuple-element.134), channel_id=1, source_target_pairs={{0,1},{1,0},{2,3},{3,2},{4,5},{5,4},{6,7},{7,6},{8,9},{9,8},{10,11... | collective-permute-start | bytes 1572872 | tf_op jit(solution)/shard_map/ppermute | solution.py:1003
  465.3 91.8 %collective-permute-start.4 = (bf16[2,64,2048]{2,1,0:T(8,128)(2,1)S(1)}, bf16[2,64,2048]{2,1,0:T(8,128)(2,1)S(1)}, u32[]{:S(2)}, u32[]{:S(2)}) collective-permute-start(bf16[2,64,2048]{2,1,0:T(8,128)(2,1)S(1)} %get-tuple-element.133), channel_id=1, source_target_pairs={{0,1},{1,0},{2,3},{3,2},{4,5},{5,4},{6,7},{7,6},{8,9},{9,8},{10,11... | collective-permute-start | bytes 1572872 | tf_op jit(solution)/shard_map/ppermute | solution.py:1003
  474.5 73.2 %copy-start.10 = (bf16[2048,768]{1,0:T(8,128)(2,1)S(1)}, bf16[2048,768]{1,0:T(8,128)(2,1)}, u32[]{:S(2)}) copy-start(bf16[2048,768]{1,0:T(8,128)(2,1)} %convolution_convert_fusion.3.wide_ref) | copy-start | bytes 9437188
  (5 other events, 7.4 us)

commit v5 on v4

--- a/solution.py
+++ b/solution.py
@@ -22,6 +22,10 @@
 VMEM_LIMIT = 48 * 1024 * 1024
 
 
+def dot(a, b, dims):
+    return lax.dot_general(a, b, (dims, ((), ())), preferred_element_type=F32)
+
+
 def place():
     f, c = lax.axis_index("fsdp"), lax.axis_index("ctx")
     return f // 2, f % 2, c // 2, c % 2
@@ -71,9 +75,41 @@
     )
 
 
+def route(ids, gates, experts, size, select_ref, high_ref, low_ref):
+    tokens, slots = ids.shape[0], select_ref.shape[1]
+    block, places = tokens // 2, size // 2
+    chosen = jnp.zeros((tokens, experts.shape[1]), F32)
+    weight = jnp.zeros((tokens, experts.shape[1]), F32)
+    for k in range(ids.shape[1]):
+        same = ids[:, k : k + 1] == experts
+        chosen = chosen + jnp.where(same, 1.0, 0.0)
+        weight = weight + jnp.where(same, gates[:, k : k + 1], 0.0)
+    t = lax.broadcasted_iota(jnp.int32, (tokens, tokens), 0)
+    u = lax.broadcasted_iota(jnp.int32, (tokens, tokens), 1)
+    earlier = jnp.logical_and(u < t, (u >= block) == (t >= block))
+    rank = dot(jnp.where(earlier, 1.0, 0.0).astype(BF16), chosen.astype(BF16), ((1,), (0,)))
+    rank = jnp.where(chosen > 0.0, rank, -1.0).astype(BF16)
+    e = lax.broadcasted_iota(jnp.int32, (experts.shape[1], slots), 0)
+    j = lax.broadcasted_iota(jnp.int32, (experts.shape[1], slots), 1)
+    spread = jnp.where(jnp.logical_and(j >= e * size, j < (e + 1) * size), 1.0, 0.0).astype(BF16)
+    j = lax.broadcasted_iota(jnp.int32, (tokens, slots), 1)
+    later = lax.broadcasted_iota(jnp.int32, (tokens, slots), 0) >= block
+    place = (j & (places - 1)).astype(F32)
+    mine = ((j & places) != 0) == later
+    there = jnp.logical_and(dot(rank, spread, ((1,), (0,))) == place, mine)
+    select_ref[...] = jnp.where(there, 1.0, 0.0).astype(BF16)
+    if high_ref is not None:
+        high = weight.astype(BF16)
+        low = (weight - high.astype(F32)).astype(BF16)
+        high_ref[...] = jnp.where(there, dot(high, spread, ((1,), (0,))), 0.0).astype(BF16)
+        low_ref[...] = jnp.where(there, dot(low, spread, ((1,), (0,))), 0.0).astype(BF16)
+
+
 def gather_kernel(
-    query_ref, key_ref, value_ref, out_ref, extra_ref, gate_ref, up_ref, down_ref,
-    a_all, b_all, gate_all, up_all, down_all, a_own, b_own, local_sem, send_sem, recv_sem, away_sem, home_sem, give_sem, take_sem,
+    query_ref, key_ref, value_ref, out_ref, extra_ref, ids_ref, gates_ref, experts_ref, cot_ref,
+    gate_ref, up_ref, down_ref,
+    a_all, b_all, gate_all, up_all, down_all, near_ref, high_ref, low_ref, rows_ref,
+    a_own, b_own, select, rows, rows_sem, local_sem, send_sem, recv_sem, away_sem, home_sem, give_sem, take_sem,
 ):
     y, core, z, x = place()
     for own, refs in ((a_own, (query_ref, key_ref, value_ref)), (b_own, (out_ref, extra_ref))):
@@ -143,6 +179,10 @@
         )
         copy.start()
         started.append(copy)
+    size = rows.shape[0] // (RING * RING * RING)
+    ids, gates = ids_ref[...], gates_ref[...]
+    route(ids, gates, experts_ref[0:1, :], size, select, high_ref, low_ref)
+    route(ids, gates, experts_ref[1:2, :], size, near_ref, None, None)
     for n in (0, 1):
         i, j = me[n]
         locals_[n].wait()
@@ -158,6 +198,14 @@
         for copy in moved:
             copy.start()
 
+    part = 256
+    for at in range(0, rows.shape[0], part):
+        lanes = slice(at, at + part)
+        total = dot(high_ref[:, lanes], cot_ref[...], ((0,), (0,)))
+        total = total + dot(low_ref[:, lanes], cot_ref[...], ((0,), (0,)))
+        rows[lanes, :] = total.astype(BF16)
+    keep_rows = pltpu.make_async_copy(rows, rows_ref, rows_sem)
+    keep_rows.start()
     for n in (0, 1):
         i, j = me[n]
         arrived(n, chunk(n, down(i), j), 1)
@@ -194,6 +242,7 @@
             arrived(n, chunk(n, it, far).at[0], base + 2)
             arrived(n, chunk(n, it, far).at[1], base + 3)
             across(n, it, far)
+    keep_rows.wait()
     for copy in homes:
         copy.wait()
     for copy in started:
@@ -205,18 +254,24 @@
             copy.wait()
 
 
-def gather_weights(query, key, value, out, extra, gate, up, down):
+def gather_weights(query, key, value, out, extra, ids, gates, experts, cot, slots, gate, up, down):
     rows = query.shape[0]
     cols = (query.shape[1] + key.shape[1] + value.shape[1], out.shape[1] + extra.shape[1])
     shape = (RING, 2, RING, 2, rows)
-    any_space = pl.BlockSpec(memory_space=pl.ANY)
-    a_all, b_all, *experts = pl.pallas_call(
+    vmem, any_space = (pl.BlockSpec(memory_space=space) for space in (pltpu.VMEM, pl.ANY))
+    tokens, width = cot.shape
+    routing = [jax.ShapeDtypeStruct((tokens, slots), BF16)] * 3
+    a_all, b_all, *rest = pl.pallas_call(
         gather_kernel,
-        in_specs=[pl.BlockSpec(memory_space=pltpu.VMEM)] * 5 + [any_space] * 3,
-        out_specs=[any_space] * 5,
+        in_specs=[vmem] * 9 + [any_space] * 3,
+        out_specs=[any_space] * 5 + [vmem] * 3 + [any_space],
         out_shape=[jax.ShapeDtypeStruct(shape + (c,), query.dtype) for c in cols]
-        + [jax.ShapeDtypeStruct(v.shape, v.dtype) for v in (gate, up, down)],
+        + [jax.ShapeDtypeStruct(v.shape, v.dtype) for v in (gate, up, down)]
+        + routing + [jax.ShapeDtypeStruct((slots, width), BF16)],
         scratch_shapes=[pltpu.VMEM((rows, c), query.dtype) for c in cols] + [
+            pltpu.VMEM((tokens, slots), BF16),
+            pltpu.VMEM((slots, width), BF16),
+            pltpu.SemaphoreType.DMA,
             pltpu.SemaphoreType.DMA((2,)),
             pltpu.SemaphoreType.DMA((2, 21)),
             pltpu.SemaphoreType.DMA((2, 21)),
@@ -225,11 +280,13 @@
             pltpu.SemaphoreType.DMA((3,)),
             pltpu.SemaphoreType.DMA((3,)),
         ],
-        compiler_params=pltpu.CompilerParams(collective_id=0, has_side_effects=True),
+        compiler_params=pltpu.CompilerParams(
+            collective_id=0, has_side_effects=True, vmem_limit_bytes=VMEM_LIMIT
+        ),
         cost_estimate=pl.CostEstimate(flops=0, bytes_accessed=250_000_000, transcendentals=0),
         name="gather_weights",
-    )(query, key, value, out, extra, gate, up, down)
-    return a_all.reshape(-1, cols[0]), b_all.reshape(-1, cols[1]), *experts
+    )(query, key, value, out, extra, ids, gates, experts, cot, gate, up, down)
+    return a_all.reshape(-1, cols[0]), b_all.reshape(-1, cols[1]), rest[:3], rest[3:]
 
 
 ORDER = (2, 1, 3, 0)
@@ -473,10 +530,6 @@
 CTX = 8
 
 
-def dot(a, b, dims):
-    return lax.dot_general(a, b, (dims, ((), ())), preferred_element_type=F32)
-
-
 def rotated(u, gain, cosine, sine):
     scaling = lax.rsqrt(jnp.mean(u * u, axis=-1, keepdims=True) + EPS)
     normed = u * scaling
@@ -748,27 +801,29 @@
 
 CHIPS = RING * RING * RING
 GROUP = 16
-MIX = 27
+MIX = 11
+AHEAD = 2
+TILE = 256
 
 
 def chip_at(slot, sign):
     f, c, t = lax.axis_index("fsdp"), lax.axis_index("ctx"), lax.axis_index("tp")
-    k = slot * MIX % CHIPS
-    turn = RING * sign
-    y = (f // 2 + turn + sign * (k // (RING * RING))) % RING
-    z = (c // 2 + turn + sign * (k // RING % RING)) % RING
-    x = (t * 2 + c % 2 + turn + sign * (k % RING)) % RING
-    return y, z, x
+    k = lax.rem(slot * MIX, CHIPS) * sign
+    turn = 0 if sign > 0 else RING
+    far = [lax.div(k, RING * RING), lax.rem(lax.div(k, RING), RING), lax.rem(k, RING)]
+    own = [lax.div(f, 2), lax.div(c, 2), t * 2 + lax.rem(c, 2)]
+    return [lax.rem(o + d + turn, RING) for o, d in zip(own, far)]
 
 
 def device_at(slot, sign):
     y, z, x = chip_at(slot, sign)
-    return {"fsdp": y * 2 + lax.axis_index("fsdp") % 2, "ctx": z * 2 + x % 2, "tp": x // 2}
+    core = lax.rem(lax.axis_index("fsdp"), 2)
+    return {"fsdp": y * 2 + core, "ctx": z * 2 + lax.rem(x, 2), "tp": lax.div(x, 2)}
 
 
 def chip_number(slot, sign):
     y, z, x = chip_at(slot, sign)
-    return (y * 2 * RING + z * 2 + x % 2) * 2 + x // 2
+    return (y * 2 * RING + z * 2 + lax.rem(x, 2)) * 2 + lax.div(x, 2)
 
 
 def other_core():
@@ -778,15 +833,15 @@
 
 def moe_kernel(
     send_ref, deo_ref, gate_ref, up_ref, down_ref, gate_far, up_far, down_far,
-    back_ref, eo_ref, rows_ref, deos_ref, z_ref, dgu_ref,
-    rows, deos, gu, down, give, take,
+    back_ref, eo_ref, wide_ref, tall_ref,
+    rows, deos, gu, down, z, dgu, wide, tall, give, take,
     go_sem, come_sem, load_sem, weight_sem, share_send, share_recv, part_send, part_recv,
-    save_sem, back_send, back_recv, eo_sem,
+    back_send, back_recv, eo_sem,
 ):
     size, hidden = send_ref.shape[1], down_ref.shape[0]
     count = GROUP * size
     groups = CHIPS // GROUP
-    total = CHIPS * size
+    width = down_ref.shape[1]
 
     def each(body, low, high):
         def step(i, carry):
@@ -824,18 +879,23 @@
             deo_ref.at[chip_number(s, -1)], deos.at[0, slot_rows(s)], load_sem.at[s]
         )
 
+    def sent_rows(n, s):
+        slot = lax.rem(lax.div(s, GROUP), 2)
+        return give.at[n, slot, slot_rows(lax.rem(s, GROUP))]
+
     def back(s):
         return remote(
-            rows.at[0, slot_rows(s)], back_ref.at[s], back_send.at[s], back_recv.at[s],
-            device_at(s, -1),
+            sent_rows(0, s), back_ref.at[s], back_send.at[s], back_recv.at[s], device_at(s, -1)
         )
 
     def back_stay():
-        return pltpu.make_async_copy(rows.at[0, slot_rows(0)], back_ref.at[0], back_recv.at[0])
+        return pltpu.make_async_copy(
+            give.at[0, 0, pl.ds(0, size)], back_ref.at[0], back_recv.at[0]
+        )
 
     def out(s):
         return pltpu.make_async_copy(
-            deos.at[0, slot_rows(s)], eo_ref.at[chip_number(s, -1)], eo_sem.at[s]
+            sent_rows(1, s), eo_ref.at[chip_number(s, -1)], eo_sem.at[s]
         )
 
     def share(n, g):
@@ -846,15 +906,10 @@
         )
 
     def part(n, g):
+        slot = lax.rem(g, 2)
         return remote(
-            give.at[n, group_rows(g)], take.at[n, group_rows(g)], part_send.at[n, g],
-            part_recv.at[n, g], other_core(),
-        )
-
-    def save(n, side, g):
-        ref, to = ((rows, rows_ref), (deos, deos_ref))[n]
-        return pltpu.make_async_copy(
-            ref.at[side, group_rows(g)], to.at[side, group_rows(g)], save_sem.at[n, side, g]
+            give.at[n, slot], take.at[n, slot], part_send.at[n, g], part_recv.at[n, g],
+            other_core(),
         )
 
     places = (gu.at[:, pl.ds(0, hidden)], gu.at[:, pl.ds(hidden, hidden)], down)
@@ -874,34 +929,40 @@
                     act(copy)
 
     stay(0).start()
-    each(lambda s: go(s).start(), 1, CHIPS)
+    each(lambda s: go(s).start(), 1, AHEAD * GROUP)
     each(lambda s: load(s).start(), 0, CHIPS)
     on_weights(lambda copy: copy.start())
 
+    def tiles(body):
+        each(lambda i: body(pl.ds(pl.multiple_of(i * TILE, TILE), TILE)), 0, width // TILE)
+
+    def clear(at):
+        wide[at, :] = jnp.zeros((TILE, 2 * hidden), F32)
+        tall[:, at] = jnp.zeros((hidden, TILE), F32)
+
+    tiles(clear)
+
     def through(side, g):
         at = group_rows(g)
-        kept = pl.ds(pl.multiple_of(side * total + g * count, count), count)
         pre = dot(rows[side, at, :], gu[...], ((1,), (0,)))
         dz = dot(deos[side, at, :], down[...], ((1,), (1,)))
         gate, u = pre[:, :hidden], pre[:, hidden:]
         sig = 1.0 / (1.0 + jnp.exp(-gate))
         act = gate * sig
-        z_ref[kept, :] = (act * u).astype(BF16)
-        dgu_ref[kept, :hidden] = (dz * u * sig * (1.0 + gate * (1.0 - sig))).astype(BF16)
-        dgu_ref[kept, hidden:] = (dz * act).astype(BF16)
-
-    def to_rows(side, g):
-        kept = pl.ds(pl.multiple_of(side * total + g * count, count), count)
-        return dot(dgu_ref[kept, :], gu[...], ((1,), (1,)))
-
-    def to_outputs(side, g):
-        kept = pl.ds(pl.multiple_of(side * total + g * count, count), count)
-        return dot(z_ref[kept, :], down[...], ((1,), (0,)))
+        z[side] = (act * u).astype(BF16)
+        dgu[side, :, :hidden] = (dz * u * sig * (1.0 + gate * (1.0 - sig))).astype(BF16)
+        dgu[side, :, hidden:] = (dz * act).astype(BF16)
+
+    def to_rows(side):
+        return dot(dgu[side], gu[...], ((1,), (1,)))
+
+    def to_outputs(side):
+        return dot(z[side], down[...], ((1,), (0,)))
 
     on_weights(lambda copy: copy.wait())
 
     def group(g):
-        first, last = g * GROUP, (g + 1) * GROUP
+        first, last, slot = g * GROUP, (g + 1) * GROUP, lax.rem(g, 2)
 
         @pl.when(g == 0)
         def _():
@@ -909,74 +970,98 @@
 
         each(lambda s: go(s).wait_recv(), lax.max(first, 1), last)
         each(lambda s: load(s).wait(), first, last)
+        each(
+            lambda s: go(s).start(), lax.min(first + AHEAD * GROUP, CHIPS),
+            lax.min(last + AHEAD * GROUP, CHIPS),
+        )
         for n in (0, 1):
             share(n, g).start()
-            save(n, 0, g).start()
         through(0, g)
         for n in (0, 1):
             share(n, g).wait_recv()
-            save(n, 1, g).start()
         through(1, g)
-        give[0, group_rows(g), :] = to_rows(1, g).astype(BF16)
+
+        @pl.when(g >= 2)
+        def _():
+            @pl.when(g == 2)
+            def _():
+                back_stay().wait()
+
+            each(lambda s: back(s).wait_send(), lax.max(first - 2 * GROUP, 1), last - 2 * GROUP)
+            each(lambda s: out(s).wait(), first - 2 * GROUP, last - 2 * GROUP)
+
+        give[0, slot] = to_rows(1).astype(BF16)
         part(0, g).start()
-        give[1, group_rows(g), :] = to_outputs(1, g).astype(BF16)
+        give[1, slot] = to_outputs(1).astype(BF16)
         part(1, g).start()
-        own = to_rows(0, g)
-        part(0, g).wait_recv()
-        share(0, g).wait_send()
-        save(0, 0, g).wait()
-        at = group_rows(g)
-        rows[0, at, :] = (own + take[0, at, :].astype(F32)).astype(BF16)
+        own = to_rows(0)
+        part(0, g).wait()
+        give[0, slot] = (own + take[0, slot].astype(F32)).astype(BF16)
 
         @pl.when(g == 0)
         def _():
             back_stay().start()
 
         each(lambda s: back(s).start(), lax.max(first, 1), last)
-        own = to_outputs(0, g)
-        part(1, g).wait_recv()
-        share(1, g).wait_send()
-        save(1, 0, g).wait()
-        deos[0, at, :] = (own + take[1, at, :].astype(F32)).astype(BF16)
+        own = to_outputs(0)
+        part(1, g).wait()
+        give[1, slot] = (own + take[1, slot].astype(F32)).astype(BF16)
         each(lambda s: out(s).start(), first, last)
+        at = group_rows(g)
+
+        def weight_grads(cols):
+            wide[cols, :] += dot(rows[0, at, cols], dgu[0], ((0,), (0,))) + dot(
+                rows[1, at, cols], dgu[1], ((0,), (0,))
+            )
+            tall[:, cols] += dot(z[0], deos[0, at, cols], ((0,), (0,))) + dot(
+                z[1], deos[1, at, cols], ((0,), (0,))
+            )
+
+        tiles(weight_grads)
 
     each(group, 0, groups)
 
-    def finish(g):
+    def store(at):
+        wide_ref[at, :] = wide[at, :].astype(BF16)
+        tall_ref[:, at] = tall[:, at].astype(BF16)
+
+    tiles(store)
+    for g in range(groups):
         for n in (0, 1):
-            part(n, g).wait_send()
-            save(n, 1, g).wait()
-
-    each(finish, 0, groups)
-    each(lambda s: out(s).wait(), 0, CHIPS)
-    back_stay().wait()
+            share(n, g).wait_send()
+    each(lambda s: out(s).wait(), (groups - 2) * GROUP, CHIPS)
+    each(lambda s: back(s).wait_send(), (groups - 2) * GROUP, CHIPS)
     each(lambda s: go(s).wait_send(), 1, CHIPS)
-    each(lambda s: back(s).wait(), 1, CHIPS)
+    each(lambda s: back(s).wait_recv(), 1, CHIPS)
 
 
 def moe(send, d_eo, own, far):
     chips, size, width = send.shape
     hidden = own[2].shape[0]
     total, groups = chips * size, chips // GROUP
+    count = GROUP * size
     vmem, any_space = (pl.BlockSpec(memory_space=space) for space in (pltpu.VMEM, pl.ANY))
-    shapes = [send.shape, send.shape, (2, total, width), (2, total, width)]
-    shapes += [(2 * total, hidden), (2 * total, 2 * hidden)]
+    shapes = [send.shape, send.shape, (width, 2 * hidden), (hidden, width)]
     dma = pltpu.SemaphoreType.DMA
     return pl.pallas_call(
         moe_kernel,
         in_specs=[any_space] * 8,
-        out_specs=[any_space] * 4 + [vmem] * 2,
+        out_specs=[any_space] * 2 + [vmem] * 2,
         out_shape=[jax.ShapeDtypeStruct(shape, BF16) for shape in shapes],
         scratch_shapes=[
             pltpu.VMEM((2, total, width), BF16),
             pltpu.VMEM((2, total, width), BF16),
             pltpu.VMEM((width, 2 * hidden), BF16),
             pltpu.VMEM((hidden, width), BF16),
-            pltpu.VMEM((2, total, width), BF16),
-            pltpu.VMEM((2, total, width), BF16),
+            pltpu.VMEM((2, count, hidden), BF16),
+            pltpu.VMEM((2, count, 2 * hidden), BF16),
+            pltpu.VMEM((width, 2 * hidden), F32),
+            pltpu.VMEM((hidden, width), F32),
+            pltpu.VMEM((2, 2, count, width), BF16),
+            pltpu.VMEM((2, 2, count, width), BF16),
             dma((chips,)), dma((chips,)), dma((chips,)), dma((3,)),
             dma((2, groups)), dma((2, groups)), dma((2, groups)), dma((2, groups)),
-            dma((2, 2, groups)), dma((chips,)), dma((chips,)), dma((chips,)),
+            dma((chips,)), dma((chips,)), dma((chips,)),
         ],
         compiler_params=pltpu.CompilerParams(
             collective_id=4, has_side_effects=True, vmem_limit_bytes=56 * 1024 * 1024
@@ -1039,35 +1124,16 @@
 
     x_first, x_second = pad(x_prompt), x_cont[:, 0]
     own_tokens = jnp.where(first, x_second, x_first).astype(F32)
-    own_cot = jnp.where(first, cot_cont[:, 0], pad(cot_prompt)).astype(F32)
+    own_cot = jnp.where(first, cot_cont[:, 0], pad(cot_prompt))
     ids_pad = jnp.pad(
         ids_prompt[:, 0], ((0, 0), (0, block - prompt_rows), (0, 0)), constant_values=-1
     )
     own_ids = jnp.where(first, ids_cont[:, 0], ids_pad)
     own_gates = jnp.where(first, gates_cont[:, 0], pad(gates_prompt))
 
-    lower = jnp.tril(jnp.ones((block, block), BF16), -1)
-    same = jnp.arange(micro)[:, None] == jnp.arange(micro)[None, :]
-    flat = (micro * block, peers * micro * slots)
-
-    def routing(experts):
-        named = own_ids[:, :, :, None] == experts
-        chosen = jnp.any(named, axis=2)
-        weight = jnp.sum(jnp.where(named, own_gates[:, :, :, None], 0.0), axis=2)
-        rank = jnp.einsum("ts,mse->mte", lower, chosen.astype(BF16), preferred_element_type=F32)
-        place = jnp.where(chosen, rank, -1.0)
-        placed = place[:, :, :, None] == jnp.arange(slots, dtype=F32)
-        both = jnp.logical_and(placed[:, :, :, None, :], same[:, None, None, :, None])
-        return both, weight[:, :, :, None, None]
-
-    placed, weight = routing(expert_of)
-    select = placed.astype(BF16).reshape(flat)
-    mixing = jnp.where(placed, weight, 0.0).reshape(flat)
-    mixing_high = mixing.astype(BF16)
-    mixing_low = (mixing - mixing_high.astype(F32)).astype(BF16)
-    slot_gate = jnp.sum(mixing, axis=0)
     y, z, x = chip_at(jnp.arange(peers, dtype=jnp.int32), 1)
-    select_near = routing((2 * y + x // 2) * ctx + 2 * z + x % 2)[0].astype(BF16).reshape(flat)
+    near = (2 * y + x // 2) * ctx + 2 * z + x % 2
+    order = jnp.pad(jnp.stack([expert_of, near]), ((0, 0), (0, HEAD_SIZE - peers)), constant_values=-2)
 
     def lanes(v):
         return jnp.pad(v, [(0, 0)] * (v.ndim - 1) + [(0, HEAD_SIZE - v.shape[-1])])
@@ -1075,9 +1141,12 @@
     extra = jnp.stack([lanes(v) for v in (norm_gain, moe_gain, query_gain, key_gain)])
     extra = jnp.pad(extra, ((0, shard_rows - extra.shape[0]), (0, 0)))
     own_experts = (expert_gate[0], expert_up[0], expert_down[0])
-    w_qkv, w_out_extra, *far_experts = gather_weights(
-        query_weight, key_matrix, value_matrix, out_weight, extra, *own_experts
+    w_qkv, w_out_extra, far_experts, routing = gather_weights(
+        query_weight, key_matrix, value_matrix, out_weight, extra,
+        own_ids.reshape(-1, TOPK), own_gates.reshape(-1, TOPK), order,
+        own_cot.reshape(-1, width), peers * micro * slots, *own_experts,
     )
+    select_near, mixing_high, mixing_low, spread = routing
     w_out = w_out_extra[:, :q_cols]
     gains = w_out_extra[:, q_cols:].reshape(peers, shard_rows, HEAD_SIZE)[:, :4].astype(F32)
     gain_in, gain_moe = (gains[:, n, :shard_rows].reshape(-1) for n in (0, 1))
@@ -1131,8 +1200,6 @@
     heads_in = (cosine, sine, gain_query[None], gain_key[None], bias)
     kv_all = share_keys(qkv, cosine, sine, gain_key[None], kv, keys, micro)
 
-    spread = dot(select, own_cot.astype(BF16).reshape(-1, width), ((0,), (0,)))
-    spread = (spread * slot_gate[:, None]).astype(BF16)
     spread, kv_all = lax.optimization_barrier((spread, kv_all))
     d_eo_rows = exchange(spread).reshape(peers, micro * slots, width)
     o = attention(qkv, cosine, sine, gain_query[None], bias, kv_all, kv)
@@ -1141,26 +1208,26 @@
     b_low = b_normed.astype(BF16)
 
     send = dot(select_near, b_low.reshape(-1, width), ((0,), (0,))).astype(BF16)
-    back, eo, rows_in, d_eo_in, z, d_gu = moe(
+    back, eo, wide_here, tall_here = moe(
         send.reshape(d_eo_rows.shape), d_eo_rows, own_experts, far_experts
     )
-    wide_here = dot(rows_in.reshape(-1, width), d_gu, ((0,), (0,))).astype(BF16)
-    tall_here = dot(z, d_eo_in.reshape(-1, width), ((0,), (0,))).astype(BF16)
     d_b = dot(select_near, back.reshape(-1, width), ((1,), (0,))).reshape(middle.shape)
     middle_from, moe_total = normalize_back(middle, b_scale, gain_moe, d_b)
-    d_h = own_cot + middle_from
+    d_h = own_cot.astype(F32) + middle_from
     d_attn = jnp.concatenate(share_rows(d_h.astype(BF16)), axis=1).reshape(-1, width)
 
     late, d_attn = lax.optimization_barrier((eo, d_attn))
     eo_back = exchange(late.reshape(-1, width))
 
     d_o = dot(d_attn, w_out, ((1,), (0,))).astype(BF16)
+    d_qkv, head_totals = attention_back(qkv, *heads_in, kv_all, d_o, kv)
+    input_part, d_attn, eo_back = lax.optimization_barrier(
+        (dot(d_qkv, w_qkv, ((1,), (1,))), d_attn, eo_back)
+    )
+    input_grad = sum_own(input_part)
     grad_out = dot(d_attn, o, ((0,), (0,))).astype(BF16)
-    d_qkv, head_totals = attention_back(qkv, *heads_in, kv_all, d_o, kv)
-    d_qkv, eo_back = lax.optimization_barrier((d_qkv, eo_back))
     moe_out = dot(mixing_high, eo_back, ((1,), (0,))) + dot(mixing_low, eo_back, ((1,), (0,)))
     out_first, out_second = share_rows((middle + moe_out.reshape(middle.shape)).astype(BF16))
-    input_grad = sum_own(dot(d_qkv, w_qkv, ((1,), (1,))))
     grad_qkv = dot(a, d_qkv, ((0,), (0,))).astype(BF16)
     scale_in = lax.rsqrt(jnp.mean(own_tokens * own_tokens, axis=-1, keepdims=True) + EPS)
     token_from, norm_total = normalize_back(own_tokens, scale_in, gain_in, input_grad)
@@ -1175,7 +1242,6 @@
     )
     extra_grads = jnp.pad(extra_grads, ((0, 0), (0, shard_rows - extra_grads.shape[1]), (0, 0)))
     extra_grads = extra_grads.reshape(-1, HEAD_SIZE).astype(BF16)
-    grad_qkv, out_first, out_second = lax.optimization_barrier((grad_qkv, out_first, out_second))
     share, share_out, wide_there, tall_there = scatter_grads(
         grad_qkv, grad_out, extra_grads, wide_here, tall_here
     )

time: 570 us -> 570 us (level)
  starting transfers between devices: 23.9 us -> 50.7 us
  matrix products: 71 us -> 52 us
  waiting for transfers between devices: 42.4 us -> 54.3 us
  Pallas kernels: 365 us -> 355 us
  other arithmetic: 32 us -> 26 us
    pallas_call x1, Pallas kernels: 150 us -> 116 us  [moe(): pl.pallas_call(moe_kernel, in_specs=[any_space] * 8, out_specs=[any_space...]
    all_to_all x2, starting transfers between devices: 12.4 us -> 38.2 us  [exchange(): lax.all_to_all(rows_of, ('fsdp', 'ctx', 'tp'), split_axis=0, concat_axis=...]
    dot_general x13 -> x10, matrix products: 70.6 us -> 52 us  [dot(): return lax.dot_general(a, b, (dims, ((), ())), preferred_element_type=F32)]
    pallas_call x1, Pallas kernels: 34.4 us -> 52.4 us  [attention_back(): pl.pallas_call(functools.partial(attention_back_kernel, kv, heads), out_s...]
    ppermute x5, waiting for transfers between devices: 42.4 us -> 54.3 us  [swap_tp(): return lax.ppermute(value, 'tp', [(0, 1), (1, 0)])]
    pallas_call x1, Pallas kernels: 73.2 us -> 79.8 us  [scatter_grads(): pl.pallas_call(scatter_kernel, in_specs=[any_space] * 5, out_specs=[pl.Bl...]
  transfers between devices with their start and end apart: 7 -> 7, of which waited for: 4 -> 4; matrix products, arithmetic and copies ran while one was open for 15% -> 11% of each run, Pallas kernels for 22% -> 12%
where the time goes in v5:
time: 570 us; the launch traced here: 563 us
  Pallas kernels  355 us (62%)
  waiting for transfers between devices  54.3 us (10%)
  matrix products  52 us (9%)
  starting transfers between devices  50.7 us (9%)
  other arithmetic  26 us (5%)
  local copies, waits for them, and re-layouts  22.6 us (4%)
    pallas_call x1, Pallas kernels, moe(): pl.pallas_call(moe_kernel, in_specs=[any_space] * 8, out_specs=[any_space...  116 us
    pallas_call x1, Pallas kernels, scatter_grads(): pl.pallas_call(scatter_kernel, in_specs=[any_space] * 5, out_specs=[pl.Bl...  79.8 us
    pallas_call x1, Pallas kernels, gather_weights(): pl.pallas_call(gather_kernel, in_specs=[vmem] * 9 + [any_space] * 3, out_...  70.5 us
    ppermute x5, waiting for transfers between devices, swap_tp(): return lax.ppermute(value, 'tp', [(0, 1), (1, 0)])  54.3 us
    pallas_call x1, Pallas kernels, attention_back(): pl.pallas_call(functools.partial(attention_back_kernel, kv, heads), out_s...  52.4 us
    dot_general x10, matrix products, dot(): return lax.dot_general(a, b, (dims, ((), ())), preferred_element_type=F32)  52 us
    all_to_all x2, starting transfers between devices, exchange(): lax.all_to_all(rows_of, ('fsdp', 'ctx', 'tp'), split_axis=0, concat_axis=...  38.2 us
    pallas_call x1, Pallas kernels, share_keys(): pl.pallas_call(functools.partial(share_kernel, kv), grid=(1,), in_specs=[...  21.1 us
  transfers between devices with their start and end apart: 7, of which 4 were waited for; matrix products, arithmetic and copies ran while one was open for 11% of the time, Pallas kernels for 12%

profile of v5, /device:TPU:0, one launch (start us, length us, event | category | flops | bytes accessed | tf_op | source)
XLA Modules:
  0.0 562.7 jit_solution(2147831239034185256)
XLA Ops:
  4.4 1.3 bitcast_select_fusion
  5.7 0.9 copy-done.18
  6.6 0.9 copy-done.19
  9.0 70.5 %gather_weights.1 = (bf16[4,2,4,2,32,2560]{5,4,3,2,1,0:T(8,128)(2,1)}, bf16[4,2,4,2,32,2176]{5,4,3,2,1,0:T(8,128)(2,1)}, bf16[2048,384]{1,0:T(8,128)(2,1)S(1)}, ...) custom-call(bf16[32,2048]{1,0:T(8,128)(2,1)S(1)} %copy-done.18, ...), custom_call_target="tpu_custom_call" | custom-call | bytes 250000000 | tf_op jit(solution)/shard_map/gather_weights/pallas_call | solution.py:264
  80.1 1.1 copy-done.9
  81.3 1.2 copy-done.10
  83.8 1.1 slice.111
  88.4 5.6 fusion.57.rows_ref.q_ref.qkv_ref
  94.1 21.1 %share_keys.1.k_ref.v_ref.kv_ref = bf16[2,640,512]{2,1,0:T(8,128)(2,1)S(1)} custom-call(f32[256,2560]{1,0:T(8,128)S(1)} %fusion.57.rows_ref.q_ref.qkv_ref, f32[128,128]{1,0:T(8,128)S(1)} %pad_maximum_fusion.1.cos_ref, f32[128,128]{1,0:T(8,128)S(1)} %pad_maximum_fusion.2.sin_ref, f32[1,128]{1,0:T(1,128)S(1)} %broadcast_in_dim_reshape_squeeze.5.gk_ref), custom_call_target="tpu_custom_call" | custom-call | bytes 50000000 | tf_op jit(solution)/shard_map/share_keys/pallas_call | solution.py:727
  115.2 1.0 copy-done.1
  116.2 6.7 %all-to-all-start = ((bf16[64,16,2048]{2,1,0:T(8,128)(2,1)}), bf16[64,16,2048]{2,1,0:T(8,128)(2,1)}, u32[]{:S(2)}, u32[]{:S(2)}) async-start(bf16[64,16,2048]{2,1,0:T(8,128)(2,1)} %bitcast.133), calls=%async_computation | async-start | bytes 8388608 | tf_op jit(solution)/shard_map/all_to_all | solution.py:1117
  123.1 0.9 select_select_fusion.bias_ref
  124.0 1.3 copy-done.2
  126.1 15.0 %attention_forward.1 = bf16[256,2048]{1,0:T(8,128)(2,1)S(1)} custom-call(f32[256,2560]{1,0:T(8,128)S(1)} %fusion.57.rows_ref.q_ref.qkv_ref, f32[128,128]{1,0:T(8,128)S(1)} %copy-done.12, f32[128,128]{1,0:T(8,128)S(1)} %pad_maximum_fusion.2.sin_ref, f32[1,128]{1,0:T(1,128)S(1)} %broadcast_in_dim_reshape_squeeze.4.gq_ref, ...), custom_call_target="tpu_custom_call" | custom-call | bytes 60000000 | tf_op jit(solution)/shard_map/attention_forward/pallas_call | solution.py:756
  141.2 7.5 %fusion.2 = f32[256,2048]{1,0:T(8,128)} fusion(bf16[256,2048]{1,0:T(8,128)(2,1)S(1)} %attention_forward.1, bf16[2048,2176]{1,0:T(8,128)(2,1)} %bitcast.142), kind=kOutput, calls=%fused_computation.4 | convolution fusion | flops 2147483648 | bytes 11534336 | tf_op jit(solution)/shard_map/dot_general | solution.py:26
  148.7 2.4 select_convert_fusion.2
  151.1 3.2 collective-permute-start
  154.6 28.1 %collective-permute-done = bf16[2,64,2048]{2,1,0:T(8,128)(2,1)S(1)} collective-permute-done((bf16[2,64,2048]{2,1,0:T(8,128)(2,1)}, bf16[2,64,2048]{2,1,0:T(8,128)(2,1)S(1)}, u32[]{:S(2)}, u32[]{:S(2)}) %collective-permute-start) | collective-permute-done | bytes 524320 | tf_op jit(solution)/shard_map/ppermute | solution.py:1088
  182.8 1.9 multiply_reduce_fusion.3
  184.9 3.3 convolution_convert_fusion.2
  188.2 116.4 %experts.1 = (bf16[64,16,2048]{2,1,0:T(8,128)(2,1)}, bf16[64,16,2048]{2,1,0:T(8,128)(2,1)}, bf16[2048,768]{1,0:T(8,128)(2,1)}, bf16[384,2048]{1,0:T(8,128)(2,1)}) custom-call(bf16[64,16,2048]{2,1,0:T(8,128)(2,1)} %bitcast.118, bf16[64,16,2048]{2,1,0:T(8,128)(2,1)} %all-to-all-done.deo_ref, bf16[2048,384]{1,0:T(8,128)(2,1)} %bitcast.124, ...), custom_call_target="tpu_custom_call" | custom-call | bytes 400000000 | tf_op jit(solution)/shard_map/experts/pallas_call | solution.py:1046
  304.6 3.2 multiply_reduce_fusion.1
  307.9 1.1 fusion.55
  309.0 2.5 collective-permute-start.1
  311.5 12.6 %collective-permute-done.1 = bf16[2,64,2048]{2,1,0:T(8,128)(2,1)S(1)} collective-permute-done((bf16[2,64,2048]{2,1,0:T(8,128)(2,1)}, bf16[2,64,2048]{2,1,0:T(8,128)(2,1)S(1)}, u32[]{:S(2)}, u32[]{:S(2)}) %collective-permute-start.1) | collective-permute-done | bytes 524320 | tf_op jit(solution)/shard_map/ppermute | solution.py:1088
  324.2 1.1 broadcast_select_fusion.1
  325.3 1.1 pad_maximum_fusion
  326.4 31.5 %all-to-all-start.1 = ((bf16[64,16,2048]{2,1,0:T(8,128)(2,1)}), bf16[64,16,2048]{2,1,0:T(8,128)(2,1)}, u32[]{:S(2)}, u32[]{:S(2)}) async-start(bf16[64,16,2048]{2,1,0:T(8,128)(2,1)} %get-tuple-element.55), calls=%async_computation.1 | async-start | bytes 8388608 | tf_op jit(solution)/shard_map/all_to_all | solution.py:1117
  358.8 1.3 fusion.8
  360.7 5.8 %fusion.4.do_ref = bf16[256,2048]{1,0:T(8,128)(2,1)S(1)} fusion(bf16[256,2048]{1,0:T(8,128)(2,1)S(1)} %bitcast.129, bf16[2048,2176]{1,0:T(8,128)(2,1)} %bitcast.143), kind=kOutput, calls=%fused_computation.10 | convolution fusion | flops 2148007936 | bytes 10485760 | tf_op jit(solution)/shard_map/dot_general | solution.py:26
  366.6 52.4 %attention_backward.1 = (bf16[256,2560]{1,0:T(8,128)(2,1)S(1)}, f32[2,128]{1,0:T(2,128)S(1)}) custom-call(f32[256,2560]{1,0:T(8,128)} %copy-done, f32[128,128]{1,0:T(8,128)S(1)} %copy-done.13, f32[128,128]{1,0:T(8,128)S(1)} %pad_maximum_fusion.2.sin_ref, f32[1,128]{1,0:T(1,128)S(1)} %broadcast_in_dim_reshape_squeeze.4.gq_ref, ...), custom_call_target="tpu_custom_call" | custom-call | bytes 120000000 | tf_op jit(solution)/shard_map/attention_backward/pallas_call | solution.py:777
  419.4 8.3 %fusion.58 = f32[256,2048]{1,0:T(8,128)} fusion(bf16[256,2560]{1,0:T(8,128)(2,1)S(1)} %get-tuple-element.54, bf16[2048,2560]{1,0:T(8,128)(2,1)} %bitcast.147), kind=kOutput, calls=%fused_computation.164 | convolution fusion | flops 2684354560 | bytes 13893632 | tf_op jit(solution)/shard_map/dot_general | solution.py:26
  427.6 5.6 %convolution_convert_fusion = bf16[2048,2560]{1,0:T(8,128)(2,1)} fusion(bf16[256,2048]{1,0:T(8,128)(2,1)S(1)} %copy-done.37, bf16[256,2560]{1,0:T(8,128)(2,1)S(1)} %get-tuple-element.54), kind=kOutput, calls=%fused_computation | convolution fusion | flops 2689597440 | bytes 12845056 | tf_op jit(solution)/shard_map/dot_general | solution.py:26
  433.3 1.6 select_convert_fusion.1
  434.9 3.2 collective-permute-start.3
  438.2 2.9 fusion.59
  441.1 4.1 convolution_add_fusion
  445.3 5.7 %convolution_convert_fusion.1 = bf16[2048,2048]{1,0:T(8,128)(2,1)} fusion(bf16[256,2048]{1,0:T(8,128)(2,1)S(1)} %bitcast.130, bf16[256,2048]{1,0:T(8,128)(2,1)S(1)} %copy-done.6), kind=kOutput, calls=%fused_computation.1 | convolution fusion | flops 2151677952 | bytes 10485760 | tf_op jit(solution)/shard_map/dot_general | solution.py:26
  451.0 1.4 fusion.17
  452.8 79.8 %scatter_grads.1 = (f32[32,2560]{1,0:T(8,128)S(1)}, f32[32,2176]{1,0:T(8,128)S(1)}, bf16[2048,768]{1,0:T(8,128)(2,1)S(1)}, bf16[384,2048]{1,0:T(8,128)(2,1)S(1)}) custom-call(bf16[4,2,4,2,32,2560]{5,4,3,2,1,0:T(8,128)(2,1)} %bitcast.116, bf16[4,2,4,2,32,2048]{5,4,3,2,1,0:T(8,128)(2,1)} %bitcast.117, bf16[4,2,4,2,32,128]{5,4,3,2,1,0:T(8,128)(2,1)S(1)} %bitcast.113, ...), custom_call_target="tpu_custom_call" | custom-call | bytes 250000000 | tf_op jit(solution)/shard_map/scatter_grads/pallas_call | solution.py:502
  536.4 1.7 collective-permute-start.2
  538.1 1.9 collective-permute-start.4
  540.5 3.1 slice_bitcast_fusion
  543.6 1.9 bitcast_convert_fusion
  545.4 7.4 %collective-permute-done.2 = bf16[2,64,2048]{2,1,0:T(8,128)(2,1)S(1)} collective-permute-done((bf16[2,64,2048]{2,1,0:T(8,128)(2,1)S(1)}, bf16[2,64,2048]{2,1,0:T(8,128)(2,1)S(1)}, u32[]{:S(2)}, u32[]{:S(2)}) %collective-permute-start.2) | collective-permute-done | bytes 524320 | tf_op jit(solution)/shard_map/ppermute | solution.py:1088
  553.7 0.8 select_bitcast_fusion.1
  554.5 6.1 %collective-permute-done.4 = bf16[2,64,2048]{2,1,0:T(8,128)(2,1)S(1)} collective-permute-done((bf16[2,64,2048]{2,1,0:T(8,128)(2,1)S(1)}, bf16[2,64,2048]{2,1,0:T(8,128)(2,1)S(1)}, u32[]{:S(2)}, u32[]{:S(2)}) %collective-permute-start.4) | collective-permute-done | bytes 524320 | tf_op jit(solution)/shard_map/ppermute | solution.py:1088
  561.4 0.8 select_bitcast_fusion
  (163 shorter events, 20.2 us)
Async XLA Ops:
  9.0 77.1 %copy-start.41 = (bf16[2,1,56,2048]{3,2,1,0:T(8,128)(2,1)S(1)}, bf16[2,1,56,2048]{3,2,1,0:T(8,128)(2,1)}, u32[]{:S(2)}) copy-start(bf16[2,1,56,2048]{3,2,1,0:T(8,128)(2,1)} %param.20) | copy-start | bytes 1376260
  83.8 2.2 copy-start.27
  86.1 2.3 copy-start.33
  87.9 6.2 %copy-start.11 = (f32[128,128]{1,0:T(8,128)}, f32[128,128]{1,0:T(8,128)S(1)}, u32[]{:S(2)}) copy-start(f32[128,128]{1,0:T(8,128)S(1)} %pad_maximum_fusion.1.cos_ref) | copy-start | bytes 196612
  94.0 30.0 %copy-start = (f32[256,2560]{1,0:T(8,128)}, f32[256,2560]{1,0:T(8,128)S(1)}, u32[]{:S(2)}) copy-start(f32[256,2560]{1,0:T(8,128)S(1)} %fusion.57.rows_ref.q_ref.qkv_ref) | copy-start | bytes 7864324
  116.2 72.0 %all-to-all-start = ((bf16[64,16,2048]{2,1,0:T(8,128)(2,1)}), bf16[64,16,2048]{2,1,0:T(8,128)(2,1)}, u32[]{:S(2)}, u32[]{:S(2)}) async-start(bf16[64,16,2048]{2,1,0:T(8,128)(2,1)} %bitcast.133), calls=%async_computation | async-start | bytes 8388608 | tf_op jit(solution)/shard_map/all_to_all | solution.py:1117
  124.0 1.3 copy-start.2
  141.1 7.5 %copy-start.5 = (bf16[256,2048]{1,0:T(8,128)(2,1)}, bf16[256,2048]{1,0:T(8,128)(2,1)S(1)}, u32[]{:S(2)}) copy-start(bf16[256,2048]{1,0:T(8,128)(2,1)S(1)} %attention_forward.1) | copy-start | bytes 3145732
  141.2 13.1 %copy-start.45 = (f32[64,32]{1,0:T(8,128)S(1)}, f32[64,32]{1,0:T(8,128)}, u32[]{:S(2)}) copy-start(f32[64,32]{1,0:T(8,128)} %get-tuple-element.101) | copy-start | bytes 24580
  141.2 13.2 %copy-start.28 = (bf16[2,1,64,2048]{3,2,1,0:T(8,128)(2,1)S(1)}, bf16[2,1,64,2048]{3,2,1,0:T(8,128)(2,1)}, u32[]{:S(2)}) copy-start(bf16[2,1,64,2048]{3,2,1,0:T(8,128)(2,1)} %param.21) | copy-start | bytes 1572868
  141.2 13.2 %copy-start.42 = (bf16[2,1,56,2048]{3,2,1,0:T(8,128)(2,1)S(1)}, bf16[2,1,56,2048]{3,2,1,0:T(8,128)(2,1)}, u32[]{:S(2)}) copy-start(bf16[2,1,56,2048]{3,2,1,0:T(8,128)(2,1)} %param.20) | copy-start | bytes 1376260
  151.1 31.7 %collective-permute-start = (bf16[2,64,2048]{2,1,0:T(8,128)(2,1)}, bf16[2,64,2048]{2,1,0:T(8,128)(2,1)S(1)}, u32[]{:S(2)}, u32[]{:S(2)}) collective-permute-start(bf16[2,64,2048]{2,1,0:T(8,128)(2,1)} %select_convert_fusion.2), channel_id=1, source_target_pairs={{0,1},{1,0},{2,3},{3,2},{4,5},{5,4},{6,7},{7,6},{8,9},{9,8},{10,11... | collective-permute-start | bytes 1572872 | tf_op jit(solution)/shard_map/ppermute | solution.py:1088
  154.3 153.5 %copy-start.43 = (f32[2048]{0:T(1024)}, f32[2048]{0:T(1024)S(1)}, u32[]{:S(2)}) copy-start(f32[2048]{0:T(1024)S(1)} %mul.252) | copy-start | bytes 24580
  154.6 30.2 %copy-start.30 = (bf16[2,64,2048]{2,1,0:T(8,128)(2,1)}, bf16[2,64,2048]{2,1,0:T(8,128)(2,1)S(1)}, u32[]{:S(2)}) copy-start(bf16[2,64,2048]{2,1,0:T(8,128)(2,1)S(1)} %get-tuple-element.109) | copy-start | bytes 1572868
  182.8 2.1 copy-start.8
  184.7 123.2 %copy-start.22 = (f32[2,64,2048]{2,1,0:T(8,128)}, f32[2,64,2048]{2,1,0:T(8,128)S(1)}, u32[]{:S(2)}) copy-start(f32[2,64,2048]{2,1,0:T(8,128)S(1)} %get-tuple-element.111) | copy-start | bytes 3145732
  184.7 123.2 %copy-start.47 = (f32[2,64]{1,0:T(2,128)}, f32[2,64]{1,0:T(2,128)S(1)}, u32[]{:S(2)}) copy-start(f32[2,64]{1,0:T(2,128)S(1)} %add_rsqrt_fusion.1) | copy-start | bytes 1540
  307.8 17.5 %copy-start.25 = (f32[2,64,2048]{2,1,0:T(8,128)}, f32[2,64,2048]{2,1,0:T(8,128)S(1)}, u32[]{:S(2)}) copy-start(f32[2,64,2048]{2,1,0:T(8,128)S(1)} %get-tuple-element.129) | copy-start | bytes 3145732
  307.8 17.5 %copy-start.49 = (f32[2,64]{1,0:T(2,128)}, f32[2,64]{1,0:T(2,128)S(1)}, u32[]{:S(2)}) copy-start(f32[2,64]{1,0:T(2,128)S(1)} %broadcast_multiply_fusion.1) | copy-start | bytes 1540
  309.0 15.1 %collective-permute-start.1 = (bf16[2,64,2048]{2,1,0:T(8,128)(2,1)}, bf16[2,64,2048]{2,1,0:T(8,128)(2,1)S(1)}, u32[]{:S(2)}, u32[]{:S(2)}) collective-permute-start(bf16[2,64,2048]{2,1,0:T(8,128)(2,1)} %fusion.55), channel_id=1, source_target_pairs={{0,1},{1,0},{2,3},{3,2},{4,5},{5,4},{6,7},{7,6},{8,9},{9,8},{10,11... | collective-permute-start | bytes 1572872 | tf_op jit(solution)/shard_map/ppermute | solution.py:1088
  326.4 32.1 %copy-start.29 = (bf16[2,1,64,2048]{3,2,1,0:T(8,128)(2,1)S(1)}, bf16[2,1,64,2048]{3,2,1,0:T(8,128)(2,1)}, u32[]{:S(2)}) copy-start(bf16[2,1,64,2048]{3,2,1,0:T(8,128)(2,1)} %param.21) | copy-start | bytes 1572868
  326.4 32.1 %copy-start.34 = (bf16[2,64,2048]{2,1,0:T(8,128)(2,1)S(1)}, bf16[2,64,2048]{2,1,0:T(8,128)(2,1)}, u32[]{:S(2)}) copy-start(bf16[2,64,2048]{2,1,0:T(8,128)(2,1)} %copy-done.33) | copy-start | bytes 1572868
  326.4 106.9 %all-to-all-start.1 = ((bf16[64,16,2048]{2,1,0:T(8,128)(2,1)}), bf16[64,16,2048]{2,1,0:T(8,128)(2,1)}, u32[]{:S(2)}, u32[]{:S(2)}) async-start(bf16[64,16,2048]{2,1,0:T(8,128)(2,1)} %get-tuple-element.55), calls=%async_computation.1 | async-start | bytes 8388608 | tf_op jit(solution)/shard_map/all_to_all | solution.py:1117
  358.7 2.0 copy-start.35
  360.7 5.8 %copy-start.3 = (bf16[2,640,512]{2,1,0:T(8,128)(2,1)S(1)}, bf16[2,640,512]{2,1,0:T(8,128)(2,1)}, u32[]{:S(2)}) copy-start(bf16[2,640,512]{2,1,0:T(8,128)(2,1)} %copy-done.1) | copy-start | bytes 3932164
  360.7 5.8 %copy-start.13 = (f32[128,128]{1,0:T(8,128)S(1)}, f32[128,128]{1,0:T(8,128)}, u32[]{:S(2)}) copy-start(f32[128,128]{1,0:T(8,128)} %copy-done.11) | copy-start | bytes 196612
  419.3 8.3 %copy-start.37 = (bf16[256,2048]{1,0:T(8,128)(2,1)S(1)}, bf16[256,2048]{1,0:T(8,128)(2,1)}, u32[]{:S(2)}) copy-start(bf16[256,2048]{1,0:T(8,128)(2,1)} %fusion.8) | copy-start | bytes 3145732
  427.6 10.5 %copy-start.17 = (bf16[128,1024]{1,0:T(8,128)(2,1)S(1)}, bf16[128,1024]{1,0:T(8,128)(2,1)}, u32[]{:S(2)}) copy-start(bf16[128,1024]{1,0:T(8,128)(2,1)} %copy-done.16) | copy-start | bytes 786436
  434.9 16.0 %collective-permute-start.3 = (bf16[2,64,2048]{2,1,0:T(8,128)(2,1)S(1)}, bf16[2,64,2048]{2,1,0:T(8,128)(2,1)S(1)}, u32[]{:S(2)}, u32[]{:S(2)}) collective-permute-start(bf16[2,64,2048]{2,1,0:T(8,128)(2,1)S(1)} %select_convert_fusion.1), channel_id=1, source_target_pairs={{0,1},{1,0},{2,3},{3,2},{4,5},{5,4},{6,7},{7,6},{8,9},{9,8},{10,11... | collective-permute-start | bytes 1572872 | tf_op jit(solution)/shard_map/ppermute | solution.py:1088
  438.2 3.0 copy-start.15
  441.1 4.1 copy-start.6
  441.1 4.1 copy-start.36
  445.2 5.7 %copy-start.31 = (bf16[2,64,2048]{2,1,0:T(8,128)(2,1)S(1)}, bf16[2,64,2048]{2,1,0:T(8,128)(2,1)}, u32[]{:S(2)}) copy-start(bf16[2,64,2048]{2,1,0:T(8,128)(2,1)} %copy-done.30) | copy-start | bytes 1572868
  445.2 5.7 %copy-start.38 = (f32[256,2048]{1,0:T(8,128)S(1)}, f32[256,2048]{1,0:T(8,128)}, u32[]{:S(2)}) copy-start(f32[256,2048]{1,0:T(8,128)} %fusion.58) | copy-start | bytes 6291460
  445.2 5.8 %copy-start.51 = (f32[2,64]{1,0:T(2,128)S(1)}, f32[2,64]{1,0:T(2,128)}, u32[]{:S(2)}) copy-start(f32[2,64]{1,0:T(2,128)} %add_rsqrt_fusion) | copy-start | bytes 1540
  451.0 1.5 copy-start.46
  451.0 1.7 copy-start.4
  452.7 83.0 %copy-start.23 = (f32[2,64,2048]{2,1,0:T(8,128)S(1)}, f32[2,64,2048]{2,1,0:T(8,128)}, u32[]{:S(2)}) copy-start(f32[2,64,2048]{2,1,0:T(8,128)} %copy-done.22) | copy-start | bytes 3145732
  452.7 83.0 %copy-start.26 = (f32[2,64,2048]{2,1,0:T(8,128)S(1)}, f32[2,64,2048]{2,1,0:T(8,128)}, u32[]{:S(2)}) copy-start(f32[2,64,2048]{2,1,0:T(8,128)} %copy-done.25) | copy-start | bytes 3145732
  452.7 83.0 %copy-start.32 = (bf16[2,64,2048]{2,1,0:T(8,128)(2,1)S(1)}, bf16[2,64,2048]{2,1,0:T(8,128)(2,1)}, u32[]{:S(2)}) copy-start(bf16[2,64,2048]{2,1,0:T(8,128)(2,1)} %copy-done.30) | copy-start | bytes 1572868
  452.7 83.0 %copy-start.39 = (f32[128,2048]{1,0:T(8,128)S(1)}, f32[128,2048]{1,0:T(8,128)}, u32[]{:S(2)}) copy-start(f32[128,2048]{1,0:T(8,128)} %convolution_add_fusion) | copy-start | bytes 3145732
  452.7 83.0 %copy-start.40 = (f32[2,64,2048]{2,1,0:T(8,128)S(1)}, f32[2,64,2048]{2,1,0:T(8,128)}, u32[]{:S(2)}) copy-start(f32[2,64,2048]{2,1,0:T(8,128)} %get-tuple-element.107) | copy-start | bytes 3145732
  452.7 83.0 %copy-start.44 = (f32[2048]{0:T(1024)S(1)}, f32[2048]{0:T(1024)}, u32[]{:S(2)}) copy-start(f32[2048]{0:T(1024)} %copy-done.43) | copy-start | bytes 24580
  452.7 83.0 %copy-start.48 = (f32[2,64]{1,0:T(2,128)S(1)}, f32[2,64]{1,0:T(2,128)}, u32[]{:S(2)}) copy-start(f32[2,64]{1,0:T(2,128)} %copy-done.47) | copy-start | bytes 1540
  452.7 83.0 %copy-start.50 = (f32[2,64]{1,0:T(2,128)S(1)}, f32[2,64]{1,0:T(2,128)}, u32[]{:S(2)}) copy-start(f32[2,64]{1,0:T(2,128)} %copy-done.49) | copy-start | bytes 1540
  535.8 4.3 copy-start.24
  536.4 16.4 %collective-permute-start.2 = (bf16[2,64,2048]{2,1,0:T(8,128)(2,1)S(1)}, bf16[2,64,2048]{2,1,0:T(8,128)(2,1)S(1)}, u32[]{:S(2)}, u32[]{:S(2)}) collective-permute-start(bf16[2,64,2048]{2,1,0:T(8,128)(2,1)S(1)} %get-tuple-element.115), channel_id=1, source_target_pairs={{0,1},{1,0},{2,3},{3,2},{4,5},{5,4},{6,7},{7,6},{8,9},{9,8},{10,11... | collective-permute-start | bytes 1572872 | tf_op jit(solution)/shard_map/ppermute | solution.py:1088
  538.1 22.5 %collective-permute-start.4 = (bf16[2,64,2048]{2,1,0:T(8,128)(2,1)S(1)}, bf16[2,64,2048]{2,1,0:T(8,128)(2,1)S(1)}, u32[]{:S(2)}, u32[]{:S(2)}) collective-permute-start(bf16[2,64,2048]{2,1,0:T(8,128)(2,1)S(1)} %get-tuple-element.114), channel_id=1, source_target_pairs={{0,1},{1,0},{2,3},{3,2},{4,5},{5,4},{6,7},{7,6},{8,9},{9,8},{10,11... | collective-permute-start | bytes 1572872 | tf_op jit(solution)/shard_map/ppermute | solution.py:1088
  (12 other events, 10.4 us)

commit v6 on v5

--- a/solution.py
+++ b/solution.py
@@ -26,6 +26,13 @@
     return lax.dot_general(a, b, (dims, ((), ())), preferred_element_type=F32)
 
 
+def remote(src, dst, send_sem, recv_sem, where):
+    return pltpu.make_async_remote_copy(
+        src_ref=src, dst_ref=dst, send_sem=send_sem, recv_sem=recv_sem, device_id=where,
+        device_id_type=MESH,
+    )
+
+
 def place():
     f, c = lax.axis_index("fsdp"), lax.axis_index("ctx")
     return f // 2, f % 2, c // 2, c % 2
@@ -75,8 +82,8 @@
     )
 
 
-def route(ids, gates, experts, size, select_ref, high_ref, low_ref):
-    tokens, slots = ids.shape[0], select_ref.shape[1]
+def route(ids, gates, experts, size, select_ref, mix_ref):
+    tokens, slots = ids.shape[0], mix_ref.shape[1]
     block, places = tokens // 2, size // 2
     chosen = jnp.zeros((tokens, experts.shape[1]), F32)
     weight = jnp.zeros((tokens, experts.shape[1]), F32)
@@ -97,19 +104,19 @@
     place = (j & (places - 1)).astype(F32)
     mine = ((j & places) != 0) == later
     there = jnp.logical_and(dot(rank, spread, ((1,), (0,))) == place, mine)
-    select_ref[...] = jnp.where(there, 1.0, 0.0).astype(BF16)
-    if high_ref is not None:
-        high = weight.astype(BF16)
-        low = (weight - high.astype(F32)).astype(BF16)
-        high_ref[...] = jnp.where(there, dot(high, spread, ((1,), (0,))), 0.0).astype(BF16)
-        low_ref[...] = jnp.where(there, dot(low, spread, ((1,), (0,))), 0.0).astype(BF16)
+    if select_ref is not None:
+        select_ref[...] = jnp.where(there, 1.0, 0.0).astype(BF16)
+    high = weight.astype(BF16)
+    low = (weight - high.astype(F32)).astype(BF16)
+    mix_ref[0:tokens, :] = jnp.where(there, dot(high, spread, ((1,), (0,))), 0.0).astype(BF16)
+    mix_ref[tokens:, :] = jnp.where(there, dot(low, spread, ((1,), (0,))), 0.0).astype(BF16)
 
 
 def gather_kernel(
     query_ref, key_ref, value_ref, out_ref, extra_ref, ids_ref, gates_ref, experts_ref, cot_ref,
     gate_ref, up_ref, down_ref,
-    a_all, b_all, gate_all, up_all, down_all, near_ref, high_ref, low_ref, rows_ref,
-    a_own, b_own, select, rows, rows_sem, local_sem, send_sem, recv_sem, away_sem, home_sem, give_sem, take_sem,
+    a_all, b_all, gate_all, up_all, down_all, near_ref, mix_ref, rows_ref,
+    a_own, b_own, mix, rows, rows_sem, local_sem, send_sem, recv_sem, away_sem, home_sem, give_sem, take_sem,
 ):
     y, core, z, x = place()
     for own, refs in ((a_own, (query_ref, key_ref, value_ref)), (b_own, (out_ref, extra_ref))):
@@ -181,8 +188,8 @@
         started.append(copy)
     size = rows.shape[0] // (RING * RING * RING)
     ids, gates = ids_ref[...], gates_ref[...]
-    route(ids, gates, experts_ref[0:1, :], size, select, high_ref, low_ref)
-    route(ids, gates, experts_ref[1:2, :], size, near_ref, None, None)
+    route(ids, gates, experts_ref[0:1, :], size, None, mix)
+    route(ids, gates, experts_ref[1:2, :], size, near_ref, mix_ref)
     for n in (0, 1):
         i, j = me[n]
         locals_[n].wait()
@@ -198,11 +205,11 @@
         for copy in moved:
             copy.start()
 
-    part = 256
+    part, tokens = 256, cot_ref.shape[0]
     for at in range(0, rows.shape[0], part):
         lanes = slice(at, at + part)
-        total = dot(high_ref[:, lanes], cot_ref[...], ((0,), (0,)))
-        total = total + dot(low_ref[:, lanes], cot_ref[...], ((0,), (0,)))
+        total = dot(mix[0:tokens, lanes], cot_ref[...], ((0,), (0,)))
+        total = total + dot(mix[tokens:, lanes], cot_ref[...], ((0,), (0,)))
         rows[lanes, :] = total.astype(BF16)
     keep_rows = pltpu.make_async_copy(rows, rows_ref, rows_sem)
     keep_rows.start()
@@ -260,16 +267,16 @@
     shape = (RING, 2, RING, 2, rows)
     vmem, any_space = (pl.BlockSpec(memory_space=space) for space in (pltpu.VMEM, pl.ANY))
     tokens, width = cot.shape
-    routing = [jax.ShapeDtypeStruct((tokens, slots), BF16)] * 3
+    routing = [jax.ShapeDtypeStruct((n * tokens, slots), BF16) for n in (1, 2)]
     a_all, b_all, *rest = pl.pallas_call(
         gather_kernel,
         in_specs=[vmem] * 9 + [any_space] * 3,
-        out_specs=[any_space] * 5 + [vmem] * 3 + [any_space],
+        out_specs=[any_space] * 5 + [vmem] * 2 + [any_space],
         out_shape=[jax.ShapeDtypeStruct(shape + (c,), query.dtype) for c in cols]
         + [jax.ShapeDtypeStruct(v.shape, v.dtype) for v in (gate, up, down)]
         + routing + [jax.ShapeDtypeStruct((slots, width), BF16)],
         scratch_shapes=[pltpu.VMEM((rows, c), query.dtype) for c in cols] + [
-            pltpu.VMEM((tokens, slots), BF16),
+            pltpu.VMEM((2 * tokens, slots), BF16),
             pltpu.VMEM((slots, width), BF16),
             pltpu.SemaphoreType.DMA,
             pltpu.SemaphoreType.DMA((2,)),
@@ -314,10 +321,11 @@
 
 
 def scatter_kernel(
-    a_ref, b_ref, extra_ref, wide_ref, tall_ref, a_out, b_out, wide_out, tall_out, a_mine, b_mine, a_theirs, b_theirs, a_one, b_one, a_two, b_two,
+    a_ref, b_ref, extra_ref, wide_ref, tall_ref, y_ref, x_ref,
+    a_out, b_out, wide_out, tall_out, y_out, x_out, a_mine, b_mine, a_theirs, b_theirs, a_one, b_one, a_two, b_two,
     a_first, b_first, a_last, b_last, a_x, b_x, load_sem, send_sem, recv_sem,
     gains_here, gains_there,
-    extra_load_sem, extra_send_sem, extra_recv_sem, give_sem, take_sem, gains_sem,
+    extra_load_sem, extra_send_sem, extra_recv_sem, give_sem, take_sem, gains_sem, token_sem,
 ):
     y, core, z, x = place()
     greet(neighbours() + [other_tp(), opposite()])
@@ -325,6 +333,16 @@
         swap_opposite(wide_ref, wide_out, give_sem.at[0], take_sem.at[0]),
         swap_opposite(tall_ref, tall_out, give_sem.at[1], take_sem.at[1]),
     ]
+
+    tokens = [
+        pltpu.make_async_remote_copy(
+            src_ref=src, dst_ref=dst, send_sem=token_sem.at[n, 0], recv_sem=token_sem.at[n, 1],
+            device_id=other_tp(), device_id_type=MESH,
+        )
+        for n, (src, dst) in enumerate(((y_ref, y_out), (x_ref, x_out)))
+    ]
+    for copy in tokens:
+        copy.start()
 
     @pl.when(jnp.logical_not(native()))
     def _():
@@ -482,6 +500,8 @@
     for slot in range(RING * RING):
         extra_copy(slot).wait_send()
     gains.wait()
+    for copy in tokens:
+        copy.wait()
     b_out[:, cols:] = gains_here[...] + gains_there[...]
 
     @pl.when(jnp.logical_not(native()))
@@ -490,7 +510,7 @@
             copy.wait()
 
 
-def scatter_grads(a, b, extra, wide, tall):
+def scatter_grads(a, b, extra, wide, tall, y, x):
     peers = RING * RING * 4
     rows = a.shape[0] // peers
     shape = (RING, 2, RING, 2, rows)
@@ -501,10 +521,10 @@
     any_space = pl.BlockSpec(memory_space=pl.ANY)
     return pl.pallas_call(
         scatter_kernel,
-        in_specs=[any_space] * 5,
-        out_specs=[pl.BlockSpec(memory_space=pltpu.VMEM)] * 2 + [any_space] * 2,
+        in_specs=[any_space] * 7,
+        out_specs=[pl.BlockSpec(memory_space=pltpu.VMEM)] * 2 + [any_space] * 4,
         out_shape=[jax.ShapeDtypeStruct((rows, c), F32) for c in cols]
-        + [jax.ShapeDtypeStruct(v.shape, v.dtype) for v in (wide, tall)],
+        + [jax.ShapeDtypeStruct(v.shape, v.dtype) for v in (wide, tall, y, x)],
         scratch_shapes=buffers + [
             pltpu.SemaphoreType.DMA((2, 16)),
             pltpu.SemaphoreType.DMA((2, 37)),
@@ -517,286 +537,14 @@
             pltpu.SemaphoreType.DMA((2,)),
             pltpu.SemaphoreType.DMA((2,)),
             pltpu.SemaphoreType.DMA((2,)),
+            pltpu.SemaphoreType.DMA((2, 2)),
         ],
         compiler_params=pltpu.CompilerParams(
             collective_id=1, has_side_effects=True, vmem_limit_bytes=44 * 1024 * 1024
         ),
         cost_estimate=pl.CostEstimate(flops=0, bytes_accessed=250_000_000, transcendentals=0),
         name="scatter_grads",
-    )(*(v.reshape(shape + (v.shape[1],)) for v in (a, b, extra)), wide, tall)
-
-
-BLOCK = 64
-CTX = 8
-
-
-def rotated(u, gain, cosine, sine):
-    scaling = lax.rsqrt(jnp.mean(u * u, axis=-1, keepdims=True) + EPS)
-    normed = u * scaling
-    n = normed * gain
-    rot = n * cosine + pltpu.roll(n, HEAD_SIZE // 2, 1) * sine
-    return rot.astype(BF16), normed, scaling
-
-
-def rotated_back(e, normed, scaling, gain, cosine, sine):
-    back = e * cosine + pltpu.roll(e * sine, HEAD_SIZE // 2, 1)
-    scaled = back * gain
-    inner = jnp.mean(scaled * normed, axis=-1, keepdims=True)
-    return scaling * (scaled - normed * inner), jnp.sum(back * normed, axis=0, keepdims=True)
-
-
-def ctx_peer(step):
-    return {"ctx": lax.rem(lax.axis_index("ctx") + step, CTX)}
-
-
-def beside():
-    c = lax.axis_index("ctx")
-    return {"ctx": c + 1 - 2 * lax.rem(c, 2)}
-
-
-def remote(src, dst, send_sem, recv_sem, where):
-    return pltpu.make_async_remote_copy(
-        src_ref=src, dst_ref=dst, send_sem=send_sem, recv_sem=recv_sem, device_id=where,
-        device_id_type=MESH,
-    )
-
-
-def softmax_parts(q_low, k, bias):
-    s = dot(q_low, k, ((1,), (1,))) * (HEAD_SIZE ** -0.5) + bias
-    e = jnp.exp(s - jnp.max(s, axis=-1, keepdims=True))
-    return e / jnp.sum(e, axis=-1, keepdims=True)
-
-
-def share_kernel(kv, rows_ref, cos_ref, sin_ref, gk_ref, kv_ref, held, send_sem, recv_sem):
-    c = lax.axis_index("ctx")
-    greet([ctx_peer(step) for step in range(1, CTX)])
-    micro, rows = held.shape[0], 2 * BLOCK
-    cosine, sine, gk = cos_ref[...], sin_ref[...], gk_ref[...]
-    mine = pl.ds(pl.multiple_of(c * BLOCK, BLOCK), BLOCK)
-    earlier, own = pl.ds(CTX * BLOCK, BLOCK), pl.ds((CTX + 1) * BLOCK, BLOCK)
-    copies = []
-    for m in range(micro):
-        span = slice(m * rows, (m + 1) * rows)
-        for h in range(2 * kv):
-            cols = slice(h * HEAD_SIZE, (h + 1) * HEAD_SIZE)
-            u = rows_ref[span, cols]
-            low = rotated(u, gk, cosine, sine)[0] if h < kv else u.astype(BF16)
-            held[m, mine, cols] = low[:BLOCK]
-            held[m, own, cols] = low[BLOCK:]
-        for step in range(1, CTX):
-            part = held.at[m, mine]
-            copies.append(
-                remote(part, part, send_sem.at[step, m], recv_sem.at[step, m], ctx_peer(step))
-            )
-        copies.append(
-            remote(
-                held.at[m, own], held.at[m, earlier], send_sem.at[0, m], recv_sem.at[0, m], beside()
-            )
-        )
-        for copy in copies[-CTX:]:
-            copy.start()
-    for m in range(micro):
-        for step in range(1, CTX):
-            source = lax.rem(c + CTX - step, CTX)
-            part = held.at[m, pl.ds(pl.multiple_of(source * BLOCK, BLOCK), BLOCK)]
-            remote(
-                part, part, send_sem.at[step, m], recv_sem.at[step, m], ctx_peer(step)
-            ).wait_recv()
-        copies[(m + 1) * CTX - 1].wait_recv()
-        kv_ref[m] = held[m]
-    for copy in copies:
-        copy.wait_send()
-
-
-def attention_kernel(heads, q_ref, cos_ref, sin_ref, gq_ref, bias_ref, k_ref, v_ref, o_ref):
-    cosine, sine, gq = cos_ref[...], sin_ref[...], gq_ref[...]
-    for e in range(heads):
-        cols = slice(e * HEAD_SIZE, (e + 1) * HEAD_SIZE)
-        q_low = rotated(q_ref[:, cols], gq, cosine, sine)[0]
-        p = softmax_parts(q_low, k_ref[...], bias_ref[...]).astype(BF16)
-        o_ref[:, cols] = dot(p, v_ref[...], ((1,), (0,))).astype(BF16)
-
-
-def attention_back_kernel(
-    kv, heads, qkv_ref, cos_ref, sin_ref, gq_ref, gk_ref, bias_ref, kv_ref, do_ref,
-    dqkv_ref, gains_ref, grads, given, given_side, p_all, ds_all, q_all, do_all,
-    send_sem, recv_sem,
-):
-    c = lax.axis_index("ctx")
-    greet([ctx_peer(step) for step in range(1, CTX)])
-    micro, rows = grads.shape[0], 2 * BLOCK
-    q_cols = kv * heads * HEAD_SIZE
-    scale = HEAD_SIZE ** -0.5
-    cosine, sine, gq, gk = cos_ref[...], sin_ref[...], gq_ref[...], gk_ref[...]
-    mine = pl.ds(pl.multiple_of(c * BLOCK, BLOCK), BLOCK)
-    earlier, own = pl.ds(CTX * BLOCK, BLOCK), pl.ds((CTX + 1) * BLOCK, BLOCK)
-
-    def head_cols(h):
-        return pl.ds(pl.multiple_of(h * HEAD_SIZE, HEAD_SIZE), HEAD_SIZE)
-
-    def keys_back(m, h, carry):
-        span = slice(m * rows, (m + 1) * rows)
-        k, v = kv_ref[m, :, head_cols(h)], kv_ref[m, :, head_cols(kv + h)]
-        for e in range(heads):
-            cols = head_cols(h * heads + e)
-            stack = slice(e * rows, (e + 1) * rows)
-            q_low = rotated(qkv_ref[span, cols], gq, cosine, sine)[0]
-            q_all[stack, :] = q_low
-            p = softmax_parts(q_low, k, bias_ref[...])
-            p_all[stack, :] = p.astype(BF16)
-            do = do_ref[span, cols]
-            do_all[stack, :] = do
-            dp = dot(do, v, ((1,), (1,)))
-            ds = (p * (dp - jnp.sum(dp * p, axis=-1, keepdims=True))).astype(BF16)
-            ds_all[m * kv + h, stack, :] = ds
-        grads[m, :, head_cols(kv + h)] = dot(p_all[...], do_all[...], ((0,), (0,))).astype(BF16)
-        d_k = dot(ds_all[m * kv + h], q_all[...], ((0,), (0,))) * scale
-        grads[m, :, head_cols(h)] = d_k.astype(BF16)
-        return carry
-
-    def queries_back(m, h, total):
-        span = slice(m * rows, (m + 1) * rows)
-        k = kv_ref[m, :, head_cols(h)]
-        for e in range(heads):
-            cols = head_cols(h * heads + e)
-            ds = ds_all[m * kv + h, e * rows : (e + 1) * rows, :]
-            dqr = (dot(ds, k, ((1,), (0,))) * scale).astype(BF16).astype(F32)
-            u = qkv_ref[span, cols]
-            scaling = lax.rsqrt(jnp.mean(u * u, axis=-1, keepdims=True) + EPS)
-            dq, part = rotated_back(dqr, u * scaling, scaling, gq, cosine, sine)
-            dqkv_ref[span, cols] = dq.astype(BF16)
-            total = total + part
-        return total
-
-    copies = []
-    for m in range(micro):
-        lax.fori_loop(0, kv, functools.partial(keys_back, m), 0)
-        for step in range(1, CTX):
-            peer = lax.rem(c + step, CTX)
-            part = grads.at[m, pl.ds(pl.multiple_of(peer * BLOCK, BLOCK), BLOCK)]
-            copies.append(
-                remote(
-                    part, given.at[step - 1, m], send_sem.at[step, m], recv_sem.at[step, m],
-                    ctx_peer(step),
-                )
-            )
-        copies.append(
-            remote(
-                grads.at[m, earlier], given_side.at[m], send_sem.at[0, m], recv_sem.at[0, m],
-                beside(),
-            )
-        )
-        for copy in copies[-CTX:]:
-            copy.start()
-    total = jnp.zeros((1, HEAD_SIZE), F32)
-    for m in range(micro):
-        total = lax.fori_loop(0, kv, functools.partial(queries_back, m), total)
-    k_total = jnp.zeros((1, HEAD_SIZE), F32)
-    for m in range(micro):
-        for copy in copies[m * CTX : (m + 1) * CTX]:
-            copy.wait_recv()
-        for h in range(2 * kv):
-            cols = slice(h * HEAD_SIZE, (h + 1) * HEAD_SIZE)
-            at = slice(q_cols + h * HEAD_SIZE, q_cols + (h + 1) * HEAD_SIZE)
-            prompt = grads[m, mine, cols].astype(F32)
-            for step in range(CTX - 1):
-                prompt = prompt + given[step, m, :, cols].astype(F32)
-            cont = grads[m, own, cols].astype(F32) + given_side[m, :, cols].astype(F32)
-            e = jnp.concatenate([prompt, cont], axis=0).astype(BF16)
-            span = slice(m * rows, (m + 1) * rows)
-            if h < kv:
-                _, normed, scaling = rotated(qkv_ref[span, at], gk, cosine, sine)
-                d, part = rotated_back(e.astype(F32), normed, scaling, gk, cosine, sine)
-                k_total = k_total + part
-                dqkv_ref[span, at] = d.astype(BF16)
-            else:
-                dqkv_ref[span, at] = e
-    gains_ref[0:1, :] = total
-    gains_ref[1:2, :] = k_total
-    for copy in copies:
-        copy.wait_send()
-
-
-def share_keys(qkv, cosine, sine, gain_key, kv, keys, micro):
-    rows, cols = qkv.shape[0], 2 * kv * HEAD_SIZE
-    last = qkv.shape[1] // cols - 1
-
-    def whole(shape):
-        return pl.BlockSpec(shape, lambda i: (0,) * len(shape))
-
-    return pl.pallas_call(
-        functools.partial(share_kernel, kv),
-        grid=(1,),
-        in_specs=[pl.BlockSpec((rows, cols), lambda i: (0, last)), whole(cosine.shape)]
-        + [whole(sine.shape), whole(gain_key.shape)],
-        out_specs=whole((micro, keys, cols)),
-        out_shape=jax.ShapeDtypeStruct((micro, keys, cols), BF16),
-        scratch_shapes=[
-            pltpu.VMEM((micro, keys, cols), BF16),
-            pltpu.SemaphoreType.DMA((CTX, micro)),
-            pltpu.SemaphoreType.DMA((CTX, micro)),
-        ],
-        compiler_params=pltpu.CompilerParams(
-            collective_id=2, has_side_effects=True, vmem_limit_bytes=VMEM_LIMIT
-        ),
-        cost_estimate=pl.CostEstimate(flops=0, bytes_accessed=50_000_000, transcendentals=0),
-        name="share_keys",
-    )(qkv, cosine, sine, gain_key)
-
-
-def attention(qkv, cosine, sine, gain_query, bias, kv_all, kv):
-    micro, keys, cols = kv_all.shape
-    rows = bias.shape[0]
-    heads = qkv.shape[1] // HEAD_SIZE // kv - 2
-    width = heads * HEAD_SIZE
-
-    def whole(v):
-        return pl.BlockSpec(v.shape, lambda m, g: (0,) * v.ndim)
-
-    return pl.pallas_call(
-        functools.partial(attention_kernel, heads),
-        grid=(micro, kv),
-        in_specs=[pl.BlockSpec((rows, width), lambda m, g: (m, g))]
-        + [whole(v) for v in (cosine, sine, gain_query, bias)]
-        + [
-            pl.BlockSpec((None, keys, HEAD_SIZE), lambda m, g: (m, 0, g)),
-            pl.BlockSpec((None, keys, HEAD_SIZE), lambda m, g: (m, 0, kv + g)),
-        ],
-        out_specs=pl.BlockSpec((rows, width), lambda m, g: (m, g)),
-        out_shape=jax.ShapeDtypeStruct((micro * rows, kv * width), BF16),
-        compiler_params=pltpu.CompilerParams(vmem_limit_bytes=VMEM_LIMIT),
-        cost_estimate=pl.CostEstimate(flops=0, bytes_accessed=60_000_000, transcendentals=0),
-        name="attention_forward",
-    )(qkv, cosine, sine, gain_query, bias, kv_all, kv_all)
-
-
-def attention_back(qkv, cosine, sine, gain_query, gain_key, bias, kv_all, d_out, kv):
-    heads = qkv.shape[1] // HEAD_SIZE // kv - 2
-    rows, keys = bias.shape
-    micro, _, kv_cols = kv_all.shape
-    return pl.pallas_call(
-        functools.partial(attention_back_kernel, kv, heads),
-        out_shape=[
-            jax.ShapeDtypeStruct(qkv.shape, BF16),
-            jax.ShapeDtypeStruct((2, HEAD_SIZE), F32),
-        ],
-        scratch_shapes=[
-            pltpu.VMEM((micro, keys, kv_cols), BF16),
-            pltpu.VMEM((CTX - 1, micro, BLOCK, kv_cols), BF16),
-            pltpu.VMEM((micro, BLOCK, kv_cols), BF16),
-            pltpu.VMEM((heads * rows, keys), BF16),
-            pltpu.VMEM((micro * kv, heads * rows, keys), BF16),
-            pltpu.VMEM((heads * rows, HEAD_SIZE), BF16),
-            pltpu.VMEM((heads * rows, HEAD_SIZE), BF16),
-            pltpu.SemaphoreType.DMA((CTX, micro)),
-            pltpu.SemaphoreType.DMA((CTX, micro)),
-        ],
-        compiler_params=pltpu.CompilerParams(
-            collective_id=3, has_side_effects=True, vmem_limit_bytes=VMEM_LIMIT
-        ),
-        cost_estimate=pl.CostEstimate(flops=0, bytes_accessed=120_000_000, transcendentals=0),
-        name="attention_backward",
-    )(qkv, cosine, sine, gain_query, gain_key, bias, kv_all, d_out)
+    )(*(v.reshape(shape + (v.shape[1],)) for v in (a, b, extra)), wide, tall, y, x)
 
 
 CHIPS = RING * RING * RING
@@ -895,7 +643,7 @@
 
     def out(s):
         return pltpu.make_async_copy(
-            sent_rows(1, s), eo_ref.at[chip_number(s, -1)], eo_sem.at[s]
+            sent_rows(1, s), eo_ref.at[s], eo_sem.at[s]
         )
 
     def share(n, g):
@@ -1071,6 +819,387 @@
     )(send, d_eo, *own, *far)
 
 
+BLOCK = 64
+CTX = 8
+WIDE = 256
+
+
+def rotated(u, gain, cosine, sine):
+    scaling = lax.rsqrt(jnp.mean(u * u, axis=-1, keepdims=True) + EPS)
+    normed = u * scaling
+    n = normed * gain
+    rot = n * cosine + pltpu.roll(n, HEAD_SIZE // 2, 1) * sine
+    return rot.astype(BF16), normed, scaling
+
+
+def rotated_back(e, normed, scaling, gain, cosine, sine):
+    back = e * cosine + pltpu.roll(e * sine, HEAD_SIZE // 2, 1)
+    scaled = back * gain
+    inner = jnp.mean(scaled * normed, axis=-1, keepdims=True)
+    return scaling * (scaled - normed * inner), jnp.sum(back * normed, axis=0, keepdims=True)
+
+
+def ctx_peer(step):
+    return {"ctx": lax.rem(lax.axis_index("ctx") + step, CTX)}
+
+
+def beside():
+    c = lax.axis_index("ctx")
+    return {"ctx": c + 1 - 2 * lax.rem(c, 2)}
+
+
+def softmax_parts(q_low, k, bias):
+    s = dot(q_low, k, ((1,), (1,))) * (HEAD_SIZE ** -0.5) + bias
+    e = jnp.exp(s - jnp.max(s, axis=-1, keepdims=True))
+    return e / jnp.sum(e, axis=-1, keepdims=True)
+
+
+def share_kernel(kv, rows_ref, cos_ref, sin_ref, gk_ref, kv_ref, held, send_sem, recv_sem):
+    c = lax.axis_index("ctx")
+    greet([ctx_peer(step) for step in range(1, CTX)])
+    micro, rows = held.shape[0], 2 * BLOCK
+    cosine, sine, gk = cos_ref[...], sin_ref[...], gk_ref[...]
+    mine = pl.ds(pl.multiple_of(c * BLOCK, BLOCK), BLOCK)
+    earlier, own = pl.ds(CTX * BLOCK, BLOCK), pl.ds((CTX + 1) * BLOCK, BLOCK)
+    copies = []
+    for m in range(micro):
+        span = slice(m * rows, (m + 1) * rows)
+        for h in range(2 * kv):
+            cols = slice(h * HEAD_SIZE, (h + 1) * HEAD_SIZE)
+            u = rows_ref[span, cols]
+            low = rotated(u, gk, cosine, sine)[0] if h < kv else u.astype(BF16)
+            held[m, mine, cols] = low[:BLOCK]
+            held[m, own, cols] = low[BLOCK:]
+        for step in range(1, CTX):
+            part = held.at[m, mine]
+            copies.append(
+                remote(part, part, send_sem.at[step, m], recv_sem.at[step, m], ctx_peer(step))
+            )
+        copies.append(
+            remote(
+                held.at[m, own], held.at[m, earlier], send_sem.at[0, m], recv_sem.at[0, m], beside()
+            )
+        )
+        for copy in copies[-CTX:]:
+            copy.start()
+    for m in range(micro):
+        for step in range(1, CTX):
+            source = lax.rem(c + CTX - step, CTX)
+            part = held.at[m, pl.ds(pl.multiple_of(source * BLOCK, BLOCK), BLOCK)]
+            remote(
+                part, part, send_sem.at[step, m], recv_sem.at[step, m], ctx_peer(step)
+            ).wait_recv()
+        copies[(m + 1) * CTX - 1].wait_recv()
+        kv_ref[m] = held[m]
+    for copy in copies:
+        copy.wait_send()
+
+
+def attention_kernel(heads, q_ref, cos_ref, sin_ref, gq_ref, bias_ref, k_ref, v_ref, o_ref):
+    cosine, sine, gq = cos_ref[...], sin_ref[...], gq_ref[...]
+    for e in range(heads):
+        cols = slice(e * HEAD_SIZE, (e + 1) * HEAD_SIZE)
+        q_low = rotated(q_ref[:, cols], gq, cosine, sine)[0]
+        p = softmax_parts(q_low, k_ref[...], bias_ref[...]).astype(BF16)
+        o_ref[:, cols] = dot(p, v_ref[...], ((1,), (0,))).astype(BF16)
+
+
+def backward_kernel(
+    kv, heads, qkv_ref, cos_ref, sin_ref, gq_ref, gk_ref, bias_ref, kv_ref, dattn_ref, o_ref, a_ref,
+    w_out_ref, w_qkv_ref, eo_ref,
+    given_grad_ref, gains_ref, grad_qkv_ref, grad_out_ref, eo_back_ref,
+    w_out, w_qkv, do_ref, dqkv_ref, part_sum, wide_tile, tall_tile, grads, given, given_side,
+    p_all, ds_all, q_all, do_all, swap_give, swap_take,
+    send_sem, recv_sem, load_sem, tile_sem, swap_sem, eo_send, eo_recv,
+):
+    c, tp = lax.axis_index("ctx"), lax.axis_index("tp")
+    width = w_out.shape[0]
+
+    def each(body, low, high):
+        def step(i, carry):
+            body(i)
+            return carry
+
+        lax.fori_loop(low, high, step, 0)
+
+    barrier = pltpu.get_barrier_semaphore()
+    each(
+        lambda s: pl.semaphore_signal(
+            barrier, inc=1, device_id=device_at(s, 1), device_id_type=MESH
+        ),
+        1, CHIPS,
+    )
+    loads = [
+        pltpu.make_async_copy(w_out_ref.at[:, pl.ds(0, w_out.shape[1])], w_out, load_sem.at[0]),
+        pltpu.make_async_copy(w_qkv_ref, w_qkv, load_sem.at[1]),
+    ]
+    for copy in loads:
+        copy.start()
+    pl.semaphore_wait(barrier, CHIPS - 1)
+
+    def output(s):
+        return remote(
+            eo_ref.at[s], eo_back_ref.at[s], eo_send.at[s], eo_recv.at[s], device_at(s, -1)
+        )
+
+    def outputs(quarter):
+        each(lambda s: output(s).start(), max(quarter * GROUP, 1), (quarter + 1) * GROUP)
+
+    stay = pltpu.make_async_copy(eo_ref.at[0], eo_back_ref.at[0], eo_recv.at[0])
+    stay.start()
+    outputs(0)
+    micro, rows = grads.shape[0], 2 * BLOCK
+    q_cols = kv * heads * HEAD_SIZE
+    scale = HEAD_SIZE ** -0.5
+    cosine, sine, gq, gk = cos_ref[...], sin_ref[...], gq_ref[...], gk_ref[...]
+    mine = pl.ds(pl.multiple_of(c * BLOCK, BLOCK), BLOCK)
+    earlier, own = pl.ds(CTX * BLOCK, BLOCK), pl.ds((CTX + 1) * BLOCK, BLOCK)
+
+    def tile(i):
+        return pl.ds(pl.multiple_of(i * WIDE, WIDE), WIDE)
+
+    loads[0].wait()
+
+    def outputs_back(i):
+        do_ref[:, tile(i)] = dot(dattn_ref[...], w_out[:, tile(i)], ((1,), (0,))).astype(BF16)
+
+    each(outputs_back, 0, w_out.shape[1] // WIDE)
+
+    def head_cols(h):
+        return pl.ds(pl.multiple_of(h * HEAD_SIZE, HEAD_SIZE), HEAD_SIZE)
+
+    def keys_back(m, h, carry):
+        span = slice(m * rows, (m + 1) * rows)
+        k, v = kv_ref[m, :, head_cols(h)], kv_ref[m, :, head_cols(kv + h)]
+        for e in range(heads):
+            cols = head_cols(h * heads + e)
+            stack = slice(e * rows, (e + 1) * rows)
+            q_low = rotated(qkv_ref[span, cols], gq, cosine, sine)[0]
+            q_all[stack, :] = q_low
+            p = softmax_parts(q_low, k, bias_ref[...])
+            p_all[stack, :] = p.astype(BF16)
+            do = do_ref[span, cols]
+            do_all[stack, :] = do
+            dp = dot(do, v, ((1,), (1,)))
+            ds = (p * (dp - jnp.sum(dp * p, axis=-1, keepdims=True))).astype(BF16)
+            ds_all[m * kv + h, stack, :] = ds
+        grads[m, :, head_cols(kv + h)] = dot(p_all[...], do_all[...], ((0,), (0,))).astype(BF16)
+        d_k = dot(ds_all[m * kv + h], q_all[...], ((0,), (0,))) * scale
+        grads[m, :, head_cols(h)] = d_k.astype(BF16)
+        return carry
+
+    def queries_back(m, h, total):
+        span = slice(m * rows, (m + 1) * rows)
+        k = kv_ref[m, :, head_cols(h)]
+        for e in range(heads):
+            cols = head_cols(h * heads + e)
+            ds = ds_all[m * kv + h, e * rows : (e + 1) * rows, :]
+            dqr = (dot(ds, k, ((1,), (0,))) * scale).astype(BF16).astype(F32)
+            u = qkv_ref[span, cols]
+            scaling = lax.rsqrt(jnp.mean(u * u, axis=-1, keepdims=True) + EPS)
+            dq, part = rotated_back(dqr, u * scaling, scaling, gq, cosine, sine)
+            dqkv_ref[span, cols] = dq.astype(BF16)
+            total = total + part
+        return total
+
+    copies = []
+    for m in range(micro):
+        lax.fori_loop(0, kv, functools.partial(keys_back, m), 0)
+        for step in range(1, CTX):
+            peer = lax.rem(c + step, CTX)
+            part = grads.at[m, pl.ds(pl.multiple_of(peer * BLOCK, BLOCK), BLOCK)]
+            copies.append(
+                remote(
+                    part, given.at[step - 1, m], send_sem.at[step, m], recv_sem.at[step, m],
+                    ctx_peer(step),
+                )
+            )
+        copies.append(
+            remote(
+                grads.at[m, earlier], given_side.at[m], send_sem.at[0, m], recv_sem.at[0, m],
+                beside(),
+            )
+        )
+        for copy in copies[-CTX:]:
+            copy.start()
+        outputs(1 + m)
+    total = jnp.zeros((1, HEAD_SIZE), F32)
+    for m in range(micro):
+        total = lax.fori_loop(0, kv, functools.partial(queries_back, m), total)
+    outputs(3)
+
+    def tiles_out(buffer, left, right, out_ref, sems):
+        def copy_out(i):
+            slot = lax.rem(i, 2)
+            return pltpu.make_async_copy(buffer.at[slot], out_ref.at[tile(i)], sems.at[i])
+
+        def step(i):
+            @pl.when(i >= 2)
+            def _():
+                copy_out(i - 2).wait()
+
+            value = dot(left[:, tile(i)], right[...], ((0,), (0,)))
+            buffer[lax.rem(i, 2)] = value.astype(BF16)
+            copy_out(i).start()
+
+        count = width // WIDE
+        each(step, 0, count)
+        return lambda: each(lambda i: copy_out(i).wait(), count - 2, count)
+
+    end_out = tiles_out(tall_tile, dattn_ref, o_ref, grad_out_ref, tile_sem.at[0])
+    loads[1].wait()
+
+    def queries_in(i):
+        part_sum[:, tile(i)] = dot(dqkv_ref[:, :q_cols], w_qkv[tile(i), :q_cols], ((1,), (1,)))
+
+    each(queries_in, 0, width // WIDE)
+    k_total = jnp.zeros((1, HEAD_SIZE), F32)
+    for m in range(micro):
+        for copy in copies[m * CTX : (m + 1) * CTX]:
+            copy.wait_recv()
+        for h in range(2 * kv):
+            cols = slice(h * HEAD_SIZE, (h + 1) * HEAD_SIZE)
+            at = slice(q_cols + h * HEAD_SIZE, q_cols + (h + 1) * HEAD_SIZE)
+            prompt = grads[m, mine, cols].astype(F32)
+            for step in range(CTX - 1):
+                prompt = prompt + given[step, m, :, cols].astype(F32)
+            cont = grads[m, own, cols].astype(F32) + given_side[m, :, cols].astype(F32)
+            e = jnp.concatenate([prompt, cont], axis=0).astype(BF16)
+            span = slice(m * rows, (m + 1) * rows)
+            if h < kv:
+                _, normed, scaling = rotated(qkv_ref[span, at], gk, cosine, sine)
+                d, part = rotated_back(e.astype(F32), normed, scaling, gk, cosine, sine)
+                k_total = k_total + part
+                dqkv_ref[span, at] = d.astype(BF16)
+            else:
+                dqkv_ref[span, at] = e
+    gains_ref[0:1, :] = total
+    gains_ref[1:2, :] = k_total
+
+    def keys_in(i):
+        part_sum[:, tile(i)] += dot(dqkv_ref[:, q_cols:], w_qkv[tile(i), q_cols:], ((1,), (1,)))
+
+    each(keys_in, 0, width // WIDE)
+    for m in range(micro):
+        away = pl.ds(pl.multiple_of(m * rows + tp * BLOCK, BLOCK), BLOCK)
+        swap_give[m * BLOCK : (m + 1) * BLOCK, :] = part_sum[away, :].astype(BF16)
+    swap = remote(swap_give, swap_take, swap_sem.at[0], swap_sem.at[1], {"tp": 1 - tp})
+    swap.start()
+    end_qkv = tiles_out(wide_tile, a_ref, dqkv_ref, grad_qkv_ref, tile_sem.at[1])
+    swap.wait()
+    for m in range(micro):
+        kept = pl.ds(pl.multiple_of(m * rows + (1 - tp) * BLOCK, BLOCK), BLOCK)
+        span = slice(m * BLOCK, (m + 1) * BLOCK)
+        given_grad_ref[span, :] = part_sum[kept, :] + swap_take[span, :].astype(F32)
+    for copy in copies:
+        copy.wait_send()
+    end_out()
+    end_qkv()
+    stay.wait()
+    each(lambda s: output(s).wait(), 1, CHIPS)
+
+
+def share_keys(qkv, cosine, sine, gain_key, kv, keys, micro):
+    rows, cols = qkv.shape[0], 2 * kv * HEAD_SIZE
+    last = qkv.shape[1] // cols - 1
+
+    def whole(shape):
+        return pl.BlockSpec(shape, lambda i: (0,) * len(shape))
+
+    return pl.pallas_call(
+        functools.partial(share_kernel, kv),
+        grid=(1,),
+        in_specs=[pl.BlockSpec((rows, cols), lambda i: (0, last)), whole(cosine.shape)]
+        + [whole(sine.shape), whole(gain_key.shape)],
+        out_specs=whole((micro, keys, cols)),
+        out_shape=jax.ShapeDtypeStruct((micro, keys, cols), BF16),
+        scratch_shapes=[
+            pltpu.VMEM((micro, keys, cols), BF16),
+            pltpu.SemaphoreType.DMA((CTX, micro)),
+            pltpu.SemaphoreType.DMA((CTX, micro)),
+        ],
+        compiler_params=pltpu.CompilerParams(
+            collective_id=2, has_side_effects=True, vmem_limit_bytes=VMEM_LIMIT
+        ),
+        cost_estimate=pl.CostEstimate(flops=0, bytes_accessed=50_000_000, transcendentals=0),
+        name="share_keys",
+    )(qkv, cosine, sine, gain_key)
+
+
+def attention(qkv, cosine, sine, gain_query, bias, kv_all, kv):
+    micro, keys, cols = kv_all.shape
+    rows = bias.shape[0]
+    heads = qkv.shape[1] // HEAD_SIZE // kv - 2
+    width = heads * HEAD_SIZE
+
+    def whole(v):
+        return pl.BlockSpec(v.shape, lambda m, g: (0,) * v.ndim)
+
+    return pl.pallas_call(
+        functools.partial(attention_kernel, heads),
+        grid=(micro, kv),
+        in_specs=[pl.BlockSpec((rows, width), lambda m, g: (m, g))]
+        + [whole(v) for v in (cosine, sine, gain_query, bias)]
+        + [
+            pl.BlockSpec((None, keys, HEAD_SIZE), lambda m, g: (m, 0, g)),
+            pl.BlockSpec((None, keys, HEAD_SIZE), lambda m, g: (m, 0, kv + g)),
+        ],
+        out_specs=pl.BlockSpec((rows, width), lambda m, g: (m, g)),
+        out_shape=jax.ShapeDtypeStruct((micro * rows, kv * width), BF16),
+        compiler_params=pltpu.CompilerParams(vmem_limit_bytes=VMEM_LIMIT),
+        cost_estimate=pl.CostEstimate(flops=0, bytes_accessed=60_000_000, transcendentals=0),
+        name="attention_forward",
+    )(qkv, cosine, sine, gain_query, bias, kv_all, kv_all)
+
+
+def backward(qkv, heads_in, kv_all, d_attn, o, a, w_out, w_qkv, eo, kv):
+    heads = qkv.shape[1] // HEAD_SIZE // kv - 2
+    bias = heads_in[-1]
+    rows, keys = bias.shape
+    micro, _, kv_cols = kv_all.shape
+    width, cols = w_qkv.shape
+    total, q_cols = qkv.shape[0], kv * heads * HEAD_SIZE
+    vmem, any_space = (pl.BlockSpec(memory_space=space) for space in (pltpu.VMEM, pl.ANY))
+    dma = pltpu.SemaphoreType.DMA
+    return pl.pallas_call(
+        functools.partial(backward_kernel, kv, heads),
+        in_specs=[vmem] * 10 + [any_space] * 3,
+        out_specs=[vmem] * 2 + [any_space] * 3,
+        out_shape=[
+            jax.ShapeDtypeStruct((micro * BLOCK, width), F32),
+            jax.ShapeDtypeStruct((2, HEAD_SIZE), F32),
+            jax.ShapeDtypeStruct((width, cols), BF16),
+            jax.ShapeDtypeStruct((width, q_cols), BF16),
+            jax.ShapeDtypeStruct(eo.shape, BF16),
+        ],
+        scratch_shapes=[
+            pltpu.VMEM((width, q_cols), BF16),
+            pltpu.VMEM((width, cols), BF16),
+            pltpu.VMEM((total, q_cols), BF16),
+            pltpu.VMEM((total, cols), BF16),
+            pltpu.VMEM((total, width), F32),
+            pltpu.VMEM((2, WIDE, cols), BF16),
+            pltpu.VMEM((2, WIDE, q_cols), BF16),
+            pltpu.VMEM((micro, keys, kv_cols), BF16),
+            pltpu.VMEM((CTX - 1, micro, BLOCK, kv_cols), BF16),
+            pltpu.VMEM((micro, BLOCK, kv_cols), BF16),
+            pltpu.VMEM((heads * rows, keys), BF16),
+            pltpu.VMEM((micro * kv, heads * rows, keys), BF16),
+            pltpu.VMEM((heads * rows, HEAD_SIZE), BF16),
+            pltpu.VMEM((heads * rows, HEAD_SIZE), BF16),
+            pltpu.VMEM((micro * BLOCK, width), BF16),
+            pltpu.VMEM((micro * BLOCK, width), BF16),
+            dma((CTX, micro)), dma((CTX, micro)), dma((2,)), dma((2, width // WIDE)), dma((2,)),
+            dma((CHIPS,)), dma((CHIPS,)),
+        ],
+        compiler_params=pltpu.CompilerParams(
+            collective_id=3, has_side_effects=True, vmem_limit_bytes=56 * 1024 * 1024
+        ),
+        cost_estimate=pl.CostEstimate(flops=0, bytes_accessed=250_000_000, transcendentals=0),
+        name="attention_backward",
+    )(qkv, *heads_in, kv_all, d_attn, o, a, w_out, w_qkv, eo)
+
+
 def normalize(rows, gain):
     scaling = lax.rsqrt(jnp.mean(rows * rows, axis=-1, keepdims=True) + EPS)
     return rows * scaling * gain, scaling
@@ -1146,7 +1275,7 @@
         own_ids.reshape(-1, TOPK), own_gates.reshape(-1, TOPK), order,
         own_cot.reshape(-1, width), peers * micro * slots, *own_experts,
     )
-    select_near, mixing_high, mixing_low, spread = routing
+    select_near, mixing, spread = routing
     w_out = w_out_extra[:, :q_cols]
     gains = w_out_extra[:, q_cols:].reshape(peers, shard_rows, HEAD_SIZE)[:, :4].astype(F32)
     gain_in, gain_moe = (gains[:, n, :shard_rows].reshape(-1) for n in (0, 1))
@@ -1184,8 +1313,7 @@
     )
     bias = jnp.where(visible, 0.0, NEG).astype(F32)
 
-    def share_rows(own):
-        other = swap_tp(own)
+    def arranged(own, other):
         return jnp.where(first, other, own), jnp.where(first, own, other)
 
     def sum_own(part):
@@ -1214,24 +1342,20 @@
     d_b = dot(select_near, back.reshape(-1, width), ((1,), (0,))).reshape(middle.shape)
     middle_from, moe_total = normalize_back(middle, b_scale, gain_moe, d_b)
     d_h = own_cot.astype(F32) + middle_from
-    d_attn = jnp.concatenate(share_rows(d_h.astype(BF16)), axis=1).reshape(-1, width)
-
-    late, d_attn = lax.optimization_barrier((eo, d_attn))
-    eo_back = exchange(late.reshape(-1, width))
-
-    d_o = dot(d_attn, w_out, ((1,), (0,))).astype(BF16)
-    d_qkv, head_totals = attention_back(qkv, *heads_in, kv_all, d_o, kv)
-    input_part, d_attn, eo_back = lax.optimization_barrier(
-        (dot(d_qkv, w_qkv, ((1,), (1,))), d_attn, eo_back)
+    d_h_low = d_h.astype(BF16)
+    d_attn = jnp.concatenate(arranged(d_h_low, swap_tp(d_h_low)), axis=1).reshape(-1, width)
+
+    input_grad, head_totals, grad_qkv, grad_out, eo_back = backward(
+        qkv, heads_in, kv_all, d_attn, o, a, w_out_extra, w_qkv, eo, kv
     )
-    input_grad = sum_own(input_part)
-    grad_out = dot(d_attn, o, ((0,), (0,))).astype(BF16)
-    moe_out = dot(mixing_high, eo_back, ((1,), (0,))) + dot(mixing_low, eo_back, ((1,), (0,)))
-    out_first, out_second = share_rows((middle + moe_out.reshape(middle.shape)).astype(BF16))
-    grad_qkv = dot(a, d_qkv, ((0,), (0,))).astype(BF16)
+    moe_out = dot(mixing, eo_back.reshape(-1, width), ((1,), (0,)))
+    moe_out = (moe_out[: micro * block] + moe_out[micro * block :]).reshape(middle.shape)
+    y_own = (middle + moe_out).astype(BF16)
     scale_in = lax.rsqrt(jnp.mean(own_tokens * own_tokens, axis=-1, keepdims=True) + EPS)
-    token_from, norm_total = normalize_back(own_tokens, scale_in, gain_in, input_grad)
-    grad_first, grad_second = share_rows((d_h + token_from).astype(BF16))
+    token_from, norm_total = normalize_back(
+        own_tokens, scale_in, gain_in, input_grad.reshape(own_tokens.shape)
+    )
+    x_own = (d_h + token_from).astype(BF16)
 
     extra_grads = jnp.stack(
         [
@@ -1242,9 +1366,11 @@
     )
     extra_grads = jnp.pad(extra_grads, ((0, 0), (0, shard_rows - extra_grads.shape[1]), (0, 0)))
     extra_grads = extra_grads.reshape(-1, HEAD_SIZE).astype(BF16)
-    share, share_out, wide_there, tall_there = scatter_grads(
-        grad_qkv, grad_out, extra_grads, wide_here, tall_here
+    share, share_out, wide_there, tall_there, y_other, x_other = scatter_grads(
+        grad_qkv, grad_out, extra_grads, wide_here, tall_here, y_own, x_own
     )
+    out_first, out_second = arranged(y_own, y_other)
+    grad_first, grad_second = arranged(x_own, x_other)
     grad_wide = jnp.where(native(), wide_here, wide_there).astype(F32)
     grad_down = jnp.where(native(), tall_here, tall_there).astype(F32)
     gain_share = share_out[:, q_cols:]

time: 570 us -> 546 us (0.958)
  Pallas kernels: 355 us -> 415 us
  starting transfers between devices: 50.7 us -> 19.4 us
  matrix products: 52 us -> 21.8 us
  waiting for transfers between devices: 54.3 us -> 39.6 us
    pallas_call x2, Pallas kernels: 132 us -> 190 us  [the longest x1 99.2 us: backward(): pl.pallas_call(functools.partial(backward_kernel, kv, heads), in_specs=[v...]
    all_to_all x2 -> x1, starting transfers between devices: 38.2 us -> 6.94 us  [exchange(): lax.all_to_all(rows_of, ('fsdp', 'ctx', 'tp'), split_axis=0, concat_axis=...]
    dot_general x10 -> x5, matrix products: 52 us -> 21.8 us  [dot(): return lax.dot_general(a, b, (dims, ((), ())), preferred_element_type=F32)]
    ppermute x5 -> x2, waiting for transfers between devices: 54.3 us -> 39.6 us  [swap_tp(): return lax.ppermute(value, 'tp', [(0, 1), (1, 0)])]
    unnamed x107 -> x73, local copies, waits for them, and re-layouts: 11.1 us -> 14.4 us
    ppermute x5 -> x2, starting transfers between devices: 12.5 us -> 12.5 us  [swap_tp(): return lax.ppermute(value, 'tp', [(0, 1), (1, 0)])]
  transfers between devices with their start and end apart: 7 -> 3, of which waited for: 4 -> 2; matrix products, arithmetic and copies ran while one was open for 11% -> 3% of each run, Pallas kernels for 12% -> 3%
where the time goes in v6:
time: 546 us; the launch traced here: 542 us
  Pallas kernels  415 us (76%)
  waiting for transfers between devices  39.6 us (7%)
  local copies, waits for them, and re-layouts  24.4 us (4%)
  matrix products  21.8 us (4%)
  other arithmetic  20.4 us (4%)
  starting transfers between devices  19.4 us (4%)
    pallas_call x1, Pallas kernels, moe(): pl.pallas_call(moe_kernel, in_specs=[any_space] * 8, out_specs=[any_space...  119 us
    pallas_call x1, Pallas kernels, backward(): pl.pallas_call(functools.partial(backward_kernel, kv, heads), in_specs=[v...  99.2 us
    pallas_call x1, Pallas kernels, scatter_grads(): pl.pallas_call(scatter_kernel, in_specs=[any_space] * 7, out_specs=[pl.Bl...  90.4 us
    pallas_call x1, Pallas kernels, gather_weights(): pl.pallas_call(gather_kernel, in_specs=[vmem] * 9 + [any_space] * 3, out_...  70.5 us
    ppermute x2, waiting for transfers between devices, swap_tp(): return lax.ppermute(value, 'tp', [(0, 1), (1, 0)])  39.6 us
    dot_general x5, matrix products, dot(): return lax.dot_general(a, b, (dims, ((), ())), preferred_element_type=F32)  21.8 us
    pallas_call x1, Pallas kernels, share_keys(): pl.pallas_call(functools.partial(share_kernel, kv), grid=(1,), in_specs=[...  21.1 us
    pallas_call x1, Pallas kernels, attention(): pl.pallas_call(functools.partial(attention_kernel, heads), grid=(micro, k...  15.1 us
  transfers between devices with their start and end apart: 3, of which 2 were waited for; matrix products, arithmetic and copies ran while one was open for 3% of the time, Pallas kernels for 3%

profile of v6, /device:TPU:0, one launch (start us, length us, event | category | flops | bytes accessed | tf_op | source)
XLA Modules:
  0.0 541.9 jit_solution(13652707012780971011)
XLA Ops:
  0.7 0.7 bitcast_select_fusion.1
  1.5 0.7 bitcast_select_fusion.2
  3.0 1.3 bitcast_select_fusion
  5.7 0.9 copy-done.13
  6.6 0.9 copy-done.14
  7.5 0.7 copy-done.15
  8.2 0.7 copy-done.16
  8.9 70.5 %gather_weights.1 = (bf16[4,2,4,2,32,2560]{5,4,3,2,1,0:T(8,128)(2,1)}, bf16[4,2,4,2,32,2176]{5,4,3,2,1,0:T(8,128)(2,1)}, bf16[2048,384]{1,0:T(8,128)(2,1)S(1)}, ...) custom-call(bf16[32,2048]{1,0:T(8,128)(2,1)S(1)} %copy-done.13, ...), custom_call_target="tpu_custom_call" | custom-call | bytes 250000000 | tf_op jit(solution)/shard_map/gather_weights/pallas_call | solution.py:271
  79.4 0.7 copy-done.6
  80.1 1.2 copy-done.8
  81.3 1.2 copy-done.9
  82.4 0.8 copy-done.19
  83.2 1.1 slice.109
  85.4 5.6 %fusion.54.rows_ref.q_ref.qkv_ref = f32[256,2560]{1,0:T(8,128)S(1)} fusion(bf16[256,2048]{1,0:T(8,128)(2,1)S(1)} %bitcast.144, bf16[2048,2560]{1,0:T(8,128)(2,1)} %bitcast.118), kind=kOutput, calls=%fused_computation.154 | convolution fusion | flops 2684354560 | bytes 14155776 | tf_op jit(solution)/shard_map/dot_general | solution.py:26
  91.5 21.1 %share_keys.1.k_ref.v_ref.kv_ref = bf16[2,640,512]{2,1,0:T(8,128)(2,1)S(1)} custom-call(f32[256,2560]{1,0:T(8,128)S(1)} %fusion.54.rows_ref.q_ref.qkv_ref, f32[128,128]{1,0:T(8,128)S(1)} %get-tuple-element.133.cos_ref, f32[128,128]{1,0:T(8,128)S(1)} %get-tuple-element.134.sin_ref, f32[1,128]{1,0:T(1,128)S(1)} %broadcast_in_dim_reshape_squeeze.5.gk_ref), custom_call_target="tpu_custom_call" | custom-call | bytes 50000000 | tf_op jit(solution)/shard_map/share_keys/pallas_call | solution.py:1109
  112.6 1.0 copy-done.1
  113.7 6.9 %all-to-all-start = ((bf16[64,16,2048]{2,1,0:T(8,128)(2,1)}), bf16[64,16,2048]{2,1,0:T(8,128)(2,1)}, u32[]{:S(2)}, u32[]{:S(2)}) async-start(bf16[64,16,2048]{2,1,0:T(8,128)(2,1)} %bitcast.139), calls=%async_computation | async-start | bytes 8388608 | tf_op jit(solution)/shard_map/all_to_all | solution.py:1246
  121.1 1.3 copy-done.2
  122.4 0.8 copy-done.12
  123.3 15.1 %attention_forward.1.o_ref = bf16[256,2048]{1,0:T(8,128)(2,1)S(1)} custom-call(f32[256,2560]{1,0:T(8,128)S(1)} %fusion.54.rows_ref.q_ref.qkv_ref, f32[128,128]{1,0:T(8,128)S(1)} %get-tuple-element.133.cos_ref, f32[128,128]{1,0:T(8,128)S(1)} %copy-done.12, f32[1,128]{1,0:T(1,128)S(1)} %broadcast_in_dim_reshape_squeeze.4.gq_ref, ...), custom_call_target="tpu_custom_call" | custom-call | bytes 60000000 | tf_op jit(solution)/shard_map/attention_forward/pallas_call | solution.py:1138
  138.4 6.1 %fusion = f32[256,2048]{1,0:T(8,128)S(1)} fusion(bf16[256,2048]{1,0:T(8,128)(2,1)S(1)} %attention_forward.1.o_ref, bf16[2048,2176]{1,0:T(8,128)(2,1)} %bitcast.122), kind=kOutput, calls=%fused_computation | convolution fusion | flops 2147483648 | bytes 11534336 | tf_op jit(solution)/shard_map/dot_general | solution.py:26
  144.6 0.9 select_convert_fusion.1
  146.0 3.3 collective-permute-start
  149.8 1.6 maximum_convert_fusion
  151.3 29.2 %collective-permute-done = bf16[2,64,2048]{2,1,0:T(8,128)(2,1)S(1)} collective-permute-done((bf16[2,64,2048]{2,1,0:T(8,128)(2,1)}, bf16[2,64,2048]{2,1,0:T(8,128)(2,1)S(1)}, u32[]{:S(2)}, u32[]{:S(2)}) %collective-permute-start) | collective-permute-done | bytes 524320 | tf_op jit(solution)/shard_map/ppermute | solution.py:1217
  181.5 3.3 convolution_convert_fusion
  184.9 118.6 %experts.1 = (bf16[64,16,2048]{2,1,0:T(8,128)(2,1)}, bf16[64,16,2048]{2,1,0:T(8,128)(2,1)}, bf16[2048,768]{1,0:T(8,128)(2,1)}, bf16[384,2048]{1,0:T(8,128)(2,1)}) custom-call(bf16[64,16,2048]{2,1,0:T(8,128)(2,1)} %bitcast.117, bf16[64,16,2048]{2,1,0:T(8,128)(2,1)} %all-to-all-done.deo_ref, bf16[2048,384]{1,0:T(8,128)(2,1)} %bitcast.131, ...), custom_call_target="tpu_custom_call" | custom-call | bytes 400000000 | tf_op jit(solution)/shard_map/experts/pallas_call | solution.py:794
  303.4 3.2 multiply_reduce_fusion.1
  307.1 9.1 %collective-permute-start.1 = (bf16[2,64,2048]{2,1,0:T(8,128)(2,1)S(1)}, bf16[2,64,2048]{2,1,0:T(8,128)(2,1)}, u32[]{:S(2)}, u32[]{:S(2)}) collective-permute-start(bf16[2,64,2048]{2,1,0:T(8,128)(2,1)S(1)} %fusion.50), channel_id=1, source_target_pairs={{0,1},{1,0},{2,3},{3,2},{4,5},{5,4},{6,7},{7,6},{8,9},{9,8},{10,11... | collective-permute-start | bytes 1572872 | tf_op jit(solution)/shard_map/ppermute | solution.py:1217
  316.2 1.2 fusion.3.a_ref
  317.5 10.4 %collective-permute-done.1 = bf16[2,64,2048]{2,1,0:T(8,128)(2,1)} collective-permute-done((bf16[2,64,2048]{2,1,0:T(8,128)(2,1)S(1)}, bf16[2,64,2048]{2,1,0:T(8,128)(2,1)}, u32[]{:S(2)}, u32[]{:S(2)}) %collective-permute-start.1) | collective-permute-done | bytes 524320 | tf_op jit(solution)/shard_map/ppermute | solution.py:1217
  327.8 1.1 broadcast_select_fusion.1
  329.0 1.1 pad_maximum_fusion
  330.0 99.2 %attention_backward.1 = (f32[128,2048]{1,0:T(8,128)}, f32[2,128]{1,0:T(2,128)}, bf16[2048,2560]{1,0:T(8,128)(2,1)}, bf16[2048,2048]{1,0:T(8,128)(2,1)}, bf16[64,16,2048]{2,1,0:T(8,128)(2,1)}) custom-call(f32[256,2560]{1,0:T(8,128)} %copy-done, f32[128,128]{1,0:T(8,128)} %copy-done.10, f32[128,128]{1,0:T(8,128)} %copy-done.11, f32[1,128]{1,0:T(1,128)} %copy-done.18, ...), custom_call_target="tpu_custom_call" | custom-call | bytes 250000000 | tf_op jit(solution)/shard_map/attention_backward/pallas_call | solution.py:1164
  429.3 2.0 fusion.8
  431.9 3.4 fusion.55
  435.5 1.1 copy-done.22
  436.7 0.7 fusion.12
  438.1 90.4 %scatter_grads.1 = (f32[32,2560]{1,0:T(8,128)S(1)}, f32[32,2176]{1,0:T(8,128)S(1)}, bf16[2048,768]{1,0:T(8,128)(2,1)S(1)}, bf16[384,2048]{1,0:T(8,128)(2,1)S(1)}...) custom-call(bf16[4,2,4,2,32,2560]{5,4,3,2,1,0:T(8,128)(2,1)} %bitcast.120, ...), custom_call_target="tpu_custom_call" | custom-call | bytes 250000000 | tf_op jit(solution)/shard_map/scatter_grads/pallas_call | solution.py:522
  528.5 0.9 select_bitcast_fusion
  529.4 0.8 fusion.14
  530.2 0.8 select_bitcast_fusion.1
  531.0 0.8 fusion.15
  531.8 0.7 slice.100
  533.2 0.7 slice.103
  535.0 1.9 bitcast_convert_fusion
  536.8 1.2 copy-done.21
  538.4 3.1 slice_bitcast_fusion
  (117 shorter events, 10.1 us)
Async XLA Ops:
  5.7 0.9 copy-start.13
  6.6 0.9 copy-start.14
  7.5 0.7 copy-start.15
  8.2 0.7 copy-start.16
  8.9 75.6 %copy-start.33 = (bf16[2,1,56,2048]{3,2,1,0:T(8,128)(2,1)S(1)}, bf16[2,1,56,2048]{3,2,1,0:T(8,128)(2,1)}, u32[]{:S(2)}) copy-start(bf16[2,1,56,2048]{3,2,1,0:T(8,128)(2,1)} %param.20) | copy-start | bytes 1376260
  79.4 0.7 copy-start.6
  80.1 1.2 copy-start.8
  81.3 1.2 copy-start.9
  82.4 0.8 copy-start.19
  83.2 1.4 copy-start.24
  84.6 0.8 copy-start.26
  85.1 6.5 %copy-start.17 = (f32[1,128]{1,0:T(1,128)}, f32[1,128]{1,0:T(1,128)S(1)}, u32[]{:S(2)}) copy-start(f32[1,128]{1,0:T(1,128)S(1)} %broadcast_in_dim_reshape_squeeze.5.gk_ref) | copy-start | bytes 1540
  91.0 30.1 %copy-start = (f32[256,2560]{1,0:T(8,128)}, f32[256,2560]{1,0:T(8,128)S(1)}, u32[]{:S(2)}) copy-start(f32[256,2560]{1,0:T(8,128)S(1)} %fusion.54.rows_ref.q_ref.qkv_ref) | copy-start | bytes 7864324
  91.5 22.2 %copy-start.11 = (f32[128,128]{1,0:T(8,128)}, f32[128,128]{1,0:T(8,128)S(1)}, u32[]{:S(2)}) copy-start(f32[128,128]{1,0:T(8,128)S(1)} %get-tuple-element.134.sin_ref) | copy-start | bytes 196612
  91.5 29.6 %copy-start.10 = (f32[128,128]{1,0:T(8,128)}, f32[128,128]{1,0:T(8,128)S(1)}, u32[]{:S(2)}) copy-start(f32[128,128]{1,0:T(8,128)S(1)} %get-tuple-element.133.cos_ref) | copy-start | bytes 196612
  112.6 1.1 copy-start.1
  113.7 71.2 %all-to-all-start = ((bf16[64,16,2048]{2,1,0:T(8,128)(2,1)}), bf16[64,16,2048]{2,1,0:T(8,128)(2,1)}, u32[]{:S(2)}, u32[]{:S(2)}) async-start(bf16[64,16,2048]{2,1,0:T(8,128)(2,1)} %bitcast.139), calls=%async_computation | async-start | bytes 8388608 | tf_op jit(solution)/shard_map/all_to_all | solution.py:1246
  120.8 17.6 %copy-start.18 = (f32[1,128]{1,0:T(1,128)}, f32[1,128]{1,0:T(1,128)S(1)}, u32[]{:S(2)}) copy-start(f32[1,128]{1,0:T(1,128)S(1)} %broadcast_in_dim_reshape_squeeze.4.gq_ref) | copy-start | bytes 1540
  121.1 1.3 copy-start.2
  122.4 0.8 copy-start.12
  123.3 15.1 %copy-start.5 = (f32[128,640]{1,0:T(8,128)}, f32[128,640]{1,0:T(8,128)S(1)}, u32[]{:S(2)}) copy-start(f32[128,640]{1,0:T(8,128)S(1)} %select_select_fusion.bias_ref) | copy-start | bytes 983044
  138.4 6.2 %copy-start.4 = (bf16[256,2048]{1,0:T(8,128)(2,1)}, bf16[256,2048]{1,0:T(8,128)(2,1)S(1)}, u32[]{:S(2)}) copy-start(bf16[256,2048]{1,0:T(8,128)(2,1)S(1)} %attention_forward.1.o_ref) | copy-start | bytes 3145732
  138.4 11.0 %copy-start.25 = (bf16[2,1,64,2048]{3,2,1,0:T(8,128)(2,1)S(1)}, bf16[2,1,64,2048]{3,2,1,0:T(8,128)(2,1)}, u32[]{:S(2)}) copy-start(bf16[2,1,64,2048]{3,2,1,0:T(8,128)(2,1)} %param.21) | copy-start | bytes 1572868
  138.4 11.0 %copy-start.34 = (bf16[2,1,56,2048]{3,2,1,0:T(8,128)(2,1)S(1)}, bf16[2,1,56,2048]{3,2,1,0:T(8,128)(2,1)}, u32[]{:S(2)}) copy-start(bf16[2,1,56,2048]{3,2,1,0:T(8,128)(2,1)} %param.20) | copy-start | bytes 1376260
  144.5 1.5 copy-start.31
  144.6 5.2 copy-start.27
  146.0 34.5 %collective-permute-start = (bf16[2,64,2048]{2,1,0:T(8,128)(2,1)}, bf16[2,64,2048]{2,1,0:T(8,128)(2,1)S(1)}, u32[]{:S(2)}, u32[]{:S(2)}) collective-permute-start(bf16[2,64,2048]{2,1,0:T(8,128)(2,1)} %select_convert_fusion.1), channel_id=1, source_target_pairs={{0,1},{1,0},{2,3},{3,2},{4,5},{5,4},{6,7},{7,6},{8,9},{9,8},{10,11... | collective-permute-start | bytes 1572872 | tf_op jit(solution)/shard_map/ppermute | solution.py:1217
  149.7 31.3 %copy-start.28 = (bf16[2,64,2048]{2,1,0:T(8,128)(2,1)}, bf16[2,64,2048]{2,1,0:T(8,128)(2,1)S(1)}, u32[]{:S(2)}) copy-start(bf16[2,64,2048]{2,1,0:T(8,128)(2,1)S(1)} %get-tuple-element.102) | copy-start | bytes 1572868
  149.7 30.8 %copy-start.32 = (f32[256,2048]{1,0:T(8,128)S(1)}, f32[256,2048]{1,0:T(8,128)}, u32[]{:S(2)}) copy-start(f32[256,2048]{1,0:T(8,128)} %copy-done.31) | copy-start | bytes 6291460
  180.6 1.0 copy-start.7
  306.7 9.5 %copy-start.23 = (f32[2,128,2048]{2,1,0:T(8,128)S(1)}, f32[2,128,2048]{2,1,0:T(8,128)}, u32[]{:S(2)}) copy-start(f32[2,128,2048]{2,1,0:T(8,128)} %maximum_convert_fusion) | copy-start | bytes 6291460
  307.1 20.8 %collective-permute-start.1 = (bf16[2,64,2048]{2,1,0:T(8,128)(2,1)S(1)}, bf16[2,64,2048]{2,1,0:T(8,128)(2,1)}, u32[]{:S(2)}, u32[]{:S(2)}) collective-permute-start(bf16[2,64,2048]{2,1,0:T(8,128)(2,1)S(1)} %fusion.50), channel_id=1, source_target_pairs={{0,1},{1,0},{2,3},{3,2},{4,5},{5,4},{6,7},{7,6},{8,9},{9,8},{10,11... | collective-permute-start | bytes 1572872 | tf_op jit(solution)/shard_map/ppermute | solution.py:1217
  330.0 99.2 %copy-start.29 = (bf16[2,64,2048]{2,1,0:T(8,128)(2,1)S(1)}, bf16[2,64,2048]{2,1,0:T(8,128)(2,1)}, u32[]{:S(2)}) copy-start(bf16[2,64,2048]{2,1,0:T(8,128)(2,1)} %copy-done.28) | copy-start | bytes 1572868
  429.3 2.1 copy-start.35
  429.3 2.6 copy-start.20
  435.4 1.2 copy-start.22
  435.4 1.3 copy-start.30
  436.7 1.4 copy-start.3
  535.0 3.0 copy-start.21

commit v7 on v6

--- a/solution.py
+++ b/solution.py
@@ -104,8 +104,7 @@
     place = (j & (places - 1)).astype(F32)
     mine = ((j & places) != 0) == later
     there = jnp.logical_and(dot(rank, spread, ((1,), (0,))) == place, mine)
-    if select_ref is not None:
-        select_ref[...] = jnp.where(there, 1.0, 0.0).astype(BF16)
+    select_ref[...] = jnp.where(there, 1.0, 0.0).astype(BF16)
     high = weight.astype(BF16)
     low = (weight - high.astype(F32)).astype(BF16)
     mix_ref[0:tokens, :] = jnp.where(there, dot(high, spread, ((1,), (0,))), 0.0).astype(BF16)
@@ -116,7 +115,7 @@
     query_ref, key_ref, value_ref, out_ref, extra_ref, ids_ref, gates_ref, experts_ref, cot_ref,
     gate_ref, up_ref, down_ref,
     a_all, b_all, gate_all, up_all, down_all, near_ref, mix_ref, rows_ref,
-    a_own, b_own, mix, rows, rows_sem, local_sem, send_sem, recv_sem, away_sem, home_sem, give_sem, take_sem,
+    a_own, b_own, rows, rows_sem, local_sem, send_sem, recv_sem, away_sem, home_sem, give_sem, take_sem,
 ):
     y, core, z, x = place()
     for own, refs in ((a_own, (query_ref, key_ref, value_ref)), (b_own, (out_ref, extra_ref))):
@@ -188,8 +187,7 @@
         started.append(copy)
     size = rows.shape[0] // (RING * RING * RING)
     ids, gates = ids_ref[...], gates_ref[...]
-    route(ids, gates, experts_ref[0:1, :], size, None, mix)
-    route(ids, gates, experts_ref[1:2, :], size, near_ref, mix_ref)
+    route(ids, gates, experts_ref[...], size, near_ref, mix_ref)
     for n in (0, 1):
         i, j = me[n]
         locals_[n].wait()
@@ -208,8 +206,8 @@
     part, tokens = 256, cot_ref.shape[0]
     for at in range(0, rows.shape[0], part):
         lanes = slice(at, at + part)
-        total = dot(mix[0:tokens, lanes], cot_ref[...], ((0,), (0,)))
-        total = total + dot(mix[tokens:, lanes], cot_ref[...], ((0,), (0,)))
+        total = dot(mix_ref[0:tokens, lanes], cot_ref[...], ((0,), (0,)))
+        total = total + dot(mix_ref[tokens:, lanes], cot_ref[...], ((0,), (0,)))
         rows[lanes, :] = total.astype(BF16)
     keep_rows = pltpu.make_async_copy(rows, rows_ref, rows_sem)
     keep_rows.start()
@@ -276,7 +274,6 @@
         + [jax.ShapeDtypeStruct(v.shape, v.dtype) for v in (gate, up, down)]
         + routing + [jax.ShapeDtypeStruct((slots, width), BF16)],
         scratch_shapes=[pltpu.VMEM((rows, c), query.dtype) for c in cols] + [
-            pltpu.VMEM((2 * tokens, slots), BF16),
             pltpu.VMEM((slots, width), BF16),
             pltpu.SemaphoreType.DMA,
             pltpu.SemaphoreType.DMA((2,)),
@@ -569,11 +566,6 @@
     return {"fsdp": y * 2 + core, "ctx": z * 2 + lax.rem(x, 2), "tp": lax.div(x, 2)}
 
 
-def chip_number(slot, sign):
-    y, z, x = chip_at(slot, sign)
-    return (y * 2 * RING + z * 2 + lax.rem(x, 2)) * 2 + lax.div(x, 2)
-
-
 def other_core():
     f = lax.axis_index("fsdp")
     return {"fsdp": f + 1 - 2 * (f % 2)}
@@ -624,7 +616,7 @@
 
     def load(s):
         return pltpu.make_async_copy(
-            deo_ref.at[chip_number(s, -1)], deos.at[0, slot_rows(s)], load_sem.at[s]
+            deo_ref.at[s], deos.at[0, slot_rows(s)], load_sem.at[s]
         )
 
     def sent_rows(n, s):
@@ -854,19 +846,88 @@
     return e / jnp.sum(e, axis=-1, keepdims=True)
 
 
-def share_kernel(kv, rows_ref, cos_ref, sin_ref, gk_ref, kv_ref, held, send_sem, recv_sem):
-    c = lax.axis_index("ctx")
-    greet([ctx_peer(step) for step in range(1, CTX)])
+def each(body, low, high):
+    def step(i, carry):
+        body(i)
+        return carry
+
+    lax.fori_loop(low, high, step, 0)
+
+
+def greet_chips():
+    barrier = pltpu.get_barrier_semaphore()
+    each(
+        lambda s: pl.semaphore_signal(
+            barrier, inc=1, device_id=device_at(s, 1), device_id_type=MESH
+        ),
+        1, CHIPS,
+    )
+    return lambda: pl.semaphore_wait(barrier, CHIPS - 1)
+
+
+def tile(i):
+    return pl.ds(pl.multiple_of(i * WIDE, WIDE), WIDE)
+
+
+def head_cols(h):
+    return pl.ds(pl.multiple_of(h * HEAD_SIZE, HEAD_SIZE), HEAD_SIZE)
+
+
+def forward_kernel(
+    kv, heads, tokens_ref, gain_in_ref, gain_moe_ref, cos_ref, sin_ref, gq_ref, gk_ref, bias_ref,
+    select_ref, w_qkv_ref, w_out_ref, rows_ref,
+    a_ref, qkv_ref, kv_ref, o_ref, middle_ref, send_ref, came_ref,
+    w_qkv, w_out, held, part_sum, swap_give, swap_take, send_rows,
+    send_sem, recv_sem, load_sem, swap_sem, out_sem, go_sem, come_sem,
+):
+    c, tp = lax.axis_index("ctx"), lax.axis_index("tp")
     micro, rows = held.shape[0], 2 * BLOCK
-    cosine, sine, gk = cos_ref[...], sin_ref[...], gk_ref[...]
+    q_cols = kv * heads * HEAD_SIZE
+    width = w_out.shape[0]
+    entered = greet_chips()
+    loads = [
+        pltpu.make_async_copy(w_qkv_ref, w_qkv, load_sem.at[0]),
+        pltpu.make_async_copy(w_out_ref.at[:, pl.ds(0, w_out.shape[1])], w_out, load_sem.at[1]),
+    ]
+    for copy in loads:
+        copy.start()
+
+    def go(s):
+        return remote(
+            rows_ref.at[s], came_ref.at[s], go_sem.at[s], come_sem.at[s], device_at(s, 1)
+        )
+
+    def rows_out(quarter):
+        each(lambda s: go(s).start(), max(quarter * GROUP, 1), (quarter + 1) * GROUP)
+
+    stay = pltpu.make_async_copy(rows_ref.at[0], came_ref.at[0], come_sem.at[0])
+    stay.start()
+    cosine, sine, gq, gk = cos_ref[...], sin_ref[...], gq_ref[...], gk_ref[...]
     mine = pl.ds(pl.multiple_of(c * BLOCK, BLOCK), BLOCK)
     earlier, own = pl.ds(CTX * BLOCK, BLOCK), pl.ds((CTX + 1) * BLOCK, BLOCK)
+
+    def block(i):
+        return pl.ds(pl.multiple_of(i * BLOCK, BLOCK), BLOCK)
+
+    def norm_in(i):
+        u = tokens_ref[block(i), :].astype(F32)
+        scaling = lax.rsqrt(jnp.mean(u * u, axis=-1, keepdims=True) + EPS)
+        a_ref[block(i), :] = (u * scaling * gain_in_ref[...]).astype(BF16)
+
+    each(norm_in, 0, micro * 2)
+    loads[0].wait()
+
+    def project(i):
+        qkv_ref[:, tile(i)] = dot(a_ref[...], w_qkv[:, tile(i)], ((1,), (0,)))
+
+    each(project, q_cols // WIDE, w_qkv.shape[1] // WIDE)
+    entered()
     copies = []
     for m in range(micro):
         span = slice(m * rows, (m + 1) * rows)
         for h in range(2 * kv):
             cols = slice(h * HEAD_SIZE, (h + 1) * HEAD_SIZE)
-            u = rows_ref[span, cols]
+            u = qkv_ref[span, q_cols + h * HEAD_SIZE : q_cols + (h + 1) * HEAD_SIZE]
             low = rotated(u, gk, cosine, sine)[0] if h < kv else u.astype(BF16)
             held[m, mine, cols] = low[:BLOCK]
             held[m, own, cols] = low[BLOCK:]
@@ -882,7 +943,20 @@
         )
         for copy in copies[-CTX:]:
             copy.start()
-    for m in range(micro):
+    rows_out(0)
+    each(project, 0, q_cols // WIDE)
+
+    def group(m, h, carry):
+        span = slice(m * rows, (m + 1) * rows)
+        k, v = held[m, :, head_cols(h)], held[m, :, head_cols(kv + h)]
+        for e in range(heads):
+            cols = head_cols(h * heads + e)
+            q_low = rotated(qkv_ref[span, cols], gq, cosine, sine)[0]
+            p = softmax_parts(q_low, k, bias_ref[...]).astype(BF16)
+            o_ref[span, cols] = dot(p, v, ((1,), (0,))).astype(BF16)
+        return carry
+
+    def arrived(m):
         for step in range(1, CTX):
             source = lax.rem(c + CTX - step, CTX)
             part = held.at[m, pl.ds(pl.multiple_of(source * BLOCK, BLOCK), BLOCK)]
@@ -890,18 +964,47 @@
                 part, part, send_sem.at[step, m], recv_sem.at[step, m], ctx_peer(step)
             ).wait_recv()
         copies[(m + 1) * CTX - 1].wait_recv()
+
+    for m in range(micro):
+        arrived(m)
+        if m == micro - 1:
+            for quarter in range(1, CHIPS // GROUP):
+                rows_out(quarter)
+        lax.fori_loop(0, kv, functools.partial(group, m), 0)
         kv_ref[m] = held[m]
+    loads[1].wait()
+
+    def join(i):
+        part_sum[:, tile(i)] = dot(o_ref[...], w_out[tile(i), :], ((1,), (1,)))
+
+    each(join, 0, width // WIDE)
+    for m in range(micro):
+        away = pl.ds(pl.multiple_of(m * rows + tp * BLOCK, BLOCK), BLOCK)
+        swap_give[m * BLOCK : (m + 1) * BLOCK, :] = part_sum[away, :].astype(BF16)
+    swap = remote(swap_give, swap_take, swap_sem.at[0], swap_sem.at[1], {"tp": 1 - tp})
+    swap.start()
+    swap.wait()
+    for m in range(micro):
+        kept = pl.ds(pl.multiple_of(m * rows + (1 - tp) * BLOCK, BLOCK), BLOCK)
+        span = slice(m * BLOCK, (m + 1) * BLOCK)
+        total = part_sum[kept, :] + swap_take[span, :].astype(F32)
+        u = tokens_ref[kept, :].astype(F32) + total
+        middle_ref[span, :] = u
+        scaling = lax.rsqrt(jnp.mean(u * u, axis=-1, keepdims=True) + EPS)
+        swap_give[span, :] = (u * scaling * gain_moe_ref[...]).astype(BF16)
+
+    def pick(i):
+        value = dot(select_ref[:, tile(i)], swap_give[...], ((0,), (0,)))
+        send_rows[tile(i), :] = value.astype(BF16)
+
+    each(pick, 0, send_rows.shape[0] // WIDE)
+    out = pltpu.make_async_copy(send_rows, send_ref, out_sem)
+    out.start()
+    out.wait()
+    stay.wait()
     for copy in copies:
         copy.wait_send()
-
-
-def attention_kernel(heads, q_ref, cos_ref, sin_ref, gq_ref, bias_ref, k_ref, v_ref, o_ref):
-    cosine, sine, gq = cos_ref[...], sin_ref[...], gq_ref[...]
-    for e in range(heads):
-        cols = slice(e * HEAD_SIZE, (e + 1) * HEAD_SIZE)
-        q_low = rotated(q_ref[:, cols], gq, cosine, sine)[0]
-        p = softmax_parts(q_low, k_ref[...], bias_ref[...]).astype(BF16)
-        o_ref[:, cols] = dot(p, v_ref[...], ((1,), (0,))).astype(BF16)
+    each(lambda s: go(s).wait(), 1, CHIPS)
 
 
 def backward_kernel(
@@ -915,27 +1018,14 @@
     c, tp = lax.axis_index("ctx"), lax.axis_index("tp")
     width = w_out.shape[0]
 
-    def each(body, low, high):
-        def step(i, carry):
-            body(i)
-            return carry
-
-        lax.fori_loop(low, high, step, 0)
-
-    barrier = pltpu.get_barrier_semaphore()
-    each(
-        lambda s: pl.semaphore_signal(
-            barrier, inc=1, device_id=device_at(s, 1), device_id_type=MESH
-        ),
-        1, CHIPS,
-    )
+    entered = greet_chips()
     loads = [
         pltpu.make_async_copy(w_out_ref.at[:, pl.ds(0, w_out.shape[1])], w_out, load_sem.at[0]),
         pltpu.make_async_copy(w_qkv_ref, w_qkv, load_sem.at[1]),
     ]
     for copy in loads:
         copy.start()
-    pl.semaphore_wait(barrier, CHIPS - 1)
+    entered()
 
     def output(s):
         return remote(
@@ -955,18 +1045,12 @@
     mine = pl.ds(pl.multiple_of(c * BLOCK, BLOCK), BLOCK)
     earlier, own = pl.ds(CTX * BLOCK, BLOCK), pl.ds((CTX + 1) * BLOCK, BLOCK)
 
-    def tile(i):
-        return pl.ds(pl.multiple_of(i * WIDE, WIDE), WIDE)
-
     loads[0].wait()
 
     def outputs_back(i):
         do_ref[:, tile(i)] = dot(dattn_ref[...], w_out[:, tile(i)], ((1,), (0,))).astype(BF16)
 
     each(outputs_back, 0, w_out.shape[1] // WIDE)
-
-    def head_cols(h):
-        return pl.ds(pl.multiple_of(h * HEAD_SIZE, HEAD_SIZE), HEAD_SIZE)
 
     def keys_back(m, h, carry):
         span = slice(m * rows, (m + 1) * rows)
@@ -1099,57 +1183,45 @@
     each(lambda s: output(s).wait(), 1, CHIPS)
 
 
-def share_keys(qkv, cosine, sine, gain_key, kv, keys, micro):
-    rows, cols = qkv.shape[0], 2 * kv * HEAD_SIZE
-    last = qkv.shape[1] // cols - 1
-
-    def whole(shape):
-        return pl.BlockSpec(shape, lambda i: (0,) * len(shape))
-
+def forward(tokens, gain_in, gain_moe, heads_in, select, w_qkv, w_out, moe_rows, kv):
+    total, width = tokens.shape
+    cols = w_qkv.shape[1]
+    heads = cols // HEAD_SIZE // kv - 2
+    q_cols, kv_cols = kv * heads * HEAD_SIZE, 2 * kv * HEAD_SIZE
+    rows, keys = heads_in[-1].shape
+    micro = total // rows
+    vmem, any_space = (pl.BlockSpec(memory_space=space) for space in (pltpu.VMEM, pl.ANY))
+    dma = pltpu.SemaphoreType.DMA
     return pl.pallas_call(
-        functools.partial(share_kernel, kv),
-        grid=(1,),
-        in_specs=[pl.BlockSpec((rows, cols), lambda i: (0, last)), whole(cosine.shape)]
-        + [whole(sine.shape), whole(gain_key.shape)],
-        out_specs=whole((micro, keys, cols)),
-        out_shape=jax.ShapeDtypeStruct((micro, keys, cols), BF16),
+        functools.partial(forward_kernel, kv, heads),
+        in_specs=[vmem] * 9 + [any_space] * 3,
+        out_specs=[vmem] * 5 + [any_space] * 2,
+        out_shape=[
+            jax.ShapeDtypeStruct((total, width), BF16),
+            jax.ShapeDtypeStruct((total, cols), F32),
+            jax.ShapeDtypeStruct((micro, keys, kv_cols), BF16),
+            jax.ShapeDtypeStruct((total, q_cols), BF16),
+            jax.ShapeDtypeStruct((micro * BLOCK, width), F32),
+            jax.ShapeDtypeStruct((select.shape[1], width), BF16),
+            jax.ShapeDtypeStruct(moe_rows.shape, BF16),
+        ],
         scratch_shapes=[
-            pltpu.VMEM((micro, keys, cols), BF16),
-            pltpu.SemaphoreType.DMA((CTX, micro)),
-            pltpu.SemaphoreType.DMA((CTX, micro)),
+            pltpu.VMEM((width, cols), BF16),
+            pltpu.VMEM((width, q_cols), BF16),
+            pltpu.VMEM((micro, keys, kv_cols), BF16),
+            pltpu.VMEM((total, width), F32),
+            pltpu.VMEM((micro * BLOCK, width), BF16),
+            pltpu.VMEM((micro * BLOCK, width), BF16),
+            pltpu.VMEM((select.shape[1], width), BF16),
+            dma((CTX, micro)), dma((CTX, micro)), dma((2,)), dma((2,)), dma,
+            dma((CHIPS,)), dma((CHIPS,)),
         ],
         compiler_params=pltpu.CompilerParams(
-            collective_id=2, has_side_effects=True, vmem_limit_bytes=VMEM_LIMIT
+            collective_id=2, has_side_effects=True, vmem_limit_bytes=56 * 1024 * 1024
         ),
-        cost_estimate=pl.CostEstimate(flops=0, bytes_accessed=50_000_000, transcendentals=0),
-        name="share_keys",
-    )(qkv, cosine, sine, gain_key)
-
-
-def attention(qkv, cosine, sine, gain_query, bias, kv_all, kv):
-    micro, keys, cols = kv_all.shape
-    rows = bias.shape[0]
-    heads = qkv.shape[1] // HEAD_SIZE // kv - 2
-    width = heads * HEAD_SIZE
-
-    def whole(v):
-        return pl.BlockSpec(v.shape, lambda m, g: (0,) * v.ndim)
-
-    return pl.pallas_call(
-        functools.partial(attention_kernel, heads),
-        grid=(micro, kv),
-        in_specs=[pl.BlockSpec((rows, width), lambda m, g: (m, g))]
-        + [whole(v) for v in (cosine, sine, gain_query, bias)]
-        + [
-            pl.BlockSpec((None, keys, HEAD_SIZE), lambda m, g: (m, 0, g)),
-            pl.BlockSpec((None, keys, HEAD_SIZE), lambda m, g: (m, 0, kv + g)),
-        ],
-        out_specs=pl.BlockSpec((rows, width), lambda m, g: (m, g)),
-        out_shape=jax.ShapeDtypeStruct((micro * rows, kv * width), BF16),
-        compiler_params=pltpu.CompilerParams(vmem_limit_bytes=VMEM_LIMIT),
-        cost_estimate=pl.CostEstimate(flops=0, bytes_accessed=60_000_000, transcendentals=0),
+        cost_estimate=pl.CostEstimate(flops=0, bytes_accessed=250_000_000, transcendentals=0),
         name="attention_forward",
-    )(qkv, cosine, sine, gain_query, bias, kv_all, kv_all)
+    )(tokens, gain_in, gain_moe, *heads_in, select, w_qkv, w_out, moe_rows)
 
 
 def backward(qkv, heads_in, kv_all, d_attn, o, a, w_out, w_qkv, eo, kv):
@@ -1200,11 +1272,6 @@
     )(qkv, *heads_in, kv_all, d_attn, o, a, w_out, w_qkv, eo)
 
 
-def normalize(rows, gain):
-    scaling = lax.rsqrt(jnp.mean(rows * rows, axis=-1, keepdims=True) + EPS)
-    return rows * scaling * gain, scaling
-
-
 def normalize_back(rows, scaling, gain, upstream):
     normed = rows * scaling
     gain_grad = jnp.sum((upstream * normed).reshape(-1, rows.shape[-1]), axis=0)
@@ -1237,17 +1304,6 @@
     hidden = expert_gate.shape[2]
     slots = cont_rows * TOPK // peers
 
-    fsdp, tp = lax.axis_size("fsdp"), lax.axis_size("tp")
-    chips = [(2 * y, c, t) for y in range(fsdp // 2) for c in range(ctx) for t in range(tp)]
-    groups = [[((f + core) * ctx + c) * tp + t for f, c, t in chips] for core in range(2)]
-    expert_of = jnp.array([(f + t) * ctx + c for f, c, t in chips], jnp.int32)
-
-    def exchange(rows_of):
-        return lax.all_to_all(
-            rows_of, ("fsdp", "ctx", "tp"), split_axis=0, concat_axis=0, tiled=True,
-            axis_index_groups=groups,
-        )
-
     def pad(v):
         return jnp.pad(v[:, 0], ((0, 0), (0, block - prompt_rows), (0, 0)))
 
@@ -1262,7 +1318,7 @@
 
     y, z, x = chip_at(jnp.arange(peers, dtype=jnp.int32), 1)
     near = (2 * y + x // 2) * ctx + 2 * z + x % 2
-    order = jnp.pad(jnp.stack([expert_of, near]), ((0, 0), (0, HEAD_SIZE - peers)), constant_values=-2)
+    order = jnp.pad(near, (0, HEAD_SIZE - peers), constant_values=-2)[None]
 
     def lanes(v):
         return jnp.pad(v, [(0, 0)] * (v.ndim - 1) + [(0, HEAD_SIZE - v.shape[-1])])
@@ -1276,7 +1332,6 @@
         own_cot.reshape(-1, width), peers * micro * slots, *own_experts,
     )
     select_near, mixing, spread = routing
-    w_out = w_out_extra[:, :q_cols]
     gains = w_out_extra[:, q_cols:].reshape(peers, shard_rows, HEAD_SIZE)[:, :4].astype(F32)
     gain_in, gain_moe = (gains[:, n, :shard_rows].reshape(-1) for n in (0, 1))
     head_rows = query_gain.shape[0]
@@ -1316,28 +1371,18 @@
     def arranged(own, other):
         return jnp.where(first, other, own), jnp.where(first, own, other)
 
-    def sum_own(part):
-        part = part.reshape(micro, rows, width)
-        given = jnp.where(first, part[:, :block], part[:, block:]).astype(BF16)
-        kept = jnp.where(first, part[:, block:], part[:, :block])
-        return kept + swap_tp(given).astype(F32)
-
-    tokens = jnp.concatenate([x_first, x_second], axis=1).astype(F32).reshape(-1, width)
-    a = normalize(tokens, gain_in)[0].astype(BF16)
-    qkv = dot(a, w_qkv, ((1,), (0,)))
     heads_in = (cosine, sine, gain_query[None], gain_key[None], bias)
-    kv_all = share_keys(qkv, cosine, sine, gain_key[None], kv, keys, micro)
-
-    spread, kv_all = lax.optimization_barrier((spread, kv_all))
-    d_eo_rows = exchange(spread).reshape(peers, micro * slots, width)
-    o = attention(qkv, cosine, sine, gain_query[None], bias, kv_all, kv)
-    middle = own_tokens + sum_own(dot(o, w_out, ((1,), (1,))))
-    b_normed, b_scale = normalize(middle, gain_moe)
-    b_low = b_normed.astype(BF16)
-
-    send = dot(select_near, b_low.reshape(-1, width), ((0,), (0,))).astype(BF16)
+    tokens = jnp.concatenate([x_first, x_second], axis=1).reshape(-1, width)
+    slot_shape = (peers, micro * slots, width)
+    a, qkv, kv_all, o, middle, send, d_eo_rows = forward(
+        tokens, gain_in[None], gain_moe[None], heads_in, select_near, w_qkv, w_out_extra,
+        spread.reshape(slot_shape), kv,
+    )
+    middle = middle.reshape(own_tokens.shape)
+    b_scale = lax.rsqrt(jnp.mean(middle * middle, axis=-1, keepdims=True) + EPS)
+
     back, eo, wide_here, tall_here = moe(
-        send.reshape(d_eo_rows.shape), d_eo_rows, own_experts, far_experts
+        send.reshape(slot_shape), d_eo_rows, own_experts, far_experts
     )
     d_b = dot(select_near, back.reshape(-1, width), ((1,), (0,))).reshape(middle.shape)
     middle_from, moe_total = normalize_back(middle, b_scale, gain_moe, d_b)

time: 546 us -> 550 us (level)
  Pallas kernels: 415 us -> 472 us
  waiting for transfers between devices: 39.6 us -> 10.4 us
  matrix products: 21.8 us -> 6.77 us
  starting transfers between devices: 19.4 us -> 9.12 us
    pallas_call x2 -> x1, Pallas kernels: 36.1 us -> 99.4 us  [forward(): pl.pallas_call(functools.partial(forward_kernel, kv, heads), in_specs=[vm...]
    ppermute x2 -> x1, waiting for transfers between devices: 39.6 us -> 10.4 us  [swap_tp(): return lax.ppermute(value, 'tp', [(0, 1), (1, 0)])]
    dot_general x5 -> x2, matrix products: 21.8 us -> 6.77 us  [dot(): return lax.dot_general(a, b, (dims, ((), ())), preferred_element_type=F32)]
    pallas_call x1, Pallas kernels: 99.2 us -> 90.5 us  [backward(): pl.pallas_call(functools.partial(backward_kernel, kv, heads), in_specs=[v...]
    all_to_all x1 -> x0, starting transfers between devices: 6.94 us -> none  [exchange(): lax.all_to_all(rows_of, ('fsdp', 'ctx', 'tp'), split_axis=0, concat_axis=...]
    unnamed x73 -> x33, local copies, waits for them, and re-layouts: 14.4 us -> 9.34 us
    ppermute x2 -> x1, starting transfers between devices: 12.5 us -> 9.12 us  [swap_tp(): return lax.ppermute(value, 'tp', [(0, 1), (1, 0)])]
  transfers between devices with their start and end apart: 3 -> 1, of which waited for: 2 -> 1; matrix products, arithmetic and copies ran while one was open for 3% -> 0% of each run, Pallas kernels for 3% -> 0%
where the time goes in v7:
time: 550 us; the launch traced here: 543 us
  Pallas kernels  472 us (86%)
  other arithmetic  22 us (4%)
  local copies, waits for them, and re-layouts  21.7 us (4%)
  waiting for transfers between devices  10.4 us (2%)
  starting transfers between devices  9.12 us (2%)
  matrix products  6.77 us (1%)
    pallas_call x1, Pallas kernels, moe(): pl.pallas_call(moe_kernel, in_specs=[any_space] * 8, out_specs=[any_space...  123 us
    pallas_call x1, Pallas kernels, forward(): pl.pallas_call(functools.partial(forward_kernel, kv, heads), in_specs=[vm...  99.4 us
    pallas_call x1, Pallas kernels, backward(): pl.pallas_call(functools.partial(backward_kernel, kv, heads), in_specs=[v...  90.5 us
    pallas_call x1, Pallas kernels, scatter_grads(): pl.pallas_call(scatter_kernel, in_specs=[any_space] * 7, out_specs=[pl.Bl...  88.7 us
    pallas_call x1, Pallas kernels, gather_weights(): pl.pallas_call(gather_kernel, in_specs=[vmem] * 9 + [any_space] * 3, out_...  70.5 us
  transfers between devices with their start and end apart: 1, of which 1 were waited for; matrix products, arithmetic and copies ran while one was open for 0% of the time, Pallas kernels for 0%

profile of v7, /device:TPU:0, one launch (start us, length us, event | category | flops | bytes accessed | tf_op | source)
XLA Modules:
  0.0 543.1 jit_solution(9233799941966284006)
XLA Ops:
  0.7 0.7 bitcast_select_fusion.1
  1.5 0.7 bitcast_select_fusion.2
  2.3 1.3 bitcast_select_fusion
  3.7 0.7 pad_bitcast_fusion.5
  4.3 0.7 pad_bitcast_fusion.7
  5.0 0.9 copy-done.5
  5.9 0.9 copy-done.6
  6.8 0.7 copy-done.7
  7.6 0.7 copy-done.8
  8.3 70.5 %gather_weights.1 = (bf16[4,2,4,2,32,2560]{5,4,3,2,1,0:T(8,128)(2,1)}, bf16[4,2,4,2,32,2176]{5,4,3,2,1,0:T(8,128)(2,1)}, bf16[2048,384]{1,0:T(8,128)(2,1)S(1)}, ...) custom-call(bf16[32,2048]{1,0:T(8,128)(2,1)S(1)} %copy-done.5, ...), custom_call_target="tpu_custom_call" | custom-call | bytes 250000000 | tf_op jit(solution)/shard_map/gather_weights/pallas_call | solution.py:269
  78.8 1.1 copy-done.1
  79.9 1.1 copy-done.2
  81.0 0.7 copy-done.3
  81.7 1.1 slice.95
  82.9 0.7 broadcast_in_dim_reshape_squeeze.15.gain_moe_ref
  83.7 0.7 broadcast_in_dim_reshape_squeeze.14.gain_in_ref
  84.4 0.6 broadcast_in_dim_reshape_squeeze.16.gq_ref
  85.0 0.6 broadcast_in_dim_reshape_squeeze.17.gk_ref
  86.0 0.7 pad_maximum_fusion.2.cos_ref
  86.8 0.7 pad_maximum_fusion.3.sin_ref
  87.5 1.1 pad_maximum_fusion
  88.6 0.9 select_select_fusion.bias_ref
  89.5 99.4 %attention_forward.1 = (bf16[256,2048]{1,0:T(8,128)(2,1)}, f32[256,2560]{1,0:T(8,128)}, bf16[2,640,512]{2,1,0:T(8,128)(2,1)}, bf16[256,2048]{1,0:T(8,128)(2,1)},...) custom-call(bf16[256,2048]{1,0:T(8,128)(2,1)} %bitcast.133, ...), custom_call_target="tpu_custom_call" | custom-call | bytes 250000000 | tf_op jit(solution)/shard_map/attention_forward/pallas_call | solution.py:1195
  189.0 1.4 multiply_reduce_fusion.2
  190.5 122.7 %experts.1 = (bf16[64,16,2048]{2,1,0:T(8,128)(2,1)}, bf16[64,16,2048]{2,1,0:T(8,128)(2,1)}, bf16[2048,768]{1,0:T(8,128)(2,1)}, bf16[384,2048]{1,0:T(8,128)(2,1)}) custom-call(bf16[64,16,2048]{2,1,0:T(8,128)(2,1)} %bitcast.132, bf16[64,16,2048]{2,1,0:T(8,128)(2,1)} %get-tuple-element.53.deo_ref, bf16[2048,384]{1,0:T(8,128)(2,1)} %bitcast.127, ...), custom_call_target="tpu_custom_call" | custom-call | bytes 400000000 | tf_op jit(solution)/shard_map/experts/pallas_call | solution.py:786
  313.2 3.3 multiply_reduce_fusion
  316.6 1.1 fusion.45
  317.7 9.1 %collective-permute-start = (bf16[2,64,2048]{2,1,0:T(8,128)(2,1)}, bf16[2,64,2048]{2,1,0:T(8,128)(2,1)}, u32[]{:S(2)}, u32[]{:S(2)}) collective-permute-start(bf16[2,64,2048]{2,1,0:T(8,128)(2,1)} %fusion.45), channel_id=1, source_target_pairs={{0,1},{1,0},{2,3},{3,2},{4,5},{5,4},{6,7},{7,6},{8,9},{9,8},{10,11... | collective-permute-start | bytes 1572872 | tf_op jit(solution)/shard_map/ppermute | solution.py:1284
  327.0 1.5 fusion.9
  328.5 10.4 %collective-permute-done = bf16[2,64,2048]{2,1,0:T(8,128)(2,1)} collective-permute-done((bf16[2,64,2048]{2,1,0:T(8,128)(2,1)}, bf16[2,64,2048]{2,1,0:T(8,128)(2,1)}, u32[]{:S(2)}, u32[]{:S(2)}) %collective-permute-start) | collective-permute-done | bytes 524320 | tf_op jit(solution)/shard_map/ppermute | solution.py:1284
  338.9 1.3 broadcast_select_fusion.2
  340.1 1.1 pad_maximum_fusion.1
  341.2 90.5 %attention_backward.1 = (f32[128,2048]{1,0:T(8,128)}, f32[2,128]{1,0:T(2,128)}, bf16[2048,2560]{1,0:T(8,128)(2,1)}, bf16[2048,2048]{1,0:T(8,128)(2,1)}, bf16[64,16,2048]{2,1,0:T(8,128)(2,1)}) custom-call(f32[256,2560]{1,0:T(8,128)} %get-tuple-element.49.qkv_ref, f32[128,128]{1,0:T(8,128)} %pad_maximum_fusion.2.cos_ref, ...), custom_call_target="tpu_custom_call" | custom-call | bytes 250000000 | tf_op jit(solution)/shard_map/attention_backward/pallas_call | solution.py:1236
  431.7 1.9 fusion.4
  434.9 3.4 fusion.49
  438.5 1.1 copy-done.11
  439.7 0.7 fusion.8
  440.4 0.7 copy-done
  441.1 88.7 %scatter_grads.1 = (f32[32,2560]{1,0:T(8,128)S(1)}, f32[32,2176]{1,0:T(8,128)S(1)}, bf16[2048,768]{1,0:T(8,128)(2,1)S(1)}, bf16[384,2048]{1,0:T(8,128)(2,1)S(1)}...) custom-call(bf16[4,2,4,2,32,2560]{5,4,3,2,1,0:T(8,128)(2,1)} %bitcast.122, ...), custom_call_target="tpu_custom_call" | custom-call | bytes 250000000 | tf_op jit(solution)/shard_map/scatter_grads/pallas_call | solution.py:519
  529.8 0.9 select_bitcast_fusion
  530.7 0.8 fusion.10
  531.5 0.8 select_bitcast_fusion.1
  532.3 0.8 fusion.11
  533.2 0.7 slice.86
  534.5 0.7 slice.89
  536.3 1.9 bitcast_convert_fusion
  538.1 1.2 copy-done.10
  539.7 3.1 slice_bitcast_fusion
  (65 shorter events, 4.6 us)
Async XLA Ops:
  5.0 0.9 copy-start.5
  5.9 0.9 copy-start.6
  6.8 0.7 copy-start.7
  7.6 0.7 copy-start.8
  8.3 79.2 %copy-start.15 = (bf16[2,1,56,2048]{3,2,1,0:T(8,128)(2,1)S(1)}, bf16[2,1,56,2048]{3,2,1,0:T(8,128)(2,1)}, u32[]{:S(2)}) copy-start(bf16[2,1,56,2048]{3,2,1,0:T(8,128)(2,1)} %param.19) | copy-start | bytes 1376260
  8.3 79.3 %copy-start.14 = (bf16[2,1,64,2048]{3,2,1,0:T(8,128)(2,1)S(1)}, bf16[2,1,64,2048]{3,2,1,0:T(8,128)(2,1)}, u32[]{:S(2)}) copy-start(bf16[2,1,64,2048]{3,2,1,0:T(8,128)(2,1)} %param.20) | copy-start | bytes 1572868
  78.7 1.1 copy-start.1
  79.9 1.1 copy-start.2
  81.0 0.7 copy-start.3
  190.5 122.8 %copy-start.4 = (bf16[128,1024]{1,0:T(8,128)(2,1)S(1)}, bf16[128,1024]{1,0:T(8,128)(2,1)}, u32[]{:S(2)}) copy-start(bf16[128,1024]{1,0:T(8,128)(2,1)} %copy-done.3) | copy-start | bytes 786436
  190.5 122.8 %copy-start.9 = (f32[128,2048]{1,0:T(8,128)S(1)}, f32[128,2048]{1,0:T(8,128)}, u32[]{:S(2)}) copy-start(f32[128,2048]{1,0:T(8,128)} %get-tuple-element.51) | copy-start | bytes 3145732
  317.7 21.1 %collective-permute-start = (bf16[2,64,2048]{2,1,0:T(8,128)(2,1)}, bf16[2,64,2048]{2,1,0:T(8,128)(2,1)}, u32[]{:S(2)}, u32[]{:S(2)}) collective-permute-start(bf16[2,64,2048]{2,1,0:T(8,128)(2,1)} %fusion.45), channel_id=1, source_target_pairs={{0,1},{1,0},{2,3},{3,2},{4,5},{5,4},{6,7},{7,6},{8,9},{9,8},{10,11... | collective-permute-start | bytes 1572872 | tf_op jit(solution)/shard_map/ppermute | solution.py:1284
  328.5 103.3 %copy-start.12 = (bf16[2,64,2048]{2,1,0:T(8,128)(2,1)}, bf16[2,64,2048]{2,1,0:T(8,128)(2,1)S(1)}, u32[]{:S(2)}) copy-start(bf16[2,64,2048]{2,1,0:T(8,128)(2,1)S(1)} %get-tuple-element.112) | copy-start | bytes 1572868
  438.4 1.2 copy-start.11
  438.4 1.3 copy-start.13
  439.7 1.4 copy-start
  536.3 3.0 copy-start.10

commit v8 on v7

--- a/solution.py
+++ b/solution.py
@@ -114,10 +114,19 @@
 def gather_kernel(
     query_ref, key_ref, value_ref, out_ref, extra_ref, ids_ref, gates_ref, experts_ref, cot_ref,
     gate_ref, up_ref, down_ref,
-    a_all, b_all, gate_all, up_all, down_all, near_ref, mix_ref, rows_ref,
-    a_own, b_own, rows, rows_sem, local_sem, send_sem, recv_sem, away_sem, home_sem, give_sem, take_sem,
+    a_all, b_all, gate_all, up_all, down_all, near_out, mix_out, rows_ref,
+    a_own, b_own, ids_own, gates_own, cot_own, near_ref, mix_ref, rows, rows_sem, small_sem, local_sem, send_sem, recv_sem, away_sem, home_sem, give_sem, take_sem,
 ):
     y, core, z, x = place()
+    smalls = [
+        pltpu.make_async_copy(src, dst, small_sem.at[n])
+        for n, (src, dst) in enumerate(
+            ((ids_ref, ids_own), (gates_ref, gates_own), (cot_ref, cot_own),
+             (near_ref, near_out), (mix_ref, mix_out))
+        )
+    ]
+    for copy in smalls[:3]:
+        copy.start()
     for own, refs in ((a_own, (query_ref, key_ref, value_ref)), (b_own, (out_ref, extra_ref))):
         at = 0
         for ref in refs:
@@ -186,8 +195,12 @@
         copy.start()
         started.append(copy)
     size = rows.shape[0] // (RING * RING * RING)
-    ids, gates = ids_ref[...], gates_ref[...]
+    for copy in smalls[:3]:
+        copy.wait()
+    ids, gates = ids_own[...], gates_own[...]
     route(ids, gates, experts_ref[...], size, near_ref, mix_ref)
+    for copy in smalls[3:]:
+        copy.start()
     for n in (0, 1):
         i, j = me[n]
         locals_[n].wait()
@@ -206,8 +219,8 @@
     part, tokens = 256, cot_ref.shape[0]
     for at in range(0, rows.shape[0], part):
         lanes = slice(at, at + part)
-        total = dot(mix_ref[0:tokens, lanes], cot_ref[...], ((0,), (0,)))
-        total = total + dot(mix_ref[tokens:, lanes], cot_ref[...], ((0,), (0,)))
+        total = dot(mix_ref[0:tokens, lanes], cot_own[...], ((0,), (0,)))
+        total = total + dot(mix_ref[tokens:, lanes], cot_own[...], ((0,), (0,)))
         rows[lanes, :] = total.astype(BF16)
     keep_rows = pltpu.make_async_copy(rows, rows_ref, rows_sem)
     keep_rows.start()
@@ -248,6 +261,8 @@
             arrived(n, chunk(n, it, far).at[1], base + 3)
             across(n, it, far)
     keep_rows.wait()
+    for copy in smalls[3:]:
+        copy.wait()
     for copy in homes:
         copy.wait()
     for copy in started:
@@ -268,14 +283,20 @@
     routing = [jax.ShapeDtypeStruct((n * tokens, slots), BF16) for n in (1, 2)]
     a_all, b_all, *rest = pl.pallas_call(
         gather_kernel,
-        in_specs=[vmem] * 9 + [any_space] * 3,
-        out_specs=[any_space] * 5 + [vmem] * 2 + [any_space],
+        in_specs=[vmem] * 5 + [any_space] * 2 + [vmem] + [any_space] * 4,
+        out_specs=[any_space] * 8,
         out_shape=[jax.ShapeDtypeStruct(shape + (c,), query.dtype) for c in cols]
         + [jax.ShapeDtypeStruct(v.shape, v.dtype) for v in (gate, up, down)]
         + routing + [jax.ShapeDtypeStruct((slots, width), BF16)],
         scratch_shapes=[pltpu.VMEM((rows, c), query.dtype) for c in cols] + [
+            pltpu.VMEM(ids.shape, ids.dtype),
+            pltpu.VMEM(gates.shape, gates.dtype),
+            pltpu.VMEM(cot.shape, cot.dtype),
+            pltpu.VMEM((tokens, slots), BF16),
+            pltpu.VMEM((2 * tokens, slots), BF16),
             pltpu.VMEM((slots, width), BF16),
             pltpu.SemaphoreType.DMA,
+            pltpu.SemaphoreType.DMA((5,)),
             pltpu.SemaphoreType.DMA((2,)),
             pltpu.SemaphoreType.DMA((2, 21)),
             pltpu.SemaphoreType.DMA((2, 21)),
@@ -547,7 +568,7 @@
 CHIPS = RING * RING * RING
 GROUP = 16
 MIX = 11
-AHEAD = 2
+EARLY = 32
 TILE = 256
 
 
@@ -566,17 +587,41 @@
     return {"fsdp": y * 2 + core, "ctx": z * 2 + lax.rem(x, 2), "tp": lax.div(x, 2)}
 
 
+def signal_chips(barrier):
+    f, c, t = lax.axis_index("fsdp"), lax.axis_index("ctx"), lax.axis_index("tp")
+    y, z, x = lax.div(f, 2), lax.div(c, 2), t * 2 + lax.rem(c, 2)
+    core = lax.rem(f, 2)
+    line = [lax.rem(x + d, RING) for d in range(RING)]
+    line = [(lax.rem(v, 2), lax.div(v, 2)) for v in line]
+
+    def plane(i, carry):
+        far_y = lax.rem(y + lax.div(i, RING), RING) * 2 + core
+        far_z = lax.rem(z + lax.rem(i, RING), RING) * 2
+        for d, (low, high) in enumerate(line):
+
+            @pl.when(jnp.logical_or(i > 0, d > 0))
+            def _(low=low, high=high):
+                pl.semaphore_signal(
+                    barrier, inc=1, device_id={"fsdp": far_y, "ctx": far_z + low, "tp": high},
+                    device_id_type=MESH,
+                )
+
+        return carry
+
+    lax.fori_loop(0, RING * RING, plane, 0)
+
+
 def other_core():
     f = lax.axis_index("fsdp")
     return {"fsdp": f + 1 - 2 * (f % 2)}
 
 
 def moe_kernel(
-    send_ref, deo_ref, gate_ref, up_ref, down_ref, gate_far, up_far, down_far,
+    send_ref, deo_ref, late_ref, gate_ref, up_ref, down_ref, gate_far, up_far, down_far,
     back_ref, eo_ref, wide_ref, tall_ref,
     rows, deos, gu, down, z, dgu, wide, tall, give, take,
     go_sem, come_sem, load_sem, weight_sem, share_send, share_recv, part_send, part_recv,
-    back_send, back_recv, eo_sem,
+    back_send, back_recv, eo_sem, late_sem,
 ):
     size, hidden = send_ref.shape[1], down_ref.shape[0]
     count = GROUP * size
@@ -591,12 +636,7 @@
         lax.fori_loop(low, high, step, 0)
 
     barrier = pltpu.get_barrier_semaphore()
-    each(
-        lambda s: pl.semaphore_signal(
-            barrier, inc=1, device_id=device_at(s, 1), device_id_type=MESH
-        ),
-        1, CHIPS,
-    )
+    signal_chips(barrier)
     pl.semaphore_signal(barrier, inc=1, device_id=other_core(), device_id_type=MESH)
     pl.semaphore_wait(barrier, CHIPS)
 
@@ -617,6 +657,12 @@
     def load(s):
         return pltpu.make_async_copy(
             deo_ref.at[s], deos.at[0, slot_rows(s)], load_sem.at[s]
+        )
+
+    def go_late(s):
+        return remote(
+            late_ref.at[s], deos.at[0, slot_rows(s)], late_sem.at[s], load_sem.at[s],
+            device_at(s, 1),
         )
 
     def sent_rows(n, s):
@@ -669,8 +715,8 @@
                     act(copy)
 
     stay(0).start()
-    each(lambda s: go(s).start(), 1, AHEAD * GROUP)
-    each(lambda s: load(s).start(), 0, CHIPS)
+    each(lambda s: go(s).start(), 1, EARLY)
+    each(lambda s: load(s).start(), 0, EARLY)
     on_weights(lambda copy: copy.start())
 
     def tiles(body):
@@ -709,11 +755,14 @@
             stay(0).wait()
 
         each(lambda s: go(s).wait_recv(), lax.max(first, 1), last)
-        each(lambda s: load(s).wait(), first, last)
-        each(
-            lambda s: go(s).start(), lax.min(first + AHEAD * GROUP, CHIPS),
-            lax.min(last + AHEAD * GROUP, CHIPS),
-        )
+        each(lambda s: load(s).wait(), lax.min(first, EARLY), lax.min(last, EARLY))
+        each(lambda s: go_late(s).wait_recv(), lax.max(first, EARLY), lax.max(last, EARLY))
+
+        def go_both(s):
+            go(s).start()
+            go_late(s).start()
+
+        each(go_both, lax.min(first + EARLY, CHIPS), lax.min(last + EARLY, CHIPS))
         for n in (0, 1):
             share(n, g).start()
         through(0, g)
@@ -772,10 +821,11 @@
     each(lambda s: out(s).wait(), (groups - 2) * GROUP, CHIPS)
     each(lambda s: back(s).wait_send(), (groups - 2) * GROUP, CHIPS)
     each(lambda s: go(s).wait_send(), 1, CHIPS)
+    each(lambda s: go_late(s).wait_send(), EARLY, CHIPS)
     each(lambda s: back(s).wait_recv(), 1, CHIPS)
 
 
-def moe(send, d_eo, own, far):
+def moe(send, d_eo, d_eo_late, own, far):
     chips, size, width = send.shape
     hidden = own[2].shape[0]
     total, groups = chips * size, chips // GROUP
@@ -785,7 +835,7 @@
     dma = pltpu.SemaphoreType.DMA
     return pl.pallas_call(
         moe_kernel,
-        in_specs=[any_space] * 8,
+        in_specs=[any_space] * 9,
         out_specs=[any_space] * 2 + [vmem] * 2,
         out_shape=[jax.ShapeDtypeStruct(shape, BF16) for shape in shapes],
         scratch_shapes=[
@@ -801,14 +851,14 @@
             pltpu.VMEM((2, 2, count, width), BF16),
             dma((chips,)), dma((chips,)), dma((chips,)), dma((3,)),
             dma((2, groups)), dma((2, groups)), dma((2, groups)), dma((2, groups)),
-            dma((chips,)), dma((chips,)), dma((chips,)),
+            dma((chips,)), dma((chips,)), dma((chips,)), dma((chips,)),
         ],
         compiler_params=pltpu.CompilerParams(
             collective_id=4, has_side_effects=True, vmem_limit_bytes=56 * 1024 * 1024
         ),
         cost_estimate=pl.CostEstimate(flops=0, bytes_accessed=400_000_000, transcendentals=0),
         name="experts",
-    )(send, d_eo, *own, *far)
+    )(send, d_eo, d_eo_late, *own, *far)
 
 
 BLOCK = 64
@@ -856,12 +906,7 @@
 
 def greet_chips():
     barrier = pltpu.get_barrier_semaphore()
-    each(
-        lambda s: pl.semaphore_signal(
-            barrier, inc=1, device_id=device_at(s, 1), device_id_type=MESH
-        ),
-        1, CHIPS,
-    )
+    signal_chips(barrier)
     return lambda: pl.semaphore_wait(barrier, CHIPS - 1)
 
 
@@ -896,9 +941,6 @@
         return remote(
             rows_ref.at[s], came_ref.at[s], go_sem.at[s], come_sem.at[s], device_at(s, 1)
         )
-
-    def rows_out(quarter):
-        each(lambda s: go(s).start(), max(quarter * GROUP, 1), (quarter + 1) * GROUP)
 
     stay = pltpu.make_async_copy(rows_ref.at[0], came_ref.at[0], come_sem.at[0])
     stay.start()
@@ -943,7 +985,7 @@
         )
         for copy in copies[-CTX:]:
             copy.start()
-    rows_out(0)
+    each(lambda s: go(s).start(), 1, EARLY)
     each(project, 0, q_cols // WIDE)
 
     def group(m, h, carry):
@@ -967,9 +1009,6 @@
 
     for m in range(micro):
         arrived(m)
-        if m == micro - 1:
-            for quarter in range(1, CHIPS // GROUP):
-                rows_out(quarter)
         lax.fori_loop(0, kv, functools.partial(group, m), 0)
         kv_ref[m] = held[m]
     loads[1].wait()
@@ -1004,7 +1043,7 @@
     stay.wait()
     for copy in copies:
         copy.wait_send()
-    each(lambda s: go(s).wait(), 1, CHIPS)
+    each(lambda s: go(s).wait(), 1, EARLY)
 
 
 def backward_kernel(
@@ -1106,11 +1145,11 @@
         )
         for copy in copies[-CTX:]:
             copy.start()
-        outputs(1 + m)
+        if m == micro - 1:
+            outputs(1)
     total = jnp.zeros((1, HEAD_SIZE), F32)
     for m in range(micro):
         total = lax.fori_loop(0, kv, functools.partial(queries_back, m), total)
-    outputs(3)
 
     def tiles_out(buffer, left, right, out_ref, sems):
         def copy_out(i):
@@ -1169,6 +1208,8 @@
         swap_give[m * BLOCK : (m + 1) * BLOCK, :] = part_sum[away, :].astype(BF16)
     swap = remote(swap_give, swap_take, swap_sem.at[0], swap_sem.at[1], {"tp": 1 - tp})
     swap.start()
+    outputs(2)
+    outputs(3)
     end_qkv = tiles_out(wide_tile, a_ref, dqkv_ref, grad_qkv_ref, tile_sem.at[1])
     swap.wait()
     for m in range(micro):
@@ -1203,7 +1244,7 @@
             jax.ShapeDtypeStruct((total, q_cols), BF16),
             jax.ShapeDtypeStruct((micro * BLOCK, width), F32),
             jax.ShapeDtypeStruct((select.shape[1], width), BF16),
-            jax.ShapeDtypeStruct(moe_rows.shape, BF16),
+            jax.ShapeDtypeStruct((EARLY,) + moe_rows.shape[1:], BF16),
         ],
         scratch_shapes=[
             pltpu.VMEM((width, cols), BF16),
@@ -1374,15 +1415,16 @@
     heads_in = (cosine, sine, gain_query[None], gain_key[None], bias)
     tokens = jnp.concatenate([x_first, x_second], axis=1).reshape(-1, width)
     slot_shape = (peers, micro * slots, width)
+    spread = spread.reshape(slot_shape)
     a, qkv, kv_all, o, middle, send, d_eo_rows = forward(
         tokens, gain_in[None], gain_moe[None], heads_in, select_near, w_qkv, w_out_extra,
-        spread.reshape(slot_shape), kv,
+        spread, kv,
     )
     middle = middle.reshape(own_tokens.shape)
     b_scale = lax.rsqrt(jnp.mean(middle * middle, axis=-1, keepdims=True) + EPS)
 
     back, eo, wide_here, tall_here = moe(
-        send.reshape(slot_shape), d_eo_rows, own_experts, far_experts
+        send.reshape(slot_shape), d_eo_rows, spread, own_experts, far_experts
     )
     d_b = dot(select_near, back.reshape(-1, width), ((1,), (0,))).reshape(middle.shape)
     middle_from, moe_total = normalize_back(middle, b_scale, gain_moe, d_b)

time: 550 us -> 556 us (1.011)
  Pallas kernels: 472 us -> 480 us
    pallas_call x2, Pallas kernels: 193 us -> 229 us  [the longest x1 158 us: moe(): pl.pallas_call(moe_kernel, in_specs=[any_space] * 9, out_specs=[any_space...]
    pallas_call x1, Pallas kernels: 99.4 us -> 73 us  [forward(): pl.pallas_call(functools.partial(forward_kernel, kv, heads), in_specs=[vm...]
where the time goes in v8:
time: 556 us; the launch traced here: 547 us
  Pallas kernels  480 us (86%)
  other arithmetic  22 us (4%)
  local copies, waits for them, and re-layouts  21.7 us (4%)
  waiting for transfers between devices  10.1 us (2%)
  matrix products  6.77 us (1%)
    pallas_call x1, Pallas kernels, moe(): pl.pallas_call(moe_kernel, in_specs=[any_space] * 9, out_specs=[any_space...  158 us
    pallas_call x1, Pallas kernels, scatter_grads(): pl.pallas_call(scatter_kernel, in_specs=[any_space] * 7, out_specs=[pl.Bl...  88.9 us
    pallas_call x1, Pallas kernels, backward(): pl.pallas_call(functools.partial(backward_kernel, kv, heads), in_specs=[v...  88.9 us
    pallas_call x1, Pallas kernels, forward(): pl.pallas_call(functools.partial(forward_kernel, kv, heads), in_specs=[vm...  73 us
    pallas_call x1, Pallas kernels, gather_weights(): pl.pallas_call(gather_kernel, in_specs=[vmem] * 5 + [any_space] * 2 + [vm...  70.6 us
  transfers between devices with their start and end apart: 1, of which 1 were waited for; matrix products, arithmetic and copies ran while one was open for 0% of the time, Pallas kernels for 0%

profile of v8, /device:TPU:0, one launch (start us, length us, event | category | flops | bytes accessed | tf_op | source)
XLA Modules:
  0.0 546.7 jit_solution(7358694271190791769)
XLA Ops:
  0.7 0.7 bitcast_select_fusion.1
  1.5 0.7 bitcast_select_fusion.2
  2.3 1.3 bitcast_select_fusion
  3.7 0.7 pad_bitcast_fusion.5
  4.3 0.7 pad_bitcast_fusion.7
  5.0 0.9 copy-done.5
  5.9 0.9 copy-done.6
  6.8 0.7 copy-done.7
  7.6 0.7 copy-done.8
  8.3 70.6 %gather_weights.1 = (bf16[4,2,4,2,32,2560]{5,4,3,2,1,0:T(8,128)(2,1)}, bf16[4,2,4,2,32,2176]{5,4,3,2,1,0:T(8,128)(2,1)}, bf16[2048,384]{1,0:T(8,128)(2,1)S(1)}, ...) custom-call(bf16[32,2048]{1,0:T(8,128)(2,1)S(1)} %copy-done.5, ...), custom_call_target="tpu_custom_call" | custom-call | bytes 250000000 | tf_op jit(solution)/shard_map/gather_weights/pallas_call | solution.py:284
  78.9 1.1 copy-done.1
  80.0 1.1 copy-done.2
  81.2 0.7 copy-done.3
  81.9 1.1 slice.95
  83.1 0.7 broadcast_in_dim_reshape_squeeze.15.gain_moe_ref
  83.8 0.7 broadcast_in_dim_reshape_squeeze.14.gain_in_ref
  84.5 0.6 broadcast_in_dim_reshape_squeeze.16.gq_ref
  85.2 0.6 broadcast_in_dim_reshape_squeeze.17.gk_ref
  86.2 0.7 pad_maximum_fusion.2.cos_ref
  86.9 0.7 pad_maximum_fusion.3.sin_ref
  87.7 1.1 pad_maximum_fusion
  88.8 0.9 select_select_fusion.bias_ref
  89.7 73.0 %attention_forward.1 = (bf16[256,2048]{1,0:T(8,128)(2,1)}, f32[256,2560]{1,0:T(8,128)}, bf16[2,640,512]{2,1,0:T(8,128)(2,1)}, bf16[256,2048]{1,0:T(8,128)(2,1)},...) custom-call(bf16[256,2048]{1,0:T(8,128)(2,1)} %bitcast.135, ...), custom_call_target="tpu_custom_call" | custom-call | bytes 250000000 | tf_op jit(solution)/shard_map/attention_forward/pallas_call | solution.py:1236
  162.7 1.4 multiply_reduce_fusion.2
  164.2 158.4 %experts.1 = (bf16[64,16,2048]{2,1,0:T(8,128)(2,1)}, bf16[64,16,2048]{2,1,0:T(8,128)(2,1)}, bf16[2048,768]{1,0:T(8,128)(2,1)}, bf16[384,2048]{1,0:T(8,128)(2,1)}) custom-call(bf16[64,16,2048]{2,1,0:T(8,128)(2,1)} %bitcast.134, bf16[32,16,2048]{2,1,0:T(8,128)(2,1)} %get-tuple-element.53.deo_ref, bf16[64,16,2048]{2,1,0:T(8,128)(2,1)} %bitcast.123, ...), custom_call_target="tpu_custom_call" | custom-call | bytes 400000000 | tf_op jit(solution)/shard_map/experts/pallas_call | solution.py:836
  322.6 3.3 multiply_reduce_fusion
  326.0 1.1 fusion.45
  327.1 4.9 collective-permute-start
  332.2 1.5 fusion.9
  333.7 10.1 %collective-permute-done = bf16[2,64,2048]{2,1,0:T(8,128)(2,1)} collective-permute-done((bf16[2,64,2048]{2,1,0:T(8,128)(2,1)}, bf16[2,64,2048]{2,1,0:T(8,128)(2,1)}, u32[]{:S(2)}, u32[]{:S(2)}) %collective-permute-start) | collective-permute-done | bytes 524320 | tf_op jit(solution)/shard_map/ppermute | solution.py:1325
  343.8 1.3 broadcast_select_fusion.2
  345.0 1.1 pad_maximum_fusion.1
  346.1 88.9 %attention_backward.1 = (f32[128,2048]{1,0:T(8,128)}, f32[2,128]{1,0:T(2,128)}, bf16[2048,2560]{1,0:T(8,128)(2,1)}, bf16[2048,2048]{1,0:T(8,128)(2,1)}, bf16[64,16,2048]{2,1,0:T(8,128)(2,1)}) custom-call(f32[256,2560]{1,0:T(8,128)} %get-tuple-element.49.qkv_ref, f32[128,128]{1,0:T(8,128)} %pad_maximum_fusion.2.cos_ref, ...), custom_call_target="tpu_custom_call" | custom-call | bytes 250000000 | tf_op jit(solution)/shard_map/attention_backward/pallas_call | solution.py:1277
  435.0 1.9 fusion.4
  438.2 3.4 fusion.49
  441.8 1.1 copy-done.11
  443.0 0.7 fusion.8
  443.7 0.7 copy-done
  444.4 88.9 %scatter_grads.1 = (f32[32,2560]{1,0:T(8,128)S(1)}, f32[32,2176]{1,0:T(8,128)S(1)}, bf16[2048,768]{1,0:T(8,128)(2,1)S(1)}, bf16[384,2048]{1,0:T(8,128)(2,1)S(1)}...) custom-call(bf16[4,2,4,2,32,2560]{5,4,3,2,1,0:T(8,128)(2,1)} %bitcast.124, ...), custom_call_target="tpu_custom_call" | custom-call | bytes 250000000 | tf_op jit(solution)/shard_map/scatter_grads/pallas_call | solution.py:540
  533.3 0.9 select_bitcast_fusion
  534.1 0.8 fusion.10
  535.0 0.8 select_bitcast_fusion.1
  535.8 0.8 fusion.11
  536.6 0.7 slice.86
  538.0 0.7 slice.89
  539.7 1.9 bitcast_convert_fusion
  541.6 1.2 copy-done.10
  543.2 3.1 slice_bitcast_fusion
  (65 shorter events, 4.6 us)
Async XLA Ops:
  5.0 0.9 copy-start.5
  5.9 0.9 copy-start.6
  6.8 0.7 copy-start.7
  7.6 0.7 copy-start.8
  8.3 79.4 %copy-start.15 = (bf16[2,1,56,2048]{3,2,1,0:T(8,128)(2,1)S(1)}, bf16[2,1,56,2048]{3,2,1,0:T(8,128)(2,1)}, u32[]{:S(2)}) copy-start(bf16[2,1,56,2048]{3,2,1,0:T(8,128)(2,1)} %param.19) | copy-start | bytes 1376260
  8.3 79.4 %copy-start.14 = (bf16[2,1,64,2048]{3,2,1,0:T(8,128)(2,1)S(1)}, bf16[2,1,64,2048]{3,2,1,0:T(8,128)(2,1)}, u32[]{:S(2)}) copy-start(bf16[2,1,64,2048]{3,2,1,0:T(8,128)(2,1)} %param.20) | copy-start | bytes 1572868
  78.9 1.1 copy-start.1
  80.0 1.1 copy-start.2
  81.2 0.7 copy-start.3
  164.2 158.4 %copy-start.4 = (bf16[128,1024]{1,0:T(8,128)(2,1)S(1)}, bf16[128,1024]{1,0:T(8,128)(2,1)}, u32[]{:S(2)}) copy-start(bf16[128,1024]{1,0:T(8,128)(2,1)} %copy-done.3) | copy-start | bytes 786436
  164.2 158.4 %copy-start.9 = (f32[128,2048]{1,0:T(8,128)S(1)}, f32[128,2048]{1,0:T(8,128)}, u32[]{:S(2)}) copy-start(f32[128,2048]{1,0:T(8,128)} %get-tuple-element.51) | copy-start | bytes 3145732
  327.1 16.7 %collective-permute-start = (bf16[2,64,2048]{2,1,0:T(8,128)(2,1)}, bf16[2,64,2048]{2,1,0:T(8,128)(2,1)}, u32[]{:S(2)}, u32[]{:S(2)}) collective-permute-start(bf16[2,64,2048]{2,1,0:T(8,128)(2,1)} %fusion.45), channel_id=1, source_target_pairs={{0,1},{1,0},{2,3},{3,2},{4,5},{5,4},{6,7},{7,6},{8,9},{9,8},{10,11... | collective-permute-start | bytes 1572872 | tf_op jit(solution)/shard_map/ppermute | solution.py:1325
  333.7 101.3 %copy-start.12 = (bf16[2,64,2048]{2,1,0:T(8,128)(2,1)}, bf16[2,64,2048]{2,1,0:T(8,128)(2,1)S(1)}, u32[]{:S(2)}) copy-start(bf16[2,64,2048]{2,1,0:T(8,128)(2,1)S(1)} %get-tuple-element.112) | copy-start | bytes 1572868
  441.6 1.2 copy-start.11
  441.6 1.3 copy-start.13
  443.0 1.4 copy-start
  539.7 3.0 copy-start.10

commit v9 on v6

--- a/solution.py
+++ b/solution.py
@@ -116,15 +116,21 @@
     query_ref, key_ref, value_ref, out_ref, extra_ref, ids_ref, gates_ref, experts_ref, cot_ref,
     gate_ref, up_ref, down_ref,
     a_all, b_all, gate_all, up_all, down_all, near_ref, mix_ref, rows_ref,
-    a_own, b_own, mix, rows, rows_sem, local_sem, send_sem, recv_sem, away_sem, home_sem, give_sem, take_sem,
+    a_own, b_own, mix, rows, rows_sem, fill_sem, local_sem, send_sem, recv_sem, away_sem, home_sem, give_sem, take_sem,
 ):
     y, core, z, x = place()
+    fills = []
     for own, refs in ((a_own, (query_ref, key_ref, value_ref)), (b_own, (out_ref, extra_ref))):
         at = 0
         for ref in refs:
-            own[:, at : at + ref.shape[1]] = ref[...]
+            part = own.at[:, pl.ds(at, ref.shape[1])]
+            fills.append(pltpu.make_async_copy(ref, part, fill_sem.at[len(fills)]))
             at += ref.shape[1]
+    for copy in fills:
+        copy.start()
     greet(neighbours() + [opposite()])
+    for copy in fills:
+        copy.wait()
     shards = ((gate_ref, gate_all), (up_ref, up_all), (down_ref, down_all))
     moved = [
         swap_opposite(p, q, give_sem.at[n], take_sem.at[n]) for n, (p, q) in enumerate(shards)
@@ -270,7 +276,7 @@
     routing = [jax.ShapeDtypeStruct((n * tokens, slots), BF16) for n in (1, 2)]
     a_all, b_all, *rest = pl.pallas_call(
         gather_kernel,
-        in_specs=[vmem] * 9 + [any_space] * 3,
+        in_specs=[any_space] * 5 + [vmem] * 4 + [any_space] * 3,
         out_specs=[any_space] * 5 + [vmem] * 2 + [any_space],
         out_shape=[jax.ShapeDtypeStruct(shape + (c,), query.dtype) for c in cols]
         + [jax.ShapeDtypeStruct(v.shape, v.dtype) for v in (gate, up, down)]
@@ -279,6 +285,7 @@
             pltpu.VMEM((2 * tokens, slots), BF16),
             pltpu.VMEM((slots, width), BF16),
             pltpu.SemaphoreType.DMA,
+            pltpu.SemaphoreType.DMA((5,)),
             pltpu.SemaphoreType.DMA((2,)),
             pltpu.SemaphoreType.DMA((2, 21)),
             pltpu.SemaphoreType.DMA((2, 21)),
@@ -574,6 +581,30 @@
     return (y * 2 * RING + z * 2 + lax.rem(x, 2)) * 2 + lax.div(x, 2)
 
 
+def signal_chips(barrier):
+    f, c, t = lax.axis_index("fsdp"), lax.axis_index("ctx"), lax.axis_index("tp")
+    y, z, x = lax.div(f, 2), lax.div(c, 2), t * 2 + lax.rem(c, 2)
+    core = lax.rem(f, 2)
+    line = [lax.rem(x + d, RING) for d in range(RING)]
+    line = [(lax.rem(v, 2), lax.div(v, 2)) for v in line]
+
+    def plane(i, carry):
+        far_y = lax.rem(y + lax.div(i, RING), RING) * 2 + core
+        far_z = lax.rem(z + lax.rem(i, RING), RING) * 2
+        for d, (low, high) in enumerate(line):
+
+            @pl.when(jnp.logical_or(i > 0, d > 0))
+            def _(low=low, high=high):
+                pl.semaphore_signal(
+                    barrier, inc=1, device_id={"fsdp": far_y, "ctx": far_z + low, "tp": high},
+                    device_id_type=MESH,
+                )
+
+        return carry
+
+    lax.fori_loop(0, RING * RING, plane, 0)
+
+
 def other_core():
     f = lax.axis_index("fsdp")
     return {"fsdp": f + 1 - 2 * (f % 2)}
@@ -599,12 +630,7 @@
         lax.fori_loop(low, high, step, 0)
 
     barrier = pltpu.get_barrier_semaphore()
-    each(
-        lambda s: pl.semaphore_signal(
-            barrier, inc=1, device_id=device_at(s, 1), device_id_type=MESH
-        ),
-        1, CHIPS,
-    )
+    signal_chips(barrier)
     pl.semaphore_signal(barrier, inc=1, device_id=other_core(), device_id_type=MESH)
     pl.semaphore_wait(barrier, CHIPS)
 
@@ -905,12 +931,12 @@
 
 
 def backward_kernel(
-    kv, heads, qkv_ref, cos_ref, sin_ref, gq_ref, gk_ref, bias_ref, kv_ref, dattn_ref, o_ref, a_ref,
-    w_out_ref, w_qkv_ref, eo_ref,
-    given_grad_ref, gains_ref, grad_qkv_ref, grad_out_ref, eo_back_ref,
-    w_out, w_qkv, do_ref, dqkv_ref, part_sum, wide_tile, tall_tile, grads, given, given_side,
+    kv, heads, qkv_ref, cos_ref, sin_ref, gq_ref, gk_ref, bias_ref, kv_ref, o_ref, a_ref,
+    select_ref, middle_ref, cot_ref, gain_moe_ref, w_out_ref, w_qkv_ref, eo_ref, back_ref,
+    given_grad_ref, gains_ref, d_h_ref, moe_ref, grad_qkv_ref, grad_out_ref, eo_back_ref,
+    w_out, w_qkv, dattn_ref, back_tile, d_b, do_ref, dqkv_ref, part_sum, wide_tile, tall_tile, grads, given, given_side,
     p_all, ds_all, q_all, do_all, swap_give, swap_take,
-    send_sem, recv_sem, load_sem, tile_sem, swap_sem, eo_send, eo_recv,
+    send_sem, recv_sem, load_sem, tile_sem, swap_sem, share_sem, back_sem, eo_send, eo_recv,
 ):
     c, tp = lax.axis_index("ctx"), lax.axis_index("tp")
     width = w_out.shape[0]
@@ -922,13 +948,18 @@
 
         lax.fori_loop(low, high, step, 0)
 
+    def tile(i):
+        return pl.ds(pl.multiple_of(i * WIDE, WIDE), WIDE)
+
+    def back_load(i):
+        slot = lax.rem(i, 2)
+        return pltpu.make_async_copy(
+            back_ref.at[:, tile(i)], back_tile.at[slot], back_sem.at[i]
+        )
+
+    back_load(0).start()
     barrier = pltpu.get_barrier_semaphore()
-    each(
-        lambda s: pl.semaphore_signal(
-            barrier, inc=1, device_id=device_at(s, 1), device_id_type=MESH
-        ),
-        1, CHIPS,
-    )
+    signal_chips(barrier)
     loads = [
         pltpu.make_async_copy(w_out_ref.at[:, pl.ds(0, w_out.shape[1])], w_out, load_sem.at[0]),
         pltpu.make_async_copy(w_qkv_ref, w_qkv, load_sem.at[1]),
@@ -955,9 +986,38 @@
     mine = pl.ds(pl.multiple_of(c * BLOCK, BLOCK), BLOCK)
     earlier, own = pl.ds(CTX * BLOCK, BLOCK), pl.ds((CTX + 1) * BLOCK, BLOCK)
 
-    def tile(i):
-        return pl.ds(pl.multiple_of(i * WIDE, WIDE), WIDE)
-
+    def combine(i):
+        @pl.when(i + 1 < width // WIDE)
+        def _():
+            back_load(i + 1).start()
+
+        back_load(i).wait()
+        d_b[:, tile(i)] = dot(select_ref[...], back_tile[lax.rem(i, 2)], ((1,), (0,)))
+
+    each(combine, 0, width // WIDE)
+    moe_total = jnp.zeros((1, width), F32)
+    shares = []
+    for m in range(micro):
+        span = slice(m * BLOCK, (m + 1) * BLOCK)
+        u, g = middle_ref[span, :], d_b[span, :]
+        scaling = lax.rsqrt(jnp.mean(u * u, axis=-1, keepdims=True) + EPS)
+        normed = u * scaling
+        moe_total = moe_total + jnp.sum(g * normed, axis=0, keepdims=True)
+        scaled = g * gain_moe_ref[...]
+        inner = jnp.mean(scaled * normed, axis=-1, keepdims=True)
+        d_h = cot_ref[span, :].astype(F32) + scaling * (scaled - normed * inner)
+        d_h_ref[span, :] = d_h
+        place = pl.ds(pl.multiple_of(m * rows + (1 - tp) * BLOCK, BLOCK), BLOCK)
+        dattn_ref[place, :] = d_h.astype(BF16)
+        part = dattn_ref.at[place]
+        shares.append(remote(part, part, share_sem.at[0, m], share_sem.at[1, m], {"tp": 1 - tp}))
+        shares[-1].start()
+    moe_ref[...] = moe_total
+    for m in range(micro):
+        place = pl.ds(pl.multiple_of(m * rows + tp * BLOCK, BLOCK), BLOCK)
+        part = dattn_ref.at[place]
+        remote(part, part, share_sem.at[0, m], share_sem.at[1, m], {"tp": 1 - tp}).wait_recv()
+    outputs(1)
     loads[0].wait()
 
     def outputs_back(i):
@@ -1022,11 +1082,11 @@
         )
         for copy in copies[-CTX:]:
             copy.start()
-        outputs(1 + m)
+        if m == micro - 1:
+            outputs(2)
     total = jnp.zeros((1, HEAD_SIZE), F32)
     for m in range(micro):
         total = lax.fori_loop(0, kv, functools.partial(queries_back, m), total)
-    outputs(3)
 
     def tiles_out(buffer, left, right, out_ref, sems):
         def copy_out(i):
@@ -1085,13 +1145,14 @@
         swap_give[m * BLOCK : (m + 1) * BLOCK, :] = part_sum[away, :].astype(BF16)
     swap = remote(swap_give, swap_take, swap_sem.at[0], swap_sem.at[1], {"tp": 1 - tp})
     swap.start()
+    outputs(3)
     end_qkv = tiles_out(wide_tile, a_ref, dqkv_ref, grad_qkv_ref, tile_sem.at[1])
     swap.wait()
     for m in range(micro):
         kept = pl.ds(pl.multiple_of(m * rows + (1 - tp) * BLOCK, BLOCK), BLOCK)
         span = slice(m * BLOCK, (m + 1) * BLOCK)
         given_grad_ref[span, :] = part_sum[kept, :] + swap_take[span, :].astype(F32)
-    for copy in copies:
+    for copy in copies + shares:
         copy.wait_send()
     end_out()
     end_qkv()
@@ -1152,7 +1213,7 @@
     )(qkv, cosine, sine, gain_query, bias, kv_all, kv_all)
 
 
-def backward(qkv, heads_in, kv_all, d_attn, o, a, w_out, w_qkv, eo, kv):
+def backward(qkv, heads_in, kv_all, o, a, moe_in, w_out, w_qkv, eo, back, kv):
     heads = qkv.shape[1] // HEAD_SIZE // kv - 2
     bias = heads_in[-1]
     rows, keys = bias.shape
@@ -1163,11 +1224,13 @@
     dma = pltpu.SemaphoreType.DMA
     return pl.pallas_call(
         functools.partial(backward_kernel, kv, heads),
-        in_specs=[vmem] * 10 + [any_space] * 3,
-        out_specs=[vmem] * 2 + [any_space] * 3,
+        in_specs=[vmem] * 13 + [any_space] * 4,
+        out_specs=[vmem] * 4 + [any_space] * 3,
         out_shape=[
             jax.ShapeDtypeStruct((micro * BLOCK, width), F32),
             jax.ShapeDtypeStruct((2, HEAD_SIZE), F32),
+            jax.ShapeDtypeStruct((micro * BLOCK, width), F32),
+            jax.ShapeDtypeStruct((1, width), F32),
             jax.ShapeDtypeStruct((width, cols), BF16),
             jax.ShapeDtypeStruct((width, q_cols), BF16),
             jax.ShapeDtypeStruct(eo.shape, BF16),
@@ -1175,6 +1238,9 @@
         scratch_shapes=[
             pltpu.VMEM((width, q_cols), BF16),
             pltpu.VMEM((width, cols), BF16),
+            pltpu.VMEM((total, width), BF16),
+            pltpu.VMEM((2, back.shape[0], WIDE), BF16),
+            pltpu.VMEM((micro * BLOCK, width), F32),
             pltpu.VMEM((total, q_cols), BF16),
             pltpu.VMEM((total, cols), BF16),
             pltpu.VMEM((total, width), F32),
@@ -1190,14 +1256,15 @@
             pltpu.VMEM((micro * BLOCK, width), BF16),
             pltpu.VMEM((micro * BLOCK, width), BF16),
             dma((CTX, micro)), dma((CTX, micro)), dma((2,)), dma((2, width // WIDE)), dma((2,)),
+            dma((2, micro)), dma((width // WIDE,)),
             dma((CHIPS,)), dma((CHIPS,)),
         ],
         compiler_params=pltpu.CompilerParams(
-            collective_id=3, has_side_effects=True, vmem_limit_bytes=56 * 1024 * 1024
+            collective_id=3, has_side_effects=True, vmem_limit_bytes=60 * 1024 * 1024
         ),
         cost_estimate=pl.CostEstimate(flops=0, bytes_accessed=250_000_000, transcendentals=0),
         name="attention_backward",
-    )(qkv, *heads_in, kv_all, d_attn, o, a, w_out, w_qkv, eo)
+    )(qkv, *heads_in, kv_all, o, a, *moe_in, w_out, w_qkv, eo, back)
 
 
 def normalize(rows, gain):
@@ -1339,15 +1406,13 @@
     back, eo, wide_here, tall_here = moe(
         send.reshape(d_eo_rows.shape), d_eo_rows, own_experts, far_experts
     )
-    d_b = dot(select_near, back.reshape(-1, width), ((1,), (0,))).reshape(middle.shape)
-    middle_from, moe_total = normalize_back(middle, b_scale, gain_moe, d_b)
-    d_h = own_cot.astype(F32) + middle_from
-    d_h_low = d_h.astype(BF16)
-    d_attn = jnp.concatenate(arranged(d_h_low, swap_tp(d_h_low)), axis=1).reshape(-1, width)
-
-    input_grad, head_totals, grad_qkv, grad_out, eo_back = backward(
-        qkv, heads_in, kv_all, d_attn, o, a, w_out_extra, w_qkv, eo, kv
+    moe_in = (
+        select_near, middle.reshape(-1, width), own_cot.reshape(-1, width), gain_moe[None]
     )
+    input_grad, head_totals, d_h, moe_total, grad_qkv, grad_out, eo_back = backward(
+        qkv, heads_in, kv_all, o, a, moe_in, w_out_extra, w_qkv, eo, back.reshape(-1, width), kv
+    )
+    d_h = d_h.reshape(middle.shape)
     moe_out = dot(mixing, eo_back.reshape(-1, width), ((1,), (0,)))
     moe_out = (moe_out[: micro * block] + moe_out[micro * block :]).reshape(middle.shape)
     y_own = (middle + moe_out).astype(BF16)

time: 546 us -> 525 us (0.962)
  waiting for transfers between devices: 39.6 us -> 25.1 us
  starting transfers between devices: 19.4 us -> 9.82 us
    ppermute x2 -> x1, waiting for transfers between devices: 39.6 us -> 25.1 us  [swap_tp(): return lax.ppermute(value, 'tp', [(0, 1), (1, 0)])]
    ppermute x2 -> x1, starting transfers between devices: 12.5 us -> 3.19 us  [swap_tp(): return lax.ppermute(value, 'tp', [(0, 1), (1, 0)])]
    unnamed x73 -> x67, local copies, waits for them, and re-layouts: 14.4 us -> 10.5 us
    dot_general x5 -> x4, matrix products: 21.8 us -> 18.4 us  [dot(): return lax.dot_general(a, b, (dims, ((), ())), preferred_element_type=F32)]
  transfers between devices with their start and end apart: 3 -> 2, of which waited for: 2 -> 1; matrix products, arithmetic and copies ran while one was open for 3% -> 4% of each run, Pallas kernels for 3% -> 3%
where the time goes in v9:
time: 525 us; the launch traced here: 518 us
  Pallas kernels  416 us (79%)
  waiting for transfers between devices  25.1 us (5%)
  other arithmetic  23.6 us (4%)
  local copies, waits for them, and re-layouts  23.3 us (4%)
  matrix products  18.4 us (4%)
  starting transfers between devices  9.82 us (2%)
    pallas_call x1, Pallas kernels, moe(): pl.pallas_call(moe_kernel, in_specs=[any_space] * 8, out_specs=[any_space...  118 us
    pallas_call x1, Pallas kernels, backward(): pl.pallas_call(functools.partial(backward_kernel, kv, heads), in_specs=[v...  101 us
    pallas_call x1, Pallas kernels, scatter_grads(): pl.pallas_call(scatter_kernel, in_specs=[any_space] * 7, out_specs=[pl.Bl...  90.6 us
    pallas_call x1, Pallas kernels, gather_weights(): pl.pallas_call(gather_kernel, in_specs=[any_space] * 5 + [vmem] * 4 + [an...  70.5 us
    ppermute x1, waiting for transfers between devices, swap_tp(): return lax.ppermute(value, 'tp', [(0, 1), (1, 0)])  25.1 us
    pallas_call x1, Pallas kernels, share_keys(): pl.pallas_call(functools.partial(share_kernel, kv), grid=(1,), in_specs=[...  21.1 us
    dot_general x4, matrix products, dot(): return lax.dot_general(a, b, (dims, ((), ())), preferred_element_type=F32)  18.4 us
    pallas_call x1, Pallas kernels, attention(): pl.pallas_call(functools.partial(attention_kernel, heads), grid=(micro, k...  15 us
  transfers between devices with their start and end apart: 2, of which 1 were waited for; matrix products, arithmetic and copies ran while one was open for 4% of the time, Pallas kernels for 3%

profile of v9, /device:TPU:0, one launch (start us, length us, event | category | flops | bytes accessed | tf_op | source)
XLA Modules:
  0.0 517.6 jit_solution(6045464133242141197)
XLA Ops:
  0.7 0.7 bitcast_select_fusion.1
  1.5 0.7 bitcast_select_fusion.2
  2.4 0.7 pad_add_fusion
  3.0 0.7 pad_bitcast_fusion.6
  3.7 0.7 pad_bitcast_fusion.4
  4.4 1.3 bitcast_select_fusion
  5.8 1.1 copy-done.12
  6.8 0.9 copy-done.13
  7.7 0.7 copy-done.14
  8.4 0.7 copy-done.15
  9.2 70.5 %gather_weights.1 = (bf16[4,2,4,2,32,2560]{5,4,3,2,1,0:T(8,128)(2,1)}, bf16[4,2,4,2,32,2176]{5,4,3,2,1,0:T(8,128)(2,1)}, bf16[2048,384]{1,0:T(8,128)(2,1)S(1)}, ...) custom-call(bf16[32,2048]{1,0:T(8,128)(2,1)S(1)} %copy-done.12, ...), custom_call_target="tpu_custom_call" | custom-call | bytes 250000000 | tf_op jit(solution)/shard_map/gather_weights/pallas_call | solution.py:277
  79.7 1.1 copy-done.8
  80.8 1.1 copy-done.9
  82.0 1.4 slice.109
  86.4 5.6 %fusion.53.rows_ref.q_ref.qkv_ref = f32[256,2560]{1,0:T(8,128)S(1)} fusion(bf16[256,2048]{1,0:T(8,128)(2,1)S(1)} %bitcast.142, bf16[2048,2560]{1,0:T(8,128)(2,1)} %bitcast.118), kind=kOutput, calls=%fused_computation.147 | convolution fusion | flops 2684354560 | bytes 14155776 | tf_op jit(solution)/shard_map/dot_general | solution.py:26
  92.2 21.1 %share_keys.1.k_ref.v_ref.kv_ref = bf16[2,640,512]{2,1,0:T(8,128)(2,1)S(1)} custom-call(f32[256,2560]{1,0:T(8,128)S(1)} %fusion.53.rows_ref.q_ref.qkv_ref, f32[128,128]{1,0:T(8,128)S(1)} %get-tuple-element.130.cos_ref, f32[128,128]{1,0:T(8,128)S(1)} %get-tuple-element.131.sin_ref, f32[1,128]{1,0:T(1,128)S(1)} %broadcast_in_dim_reshape_squeeze.7.gk_ref), custom_call_target="tpu_custom_call" | custom-call | bytes 50000000 | tf_op jit(solution)/shard_map/share_keys/pallas_call | solution.py:1170
  113.3 1.1 copy-done.1
  114.4 6.6 %all-to-all-start = ((bf16[64,16,2048]{2,1,0:T(8,128)(2,1)}), bf16[64,16,2048]{2,1,0:T(8,128)(2,1)}, u32[]{:S(2)}, u32[]{:S(2)}) async-start(bf16[64,16,2048]{2,1,0:T(8,128)(2,1)} %bitcast.138), calls=%async_computation | async-start | bytes 8388608 | tf_op jit(solution)/shard_map/all_to_all | solution.py:1313
  123.7 0.9 broadcast_in_dim_reshape_squeeze.6.gq_ref
  124.6 1.0 select_select_fusion.bias_ref
  125.7 1.3 copy-done.2
  127.0 15.0 %attention_forward.1.o_ref = bf16[256,2048]{1,0:T(8,128)(2,1)S(1)} custom-call(f32[256,2560]{1,0:T(8,128)S(1)} %fusion.53.rows_ref.q_ref.qkv_ref, f32[128,128]{1,0:T(8,128)S(1)} %get-tuple-element.130.cos_ref, f32[128,128]{1,0:T(8,128)S(1)} %get-tuple-element.131.sin_ref, f32[1,128]{1,0:T(1,128)S(1)} %broadcast_in_dim_reshape_squeeze.6.gq_ref, ...), custom_call_target="tpu_custom_call" | custom-call | bytes 60000000 | tf_op jit(solution)/shard_map/attention_forward/pallas_call | solution.py:1199
  142.0 6.1 %fusion = f32[256,2048]{1,0:T(8,128)S(1)} fusion(bf16[256,2048]{1,0:T(8,128)(2,1)S(1)} %attention_forward.1.o_ref, bf16[2048,2176]{1,0:T(8,128)(2,1)} %bitcast.121), kind=kOutput, calls=%fused_computation | convolution fusion | flops 2147483648 | bytes 11534336 | tf_op jit(solution)/shard_map/dot_general | solution.py:26
  148.2 0.9 select_convert_fusion.1
  149.1 3.2 collective-permute-start
  152.4 0.7 broadcast_in_dim_reshape_squeeze.16.gain_moe_ref
  153.0 1.3 fusion.13
  154.6 1.2 fusion.3.a_ref
  155.9 25.1 %collective-permute-done = bf16[2,64,2048]{2,1,0:T(8,128)(2,1)} collective-permute-done((bf16[2,64,2048]{2,1,0:T(8,128)(2,1)}, bf16[2,64,2048]{2,1,0:T(8,128)(2,1)}, u32[]{:S(2)}, u32[]{:S(2)}) %collective-permute-start) | collective-permute-done | bytes 524320 | tf_op jit(solution)/shard_map/ppermute | solution.py:1284
  181.0 1.4 multiply_reduce_fusion.1
  182.6 3.2 convolution_convert_fusion
  185.8 118.1 %experts.1 = (bf16[64,16,2048]{2,1,0:T(8,128)(2,1)}, bf16[64,16,2048]{2,1,0:T(8,128)(2,1)}, bf16[2048,768]{1,0:T(8,128)(2,1)}, bf16[384,2048]{1,0:T(8,128)(2,1)}) custom-call(bf16[64,16,2048]{2,1,0:T(8,128)(2,1)} %bitcast.115, bf16[64,16,2048]{2,1,0:T(8,128)(2,1)} %all-to-all-done.deo_ref, bf16[2048,384]{1,0:T(8,128)(2,1)} %bitcast.129, ...), custom_call_target="tpu_custom_call" | custom-call | bytes 400000000 | tf_op jit(solution)/shard_map/experts/pallas_call | solution.py:820
  304.0 100.5 %attention_backward.1 = (f32[128,2048]{1,0:T(8,128)}, f32[2,128]{1,0:T(2,128)}, f32[128,2048]{1,0:T(8,128)}, f32[1,2048]{1,0:T(1,128)}, bf16[2048,2560]{1,0:T(8,...) custom-call(f32[256,2560]{1,0:T(8,128)} %copy-done, f32[128,128]{1,0:T(8,128)} %copy-done.10, ...), custom_call_target="tpu_custom_call" | custom-call | bytes 250000000 | tf_op jit(solution)/shard_map/attention_backward/pallas_call | solution.py:1225
  404.5 0.7 convert.34
  405.3 0.7 convert_reduce_fusion
  406.0 1.9 fusion.8
  408.7 3.4 fusion.54
  412.3 1.1 copy-done.21
  415.0 90.6 %scatter_grads.1 = (f32[32,2560]{1,0:T(8,128)S(1)}, f32[32,2176]{1,0:T(8,128)S(1)}, bf16[2048,768]{1,0:T(8,128)(2,1)S(1)}, bf16[384,2048]{1,0:T(8,128)(2,1)S(1)}...) custom-call(bf16[4,2,4,2,32,2560]{5,4,3,2,1,0:T(8,128)(2,1)} %bitcast.117, ...), custom_call_target="tpu_custom_call" | custom-call | bytes 250000000 | tf_op jit(solution)/shard_map/scatter_grads/pallas_call | solution.py:529
  506.6 0.7 slice.103
  507.4 0.6 fusion.50
  508.0 0.7 slice.100
  508.7 0.8 fusion.15
  509.5 0.8 select_bitcast_fusion.1
  510.4 0.8 fusion.14
  511.2 0.8 select_bitcast_fusion
  512.5 1.9 bitcast_convert_fusion
  514.3 3.1 slice_bitcast_fusion
  (107 shorter events, 10.5 us)
Async XLA Ops:
  5.7 74.0 %copy-start.4 = (bf16[2,64,2048]{2,1,0:T(8,128)(2,1)}, bf16[2,64,2048]{2,1,0:T(8,128)(2,1)S(1)}, u32[]{:S(2)}) copy-start(bf16[2,64,2048]{2,1,0:T(8,128)(2,1)S(1)} %bitcast_select_fusion) | copy-start | bytes 1572868
  5.7 1.1 copy-start.12
  6.8 0.9 copy-start.13
  7.7 0.7 copy-start.14
  8.4 0.7 copy-start.15
  9.2 75.5 %copy-start.29 = (bf16[2,1,56,2048]{3,2,1,0:T(8,128)(2,1)S(1)}, bf16[2,1,56,2048]{3,2,1,0:T(8,128)(2,1)}, u32[]{:S(2)}) copy-start(bf16[2,1,56,2048]{3,2,1,0:T(8,128)(2,1)} %param.20) | copy-start | bytes 1376260
  79.7 1.1 copy-start.8
  80.8 1.1 copy-start.9
  82.0 4.4 copy-start.18
  82.0 100.6 %copy-start.7 = (bf16[128,1024]{1,0:T(8,128)(2,1)}, bf16[128,1024]{1,0:T(8,128)(2,1)S(1)}, u32[]{:S(2)}) copy-start(bf16[128,1024]{1,0:T(8,128)(2,1)S(1)} %get-tuple-element.46.select_ref) | copy-start | bytes 786436
  82.0 2.7 copy-start.24
  84.7 1.7 copy-start.25
  85.8 6.4 %copy-start.16 = (f32[1,128]{1,0:T(1,128)}, f32[1,128]{1,0:T(1,128)S(1)}, u32[]{:S(2)}) copy-start(f32[1,128]{1,0:T(1,128)S(1)} %broadcast_in_dim_reshape_squeeze.7.gk_ref) | copy-start | bytes 1540
  92.1 33.6 %copy-start = (f32[256,2560]{1,0:T(8,128)}, f32[256,2560]{1,0:T(8,128)S(1)}, u32[]{:S(2)}) copy-start(f32[256,2560]{1,0:T(8,128)S(1)} %fusion.53.rows_ref.q_ref.qkv_ref) | copy-start | bytes 7864324
  92.2 33.5 %copy-start.10 = (f32[128,128]{1,0:T(8,128)}, f32[128,128]{1,0:T(8,128)S(1)}, u32[]{:S(2)}) copy-start(f32[128,128]{1,0:T(8,128)S(1)} %get-tuple-element.130.cos_ref) | copy-start | bytes 196612
  92.2 33.5 %copy-start.11 = (f32[128,128]{1,0:T(8,128)}, f32[128,128]{1,0:T(8,128)S(1)}, u32[]{:S(2)}) copy-start(f32[128,128]{1,0:T(8,128)S(1)} %get-tuple-element.131.sin_ref) | copy-start | bytes 196612
  113.3 1.1 copy-start.1
  114.4 71.5 %all-to-all-start = ((bf16[64,16,2048]{2,1,0:T(8,128)(2,1)}), bf16[64,16,2048]{2,1,0:T(8,128)(2,1)}, u32[]{:S(2)}, u32[]{:S(2)}) async-start(bf16[64,16,2048]{2,1,0:T(8,128)(2,1)} %bitcast.138), calls=%async_computation | async-start | bytes 8388608 | tf_op jit(solution)/shard_map/all_to_all | solution.py:1313
  124.6 17.4 %copy-start.17 = (f32[1,128]{1,0:T(1,128)}, f32[1,128]{1,0:T(1,128)S(1)}, u32[]{:S(2)}) copy-start(f32[1,128]{1,0:T(1,128)S(1)} %broadcast_in_dim_reshape_squeeze.6.gq_ref) | copy-start | bytes 1540
  125.7 1.3 copy-start.2
  127.0 15.0 %copy-start.6 = (f32[128,640]{1,0:T(8,128)}, f32[128,640]{1,0:T(8,128)S(1)}, u32[]{:S(2)}) copy-start(f32[128,640]{1,0:T(8,128)S(1)} %select_select_fusion.bias_ref) | copy-start | bytes 983044
  142.0 6.2 %copy-start.5 = (bf16[256,2048]{1,0:T(8,128)(2,1)}, bf16[256,2048]{1,0:T(8,128)(2,1)S(1)}, u32[]{:S(2)}) copy-start(bf16[256,2048]{1,0:T(8,128)(2,1)S(1)} %attention_forward.1.o_ref) | copy-start | bytes 3145732
  142.0 10.3 %copy-start.31 = (f32[64,1,32]{2,0,1:T(8,128)S(1)}, f32[64,1,32]{2,0,1:T(8,128)}, u32[]{:S(2)}) copy-start(f32[64,1,32]{2,0,1:T(8,128)} %get-tuple-element.115) | copy-start | bytes 24580
  148.2 4.9 copy-start.27
  148.2 6.2 %copy-start.26 = (bf16[2,64,2048]{2,1,0:T(8,128)(2,1)S(1)}, bf16[2,64,2048]{2,1,0:T(8,128)(2,1)}, u32[]{:S(2)}) copy-start(bf16[2,64,2048]{2,1,0:T(8,128)(2,1)} %copy-done.25) | copy-start | bytes 1572868
  149.1 31.9 %collective-permute-start = (bf16[2,64,2048]{2,1,0:T(8,128)(2,1)}, bf16[2,64,2048]{2,1,0:T(8,128)(2,1)}, u32[]{:S(2)}, u32[]{:S(2)}) collective-permute-start(bf16[2,64,2048]{2,1,0:T(8,128)(2,1)} %select_convert_fusion.1), channel_id=1, source_target_pairs={{0,1},{1,0},{2,3},{3,2},{4,5},{5,4},{6,7},{7,6},{8,9},{9,8},{10,11... | collective-permute-start | bytes 1572872 | tf_op jit(solution)/shard_map/ppermute | solution.py:1284
  153.0 1.6 copy-start.32
  154.6 26.4 %copy-start.28 = (f32[256,2048]{1,0:T(8,128)S(1)}, f32[256,2048]{1,0:T(8,128)}, u32[]{:S(2)}) copy-start(f32[256,2048]{1,0:T(8,128)} %copy-done.27) | copy-start | bytes 6291460
  182.4 3.4 copy-start.20
  404.5 4.1 copy-start.19
  412.1 1.2 copy-start.21
  412.2 1.4 copy-start.23
  412.3 1.7 copy-start.30
  413.4 1.5 copy-start.3
  509.5 2.5 copy-start.22

commit v10 on v9

--- a/solution.py
+++ b/solution.py
@@ -328,8 +328,8 @@
 
 
 def scatter_kernel(
-    a_ref, b_ref, extra_ref, wide_ref, tall_ref, y_ref, x_ref,
-    a_out, b_out, wide_out, tall_out, y_out, x_out, a_mine, b_mine, a_theirs, b_theirs, a_one, b_one, a_two, b_two,
+    a_ref, b_ref, extra_ref, wide_ref, tall_ref, y_ref,
+    a_out, b_out, wide_out, tall_out, y_out, a_mine, b_mine, a_theirs, b_theirs, a_one, b_one, a_two, b_two,
     a_first, b_first, a_last, b_last, a_x, b_x, load_sem, send_sem, recv_sem,
     gains_here, gains_there,
     extra_load_sem, extra_send_sem, extra_recv_sem, give_sem, take_sem, gains_sem, token_sem,
@@ -346,7 +346,7 @@
             src_ref=src, dst_ref=dst, send_sem=token_sem.at[n, 0], recv_sem=token_sem.at[n, 1],
             device_id=other_tp(), device_id_type=MESH,
         )
-        for n, (src, dst) in enumerate(((y_ref, y_out), (x_ref, x_out)))
+        for n, (src, dst) in enumerate(((y_ref, y_out),))
     ]
     for copy in tokens:
         copy.start()
@@ -517,7 +517,7 @@
             copy.wait()
 
 
-def scatter_grads(a, b, extra, wide, tall, y, x):
+def scatter_grads(a, b, extra, wide, tall, y):
     peers = RING * RING * 4
     rows = a.shape[0] // peers
     shape = (RING, 2, RING, 2, rows)
@@ -528,10 +528,10 @@
     any_space = pl.BlockSpec(memory_space=pl.ANY)
     return pl.pallas_call(
         scatter_kernel,
-        in_specs=[any_space] * 7,
-        out_specs=[pl.BlockSpec(memory_space=pltpu.VMEM)] * 2 + [any_space] * 4,
+        in_specs=[any_space] * 6,
+        out_specs=[pl.BlockSpec(memory_space=pltpu.VMEM)] * 2 + [any_space] * 3,
         out_shape=[jax.ShapeDtypeStruct((rows, c), F32) for c in cols]
-        + [jax.ShapeDtypeStruct(v.shape, v.dtype) for v in (wide, tall, y, x)],
+        + [jax.ShapeDtypeStruct(v.shape, v.dtype) for v in (wide, tall, y)],
         scratch_shapes=buffers + [
             pltpu.SemaphoreType.DMA((2, 16)),
             pltpu.SemaphoreType.DMA((2, 37)),
@@ -551,7 +551,7 @@
         ),
         cost_estimate=pl.CostEstimate(flops=0, bytes_accessed=250_000_000, transcendentals=0),
         name="scatter_grads",
-    )(*(v.reshape(shape + (v.shape[1],)) for v in (a, b, extra)), wide, tall, y, x)
+    )(*(v.reshape(shape + (v.shape[1],)) for v in (a, b, extra)), wide, tall, y)
 
 
 CHIPS = RING * RING * RING
@@ -932,11 +932,11 @@
 
 def backward_kernel(
     kv, heads, qkv_ref, cos_ref, sin_ref, gq_ref, gk_ref, bias_ref, kv_ref, o_ref, a_ref,
-    select_ref, middle_ref, cot_ref, gain_moe_ref, w_out_ref, w_qkv_ref, eo_ref, back_ref,
-    given_grad_ref, gains_ref, d_h_ref, moe_ref, grad_qkv_ref, grad_out_ref, eo_back_ref,
-    w_out, w_qkv, dattn_ref, back_tile, d_b, do_ref, dqkv_ref, part_sum, wide_tile, tall_tile, grads, given, given_side,
+    select_ref, middle_ref, cot_ref, gain_moe_ref, tokens_ref, gain_in_ref, w_out_ref, w_qkv_ref, eo_ref, back_ref,
+    x_ref, gains_ref, norm_ref, moe_ref, x_other_ref, grad_qkv_ref, grad_out_ref, eo_back_ref,
+    w_out, w_qkv, dattn_ref, back_tile, d_b, d_h_ref, do_ref, dqkv_ref, part_sum, wide_tile, tall_tile, grads, given, given_side,
     p_all, ds_all, q_all, do_all, swap_give, swap_take,
-    send_sem, recv_sem, load_sem, tile_sem, swap_sem, share_sem, back_sem, eo_send, eo_recv,
+    send_sem, recv_sem, load_sem, tile_sem, swap_sem, share_sem, back_sem, x_sem, eo_send, eo_recv,
 ):
     c, tp = lax.axis_index("ctx"), lax.axis_index("tp")
     width = w_out.shape[0]
@@ -1148,12 +1148,25 @@
     outputs(3)
     end_qkv = tiles_out(wide_tile, a_ref, dqkv_ref, grad_qkv_ref, tile_sem.at[1])
     swap.wait()
+    norm_total = jnp.zeros((1, width), F32)
     for m in range(micro):
         kept = pl.ds(pl.multiple_of(m * rows + (1 - tp) * BLOCK, BLOCK), BLOCK)
         span = slice(m * BLOCK, (m + 1) * BLOCK)
-        given_grad_ref[span, :] = part_sum[kept, :] + swap_take[span, :].astype(F32)
+        g = part_sum[kept, :] + swap_take[span, :].astype(F32)
+        u = tokens_ref[span, :].astype(F32)
+        scaling = lax.rsqrt(jnp.mean(u * u, axis=-1, keepdims=True) + EPS)
+        normed = u * scaling
+        norm_total = norm_total + jnp.sum(g * normed, axis=0, keepdims=True)
+        scaled = g * gain_in_ref[...]
+        inner = jnp.mean(scaled * normed, axis=-1, keepdims=True)
+        x_ref[span, :] = (d_h_ref[span, :] + scaling * (scaled - normed * inner)).astype(BF16)
+        swap_give[span, :] = x_ref[span, :]
+    norm_ref[...] = norm_total
+    x_swap = remote(swap_give, x_other_ref, x_sem.at[0], x_sem.at[1], {"tp": 1 - tp})
+    x_swap.start()
     for copy in copies + shares:
         copy.wait_send()
+    x_swap.wait()
     end_out()
     end_qkv()
     stay.wait()
@@ -1224,13 +1237,14 @@
     dma = pltpu.SemaphoreType.DMA
     return pl.pallas_call(
         functools.partial(backward_kernel, kv, heads),
-        in_specs=[vmem] * 13 + [any_space] * 4,
-        out_specs=[vmem] * 4 + [any_space] * 3,
+        in_specs=[vmem] * 15 + [any_space] * 4,
+        out_specs=[vmem] * 4 + [any_space] * 4,
         out_shape=[
-            jax.ShapeDtypeStruct((micro * BLOCK, width), F32),
+            jax.ShapeDtypeStruct((micro * BLOCK, width), BF16),
             jax.ShapeDtypeStruct((2, HEAD_SIZE), F32),
-            jax.ShapeDtypeStruct((micro * BLOCK, width), F32),
             jax.ShapeDtypeStruct((1, width), F32),
+            jax.ShapeDtypeStruct((1, width), F32),
+            jax.ShapeDtypeStruct((micro * BLOCK, width), BF16),
             jax.ShapeDtypeStruct((width, cols), BF16),
             jax.ShapeDtypeStruct((width, q_cols), BF16),
             jax.ShapeDtypeStruct(eo.shape, BF16),
@@ -1240,6 +1254,7 @@
             pltpu.VMEM((width, cols), BF16),
             pltpu.VMEM((total, width), BF16),
             pltpu.VMEM((2, back.shape[0], WIDE), BF16),
+            pltpu.VMEM((micro * BLOCK, width), F32),
             pltpu.VMEM((micro * BLOCK, width), F32),
             pltpu.VMEM((total, q_cols), BF16),
             pltpu.VMEM((total, cols), BF16),
@@ -1256,7 +1271,7 @@
             pltpu.VMEM((micro * BLOCK, width), BF16),
             pltpu.VMEM((micro * BLOCK, width), BF16),
             dma((CTX, micro)), dma((CTX, micro)), dma((2,)), dma((2, width // WIDE)), dma((2,)),
-            dma((2, micro)), dma((width // WIDE,)),
+            dma((2, micro)), dma((width // WIDE,)), dma((2,)),
             dma((CHIPS,)), dma((CHIPS,)),
         ],
         compiler_params=pltpu.CompilerParams(
@@ -1407,21 +1422,16 @@
         send.reshape(d_eo_rows.shape), d_eo_rows, own_experts, far_experts
     )
     moe_in = (
-        select_near, middle.reshape(-1, width), own_cot.reshape(-1, width), gain_moe[None]
+        select_near, middle.reshape(-1, width), own_cot.reshape(-1, width), gain_moe[None],
+        own_tokens.astype(BF16).reshape(-1, width), gain_in[None],
     )
-    input_grad, head_totals, d_h, moe_total, grad_qkv, grad_out, eo_back = backward(
+    x_own, head_totals, norm_total, moe_total, x_other, grad_qkv, grad_out, eo_back = backward(
         qkv, heads_in, kv_all, o, a, moe_in, w_out_extra, w_qkv, eo, back.reshape(-1, width), kv
     )
-    d_h = d_h.reshape(middle.shape)
+    x_own, x_other = x_own.reshape(middle.shape), x_other.reshape(middle.shape)
     moe_out = dot(mixing, eo_back.reshape(-1, width), ((1,), (0,)))
     moe_out = (moe_out[: micro * block] + moe_out[micro * block :]).reshape(middle.shape)
     y_own = (middle + moe_out).astype(BF16)
-    scale_in = lax.rsqrt(jnp.mean(own_tokens * own_tokens, axis=-1, keepdims=True) + EPS)
-    token_from, norm_total = normalize_back(
-        own_tokens, scale_in, gain_in, input_grad.reshape(own_tokens.shape)
-    )
-    x_own = (d_h + token_from).astype(BF16)
-
     extra_grads = jnp.stack(
         [
             lanes(v.reshape(peers, -1))
@@ -1431,8 +1441,8 @@
     )
     extra_grads = jnp.pad(extra_grads, ((0, 0), (0, shard_rows - extra_grads.shape[1]), (0, 0)))
     extra_grads = extra_grads.reshape(-1, HEAD_SIZE).astype(BF16)
-    share, share_out, wide_there, tall_there, y_other, x_other = scatter_grads(
-        grad_qkv, grad_out, extra_grads, wide_here, tall_here, y_own, x_own
+    share, share_out, wide_there, tall_there, y_other = scatter_grads(
+        grad_qkv, grad_out, extra_grads, wide_here, tall_here, y_own
     )
     out_first, out_second = arranged(y_own, y_other)
     grad_first, grad_second = arranged(x_own, x_other)

time: 525 us -> 522 us (level)
    pallas_call x1, Pallas kernels: 90.6 us -> 77.1 us  [scatter_grads(): pl.pallas_call(scatter_kernel, in_specs=[any_space] * 6, out_specs=[pl.Bl...]
    pallas_call x1, Pallas kernels: 101 us -> 114 us  [backward(): pl.pallas_call(functools.partial(backward_kernel, kv, heads), in_specs=[v...]
where the time goes in v10:
time: 522 us; the launch traced here: 517 us
  Pallas kernels  417 us (80%)
  waiting for transfers between devices  27.4 us (5%)
  local copies, waits for them, and re-layouts  24.1 us (5%)
  other arithmetic  18.5 us (4%)
  matrix products  18.4 us (4%)
  starting transfers between devices  9.81 us (2%)
    pallas_call x1, Pallas kernels, moe(): pl.pallas_call(moe_kernel, in_specs=[any_space] * 8, out_specs=[any_space...  119 us
    pallas_call x1, Pallas kernels, backward(): pl.pallas_call(functools.partial(backward_kernel, kv, heads), in_specs=[v...  114 us
    pallas_call x1, Pallas kernels, scatter_grads(): pl.pallas_call(scatter_kernel, in_specs=[any_space] * 6, out_specs=[pl.Bl...  77.1 us
    pallas_call x1, Pallas kernels, gather_weights(): pl.pallas_call(gather_kernel, in_specs=[any_space] * 5 + [vmem] * 4 + [an...  70.5 us
    ppermute x1, waiting for transfers between devices, swap_tp(): return lax.ppermute(value, 'tp', [(0, 1), (1, 0)])  27.4 us
    pallas_call x1, Pallas kernels, share_keys(): pl.pallas_call(functools.partial(share_kernel, kv), grid=(1,), in_specs=[...  21.1 us
    dot_general x4, matrix products, dot(): return lax.dot_general(a, b, (dims, ((), ())), preferred_element_type=F32)  18.4 us
    pallas_call x1, Pallas kernels, attention(): pl.pallas_call(functools.partial(attention_kernel, heads), grid=(micro, k...  15 us
  transfers between devices with their start and end apart: 2, of which 1 were waited for; matrix products, arithmetic and copies ran while one was open for 4% of the time, Pallas kernels for 3%

profile of v10, /device:TPU:0, one launch (start us, length us, event | category | flops | bytes accessed | tf_op | source)
XLA Modules:
  0.0 516.6 jit_solution(13516272072855871878)
XLA Ops:
  0.7 0.7 bitcast_select_fusion.1
  1.5 0.7 bitcast_select_fusion.2
  2.4 0.7 pad_add_fusion
  3.0 0.7 pad_bitcast_fusion.6
  3.7 0.7 pad_bitcast_fusion.4
  4.4 1.3 bitcast_select_fusion
  5.7 1.1 copy-done.12
  6.8 0.9 copy-done.13
  7.7 0.7 copy-done.14
  8.4 0.7 copy-done.15
  9.1 70.5 %gather_weights.1 = (bf16[4,2,4,2,32,2560]{5,4,3,2,1,0:T(8,128)(2,1)}, bf16[4,2,4,2,32,2176]{5,4,3,2,1,0:T(8,128)(2,1)}, bf16[2048,384]{1,0:T(8,128)(2,1)S(1)}, ...) custom-call(bf16[32,2048]{1,0:T(8,128)(2,1)S(1)} %copy-done.12, ...), custom_call_target="tpu_custom_call" | custom-call | bytes 250000000 | tf_op jit(solution)/shard_map/gather_weights/pallas_call | solution.py:277
  79.7 1.1 copy-done.8
  80.8 1.2 copy-done.9
  82.0 1.4 slice.109
  85.9 5.6 %fusion.42.rows_ref.q_ref.qkv_ref = f32[256,2560]{1,0:T(8,128)S(1)} fusion(bf16[256,2048]{1,0:T(8,128)(2,1)S(1)} %bitcast.140, bf16[2048,2560]{1,0:T(8,128)(2,1)} %bitcast.114), kind=kOutput, calls=%fused_computation.134 | convolution fusion | flops 2684354560 | bytes 14155776 | tf_op jit(solution)/shard_map/dot_general | solution.py:26
  91.7 21.1 %share_keys.1.k_ref.v_ref.kv_ref = bf16[2,640,512]{2,1,0:T(8,128)(2,1)S(1)} custom-call(f32[256,2560]{1,0:T(8,128)S(1)} %fusion.42.rows_ref.q_ref.qkv_ref, f32[128,128]{1,0:T(8,128)S(1)} %get-tuple-element.129.cos_ref, f32[128,128]{1,0:T(8,128)S(1)} %get-tuple-element.130.sin_ref, f32[1,128]{1,0:T(1,128)S(1)} %broadcast_in_dim_reshape_squeeze.17.gk_ref), custom_call_target="tpu_custom_call" | custom-call | bytes 50000000 | tf_op jit(solution)/shard_map/share_keys/pallas_call | solution.py:1183
  112.8 1.1 copy-done.1
  113.9 6.6 %all-to-all-start = ((bf16[64,16,2048]{2,1,0:T(8,128)(2,1)}), bf16[64,16,2048]{2,1,0:T(8,128)(2,1)}, u32[]{:S(2)}, u32[]{:S(2)}) async-start(bf16[64,16,2048]{2,1,0:T(8,128)(2,1)} %bitcast.134), calls=%async_computation | async-start | bytes 8388608 | tf_op jit(solution)/shard_map/all_to_all | solution.py:1328
  121.5 0.9 broadcast_in_dim_reshape_squeeze.16.gq_ref
  122.5 0.9 select_select_fusion.bias_ref
  123.4 1.3 copy-done.2
  124.7 15.0 %attention_forward.1.o_ref = bf16[256,2048]{1,0:T(8,128)(2,1)S(1)} custom-call(f32[256,2560]{1,0:T(8,128)S(1)} %fusion.42.rows_ref.q_ref.qkv_ref, f32[128,128]{1,0:T(8,128)S(1)} %get-tuple-element.129.cos_ref, f32[128,128]{1,0:T(8,128)S(1)} %get-tuple-element.130.sin_ref, f32[1,128]{1,0:T(1,128)S(1)} %broadcast_in_dim_reshape_squeeze.16.gq_ref, ...), custom_call_target="tpu_custom_call" | custom-call | bytes 60000000 | tf_op jit(solution)/shard_map/attention_forward/pallas_call | solution.py:1212
  139.8 6.1 %fusion = f32[256,2048]{1,0:T(8,128)S(1)} fusion(bf16[256,2048]{1,0:T(8,128)(2,1)S(1)} %attention_forward.1.o_ref, bf16[2048,2176]{1,0:T(8,128)(2,1)} %bitcast.118), kind=kOutput, calls=%fused_computation | convolution fusion | flops 2147483648 | bytes 11534336 | tf_op jit(solution)/shard_map/dot_general | solution.py:26
  146.0 1.0 select_convert_fusion.1
  147.0 3.2 collective-permute-start
  150.2 0.7 broadcast_in_dim_reshape_squeeze.19.gain_in_ref
  150.9 0.7 broadcast_in_dim_reshape_squeeze.18.gain_moe_ref
  151.9 1.2 fusion.3.a_ref
  153.1 27.4 %collective-permute-done = bf16[2,64,2048]{2,1,0:T(8,128)(2,1)} collective-permute-done((bf16[2,64,2048]{2,1,0:T(8,128)(2,1)}, bf16[2,64,2048]{2,1,0:T(8,128)(2,1)}, u32[]{:S(2)}, u32[]{:S(2)}) %collective-permute-start) | collective-permute-done | bytes 524320 | tf_op jit(solution)/shard_map/ppermute | solution.py:1299
  180.5 2.2 multiply_reduce_fusion.1
  182.9 3.2 convolution_convert_fusion
  186.1 119.4 %experts.1 = (bf16[64,16,2048]{2,1,0:T(8,128)(2,1)}, bf16[64,16,2048]{2,1,0:T(8,128)(2,1)}, bf16[2048,768]{1,0:T(8,128)(2,1)}, bf16[384,2048]{1,0:T(8,128)(2,1)}) custom-call(bf16[64,16,2048]{2,1,0:T(8,128)(2,1)} %bitcast.112, bf16[64,16,2048]{2,1,0:T(8,128)(2,1)} %all-to-all-done.deo_ref, bf16[2048,384]{1,0:T(8,128)(2,1)} %bitcast.125, ...), custom_call_target="tpu_custom_call" | custom-call | bytes 400000000 | tf_op jit(solution)/shard_map/experts/pallas_call | solution.py:820
  305.6 113.8 %attention_backward.1 = (bf16[128,2048]{1,0:T(8,128)(2,1)}, f32[2,128]{1,0:T(2,128)}, f32[1,2048]{1,0:T(1,128)}, f32[1,2048]{1,0:T(1,128)}, bf16[128,2048]{1,0:T...) custom-call(f32[256,2560]{1,0:T(8,128)} %copy-done, ...), custom_call_target="tpu_custom_call" | custom-call | bytes 250000000 | tf_op jit(solution)/shard_map/attention_backward/pallas_call | solution.py:1238
  419.3 0.7 convert.34
  420.0 0.7 convert_reduce_fusion.1
  420.8 0.7 convert_reduce_fusion
  422.2 3.4 fusion.43
  425.8 1.1 copy-done.21
  427.4 77.1 %scatter_grads.1 = (f32[32,2560]{1,0:T(8,128)S(1)}, f32[32,2176]{1,0:T(8,128)S(1)}, bf16[2048,768]{1,0:T(8,128)(2,1)S(1)}, bf16[384,2048]{1,0:T(8,128)(2,1)S(1)}, bf16[2,64,2048]{2,1,0:T(8,128)(2,1)S(1)}) custom-call(bf16[4,2,4,2,32,2560]{5,4,3,2,1,0:T(8,128)(2,1)} %bitcast.116, bf16[4,2,4,2,32,2048]{5,4,3,2,1,0:T(8,128)(2,1)} %bitcast.120, ...), custom_call_target="tpu_custom_call" | custom-call | bytes 250000000 | tf_op jit(solution)/shard_map/scatter_grads/pallas_call | solution.py:529
  505.6 0.7 slice.103
  506.3 0.6 fusion.39
  506.9 0.7 slice.100
  507.7 0.8 fusion.4
  508.5 0.8 select_bitcast_fusion
  509.3 0.9 broadcast_select_fusion
  510.2 0.8 slice_bitcast_fusion.2
  511.4 1.9 bitcast_convert_fusion
  513.3 3.1 slice_bitcast_fusion
  (108 shorter events, 7.3 us)
Async XLA Ops:
  5.7 74.0 %copy-start.4 = (bf16[2,64,2048]{2,1,0:T(8,128)(2,1)}, bf16[2,64,2048]{2,1,0:T(8,128)(2,1)S(1)}, u32[]{:S(2)}) copy-start(bf16[2,64,2048]{2,1,0:T(8,128)(2,1)S(1)} %bitcast_select_fusion) | copy-start | bytes 1572868
  5.7 1.1 copy-start.12
  6.8 0.9 copy-start.13
  7.7 0.7 copy-start.14
  8.4 0.7 copy-start.15
  9.1 75.5 %copy-start.28 = (bf16[2,1,56,2048]{3,2,1,0:T(8,128)(2,1)S(1)}, bf16[2,1,56,2048]{3,2,1,0:T(8,128)(2,1)}, u32[]{:S(2)}) copy-start(bf16[2,1,56,2048]{3,2,1,0:T(8,128)(2,1)} %param.20) | copy-start | bytes 1376260
  79.7 1.1 copy-start.8
  80.8 1.2 copy-start.9
  82.0 3.9 copy-start.18
  82.0 100.9 %copy-start.7 = (bf16[128,1024]{1,0:T(8,128)(2,1)}, bf16[128,1024]{1,0:T(8,128)(2,1)S(1)}, u32[]{:S(2)}) copy-start(bf16[128,1024]{1,0:T(8,128)(2,1)S(1)} %get-tuple-element.46.select_ref) | copy-start | bytes 786436
  82.0 2.7 copy-start.23
  84.0 1.9 copy-start.33
  84.7 1.2 copy-start.24
  85.2 6.5 %copy-start.16 = (f32[1,128]{1,0:T(1,128)}, f32[1,128]{1,0:T(1,128)S(1)}, u32[]{:S(2)}) copy-start(f32[1,128]{1,0:T(1,128)S(1)} %broadcast_in_dim_reshape_squeeze.17.gk_ref) | copy-start | bytes 1540
  91.6 31.8 %copy-start = (f32[256,2560]{1,0:T(8,128)}, f32[256,2560]{1,0:T(8,128)S(1)}, u32[]{:S(2)}) copy-start(f32[256,2560]{1,0:T(8,128)S(1)} %fusion.42.rows_ref.q_ref.qkv_ref) | copy-start | bytes 7864324
  91.7 31.7 %copy-start.10 = (f32[128,128]{1,0:T(8,128)}, f32[128,128]{1,0:T(8,128)S(1)}, u32[]{:S(2)}) copy-start(f32[128,128]{1,0:T(8,128)S(1)} %get-tuple-element.129.cos_ref) | copy-start | bytes 196612
  91.7 31.7 %copy-start.11 = (f32[128,128]{1,0:T(8,128)}, f32[128,128]{1,0:T(8,128)S(1)}, u32[]{:S(2)}) copy-start(f32[128,128]{1,0:T(8,128)S(1)} %get-tuple-element.130.sin_ref) | copy-start | bytes 196612
  112.8 1.1 copy-start.1
  113.9 72.3 %all-to-all-start = ((bf16[64,16,2048]{2,1,0:T(8,128)(2,1)}), bf16[64,16,2048]{2,1,0:T(8,128)(2,1)}, u32[]{:S(2)}, u32[]{:S(2)}) async-start(bf16[64,16,2048]{2,1,0:T(8,128)(2,1)} %bitcast.134), calls=%async_computation | async-start | bytes 8388608 | tf_op jit(solution)/shard_map/all_to_all | solution.py:1328
  122.4 17.3 %copy-start.17 = (f32[1,128]{1,0:T(1,128)}, f32[1,128]{1,0:T(1,128)S(1)}, u32[]{:S(2)}) copy-start(f32[1,128]{1,0:T(1,128)S(1)} %broadcast_in_dim_reshape_squeeze.16.gq_ref) | copy-start | bytes 1540
  123.4 1.3 copy-start.2
  124.7 15.0 %copy-start.6 = (f32[128,640]{1,0:T(8,128)}, f32[128,640]{1,0:T(8,128)S(1)}, u32[]{:S(2)}) copy-start(f32[128,640]{1,0:T(8,128)S(1)} %select_select_fusion.bias_ref) | copy-start | bytes 983044
  139.8 6.2 %copy-start.5 = (bf16[256,2048]{1,0:T(8,128)(2,1)}, bf16[256,2048]{1,0:T(8,128)(2,1)S(1)}, u32[]{:S(2)}) copy-start(bf16[256,2048]{1,0:T(8,128)(2,1)S(1)} %attention_forward.1.o_ref) | copy-start | bytes 3145732
  139.8 10.4 %copy-start.34 = (f32[64,1,32]{2,0,1:T(8,128)S(1)}, f32[64,1,32]{2,0,1:T(8,128)}, u32[]{:S(2)}) copy-start(f32[64,1,32]{2,0,1:T(8,128)} %copy-done.33) | copy-start | bytes 24580
  139.8 11.0 %copy-start.32 = (f32[64,1,32]{2,0,1:T(8,128)S(1)}, f32[64,1,32]{2,0,1:T(8,128)}, u32[]{:S(2)}) copy-start(f32[64,1,32]{2,0,1:T(8,128)} %get-tuple-element.114) | copy-start | bytes 24580
  139.8 11.8 %copy-start.25 = (bf16[2,64,2048]{2,1,0:T(8,128)(2,1)S(1)}, bf16[2,64,2048]{2,1,0:T(8,128)(2,1)}, u32[]{:S(2)}) copy-start(bf16[2,64,2048]{2,1,0:T(8,128)(2,1)} %copy-done.24) | copy-start | bytes 1572868
  146.0 5.9 %copy-start.26 = (f32[256,2048]{1,0:T(8,128)}, f32[256,2048]{1,0:T(8,128)S(1)}, u32[]{:S(2)}) copy-start(f32[256,2048]{1,0:T(8,128)S(1)} %fusion) | copy-start | bytes 6291460
  147.0 33.5 %collective-permute-start = (bf16[2,64,2048]{2,1,0:T(8,128)(2,1)}, bf16[2,64,2048]{2,1,0:T(8,128)(2,1)}, u32[]{:S(2)}, u32[]{:S(2)}) collective-permute-start(bf16[2,64,2048]{2,1,0:T(8,128)(2,1)} %select_convert_fusion.1), channel_id=1, source_target_pairs={{0,1},{1,0},{2,3},{3,2},{4,5},{5,4},{6,7},{7,6},{8,9},{9,8},{10,11... | collective-permute-start | bytes 1572872 | tf_op jit(solution)/shard_map/ppermute | solution.py:1299
  151.9 28.6 %copy-start.29 = (bf16[2,1,56,2048]{3,2,1,0:T(8,128)(2,1)S(1)}, bf16[2,1,56,2048]{3,2,1,0:T(8,128)(2,1)}, u32[]{:S(2)}) copy-start(bf16[2,1,56,2048]{3,2,1,0:T(8,128)(2,1)} %param.20) | copy-start | bytes 1376260
  151.9 28.6 %copy-start.27 = (f32[256,2048]{1,0:T(8,128)S(1)}, f32[256,2048]{1,0:T(8,128)}, u32[]{:S(2)}) copy-start(f32[256,2048]{1,0:T(8,128)} %copy-done.26) | copy-start | bytes 6291460
  182.7 3.4 copy-start.20
  305.6 116.6 %copy-start.19 = (bf16[256,1024]{1,0:T(8,128)(2,1)S(1)}, bf16[256,1024]{1,0:T(8,128)(2,1)}, u32[]{:S(2)}) copy-start(bf16[256,1024]{1,0:T(8,128)(2,1)} %copy-done.18) | copy-start | bytes 1572868
  425.6 1.2 copy-start.21
  425.8 1.6 copy-start.3
  504.5 4.8 copy-start.30
  504.5 4.8 copy-start.31
  508.5 2.5 copy-start.22
